TPU v7x, 32 devices: a whole 2x2x4 slice. The times are simulated.
32 devices in a mesh: ctx: 8 (over y, x, core), exp: 4 (over z).
Axes of the slice: x: 2, y: 2, z: 4, core: 2. Of those that a mesh axis runs over, the one named last changes fastest.
Arguments:
- queries: bfloat16 [4, 2048, 2048], P(None, 'ctx', 'exp'), may hold values from -12 to 12
- rotated_key_heads: bfloat16 [4, 2048, 256], P(None, 'ctx'), may hold values from -12 to 12
- value_head_rows: bfloat16 [4, 2048, 256], P(None, 'ctx'), may hold values from -6 to 6
- out_proj: bfloat16 [2048, 2048], P('exp'), may hold values from -0.59765625 to 0.59765625
- norm_gain: float32 [2048], replicated, may hold values from 0.5 to 1.5
- expert_ids: int32 [8192, 1], P(('ctx', 'exp')), may hold values from 0 to 3; in each aligned block of 256 rows (0 to 255, 256 to 511, ...) at most 128 rows name the same one
- gate_weights: float32 [8192, 1], P(('ctx', 'exp')), may hold values from 0.25 to 1
- expert_gate: bfloat16 [4, 2048, 768], P('exp'), may hold values from -0.125 to 0.125
- expert_up: bfloat16 [4, 2048, 768], P('exp'), may hold values from -0.125 to 0.125
- expert_down: bfloat16 [4, 768, 2048], P('exp'), may hold values from -0.21875 to 0.21875
- grad_out: bfloat16 [8192, 2048], P(('ctx', 'exp')), may hold values from -0.59765625 to 0.59765625
Outputs:
- layer_out: bfloat16 [8192, 2048], P(('ctx', 'exp'))
- grad_hidden: bfloat16 [8192, 2048], P(('ctx', 'exp'))
- grad_gate: float32 [4, 2048, 768], P('exp', 'ctx')
- grad_up: float32 [4, 2048, 768], P('exp', 'ctx')
- grad_down: float32 [4, 768, 2048], P('exp', None, 'ctx')
Inputs may be any that keep to these rules, and one draw needn't show every extreme that they name: `expert_ids`: in the rows of one device no expert is named more than 128 times, and the experts named in one row differ from each other.
All inputs are finite; a program needn't handle non-finite values.
Results may differ from a plain program's by a relative error of at most 0.035.
Values may be sent and summed in bfloat16 or wider, within the bound.
No kernel may reach another device: no remote copies, remote signals or barrier semaphores. Data moves between devices by JAX's collectives and lax.ppermute only.
A program may use at most 128 MiB of HBM per device.

v0:
```python
import math

import jax
import jax.numpy as jnp
from jax import lax
from jax.sharding import PartitionSpec as P

LOCAL_QUERY_HEADS = 16
LOCAL_KEY_HEADS = 2
HEAD_SIZE = 128


epsilon = 1e-06
masked_score = -1e30


def block_fold(query_heads, query_pos):
    score_scale = 1.0 / math.sqrt(query_heads.shape[4])
    last_query = jnp.max(query_pos)

    def fold_step(running, pieces, first_row):
        key_piece, value_piece = pieces
        seq_count = key_piece.shape[0]
        kv_count = query_heads.shape[2]
        sub_rows = math.gcd(key_piece.shape[1], 512)
        sub_steps = key_piece.shape[1] // sub_rows

        def visit_block(carried, sub_index):
            key_first = sub_index * sub_rows

            def compute(current):
                old_best, weight_total, weighted = current
                key_sub = lax.dynamic_slice_in_dim(
                    key_piece, sub_index * sub_rows, sub_rows, 1
                ).reshape(seq_count, sub_rows, kv_count, -1)
                value_sub = lax.dynamic_slice_in_dim(
                    value_piece, sub_index * sub_rows, sub_rows, 1
                ).reshape(seq_count, sub_rows, kv_count, -1)
                scores = (
                    jnp.einsum(
                        "sqgrd,skgd->sgrqk",
                        query_heads,
                        key_sub,
                        preferred_element_type=jnp.float32,
                    )
                    * score_scale
                )
                allowed = (key_first + jnp.arange(sub_rows))[None, :] <= query_pos[:, None]
                scores = jnp.where(allowed, scores, masked_score)
                new_best = jnp.maximum(old_best, jnp.max(scores, axis=-1))
                weights = jnp.where(allowed, jnp.exp(scores - new_best[..., None]), 0.0)
                factor = jnp.exp(old_best - new_best)
                new_total = weight_total * factor + jnp.sum(weights, axis=-1)
                blended = jnp.einsum(
                    "sgrqk,skgd->sgrqd",
                    weights.astype(jnp.bfloat16),
                    value_sub,
                    preferred_element_type=jnp.float32,
                )
                return (new_best, new_total, weighted * factor[..., None] + blended)

            def unchanged(current):
                return current

            return (lax.cond(key_first <= last_query, compute, unchanged, carried), None)

        running, _ = lax.scan(visit_block, running, jnp.arange(sub_steps))
        return running

    return fold_step


def grouped_fold(query_heads, pos_groups, running, pieces, first_row):
    folders = [block_fold(query_heads, pos_groups[0])]
    return tuple(
        (folder(state_one, pieces, first_row) for folder, state_one in zip(folders, running))
    )


def start_state(seq_count, kv_count, repeats, block_len, head_dim):
    best_start = jnp.full((seq_count, kv_count, repeats, block_len), masked_score, jnp.float32)
    total_start = jnp.zeros((seq_count, kv_count, repeats, block_len), jnp.float32)
    weighted_start = jnp.zeros((seq_count, kv_count, repeats, block_len, head_dim), jnp.float32)
    return (best_start, total_start, weighted_start)


def grouped_start(seq_count, kv_count, repeats, block_len, group_count):
    return tuple(
        (
            start_state(seq_count, kv_count, repeats, block_len // group_count, HEAD_SIZE)
            for index in range(group_count)
        )
    )


def finish_heads(running):
    best_score, weight_total, weighted = running
    scaled = weighted / weight_total[..., None]
    seq_count, kv_count, repeats, block_len, head_dim = scaled.shape
    return (
        scaled.transpose(0, 3, 1, 2, 4)
        .reshape(seq_count, block_len, kv_count * repeats * head_dim)
        .astype(jnp.bfloat16)
    )


def grouped_finish(running):
    return jnp.concatenate([finish_heads(state_one) for state_one in running], axis=1)


def own_heads(
    queries,
    rotated_key_heads,
    value_head_rows,
    owner_index,
    pos_groups,
    heads_dev,
    query_group_width,
):
    seq_count, block_len, _ = queries.shape
    kv_count = max(1, heads_dev // query_group_width)
    repeats = heads_dev // kv_count
    kv_first = owner_index * heads_dev // query_group_width
    key_mine = lax.dynamic_slice_in_dim(
        rotated_key_heads, kv_first * HEAD_SIZE, kv_count * HEAD_SIZE, 2
    )
    value_mine = lax.dynamic_slice_in_dim(
        value_head_rows, kv_first * HEAD_SIZE, kv_count * HEAD_SIZE, 2
    )
    query_heads = queries.reshape(seq_count, block_len, kv_count, repeats, HEAD_SIZE)
    running = grouped_fold(
        query_heads,
        pos_groups,
        grouped_start(seq_count, kv_count, repeats, block_len, len(pos_groups)),
        (
            lax.all_gather(key_mine, "ctx", axis=1, tiled=True),
            lax.all_gather(value_mine, "ctx", axis=1, tiled=True),
        ),
        jnp.int32(0),
    )
    return grouped_finish(running)


def on_device(
    queries,
    rotated_key_heads,
    value_head_rows,
    out_proj,
    norm_gain,
    expert_ids,
    gate_weights,
    expert_gate,
    expert_up,
    expert_down,
    grad_out,
):
    seq_count, block_len, width = queries.shape
    heads_dev = width // HEAD_SIZE
    query_group_width = LOCAL_QUERY_HEADS // LOCAL_KEY_HEADS
    exp_count = lax.axis_size("exp")
    owner_index = lax.axis_index("exp")
    ctx_index = lax.axis_index("ctx")
    pos_groups = [ctx_index * block_len + jnp.arange(block_len)]
    attended = own_heads(
        queries,
        rotated_key_heads,
        value_head_rows,
        owner_index,
        pos_groups,
        heads_dev,
        query_group_width,
    )
    flat_heads = attended.reshape(seq_count * block_len, heads_dev * HEAD_SIZE)
    hidden = lax.psum_scatter(
        jnp.dot(flat_heads, out_proj, preferred_element_type=jnp.float32).astype(jnp.bfloat16),
        "exp",
        scatter_dimension=0,
        tiled=True,
    )
    hidden_f = hidden.astype(jnp.float32)
    inv_rms = lax.rsqrt(jnp.mean(hidden_f * hidden_f, axis=1, keepdims=True) + epsilon)
    unit = hidden_f * inv_rms
    normed = (unit * norm_gain).astype(jnp.bfloat16)
    dmodel = normed.shape[1]
    tok_rows, top_count = expert_ids.shape
    local_experts = expert_gate.shape[0]
    experts = local_experts * exp_count
    capacity = min(tok_rows, 2 * tok_rows * top_count // experts)
    flat_ids = expert_ids.reshape(-1)
    chosen = (flat_ids[:, None] == jnp.arange(experts)[None, :]).astype(jnp.int32)
    earlier = jnp.cumsum(chosen, axis=0) - chosen
    target = flat_ids * capacity + jnp.sum(earlier * chosen, axis=1)
    placed = (jnp.arange(experts * capacity)[:, None] == target[None, :]).reshape(
        experts * capacity, tok_rows, top_count
    )
    selector = jnp.any(placed, axis=2).astype(jnp.bfloat16)
    weighting = jnp.sum(jnp.where(placed, gate_weights[None, :, :], 0.0), axis=2)
    send_rows = jnp.dot(selector, normed, preferred_element_type=jnp.float32).astype(jnp.bfloat16)
    send_grads = jnp.dot(
        weighting, grad_out.astype(jnp.float32), precision=lax.Precision.HIGHEST
    ).astype(jnp.bfloat16)
    recv_rows, recv_grads = (
        lax.all_to_all(
            send_rows.reshape(experts, capacity, dmodel),
            "exp",
            split_axis=0,
            concat_axis=0,
            tiled=True,
        ),
        lax.all_to_all(
            send_grads.reshape(experts, capacity, dmodel),
            "exp",
            split_axis=0,
            concat_axis=0,
            tiled=True,
        ),
    )
    arrived = recv_rows.reshape(exp_count, local_experts, capacity, dmodel)
    cotangent = recv_grads.reshape(exp_count, local_experts, capacity, dmodel)
    gate_act = jnp.einsum(
        "nesd,edf->nesf", arrived, expert_gate, preferred_element_type=jnp.float32
    )
    up_act = jnp.einsum("nesd,edf->nesf", arrived, expert_up, preferred_element_type=jnp.float32)
    sigma = jax.nn.sigmoid(gate_act)
    gated = gate_act * sigma
    hidden_units = (gated * up_act).astype(jnp.bfloat16)
    result = jnp.einsum(
        "nesf,efd->nesd", hidden_units, expert_down, preferred_element_type=jnp.float32
    ).astype(jnp.bfloat16)
    back_units = jnp.einsum(
        "nesd,efd->nesf", cotangent, expert_down, preferred_element_type=jnp.float32
    )
    back_gate = (back_units * up_act * sigma * (1.0 + gate_act * (1.0 - sigma))).astype(
        jnp.bfloat16
    )
    back_up = (back_units * gated).astype(jnp.bfloat16)
    back_in = (
        jnp.einsum("nesf,edf->nesd", back_gate, expert_gate, preferred_element_type=jnp.float32)
        + jnp.einsum("nesf,edf->nesd", back_up, expert_up, preferred_element_type=jnp.float32)
    ).astype(jnp.bfloat16)
    part_gate = jnp.einsum("nesd,nesf->edf", arrived, back_gate, preferred_element_type=jnp.float32)
    part_up = jnp.einsum("nesd,nesf->edf", arrived, back_up, preferred_element_type=jnp.float32)
    part_down = jnp.einsum(
        "nesf,nesd->efd", hidden_units, cotangent, preferred_element_type=jnp.float32
    )
    back_result, back_rows = (
        lax.all_to_all(
            result.reshape(experts, capacity, dmodel),
            "exp",
            split_axis=0,
            concat_axis=0,
            tiled=True,
        ),
        lax.all_to_all(
            back_in.reshape(experts, capacity, dmodel),
            "exp",
            split_axis=0,
            concat_axis=0,
            tiled=True,
        ),
    )
    expert_sum = jnp.dot(
        weighting.T,
        back_result.reshape(experts * capacity, dmodel).astype(jnp.float32),
        precision=lax.Precision.HIGHEST,
    )
    layer_out = (hidden_f + expert_sum).astype(jnp.bfloat16)
    back_normed = jnp.dot(
        selector.T,
        back_rows.reshape(experts * capacity, dmodel),
        preferred_element_type=jnp.float32,
    )
    scaled_back = back_normed * norm_gain
    grad_hidden = (
        grad_out.astype(jnp.float32)
        + inv_rms * (scaled_back - unit * jnp.mean(scaled_back * unit, axis=1, keepdims=True))
    ).astype(jnp.bfloat16)
    grad_gate, grad_up, grad_down = (
        lax.psum_scatter(
            part_gate.astype(jnp.bfloat16), "ctx", scatter_dimension=1, tiled=True
        ).astype(jnp.float32),
        lax.psum_scatter(
            part_up.astype(jnp.bfloat16), "ctx", scatter_dimension=1, tiled=True
        ).astype(jnp.float32),
        lax.psum_scatter(
            part_down.astype(jnp.bfloat16), "ctx", scatter_dimension=2, tiled=True
        ).astype(jnp.float32),
    )
    return (layer_out, grad_hidden, grad_gate, grad_up, grad_down)


def solution(mesh):
    in_specs = (
        P(None, "ctx", "exp"),
        P(None, "ctx", None),
        P(None, "ctx", None),
        P("exp", None),
        P(),
        P(("ctx", "exp"), None),
        P(("ctx", "exp"), None),
        P("exp", None, None),
        P("exp", None, None),
        P("exp", None, None),
        P(("ctx", "exp"), None),
    )
    out_specs = (
        P(("ctx", "exp"), None),
        P(("ctx", "exp"), None),
        P("exp", "ctx", None),
        P("exp", "ctx", None),
        P("exp", None, "ctx"),
    )
    return jax.shard_map(
        on_device, mesh=mesh, in_specs=in_specs, out_specs=out_specs, check_vma=False
    )
```

profile of v0, /device:TPU:22, one launch (start us, length us, event | category | flops | bytes accessed | tf_op | source)
XLA Modules:
  0.0 474.5 jit_solution(6786034171650906905)
XLA Ops:
  16.1 22.4 %all-gather.3.cloned.1.call-done = bf16[4,2048,128]{2,1,0:T(8,128)(2,1)} async-done(((bf16[4,256,128]{2,1,0:T(8,128)(2,1)}), bf16[4,2048,128]{2,1,0:T(8,128)(2,1)}) %all-gather.3.cloned.1.call-update) | async-done | bytes 2097168 | tf_op jit(solution)/shard_map/all_gather | solution.py:136
  38.5 30.4 %all-gather.5.cloned.1.call-done = bf16[4,2048,128]{2,1,0:T(8,128)(2,1)} async-done(((bf16[4,256,128]{2,1,0:T(8,128)(2,1)}), bf16[4,2048,128]{2,1,0:T(8,128)(2,1)}) %all-gather.5.cloned.1.call-update) | async-done | bytes 2097168 | tf_op jit(solution)/shard_map/all_gather | solution.py:137
  70.5 48.0 %while.15 = (s32[]{:T(128)}, f32[4,1,4,256]{3,2,0,1:T(4,128)S(1)}, f32[4,1,4,256]{3,2,0,1:T(4,128)S(1)}, f32[4,1,4,256,128]{4,3,2,0,1:T(8,128)}, s32[4]{0:T(128)...) while((s32[]{:T(128)}, f32[4,1,4,256]{3,2,0,1:T(4,128)S(1)}, ...), condition=%wide.region_6.7_spmd.clone, body=%wide.region_1.6_spmd.clone.sunk | while | flops 1102197504 | bytes 49029528 | solution.py:67
  72.3 10.1 %conditional.3 = ((f32[4,1,4,256]{3,2,0,1:T(4,128)S(1)}, f32[4,1,4,256]{3,2,0,1:T(4,128)S(1)}, f32[4,1,4,256,128]{4,3,2,0,1:T(8,128)})) conditional(s32[]{:T(128)} %convert_element_type.190, (f32[4,1,4,256]{3,2,0,1:T(4,128)S(1)}, f32[4,1,4,256]{3,2,0,1:T(4,128)S(1)}, f32[4,1,4,256,128]{4,3,2,0,1:T(8,128)}) %tuple.42, (s32[]{:T(128)}, s32[]{:T(128)}, ...), branch_computations={%region_2.2_spmd, %region_3.5_spmd} | conditional | flops 1102197504 | bytes 49028244 | solution.py:65
  84.4 10.1 %conditional.3 = ((f32[4,1,4,256]{3,2,0,1:T(4,128)S(1)}, f32[4,1,4,256]{3,2,0,1:T(4,128)S(1)}, f32[4,1,4,256,128]{4,3,2,0,1:T(8,128)})) conditional(s32[]{:T(128)} %convert_element_type.190, (f32[4,1,4,256]{3,2,0,1:T(4,128)S(1)}, f32[4,1,4,256]{3,2,0,1:T(4,128)S(1)}, f32[4,1,4,256,128]{4,3,2,0,1:T(8,128)}) %tuple.42, (s32[]{:T(128)}, s32[]{:T(128)}, ...), branch_computations={%region_2.2_spmd, %region_3.5_spmd} | conditional | flops 1102197504 | bytes 49028244 | solution.py:65
  96.4 10.1 %conditional.3 = ((f32[4,1,4,256]{3,2,0,1:T(4,128)S(1)}, f32[4,1,4,256]{3,2,0,1:T(4,128)S(1)}, f32[4,1,4,256,128]{4,3,2,0,1:T(8,128)})) conditional(s32[]{:T(128)} %convert_element_type.190, (f32[4,1,4,256]{3,2,0,1:T(4,128)S(1)}, f32[4,1,4,256]{3,2,0,1:T(4,128)S(1)}, f32[4,1,4,256,128]{4,3,2,0,1:T(8,128)}) %tuple.42, (s32[]{:T(128)}, s32[]{:T(128)}, ...), branch_computations={%region_2.2_spmd, %region_3.5_spmd} | conditional | flops 1102197504 | bytes 49028244 | solution.py:65
  108.4 10.1 %conditional.3 = ((f32[4,1,4,256]{3,2,0,1:T(4,128)S(1)}, f32[4,1,4,256]{3,2,0,1:T(4,128)S(1)}, f32[4,1,4,256,128]{4,3,2,0,1:T(8,128)})) conditional(s32[]{:T(128)} %convert_element_type.190, (f32[4,1,4,256]{3,2,0,1:T(4,128)S(1)}, f32[4,1,4,256]{3,2,0,1:T(4,128)S(1)}, f32[4,1,4,256,128]{4,3,2,0,1:T(8,128)}) %tuple.42, (s32[]{:T(128)}, s32[]{:T(128)}, ...), branch_computations={%region_2.2_spmd, %region_3.5_spmd} | conditional | flops 1102197504 | bytes 49028244 | solution.py:65
  132.4 5.2 %all-to-all-start.2 = ((bf16[4,128,2048]{2,1,0:T(8,128)(2,1)}), bf16[4,128,2048]{2,1,0:T(8,128)(2,1)}, u32[]{:S(2)}, u32[]{:S(2)}) async-start(bf16[4,128,2048]{2,1,0:T(8,128)(2,1)} %bitcast.215), calls=%async_computation.3 | async-start | bytes 4194304 | tf_op jit(solution)/shard_map/all_to_all | solution.py:210
  137.7 109.9 %reduce-scatter.5.cloned.1.call-done = bf16[256,2048]{1,0:T(8,128)(2,1)} async-done(((bf16[1024,2048]{1,0:T(8,128)(2,1)}), bf16[256,2048]{1,0:T(8,128)(2,1)}) %reduce-scatter.5.cloned.1.call-update) | async-done | bytes 1048592 | tf_op jit(solution)/shard_map/reduce_scatter | solution.py:174
  252.6 4.4 all-to-all-start
  257.2 5.5 %fusion.23 = f32[4,128,768]{2,1,0:T(8,128)} fusion(bf16[4,128,2048]{2,1,0:T(8,128)(2,1)} %all-to-all-done.2, bf16[1,768,2048]{2,1,0:T(8,128)(2,1)} %param.24), kind=kOutput, calls=%fused_computation.33 | convolution fusion | flops 1610612736 | bytes 6815744 | tf_op jit(solution)/shard_map/nesd,efd->nesf/dot_general | solution.py:230
  262.8 39.7 %all-to-all-done = bf16[4,128,2048]{2,1,0:T(8,128)(2,1)} async-done(((bf16[4,128,2048]{2,1,0:T(8,128)(2,1)}), bf16[4,128,2048]{2,1,0:T(8,128)(2,1)}, u32[]{:S(2)}, u32[]{:S(2)}) %all-to-all-start) | async-done | bytes 2097184 | tf_op jit(solution)/shard_map/all_to_all | solution.py:203
  306.9 5.1 %fusion.56 = (bf16[4,1,128,768]{3,2,0,1:T(8,128)(2,1)}, bf16[4,128,768]{2,1,0:T(8,128)(2,1)}, bf16[4,128,768]{2,1,0:T(8,128)(2,1)S(1)}) fusion(f32[4,128,768]{2,1,0:T(8,128)S(1)} %copy-done.11, f32[4,128,768]{2,1,0:T(8,128)S(1)} %fusion.29, bf16[4,128,2048]{2,1,0:T(8,128)(2,1)} %all-to-all-done, bf16[1,2048,768]{2,1,0:T(8,128)(2,1)S(1)} %copy-done), kind=kOutput, calls=%fused_computation.71 | convolution fusion | flops 1616510976 | bytes 10747904 | tf_op jit(solution)/shard_map/nesd,edf->nesf/dot_general | solution.py:220
  312.9 5.1 %fusion.39 = bf16[1,2048,768]{2,1,0:T(8,128)(2,1)} fusion(bf16[4,128,2048]{2,1,0:T(8,128)(2,1)} %all-to-all-done, bf16[4,128,768]{2,1,0:T(8,128)(2,1)S(1)} %get-tuple-element.161), kind=kOutput, calls=%fused_computation.52 | convolution fusion | flops 1612185600 | bytes 6029312 | tf_op jit(solution)/shard_map/nesd,nesf->edf/dot_general | solution.py:242
  318.1 5.2 %fusion.38 = bf16[1,2048,768]{2,1,0:T(8,128)(2,1)} fusion(bf16[4,128,2048]{2,1,0:T(8,128)(2,1)} %all-to-all-done, bf16[4,1,128,768]{3,2,0,1:T(8,128)(2,1)} %get-tuple-element.159), kind=kOutput, calls=%fused_computation.51 | convolution fusion | flops 1612185600 | bytes 6029312 | tf_op jit(solution)/shard_map/nesd,nesf->edf/dot_general | solution.py:241
  330.5 7.9 %all-to-all-start.3 = ((bf16[4,128,2048]{2,1,0:T(8,128)(2,1)}), bf16[4,128,2048]{2,1,0:T(8,128)(2,1)}, u32[]{:S(2)}, u32[]{:S(2)}) async-start(bf16[4,128,2048]{2,1,0:T(8,128)(2,1)} %add_convert_fusion), calls=%async_computation.4 | async-start | bytes 4194304 | tf_op jit(solution)/shard_map/all_to_all | solution.py:254
  338.4 5.4 %fusion.40 = bf16[1,768,2048]{2,1,0:T(8,128)(2,1)} fusion(bf16[4,128,768]{2,1,0:T(8,128)(2,1)} %get-tuple-element.160, bf16[4,128,2048]{2,1,0:T(8,128)(2,1)} %all-to-all-done.2), kind=kOutput, calls=%fused_computation.53 | convolution fusion | flops 1612185600 | bytes 6029312 | tf_op jit(solution)/shard_map/nesf,nesd->efd/dot_general | solution.py:243
  343.8 5.2 %fusion.35 = bf16[4,128,2048]{2,1,0:T(8,128)(2,1)} fusion(bf16[4,128,768]{2,1,0:T(8,128)(2,1)} %get-tuple-element.160, bf16[1,768,2048]{2,1,0:T(8,128)(2,1)} %param.24), kind=kOutput, calls=%fused_computation.49 | convolution fusion | flops 1611661312 | bytes 6029312 | tf_op jit(solution)/shard_map/nesf,efd->nesd/dot_general | solution.py:227
  349.1 34.7 %all-to-all-done.3 = bf16[4,128,2048]{2,1,0:T(8,128)(2,1)} async-done(((bf16[4,128,2048]{2,1,0:T(8,128)(2,1)}), bf16[4,128,2048]{2,1,0:T(8,128)(2,1)}, u32[]{:S(2)}, u32[]{:S(2)}) %all-to-all-start.3) | async-done | bytes 2097184 | tf_op jit(solution)/shard_map/all_to_all | solution.py:254
  383.8 7.8 %all-to-all-start.1 = ((bf16[4,128,2048]{2,1,0:T(8,128)(2,1)}), bf16[4,128,2048]{2,1,0:T(8,128)(2,1)}, u32[]{:S(2)}, u32[]{:S(2)}) async-start(bf16[4,128,2048]{2,1,0:T(8,128)(2,1)} %fusion.35), calls=%async_computation.2 | async-start | bytes 4194304 | tf_op jit(solution)/shard_map/all_to_all | solution.py:247
  391.6 4.5 fusion.48
  396.1 40.0 %all-to-all-done.1 = bf16[4,128,2048]{2,1,0:T(8,128)(2,1)} async-done(((bf16[4,128,2048]{2,1,0:T(8,128)(2,1)}), bf16[4,128,2048]{2,1,0:T(8,128)(2,1)}, u32[]{:S(2)}, u32[]{:S(2)}) %all-to-all-start.1) | async-done | bytes 2097184 | tf_op jit(solution)/shard_map/all_to_all | solution.py:247
  436.1 4.8 %fusion.46 = bf16[256,2048]{1,0:T(8,128)(2,1)} fusion(bf16[512,2048]{1,0:T(8,128)(2,1)} %bitcast.38, bf16[256,2048]{1,0:T(8,128)(2,1)} %reduce-scatter.5.cloned.1.call-done, f32[256]{0:T(256)S(1)} %bitcast.223, s32[256]{0:T(256)S(1)} %multiply_add_fusion), kind=kOutput, calls=%fused_computation.58 | convolution fusion | flops 3223060480 | bytes 4196352 | tf_op jit(solution)/shard_map/dot_general | solution.py:262
  446.4 19.3 %reduce-scatter.11.cloned.1.call-done = bf16[1,768,256]{2,1,0:T(8,128)(2,1)} async-done(((bf16[1,768,2048]{2,1,0:T(8,128)(2,1)}), bf16[1,768,256]{2,1,0:T(8,128)(2,1)}) %reduce-scatter.11.cloned.1.call-update) | async-done | bytes 393232 | tf_op jit(solution)/shard_map/reduce_scatter | solution.py:285
  (131 shorter events, 89.2 us)
Async XLA Ops:
  7.2 299.8 %copy-start = (bf16[1,2048,768]{2,1,0:T(8,128)(2,1)S(1)}, bf16[1,2048,768]{2,1,0:T(8,128)(2,1)}, u32[]{:S(2)}) copy-start(bf16[1,2048,768]{2,1,0:T(8,128)(2,1)} %param.22) | copy-start | bytes 9437188
  7.2 31.3 %all-gather.3.cloned.1.call-start = ((), (), s32[]{:S(2)}) async-start(), calls=%async_computation.8 | async-start | bytes 2359296 | tf_op jit(solution)/shard_map/all_gather | solution.py:136
  9.1 59.8 %all-gather.5.cloned.1.call-start = ((), (), s32[]{:S(2)}) async-start(), calls=%async_computation.9 | async-start | bytes 2359296 | tf_op jit(solution)/shard_map/all_gather | solution.py:137
  10.8 236.8 %reduce-scatter.5.cloned.1.call-start = ((), (), s32[]{:S(2)}) async-start(), calls=%async_computation.10 | async-start | bytes 5242880 | tf_op jit(solution)/shard_map/reduce_scatter | solution.py:174
  73.2 2.9 copy-start.3
  85.2 2.9 copy-start.3
  92.4 2.0 copy-start.4
  97.2 2.9 copy-start.3
  109.2 2.9 copy-start.3
  118.5 2.9 copy-start.9
  125.8 2.3 copy-start.7
  132.4 116.7 %copy-start.6 = (f32[2048]{0:T(1024)S(1)}, f32[2048]{0:T(1024)}, u32[]{:S(2)}) copy-start(f32[2048]{0:T(1024)} %param.19) | copy-start | bytes 24580
  132.4 120.1 %all-to-all-start.2 = ((bf16[4,128,2048]{2,1,0:T(8,128)(2,1)}), bf16[4,128,2048]{2,1,0:T(8,128)(2,1)}, u32[]{:S(2)}, u32[]{:S(2)}) async-start(bf16[4,128,2048]{2,1,0:T(8,128)(2,1)} %bitcast.215), calls=%async_computation.3 | async-start | bytes 4194304 | tf_op jit(solution)/shard_map/all_to_all | solution.py:210
  252.6 49.9 %all-to-all-start = ((bf16[4,128,2048]{2,1,0:T(8,128)(2,1)}), bf16[4,128,2048]{2,1,0:T(8,128)(2,1)}, u32[]{:S(2)}, u32[]{:S(2)}) async-start(bf16[4,128,2048]{2,1,0:T(8,128)(2,1)} %bitcast.216), calls=%async_computation.1 | async-start | bytes 4194304 | tf_op jit(solution)/shard_map/all_to_all | solution.py:203
  257.0 185.6 %reduce-scatter.9.cloned.1.call-start = ((), (), s32[]{:S(2)}) async-start(), calls=%async_computation.12 | async-start | bytes 3538944 | tf_op jit(solution)/shard_map/reduce_scatter | solution.py:282
  302.5 4.4 copy-start.11
  318.0 126.5 %reduce-scatter.7.cloned.1.call-start = ((), (), s32[]{:S(2)}) async-start(), calls=%async_computation.11 | async-start | bytes 3538944 | tf_op jit(solution)/shard_map/reduce_scatter | solution.py:279
  323.3 4.0 copy-start.10
  330.5 53.3 %all-to-all-start.3 = ((bf16[4,128,2048]{2,1,0:T(8,128)(2,1)}), bf16[4,128,2048]{2,1,0:T(8,128)(2,1)}, u32[]{:S(2)}, u32[]{:S(2)}) async-start(bf16[4,128,2048]{2,1,0:T(8,128)(2,1)} %add_convert_fusion), calls=%async_computation.4 | async-start | bytes 4194304 | tf_op jit(solution)/shard_map/all_to_all | solution.py:254
  338.4 127.3 %reduce-scatter.11.cloned.1.call-start = ((), (), s32[]{:S(2)}) async-start(), calls=%async_computation.13 | async-start | bytes 3538944 | tf_op jit(solution)/shard_map/reduce_scatter | solution.py:285
  383.8 52.4 %all-to-all-start.1 = ((bf16[4,128,2048]{2,1,0:T(8,128)(2,1)}), bf16[4,128,2048]{2,1,0:T(8,128)(2,1)}, u32[]{:S(2)}, u32[]{:S(2)}) async-start(bf16[4,128,2048]{2,1,0:T(8,128)(2,1)} %fusion.35), calls=%async_computation.2 | async-start | bytes 4194304 | tf_op jit(solution)/shard_map/all_to_all | solution.py:247
  436.1 4.8 %copy-start.1 = (bf16[256,2048]{1,0:T(8,128)(2,1)S(1)}, bf16[256,2048]{1,0:T(8,128)(2,1)}, u32[]{:S(2)}) copy-start(bf16[256,2048]{1,0:T(8,128)(2,1)} %reduce-scatter.5.cloned.1.call-done) | copy-start | bytes 3145732
  436.1 4.8 %copy-start.2 = (f32[256,2048]{1,0:T(8,128)S(1)}, f32[256,2048]{1,0:T(8,128)}, u32[]{:S(2)}) copy-start(f32[256,2048]{1,0:T(8,128)} %get-tuple-element.163) | copy-start | bytes 6291460
  436.1 4.8 %copy-start.5 = (bf16[256,2048]{1,0:T(8,128)(2,1)S(1)}, bf16[256,2048]{1,0:T(8,128)(2,1)}, u32[]{:S(2)}) copy-start(bf16[256,2048]{1,0:T(8,128)(2,1)} %param.25) | copy-start | bytes 3145732
  (5 other events, 7.7 us)
Sparse Core Ops, SparseCore 0:
  10.5 27.9 all-gather.2
  41.0 27.8 all-gather.4
  125.9 121.6 reduce-scatter.4
  318.2 48.1 reduce-scatter.8
  369.6 46.2 reduce-scatter.6
  419.5 46.2 reduce-scatter.10
where the time goes:
time: 478 us; the launch traced here: 474 us
  waiting for transfers between devices  297 us (62%)
  matrix products  93 us (19%)
  starting transfers between devices  25.8 us (5%)
  other arithmetic  21.9 us (5%)
  local copies, waits for them, and re-layouts  14.6 us (3%)
  between operations  14.3 us (3%)
  loops' own time  8.28 us (2%)
    reduce_scatter x1, waiting for transfers between devices, on_device(): lax.psum_scatter(jnp.dot(flat_heads, out_proj, preferred_element_type=jnp...  110 us
    all_to_all x1, waiting for transfers between devices, on_device(): lax.all_to_all(result.reshape(experts, capacity, dmodel), 'exp', split_ax...  40 us
    all_to_all x1, waiting for transfers between devices, on_device(): lax.all_to_all(send_rows.reshape(experts, capacity, dmodel), 'exp', split...  39.7 us
    all_to_all x1, waiting for transfers between devices, on_device(): lax.all_to_all(back_in.reshape(experts, capacity, dmodel), 'exp', split_a...  34.7 us
    all_gather x1, waiting for transfers between devices, own_heads(): lax.all_gather(value_mine, 'ctx', axis=1, tiled=True)  30.4 us
    all_gather x1, waiting for transfers between devices, own_heads(): lax.all_gather(key_mine, 'ctx', axis=1, tiled=True)  22.4 us
    reduce_scatter x1, waiting for transfers between devices, on_device(): lax.psum_scatter(part_down.astype(jnp.bfloat16), 'ctx', scatter_dimension...  19.3 us
    dot_general x4, matrix products, compute(): jnp.einsum('sgrqk,skgd->sgrqd', weights.astype(jnp.bfloat16), value_sub,...  16.9 us
  transfers between devices with their start and end apart: 10, of which 7 were waited for; matrix products, arithmetic and copies ran while one was open for 13% of the time, Pallas kernels for 0%

commit v1 on v0

v1 whole, which is shorter than its diff:
```python
import functools
import math

import jax
import jax.numpy as jnp
from jax import lax
from jax.experimental import pallas as pl
from jax.experimental.pallas import tpu as pltpu
from jax.sharding import PartitionSpec as P

LOCAL_QUERY_HEADS = 16
LOCAL_KEY_HEADS = 2
HEAD_SIZE = 128
PIECE = 256
PARTS = 2

epsilon = 1e-06
masked_score = -1e30
F32 = jnp.float32
BF16 = jnp.bfloat16
MIB = 1 << 20


def dot(a, b, contract=((1,), (0,))):
    return lax.dot_general(a, b, (contract, ((), ())), preferred_element_type=F32)


def iota(shape, dim):
    return lax.broadcasted_iota(jnp.int32, shape, dim)


def slots_row(ids_row, capacity):
    n = ids_row.shape[1]
    names = iota((16, n), 0).astype(F32)
    chosen = names == ids_row
    before = (iota((n, n), 0) < iota((n, n), 1)).astype(F32).astype(BF16)
    earlier = dot(jnp.where(chosen, 1.0, 0.0).astype(BF16), before)
    return jnp.sum(jnp.where(chosen, earlier + names * capacity, 0.0), axis=0, keepdims=True)


def slots_column(ids_column, capacity):
    n = ids_column.shape[0]
    names = iota((n, 128), 1).astype(F32)
    chosen = names == ids_column
    before = (iota((n, n), 1) < iota((n, n), 0)).astype(F32).astype(BF16)
    earlier = dot(before, jnp.where(chosen, 1.0, 0.0).astype(BF16))
    return jnp.sum(jnp.where(chosen, earlier + names * capacity, 0.0), axis=1, keepdims=True)


def one_hot(matches):
    return jnp.where(matches, 1.0, 0.0).astype(BF16)


def attend_kernel(experts, capacity, heads, ctx_ref, q_ref, k_ref, v_ref, ids_ref, *rest):
    out_refs, att_scr = rest[:PARTS], rest[PARTS]
    ctx = ctx_ref[0]
    block = q_ref.shape[1]
    rows = heads * block
    factor = math.log2(math.e) / math.sqrt(HEAD_SIZE)
    q = jnp.concatenate(
        [q_ref[0, :, h * HEAD_SIZE : (h + 1) * HEAD_SIZE] for h in range(heads)], axis=0
    )

    def scores(m):
        return dot(q, k_ref[m, 0], ((1,), (1,))) * factor

    q_pos = lax.rem(iota((rows, block), 0), block)
    s = jnp.where(iota((rows, block), 1) <= q_pos, scores(0), masked_score)
    best = jnp.max(s, axis=1, keepdims=True)
    p = jnp.exp2(s - best)
    total = jnp.sum(p, axis=1, keepdims=True)
    acc = dot(p.astype(BF16), v_ref[0, 0])

    def fold(j, state):
        best, total, acc = state
        m = jnp.bitwise_xor(j, ctx)
        s = scores(m)
        new_best = jnp.maximum(best, jnp.max(s, axis=1, keepdims=True))
        p = jnp.exp2(s - new_best)
        scale = jnp.exp2(best - new_best)
        total = total * scale + jnp.sum(p, axis=1, keepdims=True)
        acc = acc * scale + dot(p.astype(BF16), v_ref[m, 0])
        return new_best, total, acc

    best, total, acc = lax.fori_loop(0, ctx, fold, (best, total, acc))
    att = (acc / total).astype(BF16)
    for h in range(heads):
        att_scr[:, h * HEAD_SIZE : (h + 1) * HEAD_SIZE] = att[h * block : (h + 1) * block]

    n = ids_ref.shape[2]
    part = capacity // PARTS
    for b in range(block // n):
        target = slots_row(ids_ref[b], capacity)
        pick = one_hot(iota((experts * capacity, n), 0).astype(F32) == target)
        picked = dot(pick, att_scr[b * n : (b + 1) * n, :]).astype(BF16)
        for e in range(experts):
            for c in range(PARTS):
                first = e * capacity + c * part
                out_refs[c][e, b] = picked[first : first + part]


def attend(ctx, queries, keys, values, ids, experts, capacity):
    seqs, block, width = queries.shape
    n_ctx = keys.shape[0]
    blocks, _, n = ids.shape
    per_seq = block // n
    heads = width // HEAD_SIZE
    part = capacity // PARTS
    return pl.pallas_call(
        functools.partial(attend_kernel, experts, capacity, heads),
        grid_spec=pltpu.PrefetchScalarGridSpec(
            num_scalar_prefetch=1,
            grid=(seqs,),
            in_specs=[
                pl.BlockSpec((1, block, width), lambda s, c: (s, 0, 0)),
                pl.BlockSpec((n_ctx, 1, block, HEAD_SIZE), lambda s, c: (0, s, 0, 0)),
                pl.BlockSpec((n_ctx, 1, block, HEAD_SIZE), lambda s, c: (0, s, 0, 0)),
                pl.BlockSpec((per_seq, 1, n), lambda s, c: (s, 0, 0)),
            ],
            out_specs=[
                pl.BlockSpec((experts, per_seq, part, width), lambda s, c: (0, s, 0, 0))
                for _ in range(PARTS)
            ],
            scratch_shapes=[pltpu.VMEM((block, width), BF16)],
        ),
        out_shape=[
            jax.ShapeDtypeStruct((experts, blocks, part, width), BF16) for _ in range(PARTS)
        ],
        compiler_params=pltpu.CompilerParams(vmem_limit_bytes=48 * MIB),
        cost_estimate=pl.CostEstimate(
            flops=4 * seqs * block * block * n_ctx * width // 2,
            bytes_accessed=8 * MIB,
            transcendentals=seqs * heads * block * block * n_ctx,
        ),
        name="attend",
    )(ctx, queries, keys, values, ids)


def place_kernel(experts, capacity, ids_ref, rows_ref, out_ref):
    n = rows_ref.shape[0]
    target = slots_row(ids_ref[...], capacity)
    pick = one_hot(iota((experts * capacity, n), 0).astype(F32) == target)
    picked = dot(pick, rows_ref[...]).astype(BF16)
    for e in range(experts):
        out_ref[e] = picked[e * capacity : (e + 1) * capacity]


def place(ids_row, rows, experts, capacity):
    n, width = rows.shape
    cols = min(width, 512)
    return pl.pallas_call(
        functools.partial(place_kernel, experts, capacity),
        grid=(width // cols,),
        in_specs=[
            pl.BlockSpec((1, n), lambda i: (0, 0)),
            pl.BlockSpec((n, cols), lambda i: (0, i)),
        ],
        out_specs=pl.BlockSpec((experts, capacity, cols), lambda i: (0, 0, i)),
        out_shape=jax.ShapeDtypeStruct((experts, capacity, width), BF16),
        compiler_params=pltpu.CompilerParams(vmem_limit_bytes=32 * MIB),
        name="place",
    )(ids_row, rows)


def restore_kernel(experts, capacity, ids_ref, *refs):
    parts, out_ref = refs[:-1], refs[-1]
    n = out_ref.shape[0]
    part = capacity // len(parts)
    target = slots_column(ids_ref[...], capacity)
    expert = jnp.floor(target / capacity)
    local = target - expert * capacity
    lane = iota((n, experts * part), 1)
    total = jnp.zeros(out_ref.shape, F32)
    for c, ref in enumerate(parts):
        where_to = jnp.where(
            (local >= c * part) & (local < (c + 1) * part),
            expert * part + local - c * part,
            -1.0,
        )
        pick = one_hot(lane.astype(F32) == where_to)
        total += dot(pick, ref[...].reshape(experts * part, -1))
    out_ref[...] = total.astype(BF16)


def restore(ids_column, parts, capacity):
    experts, part, width = parts[0].shape
    n = ids_column.shape[0]
    cols = min(width, 512)
    return pl.pallas_call(
        functools.partial(restore_kernel, experts, capacity),
        grid=(width // cols,),
        in_specs=[pl.BlockSpec((n, 1), lambda i: (0, 0))]
        + [pl.BlockSpec((experts, part, cols), lambda i: (0, 0, i)) for _ in parts],
        out_specs=pl.BlockSpec((n, cols), lambda i: (0, i)),
        out_shape=jax.ShapeDtypeStruct((n, width), BF16),
        compiler_params=pltpu.CompilerParams(vmem_limit_bytes=32 * MIB),
        name="restore",
    )(ids_column, *parts)


def expert_kernel(
    pieces,
    tiles,
    capacity,
    part_index,
    place_ref,
    att_ref,
    wa_ref,
    wb_ref,
    gain_ref,
    ids_ref,
    weight_ref,
    grad_ref,
    gate_ref,
    up_ref,
    down_ref,
    layer_ref,
    grad_hidden_ref,
    normed_ref,
    back_ref,
    units_ref,
    back_gate_ref,
    back_up_ref,
    hidden_scr,
    inv_scr,
    weight_scr,
    result_scr,
    back_in_scr,
):
    step = pl.program_id(0)
    sources, blocks, part, att_cols = att_ref.shape
    rows = blocks * part
    width = hidden_scr.shape[1]
    piece = width // pieces

    @pl.when(step < pieces)
    def _():
        total = jnp.zeros((rows, piece), F32)
        half = wa_ref.shape[1]
        for z in range(sources):
            first = z * att_cols
            source = wa_ref if first < half else wb_ref
            first = first % half
            total += dot(
                att_ref[z].reshape(rows, att_cols), source[0, first : first + att_cols, :]
            )
        column = jnp.bitwise_xor(step, place_ref[0]) * piece
        hidden_scr[:, pl.ds(pl.multiple_of(column, piece), piece)] = total.astype(BF16)

    @pl.when(step == pieces)
    def _():
        n = ids_ref.shape[2]
        owner = place_ref[1]
        weights = []
        for s in range(blocks):
            target = slots_row(ids_ref[s], capacity)
            slot = iota((part, n), 0) + (owner * capacity + part_index * part)
            weights.append(
                jnp.sum(
                    jnp.where(slot.astype(F32) == target, weight_ref[s], 0.0),
                    axis=1,
                    keepdims=True,
                )
            )
        weight = jnp.concatenate(weights, axis=0)
        weight_scr[...] = weight
        hidden = hidden_scr[...].astype(F32)
        inv = lax.rsqrt(jnp.mean(hidden * hidden, axis=1, keepdims=True) + epsilon)
        inv_scr[...] = inv
        normed_ref[...] = (hidden * inv * gain_ref[...]).astype(BF16)
        grads = grad_ref[...].reshape(rows, width).astype(F32)
        back_ref[...] = (weight * grads).astype(BF16)

    @pl.when(step >= pieces)
    def _():
        normed = normed_ref[...]
        back = back_ref[...]
        gate, up, down = gate_ref[0], up_ref[0], down_ref[0]
        gate_act = dot(normed, gate)
        up_act = dot(normed, up)
        back_units = dot(back, down, ((1,), (1,)))
        sigma = 1.0 / (1.0 + jnp.exp(-gate_act))
        gated = gate_act * sigma
        units = (gated * up_act).astype(BF16)
        back_gate = (back_units * up_act * sigma * (1.0 + gate_act * (1.0 - sigma))).astype(BF16)
        back_up = (back_units * gated).astype(BF16)
        units_ref[...] = units
        back_gate_ref[...] = back_gate
        back_up_ref[...] = back_up
        result = dot(units, down)
        back_in = dot(back_gate, gate, ((1,), (1,))) + dot(back_up, up, ((1,), (1,)))

        @pl.when(step == pieces)
        def _():
            result_scr[...] = result
            back_in_scr[...] = back_in

        @pl.when(step > pieces)
        def _():
            result_scr[...] += result
            back_in_scr[...] += back_in

    @pl.when(step == pieces + tiles - 1)
    def _():
        hidden = hidden_scr[...].astype(F32)
        inv = inv_scr[...]
        result = result_scr[...].astype(BF16).astype(F32)
        layer = hidden + weight_scr[...] * result
        layer_ref[...] = layer.astype(BF16).reshape(layer_ref.shape)
        scaled = back_in_scr[...].astype(BF16).astype(F32) * gain_ref[...]
        unit = hidden * inv
        mean = jnp.mean(scaled * unit, axis=1, keepdims=True)
        grads = grad_ref[...].reshape(rows, width).astype(F32)
        grad_hidden = grads + inv * (scaled - unit * mean)
        grad_hidden_ref[...] = grad_hidden.astype(BF16).reshape(grad_hidden_ref.shape)


def expert_part(place_of, att, wa, wb, gain, ids, weights, grads, gate, up, down, capacity, index):
    sources, blocks, part, att_cols = att.shape
    pieces, half, piece = wa.shape
    width = grads.shape[2]
    ff = gate.shape[2]
    tile = 256
    tiles = ff // tile
    rows = blocks * part
    n = ids.shape[2]
    whole = lambda *shape: pl.BlockSpec(shape, lambda i, p: (0,) * len(shape))
    tile_at = lambda i: jnp.maximum(i - pieces, 0)
    out = lambda *shape: jax.ShapeDtypeStruct(shape, BF16)
    return pl.pallas_call(
        functools.partial(expert_kernel, pieces, tiles, capacity, index),
        grid_spec=pltpu.PrefetchScalarGridSpec(
            num_scalar_prefetch=1,
            grid=(pieces + tiles,),
            in_specs=[
                whole(sources, blocks, part, att_cols),
                pl.BlockSpec((1, half, piece), lambda i, p: (jnp.minimum(i, pieces - 1), 0, 0)),
                pl.BlockSpec((1, half, piece), lambda i, p: (jnp.minimum(i, pieces - 1), 0, 0)),
                whole(1, width),
                whole(blocks, 1, n),
                whole(blocks, 1, n),
                pl.BlockSpec((blocks, part, width), lambda i, p: (0, index, 0)),
                pl.BlockSpec((1, width, tile), lambda i, p: (0, 0, tile_at(i))),
                pl.BlockSpec((1, width, tile), lambda i, p: (0, 0, tile_at(i))),
                pl.BlockSpec((1, tile, width), lambda i, p: (0, tile_at(i), 0)),
            ],
            out_specs=[
                whole(blocks, part, width),
                whole(blocks, part, width),
                whole(rows, width),
                whole(rows, width),
                pl.BlockSpec((rows, tile), lambda i, p: (0, tile_at(i))),
                pl.BlockSpec((rows, tile), lambda i, p: (0, tile_at(i))),
                pl.BlockSpec((rows, tile), lambda i, p: (0, tile_at(i))),
            ],
            scratch_shapes=[
                pltpu.VMEM((rows, width), BF16),
                pltpu.VMEM((rows, 1), F32),
                pltpu.VMEM((rows, 1), F32),
                pltpu.VMEM((rows, width), F32),
                pltpu.VMEM((rows, width), F32),
            ],
        ),
        out_shape=[
            out(blocks, part, width),
            out(blocks, part, width),
            out(rows, width),
            out(rows, width),
            out(rows, ff),
            out(rows, ff),
            out(rows, ff),
        ],
        compiler_params=pltpu.CompilerParams(vmem_limit_bytes=56 * MIB),
        cost_estimate=pl.CostEstimate(
            flops=2 * rows * width * (width + 6 * ff),
            bytes_accessed=2 * (width * width + 3 * width * ff + 8 * rows * width),
            transcendentals=rows * ff,
        ),
        name="expert",
    )(place_of, att, wa, wb, gain, ids, weights, grads, gate, up, down)


def weight_kernel(count, *refs):
    normed, back, units, back_gate, back_up = [refs[i * count : (i + 1) * count] for i in range(5)]
    gate_ref, up_ref, down_ref = refs[5 * count :]
    first = ((0,), (0,))
    gate = up = down = 0.0
    for c in range(count):
        gate += dot(normed[c][...], back_gate[c][...], first)
        up += dot(normed[c][...], back_up[c][...], first)
        down += dot(units[c][...], back[c][...], first)
    gate_ref[...] = gate.astype(BF16)
    up_ref[...] = up.astype(BF16)
    down_ref[0] = down.astype(BF16)


def weight_parts(normed, back, units, back_gate, back_up):
    count = len(normed)
    rows, width = normed[0].shape
    ff = units[0].shape[1]
    cols = PIECE
    thin = [pl.BlockSpec((rows, cols), lambda i: (0, i))] * count
    full = [pl.BlockSpec((rows, ff), lambda i: (0, 0))] * count
    return pl.pallas_call(
        functools.partial(weight_kernel, count),
        grid=(width // cols,),
        in_specs=thin + thin + full + full + full,
        out_specs=[
            pl.BlockSpec((cols, ff), lambda i: (i, 0)),
            pl.BlockSpec((cols, ff), lambda i: (i, 0)),
            pl.BlockSpec((1, ff, cols), lambda i: (i, 0, 0)),
        ],
        out_shape=[
            jax.ShapeDtypeStruct((width, ff), BF16),
            jax.ShapeDtypeStruct((width, ff), BF16),
            jax.ShapeDtypeStruct((width // cols, ff, cols), BF16),
        ],
        compiler_params=pltpu.CompilerParams(vmem_limit_bytes=40 * MIB),
        cost_estimate=pl.CostEstimate(
            flops=6 * count * rows * width * ff,
            bytes_accessed=2 * (3 * width * ff + 2 * count * rows * (width + 2 * ff)),
            transcendentals=0,
        ),
        name="weight_grads",
    )(*normed, *back, *units, *back_gate, *back_up)


def partner(axis_name, value, bit):
    count = lax.axis_size(axis_name)
    return lax.ppermute(value, axis_name, [(i, i ^ (1 << bit)) for i in range(count)])


def doubled(value, bits, order):
    shape = value.shape
    held = value.reshape((1,) * bits + shape)
    for bit in order:
        other = partner("ctx", held, bit)
        held = jnp.concatenate([held, other], axis=bits - 1 - bit)
    return held.reshape((1 << bits,) + shape)


def halved(value, bits, order, ctx):
    shape = value.shape[1:]
    held = value.reshape((2,) * bits + shape)
    for place_in_order, bit in enumerate(order):
        axis = bits - 1 - bit
        mine = (ctx >> bit) & 1
        gone = lax.dynamic_slice_in_dim(held, 1 - mine, 1, axis)
        kept = lax.dynamic_slice_in_dim(held, mine, 1, axis)
        held = kept.astype(F32) + partner("ctx", gone, bit).astype(F32)
        if place_in_order < bits - 1:
            held = held.astype(BF16)
    return held.reshape(shape)


def on_device(
    queries,
    rotated_key_heads,
    value_head_rows,
    out_proj,
    norm_gain,
    expert_ids,
    gate_weights,
    expert_gate,
    expert_up,
    expert_down,
    grad_out,
):
    seq_count, block_len, heads_width = queries.shape
    heads_dev = heads_width // HEAD_SIZE
    group = LOCAL_QUERY_HEADS // LOCAL_KEY_HEADS
    exp_count = lax.axis_size("exp")
    ctx_count = lax.axis_size("ctx")
    owner = lax.axis_index("exp")
    ctx = lax.axis_index("ctx")
    bits = ctx_count.bit_length() - 1
    n, _ = expert_ids.shape
    width = grad_out.shape[1]
    experts = exp_count * expert_gate.shape[0]
    capacity = min(n, 2 * n // experts)

    ids_f = expert_ids.astype(F32)
    info = jnp.stack([ids_f[:, 0], gate_weights[:, 0]])
    info = lax.all_to_all(
        jnp.broadcast_to(info[None], (exp_count, 2, n)), "exp", 0, 0, tiled=True
    )
    ids_all, weights_all = info[:, 0:1, :], info[:, 1:2, :]

    grads = place(ids_f.reshape(1, n), grad_out, experts, capacity)
    grads = lax.all_to_all(grads, "exp", 0, 0, tiled=True)

    first_column = (owner * heads_dev // group) * HEAD_SIZE
    low, high = list(range(1, bits)) + [0], list(range(bits - 1, 0, -1)) + [0]
    keys = lax.dynamic_slice_in_dim(rotated_key_heads, first_column, HEAD_SIZE, 2)
    values = lax.dynamic_slice_in_dim(value_head_rows, first_column, HEAD_SIZE, 2)
    keys = doubled(keys, bits, low)
    values = doubled(values, bits, high)

    pieces = min(ctx_count, width // PIECE)
    piece_bits = pieces.bit_length() - 1
    piece = width // pieces
    piece_index = ctx % pieces
    mine = lax.dynamic_slice_in_dim(out_proj, piece_index * piece, piece, 1)
    mine = lax.all_gather(mine, "exp", axis=0, tiled=True)
    half = mine.shape[0] // 2
    wa = doubled(mine[:half], piece_bits, [b for b in low if b < piece_bits])
    wb = doubled(mine[half:], piece_bits, [b for b in high if b < piece_bits])

    attended = attend(
        ctx.reshape(1).astype(jnp.int32), queries, keys, values, ids_all, experts, capacity
    )
    place_of = jnp.stack([piece_index, owner]).astype(jnp.int32)
    outs = []
    for index, sent in enumerate(attended):
        arrived = lax.all_to_all(sent, "exp", 0, 0, tiled=True)
        outs.append(
            expert_part(
                place_of,
                arrived,
                wa,
                wb,
                norm_gain.reshape(1, width),
                ids_all,
                weights_all,
                grads,
                expert_gate,
                expert_up,
                expert_down,
                capacity,
                index,
            )
        )
    layer, grad_hidden, normed, back, units, back_gate, back_up = zip(*outs)
    layer = [lax.all_to_all(x, "exp", 0, 0, tiled=True) for x in layer]
    grad_hidden = [lax.all_to_all(x, "exp", 0, 0, tiled=True) for x in grad_hidden]
    part_gate, part_up, part_down = weight_parts(normed, back, units, back_gate, back_up)

    ff = part_gate.shape[1]
    rows_dev = width // ctx_count
    part_gate = part_gate.reshape(ctx_count, rows_dev, ff)
    part_up = part_up.reshape(ctx_count, rows_dev, ff)
    if rows_dev != PIECE:
        part_down = part_down.reshape(width // PIECE, ff, PIECE // rows_dev, rows_dev)
        part_down = part_down.transpose(0, 2, 1, 3).reshape(ctx_count, ff, rows_dev)
    core_low, core_high = [0] + low[:-1], [0] + high[:-1]
    grad_gate = halved(part_gate, bits, core_low, ctx)[None]
    grad_up = halved(part_up, bits, core_high, ctx)[None]
    grad_down = halved(part_down, bits, core_low, ctx)[None]

    layer_out = restore(ids_f, layer, capacity)
    grad_hidden = restore(ids_f, grad_hidden, capacity)
    return (layer_out, grad_hidden, grad_gate, grad_up, grad_down)


def solution(mesh):
    in_specs = (
        P(None, "ctx", "exp"),
        P(None, "ctx", None),
        P(None, "ctx", None),
        P("exp", None),
        P(),
        P(("ctx", "exp"), None),
        P(("ctx", "exp"), None),
        P("exp", None, None),
        P("exp", None, None),
        P("exp", None, None),
        P(("ctx", "exp"), None),
    )
    out_specs = (
        P(("ctx", "exp"), None),
        P(("ctx", "exp"), None),
        P("exp", "ctx", None),
        P("exp", "ctx", None),
        P("exp", None, "ctx"),
    )
    return jax.shard_map(
        on_device, mesh=mesh, in_specs=in_specs, out_specs=out_specs, check_vma=False
    )
```

time: 478 us -> 349 us (0.73)
  waiting for transfers between devices: 297 us -> 120 us
  matrix products: 93 us -> 0 us
  Pallas kernels: 0 us -> 88.4 us
  starting transfers between devices: 25.8 us -> 61.3 us
  local copies, waits for them, and re-layouts: 14.6 us -> 30.2 us
  other arithmetic: 21.9 us -> 30.3 us
  loops' own time: 8.28 us -> 0 us
    reduce_scatter x4 -> x0, waiting for transfers between devices: 129 us -> none  [the longest x1 110 us: on_device(): lax.psum_scatter(jnp.dot(flat_heads, out_proj, preferred_element_type=jnp...]
    dot_general x22 -> x0, matrix products: 93 us -> none  [the longest x4 16.9 us: compute(): jnp.einsum('sgrqk,skgd->sgrqd', weights.astype(jnp.bfloat16), value_sub,...]
    pallas_call x0 -> x7, Pallas kernels: none -> 88.4 us  [the longest x2 42.2 us: expert_part(): pl.pallas_call(functools.partial(expert_kernel, pieces, tiles, capacity,...]
    all_to_all x4 -> x8, waiting for transfers between devices: 114 us -> 48.3 us  [the longest x2 24.5 us: on_device(): lax.all_to_all(x, 'exp', 0, 0, tiled=True)]
    ppermute x0 -> x21, waiting for transfers between devices: none -> 54.4 us  [partner(): lax.ppermute(value, axis_name, [(i, i ^ 1 << bit) for i in range(count)])]
    all_gather x2 -> x1, waiting for transfers between devices: 52.8 us -> 17.7 us  [on_device(): mine = lax.all_gather(mine, 'exp', axis=0, tiled=True)]
    all_to_all x4 -> x8, starting transfers between devices: 25.4 us -> 50.2 us  [the longest x2 15.4 us: on_device(): arrived = lax.all_to_all(sent, 'exp', 0, 0, tiled=True)]
    concatenate x0 -> x12, other arithmetic: none -> 15.6 us  [doubled(): held = jnp.concatenate([held, other], axis=bits - 1 - bit)]
  transfers between devices with their start and end apart: 10 -> 30, of which waited for: 7 -> 12; matrix products, arithmetic and copies ran while one was open for 13% -> 12% of each run, Pallas kernels for 0% -> 26%
where the time goes in v1:
time: 349 us; the launch traced here: 345 us
  waiting for transfers between devices  120 us (34%)
  Pallas kernels  88.4 us (25%)
  starting transfers between devices  61.3 us (18%)
  other arithmetic  30.3 us (9%)
  local copies, waits for them, and re-layouts  30.2 us (9%)
  between operations  14.4 us (4%)
    ppermute x21, waiting for transfers between devices, partner(): lax.ppermute(value, axis_name, [(i, i ^ 1 << bit) for i in range(count)])  54.4 us
    pallas_call x2, Pallas kernels, expert_part(): pl.pallas_call(functools.partial(expert_kernel, pieces, tiles, capacity,...  42.2 us
    pallas_call x1, Pallas kernels, attend(): pl.pallas_call(functools.partial(attend_kernel, experts, capacity, heads)...  27.2 us
    all_to_all x2, waiting for transfers between devices, on_device(): lax.all_to_all(x, 'exp', 0, 0, tiled=True)  24.5 us
    all_gather x1, waiting for transfers between devices, on_device(): mine = lax.all_gather(mine, 'exp', axis=0, tiled=True)  17.7 us
    unnamed x67, local copies, waits for them, and re-layouts  17.6 us
    all_to_all x2, waiting for transfers between devices, on_device(): arrived = lax.all_to_all(sent, 'exp', 0, 0, tiled=True)  17.4 us
    concatenate x12, other arithmetic, doubled(): held = jnp.concatenate([held, other], axis=bits - 1 - bit)  15.6 us
  transfers between devices with their start and end apart: 30, of which 12 were waited for; matrix products, arithmetic and copies ran while one was open for 12% of the time, Pallas kernels for 26%

profile of v1, /device:TPU:22, one launch (start us, length us, event | category | flops | bytes accessed | tf_op | source)
XLA Modules:
  0.0 345.1 jit_solution(17256514706375661798)
XLA Ops:
  11.8 5.2 %all-to-all-start = ((f32[4,2,256]{2,1,0:T(2,128)}), f32[4,2,256]{2,1,0:T(2,128)S(1)}, u32[]{:S(2)}, u32[]{:S(2)}) async-start(f32[4,2,256]{2,1,0:T(2,128)} %broadcast_in_dim.2), calls=%async_computation | async-start | bytes 16384 | tf_op jit(solution)/shard_map/all_to_all | solution.py:484
  21.4 5.7 %all-to-all-start.2 = ((bf16[4,128,2048]{2,1,0:T(8,128)(2,1)}), bf16[4,128,2048]{2,1,0:T(8,128)(2,1)}, u32[]{:S(2)}, u32[]{:S(2)}) async-start(bf16[4,128,2048]{2,1,0:T(8,128)(2,1)} %place.1), calls=%async_computation.2 | async-start | bytes 4194304 | tf_op jit(solution)/shard_map/all_to_all | solution.py:490
  28.4 5.3 %collective-permute-done.3 = bf16[1,1,1,4,256,128]{5,4,3,2,1,0:T(8,128)(2,1)S(1)} collective-permute-done((bf16[1,1,1,4,256,128]{5,4,3,2,1,0:T(8,128)(2,1)S(1)}, bf16[1,1,1,4,256,128]{5,4,3,2,1,0:T(8,128)(2,1)S(1)}, u32[]{:S(2)}, u32[]{:S(2)}) %collective-permute-start.3) | collective-permute-done | bytes 262176 | tf_op jit(solution)/shard_map/ppermute | solution.py:430
  35.0 17.7 %all-gather.2.cloned.1.call-done = bf16[2048,256]{1,0:T(8,128)(2,1)} async-done(((bf16[512,256]{1,0:T(8,128)(2,1)}), bf16[2048,256]{1,0:T(8,128)(2,1)}) %all-gather.2.cloned.1.call-update) | async-done | bytes 1048592 | tf_op jit(solution)/shard_map/all_gather | solution.py:504
  57.6 11.3 %collective-permute-done.9 = bf16[1,1,1,1024,256]{4,3,2,1,0:T(8,128)(2,1)S(1)} collective-permute-done((bf16[1,1,1,1024,256]{4,3,2,1,0:T(8,128)(2,1)S(1)}, bf16[1,1,1,1024,256]{4,3,2,1,0:T(8,128)(2,1)S(1)}, u32[]{:S(2)}, u32[]{:S(2)}) %collective-permute-start.9) | collective-permute-done | bytes 524320 | tf_op jit(solution)/shard_map/ppermute | solution.py:430
  69.7 8.8 %collective-permute-done.1 = bf16[1,2,1,4,256,128]{5,4,3,2,1,0:T(8,128)(2,1)S(1)} collective-permute-done((bf16[1,2,1,4,256,128]{5,4,3,2,1,0:T(8,128)(2,1)S(1)}, bf16[1,2,1,4,256,128]{5,4,3,2,1,0:T(8,128)(2,1)S(1)}, u32[]{:S(2)}, u32[]{:S(2)}) %collective-permute-start.1) | collective-permute-done | bytes 524320 | tf_op jit(solution)/shard_map/ppermute | solution.py:430
  82.6 10.6 %collective-permute-done.10 = bf16[2,1,1,1024,256]{4,3,2,1,0:T(8,128)(2,1)S(1)} collective-permute-done((bf16[2,1,1,1024,256]{4,3,2,1,0:T(8,128)(2,1)S(1)}, bf16[2,1,1,1024,256]{4,3,2,1,0:T(8,128)(2,1)S(1)}, u32[]{:S(2)}, u32[]{:S(2)}) %collective-permute-start.10) | collective-permute-done | bytes 1048608 | tf_op jit(solution)/shard_map/ppermute | solution.py:430
  96.1 27.2 %attend.1 = (bf16[4,4,64,512]{3,2,1,0:T(8,128)(2,1)}, bf16[4,4,64,512]{3,2,1,0:T(8,128)(2,1)}) custom-call(s32[1]{0:T(128)} %bitcast.2.ctx_ref, bf16[4,256,512]{2,1,0:T(8,128)(2,1)S(1)} %copy-done.8, bf16[8,4,256,128]{3,2,1,0:T(8,128)(2,1)S(1)} %bitcast.31, bf16[8,4,256,128]{3,2,1,0:T(8,128)(2,1)} %bitcast.40, f32[4,1,256]{2,1,0:T(1,128)S(1)} %get-tuple-element.46.ids_ref), custom_call_target="tpu_custom_call" | custom-call | flops 2147483648 | bytes 8388608 | tf_op jit(solution)/shard_map/attend/pallas_call | solution.py:109
  123.3 7.9 %all-to-all-start.4 = ((bf16[4,4,64,512]{3,2,1,0:T(8,128)(2,1)}), bf16[4,4,64,512]{3,2,1,0:T(8,128)(2,1)}, u32[]{:S(2)}, u32[]{:S(2)}) async-start(bf16[4,4,64,512]{3,2,1,0:T(8,128)(2,1)} %get-tuple-element.26), calls=%async_computation.4 | async-start | bytes 2097152 | tf_op jit(solution)/shard_map/all_to_all | solution.py:515
  136.5 17.4 %all-to-all-done.4.att_ref = bf16[4,4,64,512]{3,2,1,0:T(8,128)(2,1)} async-done(((bf16[4,4,64,512]{3,2,1,0:T(8,128)(2,1)}), bf16[4,4,64,512]{3,2,1,0:T(8,128)(2,1)}, u32[]{:S(2)}, u32[]{:S(2)}) %all-to-all-start.4) | async-done | bytes 1048608 | tf_op jit(solution)/shard_map/all_to_all | solution.py:515
  153.9 7.6 %all-to-all-start.1 = ((bf16[4,4,64,512]{3,2,1,0:T(8,128)(2,1)}), bf16[4,4,64,512]{3,2,1,0:T(8,128)(2,1)}, u32[]{:S(2)}, u32[]{:S(2)}) async-start(bf16[4,4,64,512]{3,2,1,0:T(8,128)(2,1)} %get-tuple-element.24), calls=%async_computation.1 | async-start | bytes 2097152 | tf_op jit(solution)/shard_map/all_to_all | solution.py:515
  169.2 21.1 %expert.3 = (bf16[4,64,2048]{2,1,0:T(8,128)(2,1)}, bf16[4,64,2048]{2,1,0:T(8,128)(2,1)}, bf16[256,2048]{1,0:T(8,128)(2,1)}, bf16[256,2048]{1,0:T(8,128)(2,1)}, b...) custom-call(s32[2]{0:T(128)} %pad_add_fusion.place_ref, ...), custom_call_target="tpu_custom_call" | custom-call | flops 6979321856 | bytes 26214400 | tf_op jit(solution)/shard_map/expert/pallas_call | solution.py:330
  190.3 5.1 %all-to-all-start.7 = ((bf16[4,64,2048]{2,1,0:T(8,128)(2,1)}), bf16[4,64,2048]{2,1,0:T(8,128)(2,1)S(1)}, u32[]{:S(2)}, u32[]{:S(2)}) async-start(bf16[4,64,2048]{2,1,0:T(8,128)(2,1)} %get-tuple-element.29), calls=%async_computation.7 | async-start | bytes 2097152 | tf_op jit(solution)/shard_map/all_to_all | solution.py:535
  195.4 21.1 %expert.2 = (bf16[4,64,2048]{2,1,0:T(8,128)(2,1)}, bf16[4,64,2048]{2,1,0:T(8,128)(2,1)}, bf16[256,2048]{1,0:T(8,128)(2,1)}, bf16[256,2048]{1,0:T(8,128)(2,1)}, b...) custom-call(s32[2]{0:T(128)} %pad_add_fusion.place_ref, ...), custom_call_target="tpu_custom_call" | custom-call | flops 6979321856 | bytes 26214400 | tf_op jit(solution)/shard_map/expert/pallas_call | solution.py:330
  218.6 6.9 %all-to-all-start.6 = ((bf16[4,64,2048]{2,1,0:T(8,128)(2,1)}), bf16[4,64,2048]{2,1,0:T(8,128)(2,1)S(1)}, u32[]{:S(2)}, u32[]{:S(2)}) async-start(bf16[4,64,2048]{2,1,0:T(8,128)(2,1)} %get-tuple-element.28), calls=%async_computation.6 | async-start | bytes 2097152 | tf_op jit(solution)/shard_map/all_to_all | solution.py:535
  225.5 22.4 %all-to-all-done.6.refs_0_ = bf16[4,64,2048]{2,1,0:T(8,128)(2,1)S(1)} async-done(((bf16[4,64,2048]{2,1,0:T(8,128)(2,1)}), bf16[4,64,2048]{2,1,0:T(8,128)(2,1)S(1)}, u32[]{:S(2)}, u32[]{:S(2)}) %all-to-all-start.6) | async-done | bytes 1048608 | tf_op jit(solution)/shard_map/all_to_all | solution.py:535
  247.9 6.8 %all-to-all-start.5 = ((bf16[4,64,2048]{2,1,0:T(8,128)(2,1)}), bf16[4,64,2048]{2,1,0:T(8,128)(2,1)S(1)}, u32[]{:S(2)}, u32[]{:S(2)}) async-start(bf16[4,64,2048]{2,1,0:T(8,128)(2,1)} %get-tuple-element.27), calls=%async_computation.5 | async-start | bytes 2097152 | tf_op jit(solution)/shard_map/all_to_all | solution.py:534
  264.6 8.0 %weight_grads.1 = (bf16[2048,768]{1,0:T(8,128)(2,1)S(1)}, bf16[2048,768]{1,0:T(8,128)(2,1)S(1)}, bf16[8,768,256]{2,1,0:T(8,128)(2,1)}) custom-call(bf16[256,2048]{1,0:T(8,128)(2,1)S(1)} %copy-done.11, bf16[256,2048]{1,0:T(8,128)(2,1)S(1)} %copy-done.9, bf16[256,2048]{1,0:T(8,128)(2,1)S(1)} %copy-done.12, bf16[256,2048]{1,0:T(8,128)(2,1)S(1)} %copy-done.10, ...), custom_call_target="tpu_custom_call" | custom-call | flops 4831838208 | bytes 16777216 | tf_op jit(solution)/shard_map/weight_grads/pallas_call | solution.py:404
  272.6 3.8 %constant_dynamic-slice_fusion.2 = bf16[2,2,1,768,256]{4,3,2,1,0:T(8,128)(2,1)} fusion(bf16[2,2,2,768,256]{4,3,2,1,0:T(8,128)(2,1)} %bitcast.38, s32[]{:T(128)S(6)} %select_n.53), kind=kLoop, calls=%fused_computation.27 | loop fusion | bytes 3145732 | tf_op jit(solution)/shard_map/dynamic_slice | solution.py:448
  279.5 5.1 %all-to-all-start.3 = ((bf16[4,64,2048]{2,1,0:T(8,128)(2,1)}), bf16[4,64,2048]{2,1,0:T(8,128)(2,1)}, u32[]{:S(2)}, u32[]{:S(2)}) async-start(bf16[4,64,2048]{2,1,0:T(8,128)(2,1)} %get-tuple-element.25), calls=%async_computation.3 | async-start | bytes 2097152 | tf_op jit(solution)/shard_map/all_to_all | solution.py:534
  301.4 6.3 %all-to-all-done.3.refs_0_ = bf16[4,64,2048]{2,1,0:T(8,128)(2,1)} async-done(((bf16[4,64,2048]{2,1,0:T(8,128)(2,1)}), bf16[4,64,2048]{2,1,0:T(8,128)(2,1)}, u32[]{:S(2)}, u32[]{:S(2)}) %all-to-all-start.3) | async-done | bytes 1048608 | tf_op jit(solution)/shard_map/all_to_all | solution.py:534
  307.7 4.5 %restore.2 = bf16[256,2048]{1,0:T(8,128)(2,1)} custom-call(f32[256,1]{1,0:T(8,128)S(1)} %convert_element_type.75.ids_ref, bf16[4,64,2048]{2,1,0:T(8,128)(2,1)} %all-to-all-done.3.refs_0_, bf16[4,64,2048]{2,1,0:T(8,128)(2,1)S(1)} %all-to-all-done.5.refs_1_), custom_call_target="tpu_custom_call" | custom-call | tf_op jit(solution)/shard_map/restore/pallas_call | solution.py:189
  315.6 11.1 %collective-permute-done.13 = bf16[2,1,1,256,768]{4,3,2,1,0:T(8,128)(2,1)} collective-permute-done((bf16[2,1,1,256,768]{4,3,2,1,0:T(8,128)(2,1)}, bf16[2,1,1,256,768]{4,3,2,1,0:T(8,128)(2,1)}, u32[]{:S(2)}, u32[]{:S(2)}) %collective-permute-start.13) | collective-permute-done | bytes 786464 | tf_op jit(solution)/shard_map/ppermute | solution.py:430
  329.2 4.9 %collective-permute-done.17 = bf16[1,1,1,256,768]{4,3,2,1,0:T(8,128)(2,1)S(1)} collective-permute-done((bf16[1,1,1,256,768]{4,3,2,1,0:T(8,128)(2,1)S(1)}, bf16[1,1,1,256,768]{4,3,2,1,0:T(8,128)(2,1)S(1)}, u32[]{:S(2)}, u32[]{:S(2)}) %collective-permute-start.17) | collective-permute-done | bytes 393248 | tf_op jit(solution)/shard_map/ppermute | solution.py:430
  (151 shorter events, 78.9 us)
Async XLA Ops:
  7.2 45.6 %all-gather.2.cloned.1.call-start = ((), (), s32[]{:S(2)}) async-start(), calls=%async_computation.8 | async-start | bytes 1310720 | tf_op jit(solution)/shard_map/all_gather | solution.py:504
  21.4 101.8 %all-to-all-start.2 = ((bf16[4,128,2048]{2,1,0:T(8,128)(2,1)}), bf16[4,128,2048]{2,1,0:T(8,128)(2,1)}, u32[]{:S(2)}, u32[]{:S(2)}) async-start(bf16[4,128,2048]{2,1,0:T(8,128)(2,1)} %place.1), calls=%async_computation.2 | async-start | bytes 4194304 | tf_op jit(solution)/shard_map/all_to_all | solution.py:490
  27.8 26.9 %collective-permute-start = (bf16[1,1,1,4,256,128]{5,4,3,2,1,0:T(8,128)(2,1)S(1)}, bf16[1,1,1,4,256,128]{5,4,3,2,1,0:T(8,128)(2,1)S(1)}, u32[]{:S(2)}, u32[]{:S(2)}) collective-permute-start(bf16[1,1,1,4,256,128]{5,4,3,2,1,0:T(8,128)(2,1)S(1)} %dynamic-slice_bitcast_fusion.1), channel_id=1, source_target_pairs={{0,8},{4,12},{8,0},{12,4},{16,24},{20,28},{24,16},{28,20},{1,9},{5... | collective-permute-start | bytes 786440 | tf_op jit(solution)/shard_map/ppermute | solution.py:430
  34.5 21.7 %collective-permute-start.4 = (bf16[2,1,1,4,256,128]{5,4,3,2,1,0:T(8,128)(2,1)}, bf16[2,1,1,4,256,128]{5,4,3,2,1,0:T(8,128)(2,1)S(1)}, u32[]{:S(2)}, u32[]{:S(2)}) collective-permute-start(bf16[2,1,1,4,256,128]{5,4,3,2,1,0:T(8,128)(2,1)} %pad_maximum_fusion.11), channel_id=1, source_target_pairs={{0,8},{4,12},{8,0},{12,4},{16,24},{20,28},{24,16},{28,20},{1,9},{5... | collective-permute-start | bytes 1572872 | tf_op jit(solution)/shard_map/ppermute | solution.py:430
  54.0 14.9 %collective-permute-start.9 = (bf16[1,1,1,1024,256]{4,3,2,1,0:T(8,128)(2,1)S(1)}, bf16[1,1,1,1024,256]{4,3,2,1,0:T(8,128)(2,1)S(1)}, u32[]{:S(2)}, u32[]{:S(2)}) collective-permute-start(bf16[1,1,1,1024,256]{4,3,2,1,0:T(8,128)(2,1)S(1)} %get-tuple-element.43), channel_id=1, source_target_pairs={{0,16},{4,20},{8,24},{12,28},{16,0},{20,4},{24,8},{28,12},{1,17},{... | collective-permute-start | bytes 1572872 | tf_op jit(solution)/shard_map/ppermute | solution.py:430
  54.7 23.8 %collective-permute-start.1 = (bf16[1,2,1,4,256,128]{5,4,3,2,1,0:T(8,128)(2,1)S(1)}, bf16[1,2,1,4,256,128]{5,4,3,2,1,0:T(8,128)(2,1)S(1)}, u32[]{:S(2)}, u32[]{:S(2)}) collective-permute-start(bf16[1,2,1,4,256,128]{5,4,3,2,1,0:T(8,128)(2,1)S(1)} %pad_maximum_fusion.10), channel_id=1, source_target_pairs={{0,16},{4,20},{8,24},{12,28},{16,0},{20,4},{24,8},{28,12},{1,17},{... | collective-permute-start | bytes 1572872 | tf_op jit(solution)/shard_map/ppermute | solution.py:430
  56.3 24.7 %collective-permute-start.5 = (bf16[2,2,1,4,256,128]{5,4,3,2,1,0:T(8,128)(2,1)S(1)}, bf16[2,2,1,4,256,128]{5,4,3,2,1,0:T(8,128)(2,1)S(1)}, u32[]{:S(2)}, u32[]{:S(2)}) collective-permute-start(bf16[2,2,1,4,256,128]{5,4,3,2,1,0:T(8,128)(2,1)S(1)} %pad_maximum_fusion.7), channel_id=1, source_target_pairs={{0,4},{4,0},{8,12},{12,8},{16,20},{20,16},{24,28},{28,24},{1,5},{5... | collective-permute-start | bytes 3145736 | tf_op jit(solution)/shard_map/ppermute | solution.py:430
  57.0 21.7 %collective-permute-start.6 = (bf16[1,1,1,1024,256]{4,3,2,1,0:T(8,128)(2,1)S(1)}, bf16[1,1,1,1024,256]{4,3,2,1,0:T(8,128)(2,1)S(1)}, u32[]{:S(2)}, u32[]{:S(2)}) collective-permute-start(bf16[1,1,1,1024,256]{4,3,2,1,0:T(8,128)(2,1)S(1)} %get-tuple-element.44), channel_id=1, source_target_pairs={{0,8},{4,12},{8,0},{12,4},{16,24},{20,28},{24,16},{28,20},{1,9},{5... | collective-permute-start | bytes 1572872 | tf_op jit(solution)/shard_map/ppermute | solution.py:430
  69.1 24.2 %collective-permute-start.10 = (bf16[2,1,1,1024,256]{4,3,2,1,0:T(8,128)(2,1)S(1)}, bf16[2,1,1,1024,256]{4,3,2,1,0:T(8,128)(2,1)S(1)}, u32[]{:S(2)}, u32[]{:S(2)}) collective-permute-start(bf16[2,1,1,1024,256]{4,3,2,1,0:T(8,128)(2,1)S(1)} %pad_maximum_fusion.9), channel_id=1, source_target_pairs={{0,8},{4,12},{8,0},{12,4},{16,24},{20,28},{24,16},{28,20},{1,9},{5... | collective-permute-start | bytes 3145736 | tf_op jit(solution)/shard_map/ppermute | solution.py:430
  78.7 16.2 %collective-permute-start.2 = (bf16[2,2,1,4,256,128]{5,4,3,2,1,0:T(8,128)(2,1)S(1)}, bf16[2,2,1,4,256,128]{5,4,3,2,1,0:T(8,128)(2,1)S(1)}, u32[]{:S(2)}, u32[]{:S(2)}) collective-permute-start(bf16[2,2,1,4,256,128]{5,4,3,2,1,0:T(8,128)(2,1)S(1)} %pad_maximum_fusion.6), channel_id=1, source_target_pairs={{0,4},{4,0},{8,12},{12,8},{16,20},{20,16},{24,28},{28,24},{1,5},{5... | collective-permute-start | bytes 3145736 | tf_op jit(solution)/shard_map/ppermute | solution.py:430
  79.8 51.3 %collective-permute-start.7 = (bf16[1,2,1,1024,256]{4,3,2,1,0:T(8,128)(2,1)}, bf16[1,2,1,1024,256]{4,3,2,1,0:T(8,128)(2,1)}, u32[]{:S(2)}, u32[]{:S(2)}) collective-permute-start(bf16[1,2,1,1024,256]{4,3,2,1,0:T(8,128)(2,1)} %pad_maximum_fusion.8), channel_id=1, source_target_pairs={{0,16},{4,20},{8,24},{12,28},{16,0},{20,4},{24,8},{28,12},{1,17},{... | collective-permute-start | bytes 3145736 | tf_op jit(solution)/shard_map/ppermute | solution.py:430
  94.9 67.3 %collective-permute-start.11 = (bf16[2,2,1,1024,256]{4,3,2,1,0:T(8,128)(2,1)}, bf16[2,2,1,1024,256]{4,3,2,1,0:T(8,128)(2,1)}, u32[]{:S(2)}, u32[]{:S(2)}) collective-permute-start(bf16[2,2,1,1024,256]{4,3,2,1,0:T(8,128)(2,1)} %pad_maximum_fusion.5), channel_id=1, source_target_pairs={{0,4},{4,0},{8,12},{12,8},{16,20},{20,16},{24,28},{28,24},{1,5},{5... | collective-permute-start | bytes 6291464 | tf_op jit(solution)/shard_map/ppermute | solution.py:430
  123.3 30.7 %all-to-all-start.4 = ((bf16[4,4,64,512]{3,2,1,0:T(8,128)(2,1)}), bf16[4,4,64,512]{3,2,1,0:T(8,128)(2,1)}, u32[]{:S(2)}, u32[]{:S(2)}) async-start(bf16[4,4,64,512]{3,2,1,0:T(8,128)(2,1)} %get-tuple-element.26), calls=%async_computation.4 | async-start | bytes 2097152 | tf_op jit(solution)/shard_map/all_to_all | solution.py:515
  133.9 31.6 %collective-permute-start.8 = (bf16[2,2,1,1024,256]{4,3,2,1,0:T(8,128)(2,1)}, bf16[2,2,1,1024,256]{4,3,2,1,0:T(8,128)(2,1)}, u32[]{:S(2)}, u32[]{:S(2)}) collective-permute-start(bf16[2,2,1,1024,256]{4,3,2,1,0:T(8,128)(2,1)} %pad_maximum_fusion.4), channel_id=1, source_target_pairs={{0,4},{4,0},{8,12},{12,8},{16,20},{20,16},{24,28},{28,24},{1,5},{5... | collective-permute-start | bytes 6291464 | tf_op jit(solution)/shard_map/ppermute | solution.py:430
  153.9 36.3 %all-to-all-start.1 = ((bf16[4,4,64,512]{3,2,1,0:T(8,128)(2,1)}), bf16[4,4,64,512]{3,2,1,0:T(8,128)(2,1)}, u32[]{:S(2)}, u32[]{:S(2)}) async-start(bf16[4,4,64,512]{3,2,1,0:T(8,128)(2,1)} %get-tuple-element.24), calls=%async_computation.1 | async-start | bytes 2097152 | tf_op jit(solution)/shard_map/all_to_all | solution.py:515
  190.3 28.3 %all-to-all-start.7 = ((bf16[4,64,2048]{2,1,0:T(8,128)(2,1)}), bf16[4,64,2048]{2,1,0:T(8,128)(2,1)S(1)}, u32[]{:S(2)}, u32[]{:S(2)}) async-start(bf16[4,64,2048]{2,1,0:T(8,128)(2,1)} %get-tuple-element.29), calls=%async_computation.7 | async-start | bytes 2097152 | tf_op jit(solution)/shard_map/all_to_all | solution.py:535
  218.6 29.3 %all-to-all-start.6 = ((bf16[4,64,2048]{2,1,0:T(8,128)(2,1)}), bf16[4,64,2048]{2,1,0:T(8,128)(2,1)S(1)}, u32[]{:S(2)}, u32[]{:S(2)}) async-start(bf16[4,64,2048]{2,1,0:T(8,128)(2,1)} %get-tuple-element.28), calls=%async_computation.6 | async-start | bytes 2097152 | tf_op jit(solution)/shard_map/all_to_all | solution.py:535
  247.9 31.6 %all-to-all-start.5 = ((bf16[4,64,2048]{2,1,0:T(8,128)(2,1)}), bf16[4,64,2048]{2,1,0:T(8,128)(2,1)S(1)}, u32[]{:S(2)}, u32[]{:S(2)}) async-start(bf16[4,64,2048]{2,1,0:T(8,128)(2,1)} %get-tuple-element.27), calls=%async_computation.5 | async-start | bytes 2097152 | tf_op jit(solution)/shard_map/all_to_all | solution.py:534
  279.5 28.2 %all-to-all-start.3 = ((bf16[4,64,2048]{2,1,0:T(8,128)(2,1)}), bf16[4,64,2048]{2,1,0:T(8,128)(2,1)}, u32[]{:S(2)}, u32[]{:S(2)}) async-start(bf16[4,64,2048]{2,1,0:T(8,128)(2,1)} %get-tuple-element.25), calls=%async_computation.3 | async-start | bytes 2097152 | tf_op jit(solution)/shard_map/all_to_all | solution.py:534
  289.2 23.1 %collective-permute-start.19 = (bf16[2,1,1,768,256]{4,3,2,1,0:T(8,128)(2,1)}, bf16[2,1,1,768,256]{4,3,2,1,0:T(8,128)(2,1)}, u32[]{:S(2)}, u32[]{:S(2)}) collective-permute-start(bf16[2,1,1,768,256]{4,3,2,1,0:T(8,128)(2,1)} %constant_dynamic-slice_fusion.1), channel_id=1, source_target_pairs={{0,8},{4,12},{8,0},{12,4},{16,24},{20,28},{24,16},{28,20},{1,9},{5... | collective-permute-start | bytes 2359304 | tf_op jit(solution)/shard_map/ppermute | solution.py:430
  292.2 21.6 %collective-permute-start.16 = (bf16[1,2,1,256,768]{4,3,2,1,0:T(8,128)(2,1)}, bf16[1,2,1,256,768]{4,3,2,1,0:T(8,128)(2,1)}, u32[]{:S(2)}, u32[]{:S(2)}) collective-permute-start(bf16[1,2,1,256,768]{4,3,2,1,0:T(8,128)(2,1)} %constant_dynamic-slice_fusion.4), channel_id=1, source_target_pairs={{0,16},{4,20},{8,24},{12,28},{16,0},{20,4},{24,8},{28,12},{1,17},{... | collective-permute-start | bytes 2359304 | tf_op jit(solution)/shard_map/ppermute | solution.py:430
  296.2 30.5 %collective-permute-start.13 = (bf16[2,1,1,256,768]{4,3,2,1,0:T(8,128)(2,1)}, bf16[2,1,1,256,768]{4,3,2,1,0:T(8,128)(2,1)}, u32[]{:S(2)}, u32[]{:S(2)}) collective-permute-start(bf16[2,1,1,256,768]{4,3,2,1,0:T(8,128)(2,1)} %constant_dynamic-slice_fusion.7), channel_id=1, source_target_pairs={{0,8},{4,12},{8,0},{12,4},{16,24},{20,28},{24,16},{28,20},{1,9},{5... | collective-permute-start | bytes 2359304 | tf_op jit(solution)/shard_map/ppermute | solution.py:430
  313.8 14.5 %collective-permute-start.20 = (bf16[1,1,1,768,256]{4,3,2,1,0:T(8,128)(2,1)S(1)}, bf16[1,1,1,768,256]{4,3,2,1,0:T(8,128)(2,1)S(1)}, u32[]{:S(2)}, u32[]{:S(2)}) collective-permute-start(bf16[1,1,1,768,256]{4,3,2,1,0:T(8,128)(2,1)S(1)} %constant_dynamic-slice_fusion), channel_id=1, source_target_pairs={{0,16},{4,20},{8,24},{12,28},{16,0},{20,4},{24,8},{28,12},{1,17},{... | collective-permute-start | bytes 1179656 | tf_op jit(solution)/shard_map/ppermute | solution.py:430
  315.4 18.7 %collective-permute-start.17 = (bf16[1,1,1,256,768]{4,3,2,1,0:T(8,128)(2,1)S(1)}, bf16[1,1,1,256,768]{4,3,2,1,0:T(8,128)(2,1)S(1)}, u32[]{:S(2)}, u32[]{:S(2)}) collective-permute-start(bf16[1,1,1,256,768]{4,3,2,1,0:T(8,128)(2,1)S(1)} %constant_dynamic-slice_fusion.3), channel_id=1, source_target_pairs={{0,8},{4,12},{8,0},{12,4},{16,24},{20,28},{24,16},{28,20},{1,9},{5... | collective-permute-start | bytes 1179656 | tf_op jit(solution)/shard_map/ppermute | solution.py:430
  (39 other events, 243.1 us)
Sparse Core Ops, SparseCore 0:
  10.2 42.5 all-gather.1

commit v2 on v0

v2 whole, which is shorter than its diff:
```python
import functools
import math

import jax
import jax.numpy as jnp
from jax import lax
from jax.experimental import pallas as pl
from jax.experimental.pallas import tpu as pltpu
from jax.sharding import PartitionSpec as P

LOCAL_QUERY_HEADS = 16
LOCAL_KEY_HEADS = 2
HEAD_SIZE = 128
PIECE = 256
PARTS = 2

epsilon = 1e-06
masked_score = -1e30
F32 = jnp.float32
BF16 = jnp.bfloat16
VMEM_LIMIT = 60 << 20


def dot(a, b, contract=((1,), (0,))):
    return lax.dot_general(a, b, (contract, ((), ())), preferred_element_type=F32)


def iota(shape, dim):
    return lax.broadcasted_iota(jnp.int32, shape, dim)


def slots_row(ids_row, capacity):
    n = ids_row.shape[1]
    names = iota((16, n), 0).astype(F32)
    chosen = names == ids_row
    before = (iota((n, n), 0) < iota((n, n), 1)).astype(F32).astype(BF16)
    earlier = dot(jnp.where(chosen, 1.0, 0.0).astype(BF16), before)
    return jnp.sum(jnp.where(chosen, earlier + names * capacity, 0.0), axis=0, keepdims=True)


def slots_column(ids_column, capacity):
    n = ids_column.shape[0]
    names = iota((n, 128), 1).astype(F32)
    chosen = names == ids_column
    before = (iota((n, n), 1) < iota((n, n), 0)).astype(F32).astype(BF16)
    earlier = dot(before, jnp.where(chosen, 1.0, 0.0).astype(BF16))
    return jnp.sum(jnp.where(chosen, earlier + names * capacity, 0.0), axis=1, keepdims=True)


def one_hot(matches):
    return jnp.where(matches, 1.0, 0.0).astype(BF16)


def shifted_slots(position, owner, experts, capacity):
    expert = lax.rem(position // capacity + owner, experts)
    return (expert * capacity + lax.rem(position, capacity)).astype(F32)


def kernel_params():
    return pltpu.CompilerParams(vmem_limit_bytes=VMEM_LIMIT)


def whole(*shape):
    return pl.BlockSpec(shape, lambda *_: (0,) * len(shape))


def smem():
    return pl.BlockSpec(memory_space=pltpu.SMEM)


def attend_kernel(experts, capacity, heads, n_ctx, where_ref, q_ref, ids_ref, *refs):
    k_refs, refs = refs[:n_ctx], refs[n_ctx:]
    v_refs, refs = refs[:n_ctx], refs[n_ctx:]
    out_refs, refs = refs[: experts * PARTS], refs[experts * PARTS :]
    k_scr, v_scr, best_scr, acc_scr, att_scr = refs
    ctx, owner = where_ref[0], where_ref[1]
    seq = pl.program_id(0)
    block = q_ref.shape[1]
    tile = 2 * block
    factor = math.log2(math.e) / math.sqrt(HEAD_SIZE)

    @pl.when(seq == 0)
    def _():
        v_scr[:, :, HEAD_SIZE:] = jnp.ones((n_ctx, block, HEAD_SIZE), BF16)

    for m in range(n_ctx):
        index = jnp.bitwise_xor(ctx, m)
        k_scr[index] = k_refs[m][0]
        v_scr[index, :, :HEAD_SIZE] = v_refs[m][0]

    def fold(t, last):
        key_tile = k_scr[pl.ds(2 * t, 2)].reshape(tile, HEAD_SIZE)
        value_tile = v_scr[pl.ds(2 * t, 2)].reshape(tile, 2 * HEAD_SIZE)
        for h in range(heads):
            q = q_ref[0, :, h * HEAD_SIZE : (h + 1) * HEAD_SIZE]
            s = dot(q, key_tile, ((1,), (1,)))
            if last:
                key_pos = iota((block, tile), 1) + t * tile
                query_pos = iota((block, tile), 0) + ctx * block
                s = jnp.where(key_pos <= query_pos, s, masked_score)
            best = jnp.max(s, axis=1, keepdims=True)
            if not last:
                old = best_scr[h]
                best = jnp.maximum(old, best)
            p = jnp.exp2((s - best) * factor)
            blended = dot(p.astype(BF16), value_tile)
            if last:
                acc_scr[h] = blended
            else:
                acc_scr[h] = acc_scr[h] * jnp.exp2((old - best) * factor) + blended
            best_scr[h] = best

    fold(ctx // 2, True)

    @pl.loop(0, ctx // 2)
    def _(t):
        fold(t, False)

    for h in range(heads):
        acc = acc_scr[h]
        att = acc[:, :HEAD_SIZE] / acc[:, HEAD_SIZE:]
        att_scr[:, h * HEAD_SIZE : (h + 1) * HEAD_SIZE] = att.astype(BF16)

    n = ids_ref.shape[2]
    part = capacity // PARTS
    per_seq = block // n
    position = iota((experts * capacity, n), 0)
    slots = shifted_slots(position, owner, experts, capacity)
    for b in range(per_seq):
        source = seq * per_seq + b
        target = slots_row(ids_ref[lax.rem(owner - source + experts, experts)], capacity)
        picked = dot(one_hot(slots == target), att_scr[b * n : (b + 1) * n, :]).astype(BF16)
        for d in range(experts):
            rank = lax.rem(owner + d - source + experts, experts)
            for c in range(PARTS):
                first = d * capacity + c * part
                out_refs[c * experts + d][rank] = picked[first : first + part]


def attend(where, queries, keys, values, ids, capacity):
    seqs, block, width = queries.shape
    n_ctx = len(keys)
    experts, _, n = ids.shape
    heads = width // HEAD_SIZE
    part = capacity // PARTS
    by_seq = pl.BlockSpec((1, block, HEAD_SIZE), lambda s: (s, 0, 0))
    outs = pl.pallas_call(
        functools.partial(attend_kernel, experts, capacity, heads, n_ctx),
        grid=(seqs,),
        in_specs=[
            smem(),
            pl.BlockSpec((1, block, width), lambda s: (s, 0, 0)),
            whole(experts, 1, n),
        ]
        + [by_seq] * (2 * n_ctx),
        out_specs=[whole(experts, part, width)] * (PARTS * experts),
        scratch_shapes=[
            pltpu.VMEM((n_ctx, block, HEAD_SIZE), BF16),
            pltpu.VMEM((n_ctx, block, 2 * HEAD_SIZE), BF16),
            pltpu.VMEM((heads, block, 1), F32),
            pltpu.VMEM((heads, block, 2 * HEAD_SIZE), F32),
            pltpu.VMEM((block, width), BF16),
        ],
        out_shape=[jax.ShapeDtypeStruct((experts, part, width), BF16)] * (PARTS * experts),
        compiler_params=kernel_params(),
        cost_estimate=pl.CostEstimate(
            flops=4 * seqs * block * block * n_ctx * width,
            bytes_accessed=8 << 20,
            transcendentals=seqs * heads * block * block * n_ctx,
        ),
        name="attend",
    )(where, queries, ids, *keys, *values)
    return [outs[c * experts : (c + 1) * experts] for c in range(PARTS)]


def place_kernel(experts, capacity, where_ref, ids_ref, rows_ref, *refs):
    out_refs, pick_scr = refs[:-1], refs[-1]

    @pl.when(pl.program_id(0) == 0)
    def _():
        position = iota(pick_scr.shape, 0)
        slots = shifted_slots(position, where_ref[1], experts, capacity)
        pick_scr[...] = one_hot(slots == slots_row(ids_ref[...], capacity))

    picked = dot(pick_scr[...], rows_ref[...]).astype(BF16)
    for d, ref in enumerate(out_refs):
        ref[...] = picked[d * capacity : (d + 1) * capacity]


def place(where, ids_row, rows, experts, capacity):
    n, width = rows.shape
    cols = min(width, 1024)
    return pl.pallas_call(
        functools.partial(place_kernel, experts, capacity),
        grid=(width // cols,),
        in_specs=[smem(), whole(1, n), pl.BlockSpec((n, cols), lambda i: (0, i))],
        out_specs=[pl.BlockSpec((capacity, cols), lambda i: (0, i))] * experts,
        out_shape=[jax.ShapeDtypeStruct((capacity, width), BF16)] * experts,
        scratch_shapes=[pltpu.VMEM((experts * capacity, n), BF16)],
        compiler_params=kernel_params(),
        name="place",
    )(where, ids_row, rows)


def restore_kernel(experts, capacity, tiles, where_ref, ids_ref, *refs):
    parts, refs = refs[: experts * PARTS], refs[experts * PARTS :]
    layer_ref, grad_ref, pick_scr = refs
    step = pl.program_id(0)

    @pl.when(step == 0)
    def _():
        slots = shifted_slots(iota(pick_scr.shape, 1), where_ref[1], experts, capacity)
        pick_scr[...] = one_hot(slots == slots_column(ids_ref[...], capacity))

    rows = jnp.concatenate([ref[...] for ref in parts], axis=0)
    out = dot(pick_scr[...], rows).astype(BF16)

    @pl.when(step < tiles)
    def _():
        layer_ref[...] = out

    @pl.when(step >= tiles)
    def _():
        grad_ref[...] = out


def restore(where, ids_column, parts, experts, capacity):
    n = ids_column.shape[0]
    part, both = parts[0][0].shape
    width = both // 2
    cols = min(width, 1024)
    tiles = width // cols
    return pl.pallas_call(
        functools.partial(restore_kernel, experts, capacity, tiles),
        grid=(2 * tiles,),
        in_specs=[smem(), whole(n, 1)]
        + [pl.BlockSpec((part, cols), lambda i: (0, i))] * (experts * PARTS),
        out_specs=[
            pl.BlockSpec((n, cols), lambda i: (0, jnp.minimum(i, tiles - 1))),
            pl.BlockSpec((n, cols), lambda i: (0, jnp.maximum(i - tiles, 0))),
        ],
        out_shape=[jax.ShapeDtypeStruct((n, width), BF16)] * 2,
        scratch_shapes=[pltpu.VMEM((n, experts * capacity), BF16)],
        compiler_params=kernel_params(),
        name="restore",
    )(where, ids_column, *[parts[c][d] for d in range(experts) for c in range(PARTS)])


def expert_kernel(pieces, experts, capacity, part_index, where_ref, *refs):
    att_refs, refs = refs[:experts], refs[experts:]
    grad_refs, refs = refs[:experts], refs[experts:]
    wa_refs, refs = refs[:pieces], refs[pieces:]
    wb_refs, refs = refs[:pieces], refs[pieces:]
    gate_hbm, up_hbm, down_hbm, gain_ref, ids_ref, weight_ref = refs[:6]
    refs = refs[6:]
    out_refs, refs = refs[:experts], refs[experts:]
    normed_ref, back_ref, units_ref, back_gate_ref, back_up_ref = refs[:5]
    w_scr, gate_scr, up_scr, down_scr, hidden_scr, back_in_scr, sems = refs[5:]
    part, width = grad_refs[0].shape
    rows = experts * part
    att_cols = att_refs[0].shape[2]
    half, piece = wa_refs[0].shape
    ff = units_ref.shape[1]
    piece_index, owner = where_ref[2], where_ref[1]

    copies = []
    for m in range(pieces):
        copies.append(
            (
                pltpu.make_async_copy(wa_refs[m], w_scr.at[m, pl.ds(0, half)], sems.at[2 * m]),
                pltpu.make_async_copy(
                    wb_refs[m], w_scr.at[m, pl.ds(half, half)], sems.at[2 * m + 1]
                ),
            )
        )
    first = 2 * pieces
    weight_copies = (
        pltpu.make_async_copy(gate_hbm.at[0], gate_scr, sems.at[first]),
        pltpu.make_async_copy(up_hbm.at[0], up_scr, sems.at[first + 1]),
        pltpu.make_async_copy(down_hbm.at[0], down_scr, sems.at[first + 2]),
    )
    for pair in copies:
        for copy in pair:
            copy.start()
    for copy in weight_copies:
        copy.start()

    n = ids_ref.shape[2]
    weights = []
    for s in range(experts):
        target = slots_row(ids_ref[s], capacity)
        slot = iota((part, n), 0) + (owner * capacity + part_index * part)
        weights.append(
            jnp.sum(
                jnp.where(slot.astype(F32) == target, weight_ref[s], 0.0), axis=1, keepdims=True
            )
        )
        grads = grad_refs[s][...].astype(F32)
        back_ref[s * part : (s + 1) * part, :] = (weights[s] * grads).astype(BF16)

    for m in range(pieces):
        for copy in copies[m]:
            copy.wait()
        total = jnp.zeros((rows, piece), F32)
        for d in range(experts):
            source = lax.rem(owner - d + experts, experts)
            at = pl.multiple_of(source * att_cols, att_cols)
            total += dot(
                att_refs[d][...].reshape(rows, att_cols), w_scr[m, pl.ds(at, att_cols), :]
            )
        column = pl.multiple_of(jnp.bitwise_xor(piece_index, m) * piece, piece)
        hidden_scr[:, pl.ds(column, piece)] = total.astype(BF16)

    squares = jnp.zeros((rows, 1), F32)
    for t in range(0, width, PIECE):
        hidden = hidden_scr[:, t : t + PIECE].astype(F32)
        squares += jnp.sum(hidden * hidden, axis=1, keepdims=True)
    inv = lax.rsqrt(squares / width + epsilon)
    for t in range(0, width, PIECE):
        hidden = hidden_scr[:, t : t + PIECE].astype(F32)
        normed_ref[:, t : t + PIECE] = (hidden * inv * gain_ref[:, t : t + PIECE]).astype(BF16)

    for copy in weight_copies:
        copy.wait()
    for f in range(0, ff, 256):
        gate_act = dot(normed_ref[...], gate_scr[:, f : f + 256])
        up_act = dot(normed_ref[...], up_scr[:, f : f + 256])
        back_units = dot(back_ref[...], down_scr[f : f + 256, :], ((1,), (1,)))
        sigma = 1.0 / (1.0 + jnp.exp(-gate_act))
        gated = gate_act * sigma
        units_ref[:, f : f + 256] = (gated * up_act).astype(BF16)
        back_gate = back_units * up_act * sigma * (1.0 + gate_act * (1.0 - sigma))
        back_gate_ref[:, f : f + 256] = back_gate.astype(BF16)
        back_up_ref[:, f : f + 256] = (back_units * gated).astype(BF16)

    weight = jnp.concatenate(weights, axis=0)
    moment = jnp.zeros((rows, 1), F32)
    for t in range(0, width, PIECE):
        hidden = hidden_scr[:, t : t + PIECE].astype(F32)
        result = dot(units_ref[...], down_scr[:, t : t + PIECE]).astype(BF16).astype(F32)
        layer = (hidden + weight * result).astype(BF16)
        for s in range(experts):
            out_refs[s][:, t : t + PIECE] = layer[s * part : (s + 1) * part]
        back_in = dot(back_gate_ref[...], gate_scr[t : t + PIECE, :], ((1,), (1,)))
        back_in += dot(back_up_ref[...], up_scr[t : t + PIECE, :], ((1,), (1,)))
        back_in = back_in.astype(BF16)
        back_in_scr[:, t : t + PIECE] = back_in
        scaled = back_in.astype(F32) * gain_ref[:, t : t + PIECE]
        moment += jnp.sum(scaled * (hidden * inv), axis=1, keepdims=True)
    moment = moment / width
    for t in range(0, width, PIECE):
        unit = hidden_scr[:, t : t + PIECE].astype(F32) * inv
        scaled = back_in_scr[:, t : t + PIECE].astype(F32) * gain_ref[:, t : t + PIECE]
        change = inv * (scaled - unit * moment)
        for s in range(experts):
            grads = grad_refs[s][:, t : t + PIECE].astype(F32)
            out_refs[s][:, width + t : width + t + PIECE] = (
                grads + change[s * part : (s + 1) * part]
            ).astype(BF16)


def expert_part(where, att, grads, wa, wb, gate, up, down, gain, ids, weights, capacity, index):
    experts, part, att_cols = att[0].shape
    pieces = len(wa)
    half, piece = wa[0].shape
    width = grads[0].shape[1]
    ff = gate.shape[2]
    rows = experts * part
    n = ids.shape[2]
    out = lambda *shape: jax.ShapeDtypeStruct(shape, BF16)
    in_hbm = pl.BlockSpec(memory_space=pl.ANY)
    outs = pl.pallas_call(
        functools.partial(expert_kernel, pieces, experts, capacity, index),
        grid=(1,),
        in_specs=[smem()]
        + [whole(experts, part, att_cols)] * experts
        + [pl.BlockSpec((part, width), lambda i: (index, 0))] * experts
        + [in_hbm] * (2 * pieces + 3)
        + [whole(1, width), whole(experts, 1, n), whole(experts, 1, n)],
        out_specs=[whole(part, 2 * width)] * experts
        + [whole(rows, width)] * 2
        + [whole(rows, ff)] * 3,
        scratch_shapes=[
            pltpu.VMEM((pieces, 2 * half, piece), BF16),
            pltpu.VMEM((width, ff), BF16),
            pltpu.VMEM((width, ff), BF16),
            pltpu.VMEM((ff, width), BF16),
            pltpu.VMEM((rows, width), BF16),
            pltpu.VMEM((rows, width), BF16),
            pltpu.SemaphoreType.DMA((2 * pieces + 3,)),
        ],
        out_shape=[out(part, 2 * width)] * experts + [out(rows, width)] * 2 + [out(rows, ff)] * 3,
        compiler_params=kernel_params(),
        cost_estimate=pl.CostEstimate(
            flops=2 * rows * width * (width + 6 * ff),
            bytes_accessed=2 * (width * width + 3 * width * ff + 8 * rows * width),
            transcendentals=rows * ff,
        ),
        name="expert",
    )(where, *att, *grads, *wa, *wb, gate, up, down, gain, ids, weights)
    return outs[:experts], outs[experts:]


def weight_kernel(count, lead, *refs):
    normed, back, units, back_gate, back_up = [refs[i * count : (i + 1) * count] for i in range(5)]
    outs = refs[5 * count :]
    first = ((0,), (0,))
    gate = up = down = 0.0
    for c in range(count):
        gate += dot(normed[c][...], back_gate[c][...], first)
        up += dot(normed[c][...], back_up[c][...], first)
        down += dot(units[c][...], back[c][...], first)

    def put(gate_ref, up_ref, down_ref):
        gate_ref[0] = gate.astype(BF16)
        up_ref[0] = up.astype(BF16)
        down_ref[0] = down.astype(BF16)

    if len(outs) == 3:
        put(*outs)
        return

    @pl.when(pl.program_id(0) < lead)
    def _():
        put(*outs[:3])

    @pl.when(pl.program_id(0) >= lead)
    def _():
        put(*outs[3:])


def weight_parts(where, normed, back, units, back_gate, back_up, exchange):
    count = len(normed)
    rows, width = normed[0].shape
    ff = units[0].shape[1]
    cols = PIECE
    blocks = width // cols
    lead = blocks // 2 if exchange else blocks

    def block_of(i, where_ref):
        if not exchange:
            return i
        mask = jnp.where(i < lead, 2 * i + 1, 2 * (i - lead))
        return jnp.bitwise_xor(where_ref[0], mask)

    thin = [pl.BlockSpec((rows, cols), lambda i, w: (0, block_of(i, w)))] * count
    full = [pl.BlockSpec((rows, ff), lambda i, w: (0, 0))] * count
    early = lambda i, w: (jnp.minimum(i, lead - 1), 0, 0)
    late = lambda i, w: (jnp.maximum(i - lead, 0), 0, 0)
    shapes = [(cols, ff), (cols, ff), (ff, cols)]
    groups = [early, late] if exchange else [early]
    kernel = lambda where_ref, *refs: weight_kernel(count, lead, *refs)
    outs = pl.pallas_call(
        kernel,
        grid_spec=pltpu.PrefetchScalarGridSpec(
            num_scalar_prefetch=1,
            grid=(blocks,),
            in_specs=thin + thin + full + full + full,
            out_specs=[pl.BlockSpec((1,) + shape, at) for at in groups for shape in shapes],
        ),
        out_shape=[jax.ShapeDtypeStruct((lead,) + shape, BF16) for _ in groups for shape in shapes],
        compiler_params=kernel_params(),
        cost_estimate=pl.CostEstimate(
            flops=6 * count * rows * width * ff,
            bytes_accessed=2 * (3 * width * ff + 2 * count * rows * (width + 2 * ff)),
            transcendentals=0,
        ),
        name="weight_grads",
    )(where, *normed, *back, *units, *back_gate, *back_up)
    return outs[:3], outs[3:]


def partner(value, bit):
    count = lax.axis_size("ctx")
    return lax.ppermute(value, "ctx", [(i, i ^ (1 << bit)) for i in range(count)])


def shift(value, by):
    count = lax.axis_size("exp")
    return lax.ppermute(value, "exp", [(i, (i + by) % count) for i in range(count)])


def spread(value, order):
    held = {0: value}
    for bit in order:
        for m in list(held):
            held[m | 1 << bit] = partner(held[m], bit)
    return [held[m] for m in sorted(held)]


def halved(value, bits, order, ctx):
    shape = value.shape[1:]
    held = value.reshape((2,) * bits + shape)
    for place_in_order, bit in enumerate(order):
        axis = bits - 1 - bit
        mine = (ctx >> bit) & 1
        gone = lax.dynamic_slice_in_dim(held, 1 - mine, 1, axis)
        kept = lax.dynamic_slice_in_dim(held, mine, 1, axis)
        held = kept.astype(F32) + partner(gone, bit).astype(F32)
        if place_in_order < bits - 1:
            held = held.astype(BF16)
    return held.reshape(shape)


def halved_relative(gone, kept, bits, order):
    shape = kept.shape[1:]
    arrived = partner(gone, 0).astype(F32).reshape((2,) * (bits - 1) + shape)
    held = kept.astype(F32).reshape((2,) * (bits - 1) + shape)
    for bit in order:
        axis = bits - 1 - bit
        take = lambda x, i: lax.slice_in_dim(x, i, i + 1, axis=axis)
        gone = (take(held, 1) + take(arrived, 1)).astype(BF16)
        held = (take(held, 0) + take(arrived, 0)).astype(BF16).astype(F32)
        arrived = partner(gone, bit).astype(F32)
    return (held + arrived).reshape(shape)


def on_device(
    queries,
    rotated_key_heads,
    value_head_rows,
    out_proj,
    norm_gain,
    expert_ids,
    gate_weights,
    expert_gate,
    expert_up,
    expert_down,
    grad_out,
):
    heads_dev = queries.shape[2] // HEAD_SIZE
    group = LOCAL_QUERY_HEADS // LOCAL_KEY_HEADS
    exp_count = lax.axis_size("exp")
    ctx_count = lax.axis_size("ctx")
    owner = lax.axis_index("exp")
    ctx = lax.axis_index("ctx")
    bits = ctx_count.bit_length() - 1
    n, _ = expert_ids.shape
    width = grad_out.shape[1]
    experts = exp_count
    capacity = min(n, 2 * n // experts)
    pieces = min(ctx_count, width // PIECE)
    piece_bits = pieces.bit_length() - 1
    piece = width // pieces
    piece_index = ctx % pieces
    where = jnp.stack([ctx, owner, piece_index]).astype(jnp.int32)

    first_column = (owner * heads_dev // group) * HEAD_SIZE
    low, high = list(range(1, bits)) + [0], list(range(bits - 1, 0, -1)) + [0]
    keys = lax.dynamic_slice_in_dim(rotated_key_heads, first_column, HEAD_SIZE, 2)
    values = lax.dynamic_slice_in_dim(value_head_rows, first_column, HEAD_SIZE, 2)
    keys = spread(keys, low)
    values = spread(values, high)

    ids_f = expert_ids.astype(F32)
    info = jnp.stack([ids_f[:, 0], gate_weights[:, 0]])
    info = jnp.stack([info] + [shift(info, d) for d in range(1, experts)])
    ids_all, weights_all = info[:, 0:1, :], info[:, 1:2, :]

    grads = place(where, ids_f.reshape(1, n), grad_out, experts, capacity)
    grads = [grads[0]] + [shift(grads[d], d) for d in range(1, experts)]

    mine = lax.dynamic_slice_in_dim(out_proj, piece_index * piece, piece, 1)
    mine = lax.all_gather(mine, "exp", axis=0, tiled=True)
    half = mine.shape[0] // 2
    mine, keys, values = lax.optimization_barrier((mine, keys, values))
    wa = spread(mine[:half], [b for b in low if b < piece_bits])
    wb = spread(mine[half:], [b for b in high if b < piece_bits])

    attended = attend(where, queries, keys, values, ids_all, capacity)
    returned, kept = [], []
    for index, sent in enumerate(attended):
        arrived = [sent[0]] + [shift(sent[d], d) for d in range(1, experts)]
        rows, saved = expert_part(
            where,
            arrived,
            grads,
            wa,
            wb,
            expert_gate,
            expert_up,
            expert_down,
            norm_gain.reshape(1, width),
            ids_all,
            weights_all,
            capacity,
            index,
        )
        returned.append([rows[0]] + [shift(rows[d], -d) for d in range(1, experts)])
        kept.append(saved)

    rows_dev = width // ctx_count
    exchange = rows_dev == PIECE
    gone, stay = weight_parts(where, *zip(*kept), exchange)
    if exchange:
        orders = low[:-1], high[:-1], low[:-1]
        grad_gate, grad_up, grad_down = [
            halved_relative(g, s, bits, order)[None] for g, s, order in zip(gone, stay, orders)
        ]
    else:
        ff = expert_gate.shape[2]
        part_gate, part_up = [x.reshape(ctx_count, rows_dev, ff) for x in gone[:2]]
        part_down = gone[2].reshape(width // PIECE, ff, PIECE // rows_dev, rows_dev)
        part_down = part_down.transpose(0, 2, 1, 3).reshape(ctx_count, ff, rows_dev)
        core_low, core_high = [0] + low[:-1], [0] + high[:-1]
        grad_gate = halved(part_gate, bits, core_low, ctx)[None]
        grad_up = halved(part_up, bits, core_high, ctx)[None]
        grad_down = halved(part_down, bits, core_low, ctx)[None]

    layer_out, grad_hidden = restore(where, ids_f, returned, experts, capacity)
    return (layer_out, grad_hidden, grad_gate, grad_up, grad_down)


def solution(mesh):
    in_specs = (
        P(None, "ctx", "exp"),
        P(None, "ctx", None),
        P(None, "ctx", None),
        P("exp", None),
        P(),
        P(("ctx", "exp"), None),
        P(("ctx", "exp"), None),
        P("exp", None, None),
        P("exp", None, None),
        P("exp", None, None),
        P(("ctx", "exp"), None),
    )
    out_specs = (
        P(("ctx", "exp"), None),
        P(("ctx", "exp"), None),
        P("exp", "ctx", None),
        P("exp", "ctx", None),
        P("exp", None, "ctx"),
    )
    return jax.shard_map(
        on_device, mesh=mesh, in_specs=in_specs, out_specs=out_specs, check_vma=False
    )
```

time: 478 us -> 330 us (0.69)
  waiting for transfers between devices: 297 us -> 164 us
  matrix products: 93 us -> 0 us
  Pallas kernels: 0 us -> 80.4 us
  starting transfers between devices: 25.8 us -> 39.5 us
  loops' own time: 8.28 us -> 0 us
  other arithmetic: 21.9 us -> 14.8 us
    ppermute x0 -> x55, waiting for transfers between devices: none -> 164 us  [the longest x18 127 us: shift(): lax.ppermute(value, 'exp', [(i, (i + by) % count) for i in range(count)])]
    reduce_scatter x4 -> x0, waiting for transfers between devices: 129 us -> none  [the longest x1 110 us: on_device(): lax.psum_scatter(jnp.dot(flat_heads, out_proj, preferred_element_type=jnp...]
    all_to_all x4 -> x0, waiting for transfers between devices: 114 us -> none  [the longest x1 40 us: on_device(): lax.all_to_all(result.reshape(experts, capacity, dmodel), 'exp', split_ax...]
    dot_general x22 -> x0, matrix products: 93 us -> none  [the longest x4 16.9 us: compute(): jnp.einsum('sgrqk,skgd->sgrqd', weights.astype(jnp.bfloat16), value_sub,...]
    pallas_call x0 -> x6, Pallas kernels: none -> 80.4 us  [the longest x2 32.7 us: expert_part(): pl.pallas_call(functools.partial(expert_kernel, pieces, experts, capacity...]
    all_gather x2 -> x1, waiting for transfers between devices: 52.8 us -> 0.01 us  [on_device(): mine = lax.all_gather(mine, 'exp', axis=0, tiled=True)]
    ppermute x0 -> x55, starting transfers between devices: none -> 39.5 us  [the longest x18 22.1 us: shift(): lax.ppermute(value, 'exp', [(i, (i + by) % count) for i in range(count)])]
    all_to_all x4 -> x0, starting transfers between devices: 25.4 us -> none  [the longest x1 7.88 us: on_device(): lax.all_to_all(back_in.reshape(experts, capacity, dmodel), 'exp', split_a...]
  transfers between devices with their start and end apart: 10 -> 56, of which waited for: 7 -> 23; matrix products, arithmetic and copies ran while one was open for 13% -> 5% of each run, Pallas kernels for 0% -> 16%
where the time goes in v2:
time: 330 us; the launch traced here: 324 us
  waiting for transfers between devices  164 us (50%)
  Pallas kernels  80.4 us (24%)
  starting transfers between devices  39.5 us (12%)
  other arithmetic  14.8 us (4%)
  between operations  14.8 us (4%)
  local copies, waits for them, and re-layouts  10.7 us (3%)
    ppermute x18, waiting for transfers between devices, shift(): lax.ppermute(value, 'exp', [(i, (i + by) % count) for i in range(count)])  127 us
    ppermute x37, waiting for transfers between devices, partner(): return lax.ppermute(value, 'ctx', [(i, i ^ 1 << bit) for i in range(count)])  37.2 us
    pallas_call x2, Pallas kernels, expert_part(): pl.pallas_call(functools.partial(expert_kernel, pieces, experts, capacity...  32.7 us
    pallas_call x1, Pallas kernels, attend(): pl.pallas_call(functools.partial(attend_kernel, experts, capacity, heads,...  25.4 us
    ppermute x18, starting transfers between devices, shift(): lax.ppermute(value, 'exp', [(i, (i + by) % count) for i in range(count)])  22.1 us
    ppermute x37, starting transfers between devices, partner(): return lax.ppermute(value, 'ctx', [(i, i ^ 1 << bit) for i in range(count)])  17.4 us
    pallas_call x1, Pallas kernels, weight_parts(): pl.pallas_call(kernel, grid_spec=pltpu.PrefetchScalarGridSpec(num_scalar_...  13.3 us
    unnamed x119, local copies, waits for them, and re-layouts  8.28 us
  transfers between devices with their start and end apart: 56, of which 23 were waited for; matrix products, arithmetic and copies ran while one was open for 5% of the time, Pallas kernels for 16%

profile of v2, /device:TPU:22, one launch (start us, length us, event | category | flops | bytes accessed | tf_op | source)
XLA Modules:
  0.0 324.2 jit_solution(4101191113610051695)
XLA Ops:
  14.0 4.1 %collective-permute-done.1 = f32[2,256]{1,0:T(2,128)S(1)} collective-permute-done((f32[2,256]{1,0:T(2,128)S(1)}, f32[2,256]{1,0:T(2,128)S(1)}, u32[]{:S(2)}, u32[]{:S(2)}) %collective-permute-start.1) | collective-permute-done | bytes 2080 | tf_op jit(solution)/shard_map/ppermute | solution.py:480
  22.2 3.3 %collective-permute-done.2 = f32[2,256]{1,0:T(2,128)S(1)} collective-permute-done((f32[2,256]{1,0:T(2,128)S(1)}, f32[2,256]{1,0:T(2,128)S(1)}, u32[]{:S(2)}, u32[]{:S(2)}) %collective-permute-start.2) | collective-permute-done | bytes 2080 | tf_op jit(solution)/shard_map/ppermute | solution.py:480
  28.9 3.1 place.1
  38.9 3.2 collective-permute-start.20
  44.8 25.4 %attend.1 = (bf16[4,64,512]{2,1,0:T(8,128)(2,1)}, bf16[4,64,512]{2,1,0:T(8,128)(2,1)}, bf16[4,64,512]{2,1,0:T(8,128)(2,1)}, bf16[4,64,512]{2,1,0:T(8,128)(2,1)},...) custom-call(s32[3]{0:T(128)} %pad_add_fusion.where_ref, ...), custom_call_target="tpu_custom_call" | custom-call | flops 4294967296 | bytes 8388608 | tf_op jit(solution)/shard_map/attend/pallas_call | solution.py:147
  73.7 3.0 collective-permute-done.21.refs_6_
  77.2 21.8 %collective-permute-done.22.refs_7_ = bf16[128,2048]{1,0:T(8,128)(2,1)S(1)} collective-permute-done((bf16[128,2048]{1,0:T(8,128)(2,1)}, bf16[128,2048]{1,0:T(8,128)(2,1)S(1)}, u32[]{:S(2)}, u32[]{:S(2)}) %collective-permute-start.22) | collective-permute-done | bytes 524320 | tf_op jit(solution)/shard_map/ppermute | solution.py:480
  99.6 5.0 %collective-permute-done.38.refs_2_ = bf16[4,64,512]{2,1,0:T(8,128)(2,1)S(1)} collective-permute-done((bf16[4,64,512]{2,1,0:T(8,128)(2,1)}, bf16[4,64,512]{2,1,0:T(8,128)(2,1)S(1)}, u32[]{:S(2)}, u32[]{:S(2)}) %collective-permute-start.38) | collective-permute-done | bytes 262176 | tf_op jit(solution)/shard_map/ppermute | solution.py:480
  104.6 8.4 %collective-permute-done.39.refs_3_ = bf16[4,64,512]{2,1,0:T(8,128)(2,1)} collective-permute-done((bf16[4,64,512]{2,1,0:T(8,128)(2,1)S(1)}, bf16[4,64,512]{2,1,0:T(8,128)(2,1)}, u32[]{:S(2)}, u32[]{:S(2)}) %collective-permute-start.39) | collective-permute-done | bytes 262176 | tf_op jit(solution)/shard_map/ppermute | solution.py:480
  115.8 12.0 %collective-permute-done.26.refs_12_ = bf16[1024,256]{1,0:T(8,128)(2,1)S(1)} collective-permute-done((bf16[1024,256]{1,0:T(8,128)(2,1)S(1)}, bf16[1024,256]{1,0:T(8,128)(2,1)S(1)}, u32[]{:S(2)}, u32[]{:S(2)}) %collective-permute-start.26) | collective-permute-done | bytes 524320 | tf_op jit(solution)/shard_map/ppermute | solution.py:475
  129.5 7.8 %collective-permute-done.28.refs_14_ = bf16[1024,256]{1,0:T(8,128)(2,1)S(1)} collective-permute-done((bf16[1024,256]{1,0:T(8,128)(2,1)S(1)}, bf16[1024,256]{1,0:T(8,128)(2,1)S(1)}, u32[]{:S(2)}, u32[]{:S(2)}) %collective-permute-start.28) | collective-permute-done | bytes 524320 | tf_op jit(solution)/shard_map/ppermute | solution.py:475
  137.4 3.4 %collective-permute-start.17 = (bf16[4,64,512]{2,1,0:T(8,128)(2,1)}, bf16[4,64,512]{2,1,0:T(8,128)(2,1)}, u32[]{:S(2)}, u32[]{:S(2)}) collective-permute-start(bf16[4,64,512]{2,1,0:T(8,128)(2,1)} %get-tuple-element.77), channel_id=1, source_target_pairs={{0,1},{1,2},{2,3},{3,0},{4,5},{5,6},{6,7},{7,4},{8,9},{9,10},{10,1... | collective-permute-start | bytes 786440 | tf_op jit(solution)/shard_map/ppermute | solution.py:480
  140.8 3.1 collective-permute-start.19
  144.9 16.3 %expert.3 = (bf16[64,4096]{1,0:T(8,128)(2,1)}, bf16[64,4096]{1,0:T(8,128)(2,1)}, bf16[64,4096]{1,0:T(8,128)(2,1)}, bf16[64,4096]{1,0:T(8,128)(2,1)}, bf16[256,20...) custom-call(s32[3]{0:T(128)} %pad_add_fusion.where_ref, ...), custom_call_target="tpu_custom_call" | custom-call | flops 6979321856 | bytes 26214400 | tf_op jit(solution)/shard_map/expert/pallas_call | solution.py:372
  164.1 16.4 %expert.2 = (bf16[64,4096]{1,0:T(8,128)(2,1)}, bf16[64,4096]{1,0:T(8,128)(2,1)}, bf16[64,4096]{1,0:T(8,128)(2,1)}, bf16[64,4096]{1,0:T(8,128)(2,1)}, bf16[256,20...) custom-call(s32[3]{0:T(128)} %pad_add_fusion.where_ref, ...), custom_call_target="tpu_custom_call" | custom-call | flops 6979321856 | bytes 26214400 | tf_op jit(solution)/shard_map/expert/pallas_call | solution.py:372
  180.5 13.3 %weight_grads.1 = (bf16[4,256,768]{2,1,0:T(8,128)(2,1)}, bf16[4,256,768]{2,1,0:T(8,128)(2,1)}, bf16[4,768,256]{2,1,0:T(8,128)(2,1)}, bf16[4,256,768]{2,1,0:T(8,1...) custom-call(s32[3]{0:T(128)} %pad_add_fusion.where_ref, ...), custom_call_target="tpu_custom_call" | custom-call | flops 4831838208 | bytes 16777216 | tf_op jit(solution)/shard_map/weight_grads/pallas_call | solution.py:453
  207.5 24.6 %collective-permute-done.41.refs_3_ = bf16[64,4096]{1,0:T(8,128)(2,1)S(1)} collective-permute-done((bf16[64,4096]{1,0:T(8,128)(2,1)}, bf16[64,4096]{1,0:T(8,128)(2,1)S(1)}, u32[]{:S(2)}, u32[]{:S(2)}) %collective-permute-start.41) | collective-permute-done | bytes 524320 | tf_op jit(solution)/shard_map/ppermute | solution.py:480
  232.1 22.5 %collective-permute-done.43.refs_5_ = bf16[64,4096]{1,0:T(8,128)(2,1)S(1)} collective-permute-done((bf16[64,4096]{1,0:T(8,128)(2,1)}, bf16[64,4096]{1,0:T(8,128)(2,1)S(1)}, u32[]{:S(2)}, u32[]{:S(2)}) %collective-permute-start.43) | collective-permute-done | bytes 524320 | tf_op jit(solution)/shard_map/ppermute | solution.py:480
  254.6 11.7 %collective-permute-done.45.refs_7_ = bf16[64,4096]{1,0:T(8,128)(2,1)S(1)} collective-permute-done((bf16[64,4096]{1,0:T(8,128)(2,1)S(1)}, bf16[64,4096]{1,0:T(8,128)(2,1)S(1)}, u32[]{:S(2)}, u32[]{:S(2)}) %collective-permute-start.45) | collective-permute-done | bytes 524320 | tf_op jit(solution)/shard_map/ppermute | solution.py:480
  269.6 7.4 %collective-permute-done.40.refs_2_ = bf16[64,4096]{1,0:T(8,128)(2,1)S(1)} collective-permute-done((bf16[64,4096]{1,0:T(8,128)(2,1)S(1)}, bf16[64,4096]{1,0:T(8,128)(2,1)S(1)}, u32[]{:S(2)}, u32[]{:S(2)}) %collective-permute-start.40) | collective-permute-done | bytes 524320 | tf_op jit(solution)/shard_map/ppermute | solution.py:480
  278.1 9.6 %collective-permute-done.42.refs_4_ = bf16[64,4096]{1,0:T(8,128)(2,1)S(1)} collective-permute-done((bf16[64,4096]{1,0:T(8,128)(2,1)S(1)}, bf16[64,4096]{1,0:T(8,128)(2,1)S(1)}, u32[]{:S(2)}, u32[]{:S(2)}) %collective-permute-start.42) | collective-permute-done | bytes 524320 | tf_op jit(solution)/shard_map/ppermute | solution.py:480
  289.5 5.9 %restore.1 = (bf16[256,2048]{1,0:T(8,128)(2,1)}, bf16[256,2048]{1,0:T(8,128)(2,1)}) custom-call(s32[3]{0:T(128)} %pad_add_fusion.where_ref, f32[256,1]{1,0:T(8,128)} %convert_element_type.92.ids_ref, bf16[64,4096]{1,0:T(8,128)(2,1)} %get-tuple-element.85.refs_0_, bf16[64,4096]{1,0:T(8,128)(2,1)} %get-tuple-element.90.refs_1_, bf16[64,4096]{1,0:T(8,128)(2,1)} %copy-done.11, ...), custom_call_target="tpu_custom_call" | custom-call | tf_op jit(solution)/shard_map/restore/pallas_call | solution.py:233
  302.2 6.5 %collective-permute-done.48 = bf16[1,1,256,768]{3,2,1,0:T(8,128)(2,1)S(1)} collective-permute-done((bf16[1,1,256,768]{3,2,1,0:T(8,128)(2,1)S(1)}, bf16[1,1,256,768]{3,2,1,0:T(8,128)(2,1)S(1)}, u32[]{:S(2)}, u32[]{:S(2)}) %collective-permute-start.48) | collective-permute-done | bytes 393248 | tf_op jit(solution)/shard_map/ppermute | solution.py:475
  311.7 4.7 %collective-permute-done.54 = bf16[1,1,768,256]{3,2,1,0:T(8,128)(2,1)S(1)} collective-permute-done((bf16[1,1,768,256]{3,2,1,0:T(8,128)(2,1)S(1)}, bf16[1,1,768,256]{3,2,1,0:T(8,128)(2,1)S(1)}, u32[]{:S(2)}, u32[]{:S(2)}) %collective-permute-start.54) | collective-permute-done | bytes 393248 | tf_op jit(solution)/shard_map/ppermute | solution.py:475
  (242 shorter events, 66.8 us)
Async XLA Ops:
  7.2 37.6 %all-gather.2.cloned.1.call-start = ((), (), s32[]{:S(2)}) async-start(), calls=%async_computation | async-start | bytes 1310720 | tf_op jit(solution)/shard_map/all_gather | solution.py:564
  10.6 16.3 %collective-permute-start.13 = (bf16[4,256,128]{2,1,0:T(8,128)(2,1)S(1)}, bf16[4,256,128]{2,1,0:T(8,128)(2,1)S(1)}, u32[]{:S(2)}, u32[]{:S(2)}) collective-permute-start(bf16[4,256,128]{2,1,0:T(8,128)(2,1)S(1)} %constant_dynamic-slice_fusion.refs_8_), channel_id=1, source_target_pairs={{0,16},{4,20},{8,24},{12,28},{16,0},{20,4},{24,8},{28,12},{1,17},{... | collective-permute-start | bytes 786440 | tf_op jit(solution)/shard_map/ppermute | solution.py:475
  38.9 34.7 %collective-permute-start.20 = (bf16[128,2048]{1,0:T(8,128)(2,1)}, bf16[128,2048]{1,0:T(8,128)(2,1)S(1)}, u32[]{:S(2)}, u32[]{:S(2)}) collective-permute-start(bf16[128,2048]{1,0:T(8,128)(2,1)} %get-tuple-element.81), channel_id=1, source_target_pairs={{0,1},{1,2},{2,3},{3,0},{4,5},{5,6},{6,7},{7,4},{8,9},{9,10},{10,1... | collective-permute-start | bytes 1572872 | tf_op jit(solution)/shard_map/ppermute | solution.py:480
  42.1 34.6 %collective-permute-start.21 = (bf16[128,2048]{1,0:T(8,128)(2,1)}, bf16[128,2048]{1,0:T(8,128)(2,1)S(1)}, u32[]{:S(2)}, u32[]{:S(2)}) collective-permute-start(bf16[128,2048]{1,0:T(8,128)(2,1)} %get-tuple-element.82), channel_id=1, source_target_pairs={{0,2},{1,3},{2,0},{3,1},{4,6},{5,7},{6,4},{7,5},{8,10},{9,11},{10,... | collective-permute-start | bytes 1572872 | tf_op jit(solution)/shard_map/ppermute | solution.py:480
  42.3 56.8 %collective-permute-start.22 = (bf16[128,2048]{1,0:T(8,128)(2,1)}, bf16[128,2048]{1,0:T(8,128)(2,1)S(1)}, u32[]{:S(2)}, u32[]{:S(2)}) collective-permute-start(bf16[128,2048]{1,0:T(8,128)(2,1)} %get-tuple-element.83), channel_id=1, source_target_pairs={{0,3},{1,0},{2,1},{3,2},{4,7},{5,4},{6,5},{7,6},{8,11},{9,8},{10,9... | collective-permute-start | bytes 1572872 | tf_op jit(solution)/shard_map/ppermute | solution.py:480
  70.2 28.8 %collective-permute-start.37 = (bf16[4,64,512]{2,1,0:T(8,128)(2,1)}, bf16[4,64,512]{2,1,0:T(8,128)(2,1)S(1)}, u32[]{:S(2)}, u32[]{:S(2)}) collective-permute-start(bf16[4,64,512]{2,1,0:T(8,128)(2,1)} %get-tuple-element.87), channel_id=1, source_target_pairs={{0,1},{1,2},{2,3},{3,0},{4,5},{5,6},{6,7},{7,4},{8,9},{9,10},{10,1... | collective-permute-start | bytes 786440 | tf_op jit(solution)/shard_map/ppermute | solution.py:480
  70.6 34.0 %collective-permute-start.38 = (bf16[4,64,512]{2,1,0:T(8,128)(2,1)}, bf16[4,64,512]{2,1,0:T(8,128)(2,1)S(1)}, u32[]{:S(2)}, u32[]{:S(2)}) collective-permute-start(bf16[4,64,512]{2,1,0:T(8,128)(2,1)} %get-tuple-element.88), channel_id=1, source_target_pairs={{0,2},{1,3},{2,0},{3,1},{4,6},{5,7},{6,4},{7,5},{8,10},{9,11},{10,... | collective-permute-start | bytes 786440 | tf_op jit(solution)/shard_map/ppermute | solution.py:480
  73.6 41.0 %collective-permute-start.33 = (bf16[1024,256]{1,0:T(8,128)(2,1)S(1)}, bf16[1024,256]{1,0:T(8,128)(2,1)S(1)}, u32[]{:S(2)}, u32[]{:S(2)}) collective-permute-start(bf16[1024,256]{1,0:T(8,128)(2,1)S(1)} %get-tuple-element.121.refs_16_), channel_id=1, source_target_pairs={{0,16},{4,20},{8,24},{12,28},{16,0},{20,4},{24,8},{28,12},{1,17},{... | collective-permute-start | bytes 1572872 | tf_op jit(solution)/shard_map/ppermute | solution.py:475
  76.7 37.9 %collective-permute-start.31 = (bf16[1024,256]{1,0:T(8,128)(2,1)S(1)}, bf16[1024,256]{1,0:T(8,128)(2,1)S(1)}, u32[]{:S(2)}, u32[]{:S(2)}) collective-permute-start(bf16[1024,256]{1,0:T(8,128)(2,1)S(1)} %get-tuple-element.121.refs_16_), channel_id=1, source_target_pairs={{0,8},{4,12},{8,0},{12,4},{16,24},{20,28},{24,16},{28,20},{1,9},{5... | collective-permute-start | bytes 1572872 | tf_op jit(solution)/shard_map/ppermute | solution.py:475
  99.0 16.3 %collective-permute-start.30 = (bf16[1024,256]{1,0:T(8,128)(2,1)S(1)}, bf16[1024,256]{1,0:T(8,128)(2,1)S(1)}, u32[]{:S(2)}, u32[]{:S(2)}) collective-permute-start(bf16[1024,256]{1,0:T(8,128)(2,1)S(1)} %get-tuple-element.121.refs_16_), channel_id=1, source_target_pairs={{0,4},{4,0},{8,12},{12,8},{16,20},{20,16},{24,28},{28,24},{1,5},{5... | collective-permute-start | bytes 1572872 | tf_op jit(solution)/shard_map/ppermute | solution.py:475
  99.1 16.4 %collective-permute-start.24 = (bf16[1024,256]{1,0:T(8,128)(2,1)S(1)}, bf16[1024,256]{1,0:T(8,128)(2,1)S(1)}, u32[]{:S(2)}, u32[]{:S(2)}) collective-permute-start(bf16[1024,256]{1,0:T(8,128)(2,1)S(1)} %get-tuple-element.122.refs_8_), channel_id=1, source_target_pairs={{0,8},{4,12},{8,0},{12,4},{16,24},{20,28},{24,16},{28,20},{1,9},{5... | collective-permute-start | bytes 1572872 | tf_op jit(solution)/shard_map/ppermute | solution.py:475
  115.5 21.8 %collective-permute-start.28 = (bf16[1024,256]{1,0:T(8,128)(2,1)S(1)}, bf16[1024,256]{1,0:T(8,128)(2,1)S(1)}, u32[]{:S(2)}, u32[]{:S(2)}) collective-permute-start(bf16[1024,256]{1,0:T(8,128)(2,1)S(1)} %collective-permute-done.24.refs_10_), channel_id=1, source_target_pairs={{0,16},{4,20},{8,24},{12,28},{16,0},{20,4},{24,8},{28,12},{1,17},{... | collective-permute-start | bytes 1572872 | tf_op jit(solution)/shard_map/ppermute | solution.py:475
  137.4 23.8 %collective-permute-start.17 = (bf16[4,64,512]{2,1,0:T(8,128)(2,1)}, bf16[4,64,512]{2,1,0:T(8,128)(2,1)}, u32[]{:S(2)}, u32[]{:S(2)}) collective-permute-start(bf16[4,64,512]{2,1,0:T(8,128)(2,1)} %get-tuple-element.77), channel_id=1, source_target_pairs={{0,1},{1,2},{2,3},{3,0},{4,5},{5,6},{6,7},{7,4},{8,9},{9,10},{10,1... | collective-permute-start | bytes 786440 | tf_op jit(solution)/shard_map/ppermute | solution.py:480
  140.7 20.5 %collective-permute-start.18 = (bf16[4,64,512]{2,1,0:T(8,128)(2,1)}, bf16[4,64,512]{2,1,0:T(8,128)(2,1)}, u32[]{:S(2)}, u32[]{:S(2)}) collective-permute-start(bf16[4,64,512]{2,1,0:T(8,128)(2,1)} %get-tuple-element.78), channel_id=1, source_target_pairs={{0,2},{1,3},{2,0},{3,1},{4,6},{5,7},{6,4},{7,5},{8,10},{9,11},{10,... | collective-permute-start | bytes 786440 | tf_op jit(solution)/shard_map/ppermute | solution.py:480
  140.8 23.3 %collective-permute-start.19 = (bf16[4,64,512]{2,1,0:T(8,128)(2,1)S(1)}, bf16[4,64,512]{2,1,0:T(8,128)(2,1)}, u32[]{:S(2)}, u32[]{:S(2)}) collective-permute-start(bf16[4,64,512]{2,1,0:T(8,128)(2,1)S(1)} %copy-done.43), channel_id=1, source_target_pairs={{0,3},{1,0},{2,1},{3,2},{4,7},{5,4},{6,5},{7,6},{8,11},{9,8},{10,9... | collective-permute-start | bytes 786440 | tf_op jit(solution)/shard_map/ppermute | solution.py:480
  194.5 37.6 %collective-permute-start.41 = (bf16[64,4096]{1,0:T(8,128)(2,1)}, bf16[64,4096]{1,0:T(8,128)(2,1)S(1)}, u32[]{:S(2)}, u32[]{:S(2)}) collective-permute-start(bf16[64,4096]{1,0:T(8,128)(2,1)} %get-tuple-element.92), channel_id=1, source_target_pairs={{0,3},{1,0},{2,1},{3,2},{4,7},{5,4},{6,5},{7,6},{8,11},{9,8},{10,9... | collective-permute-start | bytes 1572872 | tf_op jit(solution)/shard_map/ppermute | solution.py:480
  197.1 57.5 %collective-permute-start.43 = (bf16[64,4096]{1,0:T(8,128)(2,1)}, bf16[64,4096]{1,0:T(8,128)(2,1)S(1)}, u32[]{:S(2)}, u32[]{:S(2)}) collective-permute-start(bf16[64,4096]{1,0:T(8,128)(2,1)} %get-tuple-element.94), channel_id=1, source_target_pairs={{0,2},{1,3},{2,0},{3,1},{4,6},{5,7},{6,4},{7,5},{8,10},{9,11},{10,... | collective-permute-start | bytes 1572872 | tf_op jit(solution)/shard_map/ppermute | solution.py:480
  201.8 64.4 %collective-permute-start.45 = (bf16[64,4096]{1,0:T(8,128)(2,1)S(1)}, bf16[64,4096]{1,0:T(8,128)(2,1)S(1)}, u32[]{:S(2)}, u32[]{:S(2)}) collective-permute-start(bf16[64,4096]{1,0:T(8,128)(2,1)S(1)} %copy-done.29), channel_id=1, source_target_pairs={{0,1},{1,2},{2,3},{3,0},{4,5},{5,6},{6,7},{7,4},{8,9},{9,10},{10,1... | collective-permute-start | bytes 1572872 | tf_op jit(solution)/shard_map/ppermute | solution.py:480
  204.2 72.8 %collective-permute-start.40 = (bf16[64,4096]{1,0:T(8,128)(2,1)S(1)}, bf16[64,4096]{1,0:T(8,128)(2,1)S(1)}, u32[]{:S(2)}, u32[]{:S(2)}) collective-permute-start(bf16[64,4096]{1,0:T(8,128)(2,1)S(1)} %copy-done.32), channel_id=1, source_target_pairs={{0,3},{1,0},{2,1},{3,2},{4,7},{5,4},{6,5},{7,6},{8,11},{9,8},{10,9... | collective-permute-start | bytes 1572872 | tf_op jit(solution)/shard_map/ppermute | solution.py:480
  205.5 89.9 %collective-permute-start.47 = (bf16[2,1,256,768]{3,2,1,0:T(8,128)(2,1)S(1)}, bf16[2,1,256,768]{3,2,1,0:T(8,128)(2,1)}, u32[]{:S(2)}, u32[]{:S(2)}) collective-permute-start(bf16[2,1,256,768]{3,2,1,0:T(8,128)(2,1)S(1)} %get-tuple-element.120), channel_id=1, source_target_pairs={{0,8},{4,12},{8,0},{12,4},{16,24},{20,28},{24,16},{28,20},{1,9},{5... | collective-permute-start | bytes 2359304 | tf_op jit(solution)/shard_map/ppermute | solution.py:475
  232.1 55.6 %collective-permute-start.42 = (bf16[64,4096]{1,0:T(8,128)(2,1)S(1)}, bf16[64,4096]{1,0:T(8,128)(2,1)S(1)}, u32[]{:S(2)}, u32[]{:S(2)}) collective-permute-start(bf16[64,4096]{1,0:T(8,128)(2,1)S(1)} %copy-done.31), channel_id=1, source_target_pairs={{0,2},{1,3},{2,0},{3,1},{4,6},{5,7},{6,4},{7,5},{8,10},{9,11},{10,... | collective-permute-start | bytes 1572872 | tf_op jit(solution)/shard_map/ppermute | solution.py:480
  254.6 34.1 %collective-permute-start.44 = (bf16[64,4096]{1,0:T(8,128)(2,1)S(1)}, bf16[64,4096]{1,0:T(8,128)(2,1)S(1)}, u32[]{:S(2)}, u32[]{:S(2)}) collective-permute-start(bf16[64,4096]{1,0:T(8,128)(2,1)S(1)} %copy-done.30), channel_id=1, source_target_pairs={{0,1},{1,2},{2,3},{3,0},{4,5},{5,6},{6,7},{7,4},{8,9},{9,10},{10,1... | collective-permute-start | bytes 1572872 | tf_op jit(solution)/shard_map/ppermute | solution.py:480
  266.3 32.1 %collective-permute-start.50 = (bf16[1,2,256,768]{3,2,1,0:T(8,128)(2,1)}, bf16[1,2,256,768]{3,2,1,0:T(8,128)(2,1)}, u32[]{:S(2)}, u32[]{:S(2)}) collective-permute-start(bf16[1,2,256,768]{3,2,1,0:T(8,128)(2,1)} %get-tuple-element.118), channel_id=1, source_target_pairs={{0,16},{4,20},{8,24},{12,28},{16,0},{20,4},{24,8},{28,12},{1,17},{... | collective-permute-start | bytes 2359304 | tf_op jit(solution)/shard_map/ppermute | solution.py:475
  277.0 23.5 %collective-permute-start.53 = (bf16[2,1,768,256]{3,2,1,0:T(8,128)(2,1)}, bf16[2,1,768,256]{3,2,1,0:T(8,128)(2,1)}, u32[]{:S(2)}, u32[]{:S(2)}) collective-permute-start(bf16[2,1,768,256]{3,2,1,0:T(8,128)(2,1)} %get-tuple-element.116), channel_id=1, source_target_pairs={{0,8},{4,12},{8,0},{12,4},{16,24},{20,28},{24,16},{28,20},{1,9},{5... | collective-permute-start | bytes 2359304 | tf_op jit(solution)/shard_map/ppermute | solution.py:475
  (91 other events, 1501.9 us)
Sparse Core Ops, SparseCore 0:
  9.7 28.4 all-gather.1

commit v3 on v2

--- a/solution.py
+++ b/solution.py
@@ -60,6 +60,10 @@
     return pltpu.CompilerParams(vmem_limit_bytes=VMEM_LIMIT)
 
 
+def brief():
+    return pl.CostEstimate(flops=1000, bytes_accessed=1000, transcendentals=0)
+
+
 def whole(*shape):
     return pl.BlockSpec(shape, lambda *_: (0,) * len(shape))
 
@@ -69,8 +73,7 @@
 
 
 def attend_kernel(experts, capacity, heads, n_ctx, where_ref, q_ref, ids_ref, *refs):
-    k_refs, refs = refs[:n_ctx], refs[n_ctx:]
-    v_refs, refs = refs[:n_ctx], refs[n_ctx:]
+    kv_refs, refs = refs[:n_ctx], refs[n_ctx:]
     out_refs, refs = refs[: experts * PARTS], refs[experts * PARTS :]
     k_scr, v_scr, best_scr, acc_scr, att_scr = refs
     ctx, owner = where_ref[0], where_ref[1]
@@ -85,8 +88,8 @@
 
     for m in range(n_ctx):
         index = jnp.bitwise_xor(ctx, m)
-        k_scr[index] = k_refs[m][0]
-        v_scr[index, :, :HEAD_SIZE] = v_refs[m][0]
+        k_scr[index] = kv_refs[m][0, :, :HEAD_SIZE]
+        v_scr[index, :, :HEAD_SIZE] = kv_refs[m][0, :, HEAD_SIZE:]
 
     def fold(t, last):
         key_tile = k_scr[pl.ds(2 * t, 2)].reshape(tile, HEAD_SIZE)
@@ -137,13 +140,13 @@
                 out_refs[c * experts + d][rank] = picked[first : first + part]
 
 
-def attend(where, queries, keys, values, ids, capacity):
+def attend(where, queries, key_values, ids, capacity):
     seqs, block, width = queries.shape
-    n_ctx = len(keys)
+    n_ctx = len(key_values)
     experts, _, n = ids.shape
     heads = width // HEAD_SIZE
     part = capacity // PARTS
-    by_seq = pl.BlockSpec((1, block, HEAD_SIZE), lambda s: (s, 0, 0))
+    by_seq = pl.BlockSpec((1, block, 2 * HEAD_SIZE), lambda s: (s, 0, 0))
     outs = pl.pallas_call(
         functools.partial(attend_kernel, experts, capacity, heads, n_ctx),
         grid=(seqs,),
@@ -152,7 +155,7 @@
             pl.BlockSpec((1, block, width), lambda s: (s, 0, 0)),
             whole(experts, 1, n),
         ]
-        + [by_seq] * (2 * n_ctx),
+        + [by_seq] * n_ctx,
         out_specs=[whole(experts, part, width)] * (PARTS * experts),
         scratch_shapes=[
             pltpu.VMEM((n_ctx, block, HEAD_SIZE), BF16),
@@ -163,13 +166,9 @@
         ],
         out_shape=[jax.ShapeDtypeStruct((experts, part, width), BF16)] * (PARTS * experts),
         compiler_params=kernel_params(),
-        cost_estimate=pl.CostEstimate(
-            flops=4 * seqs * block * block * n_ctx * width,
-            bytes_accessed=8 << 20,
-            transcendentals=seqs * heads * block * block * n_ctx,
-        ),
+        cost_estimate=brief(),
         name="attend",
-    )(where, queries, ids, *keys, *values)
+    )(where, queries, ids, *key_values)
     return [outs[c * experts : (c + 1) * experts] for c in range(PARTS)]
 
 
@@ -198,6 +197,7 @@
         out_shape=[jax.ShapeDtypeStruct((capacity, width), BF16)] * experts,
         scratch_shapes=[pltpu.VMEM((experts * capacity, n), BF16)],
         compiler_params=kernel_params(),
+        cost_estimate=brief(),
         name="place",
     )(where, ids_row, rows)
 
@@ -242,6 +242,7 @@
         out_shape=[jax.ShapeDtypeStruct((n, width), BF16)] * 2,
         scratch_shapes=[pltpu.VMEM((n, experts * capacity), BF16)],
         compiler_params=kernel_params(),
+        cost_estimate=brief(),
         name="restore",
     )(where, ids_column, *[parts[c][d] for d in range(experts) for c in range(PARTS)])
 
@@ -249,8 +250,7 @@
 def expert_kernel(pieces, experts, capacity, part_index, where_ref, *refs):
     att_refs, refs = refs[:experts], refs[experts:]
     grad_refs, refs = refs[:experts], refs[experts:]
-    wa_refs, refs = refs[:pieces], refs[pieces:]
-    wb_refs, refs = refs[:pieces], refs[pieces:]
+    w_refs, refs = refs[:pieces], refs[pieces:]
     gate_hbm, up_hbm, down_hbm, gain_ref, ids_ref, weight_ref = refs[:6]
     refs = refs[6:]
     out_refs, refs = refs[:experts], refs[experts:]
@@ -259,29 +259,21 @@
     part, width = grad_refs[0].shape
     rows = experts * part
     att_cols = att_refs[0].shape[2]
-    half, piece = wa_refs[0].shape
+    piece = w_refs[0].shape[1]
     ff = units_ref.shape[1]
     piece_index, owner = where_ref[2], where_ref[1]
 
-    copies = []
-    for m in range(pieces):
-        copies.append(
-            (
-                pltpu.make_async_copy(wa_refs[m], w_scr.at[m, pl.ds(0, half)], sems.at[2 * m]),
-                pltpu.make_async_copy(
-                    wb_refs[m], w_scr.at[m, pl.ds(half, half)], sems.at[2 * m + 1]
-                ),
-            )
-        )
-    first = 2 * pieces
+    copies = [
+        pltpu.make_async_copy(w_refs[m], w_scr.at[m], sems.at[m]) for m in range(pieces)
+    ]
+    first = pieces
     weight_copies = (
         pltpu.make_async_copy(gate_hbm.at[0], gate_scr, sems.at[first]),
         pltpu.make_async_copy(up_hbm.at[0], up_scr, sems.at[first + 1]),
         pltpu.make_async_copy(down_hbm.at[0], down_scr, sems.at[first + 2]),
     )
-    for pair in copies:
-        for copy in pair:
-            copy.start()
+    for copy in copies:
+        copy.start()
     for copy in weight_copies:
         copy.start()
 
@@ -299,8 +291,7 @@
         back_ref[s * part : (s + 1) * part, :] = (weights[s] * grads).astype(BF16)
 
     for m in range(pieces):
-        for copy in copies[m]:
-            copy.wait()
+        copies[m].wait()
         total = jnp.zeros((rows, piece), F32)
         for d in range(experts):
             source = lax.rem(owner - d + experts, experts)
@@ -359,10 +350,10 @@
             ).astype(BF16)
 
 
-def expert_part(where, att, grads, wa, wb, gate, up, down, gain, ids, weights, capacity, index):
+def expert_part(where, att, grads, projection, gate, up, down, gain, ids, weights, capacity, index):
     experts, part, att_cols = att[0].shape
-    pieces = len(wa)
-    half, piece = wa[0].shape
+    pieces = len(projection)
+    depth, piece = projection[0].shape
     width = grads[0].shape[1]
     ff = gate.shape[2]
     rows = experts * part
@@ -375,104 +366,83 @@
         in_specs=[smem()]
         + [whole(experts, part, att_cols)] * experts
         + [pl.BlockSpec((part, width), lambda i: (index, 0))] * experts
-        + [in_hbm] * (2 * pieces + 3)
+        + [in_hbm] * (pieces + 3)
         + [whole(1, width), whole(experts, 1, n), whole(experts, 1, n)],
         out_specs=[whole(part, 2 * width)] * experts
         + [whole(rows, width)] * 2
         + [whole(rows, ff)] * 3,
         scratch_shapes=[
-            pltpu.VMEM((pieces, 2 * half, piece), BF16),
+            pltpu.VMEM((pieces, depth, piece), BF16),
             pltpu.VMEM((width, ff), BF16),
             pltpu.VMEM((width, ff), BF16),
             pltpu.VMEM((ff, width), BF16),
             pltpu.VMEM((rows, width), BF16),
             pltpu.VMEM((rows, width), BF16),
-            pltpu.SemaphoreType.DMA((2 * pieces + 3,)),
+            pltpu.SemaphoreType.DMA((pieces + 3,)),
         ],
         out_shape=[out(part, 2 * width)] * experts + [out(rows, width)] * 2 + [out(rows, ff)] * 3,
         compiler_params=kernel_params(),
-        cost_estimate=pl.CostEstimate(
-            flops=2 * rows * width * (width + 6 * ff),
-            bytes_accessed=2 * (width * width + 3 * width * ff + 8 * rows * width),
-            transcendentals=rows * ff,
-        ),
+        cost_estimate=brief(),
         name="expert",
-    )(where, *att, *grads, *wa, *wb, gate, up, down, gain, ids, weights)
+    )(where, *att, *grads, *projection, gate, up, down, gain, ids, weights)
     return outs[:experts], outs[experts:]
 
 
-def weight_kernel(count, lead, *refs):
+def weight_kernel(count, *refs):
     normed, back, units, back_gate, back_up = [refs[i * count : (i + 1) * count] for i in range(5)]
     outs = refs[5 * count :]
     first = ((0,), (0,))
-    gate = up = down = 0.0
-    for c in range(count):
-        gate += dot(normed[c][...], back_gate[c][...], first)
-        up += dot(normed[c][...], back_up[c][...], first)
-        down += dot(units[c][...], back[c][...], first)
-
-    def put(gate_ref, up_ref, down_ref):
-        gate_ref[0] = gate.astype(BF16)
-        up_ref[0] = up.astype(BF16)
-        down_ref[0] = down.astype(BF16)
-
+
+    def total(left, right):
+        return sum(dot(a[...], b[...], first) for a, b in zip(left, right)).astype(BF16)
+
+    gate, up, down = total(normed, back_gate), total(normed, back_up), total(units, back)
     if len(outs) == 3:
-        put(*outs)
+        outs[0][0], outs[1][0], outs[2][0] = gate, up, down
         return
-
-    @pl.when(pl.program_id(0) < lead)
-    def _():
-        put(*outs[:3])
-
-    @pl.when(pl.program_id(0) >= lead)
-    def _():
-        put(*outs[3:])
-
-
-def weight_parts(where, normed, back, units, back_gate, back_up, exchange):
+    packed = outs[0]
+    packed[0, 0] = gate
+    packed[0, 1] = up
+    cols = down.shape[1]
+    for t in range(0, down.shape[0], cols):
+        packed[0, 2, :, t : t + cols] = down[t : t + cols]
+
+
+def weight_blocks(where, normed, back, units, back_gate, back_up, first=None):
     count = len(normed)
     rows, width = normed[0].shape
     ff = units[0].shape[1]
     cols = PIECE
-    blocks = width // cols
-    lead = blocks // 2 if exchange else blocks
+    packed = first is not None
+    blocks = width // cols // 2 if packed else width // cols
 
     def block_of(i, where_ref):
-        if not exchange:
-            return i
-        mask = jnp.where(i < lead, 2 * i + 1, 2 * (i - lead))
-        return jnp.bitwise_xor(where_ref[0], mask)
+        return jnp.bitwise_xor(where_ref[0], 2 * i + first) if packed else i
 
     thin = [pl.BlockSpec((rows, cols), lambda i, w: (0, block_of(i, w)))] * count
     full = [pl.BlockSpec((rows, ff), lambda i, w: (0, 0))] * count
-    early = lambda i, w: (jnp.minimum(i, lead - 1), 0, 0)
-    late = lambda i, w: (jnp.maximum(i - lead, 0), 0, 0)
-    shapes = [(cols, ff), (cols, ff), (ff, cols)]
-    groups = [early, late] if exchange else [early]
-    kernel = lambda where_ref, *refs: weight_kernel(count, lead, *refs)
-    outs = pl.pallas_call(
-        kernel,
+    shapes = [(3, cols, ff)] if packed else [(cols, ff), (cols, ff), (ff, cols)]
+    return pl.pallas_call(
+        lambda where_ref, *refs: weight_kernel(count, *refs),
         grid_spec=pltpu.PrefetchScalarGridSpec(
             num_scalar_prefetch=1,
             grid=(blocks,),
             in_specs=thin + thin + full + full + full,
-            out_specs=[pl.BlockSpec((1,) + shape, at) for at in groups for shape in shapes],
+            out_specs=[
+                pl.BlockSpec((1,) + shape, lambda i, w, zeros=(0,) * len(shape): (i,) + zeros)
+                for shape in shapes
+            ],
         ),
-        out_shape=[jax.ShapeDtypeStruct((lead,) + shape, BF16) for _ in groups for shape in shapes],
+        out_shape=[jax.ShapeDtypeStruct((blocks,) + shape, BF16) for shape in shapes],
         compiler_params=kernel_params(),
-        cost_estimate=pl.CostEstimate(
-            flops=6 * count * rows * width * ff,
-            bytes_accessed=2 * (3 * width * ff + 2 * count * rows * (width + 2 * ff)),
-            transcendentals=0,
-        ),
+        cost_estimate=brief(),
         name="weight_grads",
     )(where, *normed, *back, *units, *back_gate, *back_up)
-    return outs[:3], outs[3:]
-
-
-def partner(value, bit):
+
+
+def partner(value, mask):
     count = lax.axis_size("ctx")
-    return lax.ppermute(value, "ctx", [(i, i ^ (1 << bit)) for i in range(count)])
+    return lax.ppermute(value, "ctx", [(i, i ^ mask) for i in range(count)])
 
 
 def shift(value, by):
@@ -480,12 +450,12 @@
     return lax.ppermute(value, "exp", [(i, (i + by) % count) for i in range(count)])
 
 
-def spread(value, order):
-    held = {0: value}
-    for bit in order:
-        for m in list(held):
-            held[m | 1 << bit] = partner(held[m], bit)
-    return [held[m] for m in sorted(held)]
+def from_chips(value, count):
+    return [value] + [partner(value, m) for m in range(2, count, 2)]
+
+
+def with_cores(held):
+    return [x for value in held for x in (value, partner(value, 1))]
 
 
 def halved(value, bits, order, ctx):
@@ -496,23 +466,10 @@
         mine = (ctx >> bit) & 1
         gone = lax.dynamic_slice_in_dim(held, 1 - mine, 1, axis)
         kept = lax.dynamic_slice_in_dim(held, mine, 1, axis)
-        held = kept.astype(F32) + partner(gone, bit).astype(F32)
+        held = kept.astype(F32) + partner(gone, 1 << bit).astype(F32)
         if place_in_order < bits - 1:
             held = held.astype(BF16)
     return held.reshape(shape)
-
-
-def halved_relative(gone, kept, bits, order):
-    shape = kept.shape[1:]
-    arrived = partner(gone, 0).astype(F32).reshape((2,) * (bits - 1) + shape)
-    held = kept.astype(F32).reshape((2,) * (bits - 1) + shape)
-    for bit in order:
-        axis = bits - 1 - bit
-        take = lambda x, i: lax.slice_in_dim(x, i, i + 1, axis=axis)
-        gone = (take(held, 1) + take(arrived, 1)).astype(BF16)
-        held = (take(held, 0) + take(arrived, 0)).astype(BF16).astype(F32)
-        arrived = partner(gone, bit).astype(F32)
-    return (held + arrived).reshape(shape)
 
 
 def on_device(
@@ -540,17 +497,15 @@
     experts = exp_count
     capacity = min(n, 2 * n // experts)
     pieces = min(ctx_count, width // PIECE)
-    piece_bits = pieces.bit_length() - 1
     piece = width // pieces
     piece_index = ctx % pieces
     where = jnp.stack([ctx, owner, piece_index]).astype(jnp.int32)
 
     first_column = (owner * heads_dev // group) * HEAD_SIZE
-    low, high = list(range(1, bits)) + [0], list(range(bits - 1, 0, -1)) + [0]
     keys = lax.dynamic_slice_in_dim(rotated_key_heads, first_column, HEAD_SIZE, 2)
     values = lax.dynamic_slice_in_dim(value_head_rows, first_column, HEAD_SIZE, 2)
-    keys = spread(keys, low)
-    values = spread(values, high)
+    key_values = jnp.concatenate([keys, values], axis=2)
+    key_values = with_cores(from_chips(key_values, ctx_count))
 
     ids_f = expert_ids.astype(F32)
     info = jnp.stack([ids_f[:, 0], gate_weights[:, 0]])
@@ -562,21 +517,22 @@
 
     mine = lax.dynamic_slice_in_dim(out_proj, piece_index * piece, piece, 1)
     mine = lax.all_gather(mine, "exp", axis=0, tiled=True)
-    half = mine.shape[0] // 2
-    mine, keys, values = lax.optimization_barrier((mine, keys, values))
-    wa = spread(mine[:half], [b for b in low if b < piece_bits])
-    wb = spread(mine[half:], [b for b in high if b < piece_bits])
-
-    attended = attend(where, queries, keys, values, ids_all, capacity)
-    returned, kept = [], []
-    for index, sent in enumerate(attended):
-        arrived = [sent[0]] + [shift(sent[d], d) for d in range(1, experts)]
-        rows, saved = expert_part(
+    mine, key_values = lax.optimization_barrier((mine, key_values))
+    projection = from_chips(mine, pieces)
+
+    attended = attend(where, queries, key_values, ids_all, capacity)
+    arrived = [[sent[0]] + [shift(sent[d], d) for d in range(1, experts)] for sent in attended[:1]]
+    projection, later = lax.optimization_barrier((projection, attended[1:]))
+    projection = with_cores(projection)
+    arrived += [[sent[0]] + [shift(sent[d], d) for d in range(1, experts)] for sent in later]
+
+    rows, kept = [], []
+    for index, att in enumerate(arrived):
+        out, saved = expert_part(
             where,
-            arrived,
+            att,
             grads,
-            wa,
-            wb,
+            projection,
             expert_gate,
             expert_up,
             expert_down,
@@ -586,26 +542,38 @@
             capacity,
             index,
         )
-        returned.append([rows[0]] + [shift(rows[d], -d) for d in range(1, experts)])
+        rows.append(out)
         kept.append(saved)
+    returned = [[rows[0][0]] + [shift(rows[0][d], -d) for d in range(1, experts)]]
 
     rows_dev = width // ctx_count
-    exchange = rows_dev == PIECE
-    gone, stay = weight_parts(where, *zip(*kept), exchange)
-    if exchange:
-        orders = low[:-1], high[:-1], low[:-1]
-        grad_gate, grad_up, grad_down = [
-            halved_relative(g, s, bits, order)[None] for g, s, order in zip(gone, stay, orders)
-        ]
+    ff = expert_gate.shape[2]
+    if rows_dev == PIECE:
+        (gone,) = weight_blocks(where, *zip(*kept), first=1)
+        near = partner(gone, 1)
+        (stay,) = weight_blocks(where, *zip(*kept), first=0)
+        pair = [(stay[j].astype(F32) + near[j].astype(F32)) for j in range(ctx_count // 2)]
+        far = [x.astype(BF16) for x in pair[1:]]
+        far, later = lax.optimization_barrier((far, rows[1:]))
+        far = [partner(x, 2 * j + 2) for j, x in enumerate(far)]
+        total = sum([x.astype(F32) for x in far], pair[0])
+        grad_gate, grad_up = total[0][None], total[1][None]
+        grad_down = total[2].reshape(PIECE, ff // PIECE, PIECE).transpose(1, 0, 2)
+        grad_down = grad_down.reshape(1, ff, PIECE)
     else:
-        ff = expert_gate.shape[2]
+        gone = weight_blocks(where, *zip(*kept))
+        later = rows[1:]
         part_gate, part_up = [x.reshape(ctx_count, rows_dev, ff) for x in gone[:2]]
         part_down = gone[2].reshape(width // PIECE, ff, PIECE // rows_dev, rows_dev)
         part_down = part_down.transpose(0, 2, 1, 3).reshape(ctx_count, ff, rows_dev)
-        core_low, core_high = [0] + low[:-1], [0] + high[:-1]
-        grad_gate = halved(part_gate, bits, core_low, ctx)[None]
-        grad_up = halved(part_up, bits, core_high, ctx)[None]
-        grad_down = halved(part_down, bits, core_low, ctx)[None]
+        order = list(range(bits))
+        grad_gate, grad_up, grad_down = [
+            halved(x, bits, order, ctx)[None] for x in (part_gate, part_up, part_down)
+        ]
+    returned += [[out[0]] + [shift(out[d], -d) for d in range(1, experts)] for out in later]
+    returned, grad_gate, grad_up, grad_down = lax.optimization_barrier(
+        (returned, grad_gate, grad_up, grad_down)
+    )
 
     layer_out, grad_hidden = restore(where, ids_f, returned, experts, capacity)
     return (layer_out, grad_hidden, grad_gate, grad_up, grad_down)

time: 330 us -> 303 us (0.918)
  waiting for transfers between devices: 164 us -> 146 us
  other arithmetic: 14.8 us -> 7.77 us
    ppermute x18, waiting for transfers between devices: 127 us -> 100 us  [shift(): lax.ppermute(value, 'exp', [(i, (i + by) % count) for i in range(count)])]
    ppermute x37 -> x18, waiting for transfers between devices: 37.2 us -> 45.6 us  [partner(): return lax.ppermute(value, 'ctx', [(i, i ^ mask) for i in range(count)])]
    ppermute x37 -> x18, starting transfers between devices: 17.4 us -> 11.7 us  [partner(): return lax.ppermute(value, 'ctx', [(i, i ^ mask) for i in range(count)])]
    ppermute x18, starting transfers between devices: 22.1 us -> 27.2 us  [shift(): lax.ppermute(value, 'exp', [(i, (i + by) % count) for i in range(count)])]
    convert_element_type x11 -> x1, other arithmetic: 7.91 us -> 3.96 us  [on_device(): far = [x.astype(BF16) for x in pair[1:]]]
    unnamed x119 -> x59, local copies, waits for them, and re-layouts: 8.28 us -> 4.51 us
    pallas_call x1 -> x2, Pallas kernels: 13.3 us -> 15.3 us  [weight_blocks(): pl.pallas_call(lambda where_ref, *refs: weight_kernel(count, *refs), grid...]
  transfers between devices with their start and end apart: 56 -> 37, of which waited for: 23 -> 17; matrix products, arithmetic and copies ran while one was open for 5% -> 3% of each run, Pallas kernels for 16% -> 18%
where the time goes in v3:
time: 303 us; the launch traced here: 299 us
  waiting for transfers between devices  146 us (48%)
  Pallas kernels  82.5 us (27%)
  starting transfers between devices  39 us (13%)
  between operations  14.4 us (5%)
  local copies, waits for them, and re-layouts  9.62 us (3%)
  other arithmetic  7.77 us (3%)
    ppermute x18, waiting for transfers between devices, shift(): lax.ppermute(value, 'exp', [(i, (i + by) % count) for i in range(count)])  100 us
    ppermute x18, waiting for transfers between devices, partner(): return lax.ppermute(value, 'ctx', [(i, i ^ mask) for i in range(count)])  45.6 us
    pallas_call x2, Pallas kernels, expert_part(): pl.pallas_call(functools.partial(expert_kernel, pieces, experts, capacity...  32.5 us
    ppermute x18, starting transfers between devices, shift(): lax.ppermute(value, 'exp', [(i, (i + by) % count) for i in range(count)])  27.2 us
    pallas_call x1, Pallas kernels, attend(): pl.pallas_call(functools.partial(attend_kernel, experts, capacity, heads,...  25.7 us
    pallas_call x2, Pallas kernels, weight_blocks(): pl.pallas_call(lambda where_ref, *refs: weight_kernel(count, *refs), grid...  15.3 us
    ppermute x18, starting transfers between devices, partner(): return lax.ppermute(value, 'ctx', [(i, i ^ mask) for i in range(count)])  11.7 us
  transfers between devices with their start and end apart: 37, of which 17 were waited for; matrix products, arithmetic and copies ran while one was open for 3% of the time, Pallas kernels for 18%

profile of v3, /device:TPU:22, one launch (start us, length us, event | category | flops | bytes accessed | tf_op | source)
XLA Modules:
  0.0 299.1 jit_solution(15269313047910074235)
XLA Ops:
  14.3 12.2 %collective-permute-done.8.refs_6_ = bf16[4,256,256]{2,1,0:T(8,128)(2,1)S(1)} collective-permute-done((bf16[4,256,256]{2,1,0:T(8,128)(2,1)S(1)}, bf16[4,256,256]{2,1,0:T(8,128)(2,1)S(1)}, u32[]{:S(2)}, u32[]{:S(2)}) %collective-permute-start.8) | collective-permute-done | bytes 524320 | tf_op jit(solution)/shard_map/ppermute | solution.py:445
  26.5 9.4 %collective-permute-done.6.refs_4_ = bf16[4,256,256]{2,1,0:T(8,128)(2,1)S(1)} collective-permute-done((bf16[4,256,256]{2,1,0:T(8,128)(2,1)S(1)}, bf16[4,256,256]{2,1,0:T(8,128)(2,1)S(1)}, u32[]{:S(2)}, u32[]{:S(2)}) %collective-permute-start.6) | collective-permute-done | bytes 524320 | tf_op jit(solution)/shard_map/ppermute | solution.py:445
  44.5 2.6 collective-permute-done.1
  48.2 3.2 %place.1 = (bf16[128,2048]{1,0:T(8,128)(2,1)}, bf16[128,2048]{1,0:T(8,128)(2,1)}, bf16[128,2048]{1,0:T(8,128)(2,1)}, bf16[128,2048]{1,0:T(8,128)(2,1)}) custom-call(s32[3]{0:T(128)} %pad_add_fusion.where_ref, f32[1,256]{1,0:T(1,128)} %bitcast.32, bf16[256,2048]{1,0:T(8,128)(2,1)} %rows_ref.1), custom_call_target="tpu_custom_call" | custom-call | flops 1000 | bytes 1000 | tf_op jit(solution)/shard_map/place/pallas_call | solution.py:192
  54.9 10.9 %collective-permute-done.18.refs_14_ = bf16[2048,256]{1,0:T(8,128)(2,1)S(1)} collective-permute-done((bf16[2048,256]{1,0:T(8,128)(2,1)}, bf16[2048,256]{1,0:T(8,128)(2,1)S(1)}, u32[]{:S(2)}, u32[]{:S(2)}) %collective-permute-start.18) | collective-permute-done | bytes 1048608 | tf_op jit(solution)/shard_map/ppermute | solution.py:445
  67.0 25.7 %attend.1 = (bf16[4,64,512]{2,1,0:T(8,128)(2,1)}, bf16[4,64,512]{2,1,0:T(8,128)(2,1)}, bf16[4,64,512]{2,1,0:T(8,128)(2,1)}, bf16[4,64,512]{2,1,0:T(8,128)(2,1)},...) custom-call(s32[3]{0:T(128)} %pad_add_fusion.where_ref, ...), custom_call_target="tpu_custom_call" | custom-call | flops 1000 | bytes 1000 | tf_op jit(solution)/shard_map/attend/pallas_call | solution.py:150
  94.9 9.3 %collective-permute-done.15.refs_7_ = bf16[128,2048]{1,0:T(8,128)(2,1)} collective-permute-done((bf16[128,2048]{1,0:T(8,128)(2,1)}, bf16[128,2048]{1,0:T(8,128)(2,1)}, u32[]{:S(2)}, u32[]{:S(2)}) %collective-permute-start.15) | collective-permute-done | bytes 524320 | tf_op jit(solution)/shard_map/ppermute | solution.py:450
  104.2 3.0 collective-permute-start.27
  107.2 10.8 %collective-permute-done.27.refs_2_ = bf16[4,64,512]{2,1,0:T(8,128)(2,1)S(1)} collective-permute-done((bf16[4,64,512]{2,1,0:T(8,128)(2,1)}, bf16[4,64,512]{2,1,0:T(8,128)(2,1)S(1)}, u32[]{:S(2)}, u32[]{:S(2)}) %collective-permute-start.27) | collective-permute-done | bytes 262176 | tf_op jit(solution)/shard_map/ppermute | solution.py:450
  119.1 8.4 %collective-permute-done.28.refs_3_ = bf16[4,64,512]{2,1,0:T(8,128)(2,1)S(1)} collective-permute-done((bf16[4,64,512]{2,1,0:T(8,128)(2,1)}, bf16[4,64,512]{2,1,0:T(8,128)(2,1)S(1)}, u32[]{:S(2)}, u32[]{:S(2)}) %collective-permute-start.28) | collective-permute-done | bytes 262176 | tf_op jit(solution)/shard_map/ppermute | solution.py:450
  127.4 3.8 %collective-permute-start.10 = (bf16[4,64,512]{2,1,0:T(8,128)(2,1)}, bf16[4,64,512]{2,1,0:T(8,128)(2,1)S(1)}, u32[]{:S(2)}, u32[]{:S(2)}) collective-permute-start(bf16[4,64,512]{2,1,0:T(8,128)(2,1)} %get-tuple-element.81), channel_id=1, source_target_pairs={{0,1},{1,2},{2,3},{3,0},{4,5},{5,6},{6,7},{7,4},{8,9},{9,10},{10,1... | collective-permute-start | bytes 786440 | tf_op jit(solution)/shard_map/ppermute | solution.py:450
  134.1 16.1 %expert.3 = (bf16[64,4096]{1,0:T(8,128)(2,1)}, bf16[64,4096]{1,0:T(8,128)(2,1)}, bf16[64,4096]{1,0:T(8,128)(2,1)}, bf16[64,4096]{1,0:T(8,128)(2,1)}, bf16[256,20...) custom-call(s32[3]{0:T(128)} %pad_add_fusion.where_ref, ...), custom_call_target="tpu_custom_call" | custom-call | flops 1000 | bytes 1000 | tf_op jit(solution)/shard_map/expert/pallas_call | solution.py:363
  153.3 16.3 %expert.2 = (bf16[64,4096]{1,0:T(8,128)(2,1)}, bf16[64,4096]{1,0:T(8,128)(2,1)}, bf16[64,4096]{1,0:T(8,128)(2,1)}, bf16[64,4096]{1,0:T(8,128)(2,1)}, bf16[256,20...) custom-call(s32[3]{0:T(128)} %pad_add_fusion.where_ref, ...), custom_call_target="tpu_custom_call" | custom-call | flops 1000 | bytes 1000 | tf_op jit(solution)/shard_map/expert/pallas_call | solution.py:363
  169.6 7.7 %weight_grads.3 = bf16[4,3,256,768]{3,2,1,0:T(8,128)(2,1)} custom-call(s32[3]{0:T(128)} %pad_add_fusion.where_ref, bf16[256,2048]{1,0:T(8,128)(2,1)} %get-tuple-element.101.refs_0_, bf16[256,2048]{1,0:T(8,128)(2,1)} %get-tuple-element.106.refs_1_, bf16[256,2048]{1,0:T(8,128)(2,1)} %get-tuple-element.107.refs_2_, ...), custom_call_target="tpu_custom_call" | custom-call | flops 1000 | bytes 1000 | tf_op jit(solution)/shard_map/weight_grads/pallas_call | solution.py:425
  177.3 7.6 %weight_grads.2 = bf16[4,3,256,768]{3,2,1,0:T(8,128)(2,1)} custom-call(s32[3]{0:T(128)} %pad_add_fusion.where_ref, bf16[256,2048]{1,0:T(8,128)(2,1)} %get-tuple-element.101.refs_0_, bf16[256,2048]{1,0:T(8,128)(2,1)} %get-tuple-element.106.refs_1_, bf16[256,2048]{1,0:T(8,128)(2,1)} %get-tuple-element.107.refs_2_, ...), custom_call_target="tpu_custom_call" | custom-call | flops 1000 | bytes 1000 | tf_op jit(solution)/shard_map/weight_grads/pallas_call | solution.py:425
  185.6 4.0 %fusion.4 = (bf16[3,256,768]{2,1,0:T(8,128)(2,1)S(1)}, bf16[3,256,768]{2,1,0:T(8,128)(2,1)S(1)}, bf16[3,256,768]{2,1,0:T(8,128)(2,1)S(1)}) fusion(bf16[4,3,256,768]{3,2,1,0:T(8,128)(2,1)} %collective-permute-done.29, bf16[4,3,256,768]{3,2,1,0:T(8,128)(2,1)} %weight_grads.2), kind=kLoop, calls=%fused_computation.8 | loop fusion | flops 7077888 | bytes 10616832 | tf_op jit(solution)/shard_map/convert_element_type | solution.py:556
  197.2 33.2 %collective-permute-done.23.refs_2_ = bf16[64,4096]{1,0:T(8,128)(2,1)S(1)} collective-permute-done((bf16[64,4096]{1,0:T(8,128)(2,1)S(1)}, bf16[64,4096]{1,0:T(8,128)(2,1)S(1)}, u32[]{:S(2)}, u32[]{:S(2)}) %collective-permute-start.23) | collective-permute-done | bytes 524320 | tf_op jit(solution)/shard_map/ppermute | solution.py:450
  230.4 2.5 collective-permute-start.30
  232.9 11.0 %collective-permute-done.34 = bf16[3,256,768]{2,1,0:T(8,128)(2,1)S(1)} collective-permute-done((bf16[3,256,768]{2,1,0:T(8,128)(2,1)S(1)}, bf16[3,256,768]{2,1,0:T(8,128)(2,1)S(1)}, u32[]{:S(2)}, u32[]{:S(2)}) %collective-permute-start.34) | collective-permute-done | bytes 1179680 | tf_op jit(solution)/shard_map/ppermute | solution.py:445
  243.9 3.8 %collective-permute-start.32 = (bf16[64,4096]{1,0:T(8,128)(2,1)}, bf16[64,4096]{1,0:T(8,128)(2,1)}, u32[]{:S(2)}, u32[]{:S(2)}) collective-permute-start(bf16[64,4096]{1,0:T(8,128)(2,1)} %get-tuple-element.122), channel_id=1, source_target_pairs={{0,1},{1,2},{2,3},{3,0},{4,5},{5,6},{6,7},{7,4},{8,9},{9,10},{10,1... | collective-permute-start | bytes 1572872 | tf_op jit(solution)/shard_map/ppermute | solution.py:450
  252.8 11.4 %collective-permute-done.24.refs_4_ = bf16[64,4096]{1,0:T(8,128)(2,1)S(1)} collective-permute-done((bf16[64,4096]{1,0:T(8,128)(2,1)}, bf16[64,4096]{1,0:T(8,128)(2,1)S(1)}, u32[]{:S(2)}, u32[]{:S(2)}) %collective-permute-start.24) | collective-permute-done | bytes 524320 | tf_op jit(solution)/shard_map/ppermute | solution.py:450
  264.2 11.2 %collective-permute-done.30.refs_3_ = bf16[64,4096]{1,0:T(8,128)(2,1)} collective-permute-done((bf16[64,4096]{1,0:T(8,128)(2,1)}, bf16[64,4096]{1,0:T(8,128)(2,1)}, u32[]{:S(2)}, u32[]{:S(2)}) %collective-permute-start.30) | collective-permute-done | bytes 524320 | tf_op jit(solution)/shard_map/ppermute | solution.py:450
  275.4 9.5 %collective-permute-done.31.refs_5_ = bf16[64,4096]{1,0:T(8,128)(2,1)} collective-permute-done((bf16[64,4096]{1,0:T(8,128)(2,1)}, bf16[64,4096]{1,0:T(8,128)(2,1)}, u32[]{:S(2)}, u32[]{:S(2)}) %collective-permute-start.31) | collective-permute-done | bytes 524320 | tf_op jit(solution)/shard_map/ppermute | solution.py:450
  286.4 5.9 %restore.1 = (bf16[256,2048]{1,0:T(8,128)(2,1)}, bf16[256,2048]{1,0:T(8,128)(2,1)}) custom-call(s32[3]{0:T(128)} %pad_add_fusion.where_ref, f32[256,1]{1,0:T(8,128)} %convert_element_type.62.ids_ref, bf16[64,4096]{1,0:T(8,128)(2,1)} %get-tuple-element.126.refs_0_, bf16[64,4096]{1,0:T(8,128)(2,1)} %get-tuple-element.127.refs_1_, bf16[64,4096]{1,0:T(8,128)(2,1)} %copy-done.17, ...), custom_call_target="tpu_custom_call" | custom-call | flops 1000 | bytes 1000 | tf_op jit(solution)/shard_map/restore/pallas_call | solution.py:233
  (131 shorter events, 45.2 us)
Async XLA Ops:
  7.2 31.5 %all-gather.2.cloned.1.call-start = ((), (), s32[]{:S(2)}) async-start(), calls=%async_computation | async-start | bytes 1310720 | tf_op jit(solution)/shard_map/all_gather | solution.py:519
  11.2 24.6 %collective-permute-start.6 = (bf16[4,256,256]{2,1,0:T(8,128)(2,1)S(1)}, bf16[4,256,256]{2,1,0:T(8,128)(2,1)S(1)}, u32[]{:S(2)}, u32[]{:S(2)}) collective-permute-start(bf16[4,256,256]{2,1,0:T(8,128)(2,1)S(1)} %pad_maximum_fusion.refs_0_), channel_id=1, source_target_pairs={{0,16},{4,20},{8,24},{12,28},{16,0},{20,4},{24,8},{28,12},{1,17},{... | collective-permute-start | bytes 1572872 | tf_op jit(solution)/shard_map/ppermute | solution.py:445
  12.8 23.1 %collective-permute-start.4 = (bf16[4,256,256]{2,1,0:T(8,128)(2,1)S(1)}, bf16[4,256,256]{2,1,0:T(8,128)(2,1)S(1)}, u32[]{:S(2)}, u32[]{:S(2)}) collective-permute-start(bf16[4,256,256]{2,1,0:T(8,128)(2,1)S(1)} %pad_maximum_fusion.refs_0_), channel_id=1, source_target_pairs={{0,8},{4,12},{8,0},{12,4},{16,24},{20,28},{24,16},{28,20},{1,9},{5... | collective-permute-start | bytes 1572872 | tf_op jit(solution)/shard_map/ppermute | solution.py:445
  14.3 22.1 %collective-permute-start.3 = (bf16[4,256,256]{2,1,0:T(8,128)(2,1)S(1)}, bf16[4,256,256]{2,1,0:T(8,128)(2,1)S(1)}, u32[]{:S(2)}, u32[]{:S(2)}) collective-permute-start(bf16[4,256,256]{2,1,0:T(8,128)(2,1)S(1)} %pad_maximum_fusion.refs_0_), channel_id=1, source_target_pairs={{0,4},{4,0},{8,12},{12,8},{16,20},{20,16},{24,28},{28,24},{1,5},{5... | collective-permute-start | bytes 1572872 | tf_op jit(solution)/shard_map/ppermute | solution.py:445
  38.7 27.2 %collective-permute-start.18 = (bf16[2048,256]{1,0:T(8,128)(2,1)}, bf16[2048,256]{1,0:T(8,128)(2,1)S(1)}, u32[]{:S(2)}, u32[]{:S(2)}) collective-permute-start(bf16[2048,256]{1,0:T(8,128)(2,1)} %all-gather.2.cloned.1.call-done.refs_8_), channel_id=1, source_target_pairs={{0,24},{4,28},{8,16},{12,20},{16,8},{20,12},{24,0},{28,4},{1,25},{... | collective-permute-start | bytes 3145736 | tf_op jit(solution)/shard_map/ppermute | solution.py:445
  39.9 52.7 %collective-permute-start.17 = (bf16[2048,256]{1,0:T(8,128)(2,1)}, bf16[2048,256]{1,0:T(8,128)(2,1)S(1)}, u32[]{:S(2)}, u32[]{:S(2)}) collective-permute-start(bf16[2048,256]{1,0:T(8,128)(2,1)} %all-gather.2.cloned.1.call-done.refs_8_), channel_id=1, source_target_pairs={{0,16},{4,20},{8,24},{12,28},{16,0},{20,4},{24,8},{28,12},{1,17},{... | collective-permute-start | bytes 3145736 | tf_op jit(solution)/shard_map/ppermute | solution.py:445
  41.4 51.2 %collective-permute-start.16 = (bf16[2048,256]{1,0:T(8,128)(2,1)}, bf16[2048,256]{1,0:T(8,128)(2,1)}, u32[]{:S(2)}, u32[]{:S(2)}) collective-permute-start(bf16[2048,256]{1,0:T(8,128)(2,1)} %all-gather.2.cloned.1.call-done.refs_8_), channel_id=1, source_target_pairs={{0,8},{4,12},{8,0},{12,4},{16,24},{20,28},{24,16},{28,20},{1,9},{5... | collective-permute-start | bytes 3145736 | tf_op jit(solution)/shard_map/ppermute | solution.py:445
  51.3 42.0 %collective-permute-start.13 = (bf16[128,2048]{1,0:T(8,128)(2,1)}, bf16[128,2048]{1,0:T(8,128)(2,1)S(1)}, u32[]{:S(2)}, u32[]{:S(2)}) collective-permute-start(bf16[128,2048]{1,0:T(8,128)(2,1)} %get-tuple-element.85), channel_id=1, source_target_pairs={{0,1},{1,2},{2,3},{3,0},{4,5},{5,6},{6,7},{7,4},{8,9},{9,10},{10,1... | collective-permute-start | bytes 1572872 | tf_op jit(solution)/shard_map/ppermute | solution.py:450
  52.9 41.9 %collective-permute-start.14 = (bf16[128,2048]{1,0:T(8,128)(2,1)}, bf16[128,2048]{1,0:T(8,128)(2,1)}, u32[]{:S(2)}, u32[]{:S(2)}) collective-permute-start(bf16[128,2048]{1,0:T(8,128)(2,1)} %get-tuple-element.86), channel_id=1, source_target_pairs={{0,2},{1,3},{2,0},{3,1},{4,6},{5,7},{6,4},{7,5},{8,10},{9,11},{10,... | collective-permute-start | bytes 1572872 | tf_op jit(solution)/shard_map/ppermute | solution.py:450
  65.9 38.3 %collective-permute-start.15 = (bf16[128,2048]{1,0:T(8,128)(2,1)}, bf16[128,2048]{1,0:T(8,128)(2,1)}, u32[]{:S(2)}, u32[]{:S(2)}) collective-permute-start(bf16[128,2048]{1,0:T(8,128)(2,1)} %get-tuple-element.87), channel_id=1, source_target_pairs={{0,3},{1,0},{2,1},{3,2},{4,7},{5,4},{6,5},{7,6},{8,11},{9,8},{10,9... | collective-permute-start | bytes 1572872 | tf_op jit(solution)/shard_map/ppermute | solution.py:450
  92.7 38.5 %collective-permute-start.19 = (bf16[2048,256]{1,0:T(8,128)(2,1)S(1)}, bf16[2048,256]{1,0:T(8,128)(2,1)S(1)}, u32[]{:S(2)}, u32[]{:S(2)}) collective-permute-start(bf16[2048,256]{1,0:T(8,128)(2,1)S(1)} %copy-done.2), channel_id=1, source_target_pairs={{0,4},{4,0},{8,12},{12,8},{16,20},{20,16},{24,28},{28,24},{1,5},{5... | collective-permute-start | bytes 3145736 | tf_op jit(solution)/shard_map/ppermute | solution.py:445
  92.8 38.4 %collective-permute-start.20 = (bf16[2048,256]{1,0:T(8,128)(2,1)}, bf16[2048,256]{1,0:T(8,128)(2,1)S(1)}, u32[]{:S(2)}, u32[]{:S(2)}) collective-permute-start(bf16[2048,256]{1,0:T(8,128)(2,1)} %collective-permute-done.16.refs_10_), channel_id=1, source_target_pairs={{0,4},{4,0},{8,12},{12,8},{16,20},{20,16},{24,28},{28,24},{1,5},{5... | collective-permute-start | bytes 3145736 | tf_op jit(solution)/shard_map/ppermute | solution.py:445
  94.9 37.9 %collective-permute-start.21 = (bf16[2048,256]{1,0:T(8,128)(2,1)S(1)}, bf16[2048,256]{1,0:T(8,128)(2,1)S(1)}, u32[]{:S(2)}, u32[]{:S(2)}) collective-permute-start(bf16[2048,256]{1,0:T(8,128)(2,1)S(1)} %collective-permute-done.17.refs_12_), channel_id=1, source_target_pairs={{0,4},{4,0},{8,12},{12,8},{16,20},{20,16},{24,28},{28,24},{1,5},{5... | collective-permute-start | bytes 3145736 | tf_op jit(solution)/shard_map/ppermute | solution.py:445
  104.1 28.6 %collective-permute-start.22 = (bf16[2048,256]{1,0:T(8,128)(2,1)S(1)}, bf16[2048,256]{1,0:T(8,128)(2,1)S(1)}, u32[]{:S(2)}, u32[]{:S(2)}) collective-permute-start(bf16[2048,256]{1,0:T(8,128)(2,1)S(1)} %collective-permute-done.18.refs_14_), channel_id=1, source_target_pairs={{0,4},{4,0},{8,12},{12,8},{16,20},{20,16},{24,28},{28,24},{1,5},{5... | collective-permute-start | bytes 3145736 | tf_op jit(solution)/shard_map/ppermute | solution.py:445
  127.4 22.8 %collective-permute-start.10 = (bf16[4,64,512]{2,1,0:T(8,128)(2,1)}, bf16[4,64,512]{2,1,0:T(8,128)(2,1)S(1)}, u32[]{:S(2)}, u32[]{:S(2)}) collective-permute-start(bf16[4,64,512]{2,1,0:T(8,128)(2,1)} %get-tuple-element.81), channel_id=1, source_target_pairs={{0,1},{1,2},{2,3},{3,0},{4,5},{5,6},{6,7},{7,4},{8,9},{9,10},{10,1... | collective-permute-start | bytes 786440 | tf_op jit(solution)/shard_map/ppermute | solution.py:450
  189.5 40.8 %collective-permute-start.33 = (bf16[3,256,768]{2,1,0:T(8,128)(2,1)S(1)}, bf16[3,256,768]{2,1,0:T(8,128)(2,1)S(1)}, u32[]{:S(2)}, u32[]{:S(2)}) collective-permute-start(bf16[3,256,768]{2,1,0:T(8,128)(2,1)S(1)} %get-tuple-element.123), channel_id=1, source_target_pairs={{0,8},{4,12},{8,0},{12,4},{16,24},{20,28},{24,16},{28,20},{1,9},{5... | collective-permute-start | bytes 3538952 | tf_op jit(solution)/shard_map/ppermute | solution.py:445
  190.9 53.0 %collective-permute-start.34 = (bf16[3,256,768]{2,1,0:T(8,128)(2,1)S(1)}, bf16[3,256,768]{2,1,0:T(8,128)(2,1)S(1)}, u32[]{:S(2)}, u32[]{:S(2)}) collective-permute-start(bf16[3,256,768]{2,1,0:T(8,128)(2,1)S(1)} %get-tuple-element.124), channel_id=1, source_target_pairs={{0,16},{4,20},{8,24},{12,28},{16,0},{20,4},{24,8},{28,12},{1,17},{... | collective-permute-start | bytes 3538952 | tf_op jit(solution)/shard_map/ppermute | solution.py:445
  191.4 52.5 %collective-permute-start.35 = (bf16[3,256,768]{2,1,0:T(8,128)(2,1)S(1)}, bf16[3,256,768]{2,1,0:T(8,128)(2,1)S(1)}, u32[]{:S(2)}, u32[]{:S(2)}) collective-permute-start(bf16[3,256,768]{2,1,0:T(8,128)(2,1)S(1)} %get-tuple-element.125), channel_id=1, source_target_pairs={{0,24},{4,28},{8,16},{12,20},{16,8},{20,12},{24,0},{28,4},{1,25},{... | collective-permute-start | bytes 3538952 | tf_op jit(solution)/shard_map/ppermute | solution.py:445
  193.1 37.3 %collective-permute-start.23 = (bf16[64,4096]{1,0:T(8,128)(2,1)S(1)}, bf16[64,4096]{1,0:T(8,128)(2,1)S(1)}, u32[]{:S(2)}, u32[]{:S(2)}) collective-permute-start(bf16[64,4096]{1,0:T(8,128)(2,1)S(1)} %copy-done.28), channel_id=1, source_target_pairs={{0,3},{1,0},{2,1},{3,2},{4,7},{5,4},{6,5},{7,6},{8,11},{9,8},{10,9... | collective-permute-start | bytes 1572872 | tf_op jit(solution)/shard_map/ppermute | solution.py:450
  196.1 68.0 %collective-permute-start.24 = (bf16[64,4096]{1,0:T(8,128)(2,1)}, bf16[64,4096]{1,0:T(8,128)(2,1)S(1)}, u32[]{:S(2)}, u32[]{:S(2)}) collective-permute-start(bf16[64,4096]{1,0:T(8,128)(2,1)} %get-tuple-element.99), channel_id=1, source_target_pairs={{0,2},{1,3},{2,0},{3,1},{4,6},{5,7},{6,4},{7,5},{8,10},{9,11},{10,... | collective-permute-start | bytes 1572872 | tf_op jit(solution)/shard_map/ppermute | solution.py:450
  230.4 33.8 %collective-permute-start.25 = (bf16[64,4096]{1,0:T(8,128)(2,1)}, bf16[64,4096]{1,0:T(8,128)(2,1)}, u32[]{:S(2)}, u32[]{:S(2)}) collective-permute-start(bf16[64,4096]{1,0:T(8,128)(2,1)} %get-tuple-element.100), channel_id=1, source_target_pairs={{0,1},{1,2},{2,3},{3,0},{4,5},{5,6},{6,7},{7,4},{8,9},{9,10},{10,1... | collective-permute-start | bytes 1572872 | tf_op jit(solution)/shard_map/ppermute | solution.py:450
  230.4 45.0 %collective-permute-start.30 = (bf16[64,4096]{1,0:T(8,128)(2,1)}, bf16[64,4096]{1,0:T(8,128)(2,1)}, u32[]{:S(2)}, u32[]{:S(2)}) collective-permute-start(bf16[64,4096]{1,0:T(8,128)(2,1)} %get-tuple-element.120), channel_id=1, source_target_pairs={{0,3},{1,0},{2,1},{3,2},{4,7},{5,4},{6,5},{7,6},{8,11},{9,8},{10,9... | collective-permute-start | bytes 1572872 | tf_op jit(solution)/shard_map/ppermute | solution.py:450
  243.9 41.0 %collective-permute-start.31 = (bf16[64,4096]{1,0:T(8,128)(2,1)}, bf16[64,4096]{1,0:T(8,128)(2,1)}, u32[]{:S(2)}, u32[]{:S(2)}) collective-permute-start(bf16[64,4096]{1,0:T(8,128)(2,1)} %get-tuple-element.121), channel_id=1, source_target_pairs={{0,2},{1,3},{2,0},{3,1},{4,6},{5,7},{6,4},{7,5},{8,10},{9,11},{10,... | collective-permute-start | bytes 1572872 | tf_op jit(solution)/shard_map/ppermute | solution.py:450
  243.9 42.5 %collective-permute-start.32 = (bf16[64,4096]{1,0:T(8,128)(2,1)}, bf16[64,4096]{1,0:T(8,128)(2,1)}, u32[]{:S(2)}, u32[]{:S(2)}) collective-permute-start(bf16[64,4096]{1,0:T(8,128)(2,1)} %get-tuple-element.122), channel_id=1, source_target_pairs={{0,1},{1,2},{2,3},{3,0},{4,5},{5,6},{6,7},{7,4},{8,9},{9,10},{10,1... | collective-permute-start | bytes 1572872 | tf_op jit(solution)/shard_map/ppermute | solution.py:450
  (42 other events, 612.1 us)
Sparse Core Ops, SparseCore 0:
  9.6 28.4 all-gather.1

commit v4 on v3

--- a/solution.py
+++ b/solution.py
@@ -13,6 +13,8 @@
 HEAD_SIZE = 128
 PIECE = 256
 PARTS = 2
+SENT_STACKED = (False, True)
+BACK_STACKED = (True, False)
 
 epsilon = 1e-06
 masked_score = -1e30
@@ -52,7 +54,7 @@
 
 
 def shifted_slots(position, owner, experts, capacity):
-    expert = lax.rem(position // capacity + owner, experts)
+    expert = jnp.bitwise_xor(position // capacity, owner)
     return (expert * capacity + lax.rem(position, capacity)).astype(F32)
 
 
@@ -60,6 +62,14 @@
     return pltpu.CompilerParams(vmem_limit_bytes=VMEM_LIMIT)
 
 
+def entry(refs, d, owner):
+    return refs[0].at[jnp.bitwise_xor(owner, d)] if len(refs) == 1 else refs[d]
+
+
+def arrays(stacked, experts, shape):
+    return [(experts,) + shape] if stacked else [shape] * experts
+
+
 def brief():
     return pl.CostEstimate(flops=1000, bytes_accessed=1000, transcendentals=0)
 
@@ -73,8 +83,17 @@
 
 
 def attend_kernel(experts, capacity, heads, n_ctx, where_ref, q_ref, ids_ref, *refs):
-    kv_refs, refs = refs[:n_ctx], refs[n_ctx:]
-    out_refs, refs = refs[: experts * PARTS], refs[experts * PARTS :]
+    count = n_ctx // 2 + 2
+    own, own_core, *chips, cores = refs[:count]
+    refs = refs[count:]
+    blocks = [own, own_core]
+    for j, chip in enumerate(chips):
+        blocks += [chip, cores.at[j]]
+    out_refs = []
+    for stacked in SENT_STACKED:
+        count = 1 if stacked else experts
+        out_refs.append(refs[:count])
+        refs = refs[count:]
     k_scr, v_scr, best_scr, acc_scr, att_scr = refs
     ctx, owner = where_ref[0], where_ref[1]
     seq = pl.program_id(0)
@@ -88,8 +107,8 @@
 
     for m in range(n_ctx):
         index = jnp.bitwise_xor(ctx, m)
-        k_scr[index] = kv_refs[m][0, :, :HEAD_SIZE]
-        v_scr[index, :, :HEAD_SIZE] = kv_refs[m][0, :, HEAD_SIZE:]
+        k_scr[index] = blocks[m][0, :, :HEAD_SIZE]
+        v_scr[index, :, :HEAD_SIZE] = blocks[m][0, :, HEAD_SIZE:]
 
     def fold(t, last):
         key_tile = k_scr[pl.ds(2 * t, 2)].reshape(tile, HEAD_SIZE)
@@ -131,22 +150,25 @@
     slots = shifted_slots(position, owner, experts, capacity)
     for b in range(per_seq):
         source = seq * per_seq + b
-        target = slots_row(ids_ref[lax.rem(owner - source + experts, experts)], capacity)
+        target = slots_row(ids_ref[source], capacity)
         picked = dot(one_hot(slots == target), att_scr[b * n : (b + 1) * n, :]).astype(BF16)
         for d in range(experts):
-            rank = lax.rem(owner + d - source + experts, experts)
+            rank = jnp.bitwise_xor(jnp.bitwise_xor(owner, d), source)
             for c in range(PARTS):
                 first = d * capacity + c * part
-                out_refs[c * experts + d][rank] = picked[first : first + part]
+                entry(out_refs[c], d, owner)[rank] = picked[first : first + part]
 
 
 def attend(where, queries, key_values, ids, capacity):
     seqs, block, width = queries.shape
-    n_ctx = len(key_values)
+    n_ctx = 2 * (len(key_values) - 2)
     experts, _, n = ids.shape
     heads = width // HEAD_SIZE
     part = capacity // PARTS
     by_seq = pl.BlockSpec((1, block, 2 * HEAD_SIZE), lambda s: (s, 0, 0))
+    shapes = []
+    for stacked in SENT_STACKED:
+        shapes += arrays(stacked, experts, (experts, part, width))
     outs = pl.pallas_call(
         functools.partial(attend_kernel, experts, capacity, heads, n_ctx),
         grid=(seqs,),
@@ -155,8 +177,9 @@
             pl.BlockSpec((1, block, width), lambda s: (s, 0, 0)),
             whole(experts, 1, n),
         ]
-        + [by_seq] * n_ctx,
-        out_specs=[whole(experts, part, width)] * (PARTS * experts),
+        + [by_seq] * (len(key_values) - 1)
+        + [pl.BlockSpec((n_ctx // 2 - 1, 1, block, 2 * HEAD_SIZE), lambda s: (0, s, 0, 0))],
+        out_specs=[whole(*shape) for shape in shapes],
         scratch_shapes=[
             pltpu.VMEM((n_ctx, block, HEAD_SIZE), BF16),
             pltpu.VMEM((n_ctx, block, 2 * HEAD_SIZE), BF16),
@@ -164,55 +187,61 @@
             pltpu.VMEM((heads, block, 2 * HEAD_SIZE), F32),
             pltpu.VMEM((block, width), BF16),
         ],
-        out_shape=[jax.ShapeDtypeStruct((experts, part, width), BF16)] * (PARTS * experts),
+        out_shape=[jax.ShapeDtypeStruct(shape, BF16) for shape in shapes],
         compiler_params=kernel_params(),
         cost_estimate=brief(),
         name="attend",
     )(where, queries, ids, *key_values)
-    return [outs[c * experts : (c + 1) * experts] for c in range(PARTS)]
-
-
-def place_kernel(experts, capacity, where_ref, ids_ref, rows_ref, *refs):
-    out_refs, pick_scr = refs[:-1], refs[-1]
-
+    sent = []
+    for stacked in SENT_STACKED:
+        count = 1 if stacked else experts
+        sent.append(list(outs[:count]))
+        outs = outs[count:]
+    return sent
+
+
+def place_kernel(capacity, ids_ref, rows_ref, out_ref, pick_scr):
     @pl.when(pl.program_id(0) == 0)
     def _():
         position = iota(pick_scr.shape, 0)
-        slots = shifted_slots(position, where_ref[1], experts, capacity)
-        pick_scr[...] = one_hot(slots == slots_row(ids_ref[...], capacity))
-
-    picked = dot(pick_scr[...], rows_ref[...]).astype(BF16)
-    for d, ref in enumerate(out_refs):
-        ref[...] = picked[d * capacity : (d + 1) * capacity]
-
-
-def place(where, ids_row, rows, experts, capacity):
+        pick_scr[...] = one_hot(position.astype(F32) == slots_row(ids_ref[...], capacity))
+
+    out_ref[...] = dot(pick_scr[...], rows_ref[...]).astype(BF16).reshape(out_ref.shape)
+
+
+def place(ids_row, rows, experts, capacity):
     n, width = rows.shape
     cols = min(width, 1024)
     return pl.pallas_call(
-        functools.partial(place_kernel, experts, capacity),
+        functools.partial(place_kernel, capacity),
         grid=(width // cols,),
-        in_specs=[smem(), whole(1, n), pl.BlockSpec((n, cols), lambda i: (0, i))],
-        out_specs=[pl.BlockSpec((capacity, cols), lambda i: (0, i))] * experts,
-        out_shape=[jax.ShapeDtypeStruct((capacity, width), BF16)] * experts,
+        in_specs=[whole(1, n), pl.BlockSpec((n, cols), lambda i: (0, i))],
+        out_specs=pl.BlockSpec((experts, capacity, cols), lambda i: (0, 0, i)),
+        out_shape=jax.ShapeDtypeStruct((experts, capacity, width), BF16),
         scratch_shapes=[pltpu.VMEM((experts * capacity, n), BF16)],
         compiler_params=kernel_params(),
         cost_estimate=brief(),
         name="place",
-    )(where, ids_row, rows)
+    )(ids_row, rows)
 
 
 def restore_kernel(experts, capacity, tiles, where_ref, ids_ref, *refs):
-    parts, refs = refs[: experts * PARTS], refs[experts * PARTS :]
-    layer_ref, grad_ref, pick_scr = refs
+    *refs, layer_ref, grad_ref, pick_scr = refs
+    parts = []
+    for stacked in BACK_STACKED:
+        count = 1 if stacked else experts
+        parts.append(refs[:count])
+        refs = refs[count:]
+    owner = where_ref[1]
     step = pl.program_id(0)
 
     @pl.when(step == 0)
     def _():
-        slots = shifted_slots(iota(pick_scr.shape, 1), where_ref[1], experts, capacity)
+        slots = shifted_slots(iota(pick_scr.shape, 1), owner, experts, capacity)
         pick_scr[...] = one_hot(slots == slots_column(ids_ref[...], capacity))
 
-    rows = jnp.concatenate([ref[...] for ref in parts], axis=0)
+    rows = [entry(parts[c], d, owner)[...] for d in range(experts) for c in range(PARTS)]
+    rows = jnp.concatenate(rows, axis=0)
     out = dot(pick_scr[...], rows).astype(BF16)
 
     @pl.when(step < tiles)
@@ -226,15 +255,19 @@
 
 def restore(where, ids_column, parts, experts, capacity):
     n = ids_column.shape[0]
-    part, both = parts[0][0].shape
+    part, both = parts[0][0].shape[-2:]
     width = both // 2
     cols = min(width, 1024)
     tiles = width // cols
+    flat = [x for values in parts for x in values]
     return pl.pallas_call(
         functools.partial(restore_kernel, experts, capacity, tiles),
         grid=(2 * tiles,),
         in_specs=[smem(), whole(n, 1)]
-        + [pl.BlockSpec((part, cols), lambda i: (0, i))] * (experts * PARTS),
+        + [
+            pl.BlockSpec(x.shape[:-1] + (cols,), lambda i, zeros=(0,) * (x.ndim - 1): zeros + (i,))
+            for x in flat
+        ],
         out_specs=[
             pl.BlockSpec((n, cols), lambda i: (0, jnp.minimum(i, tiles - 1))),
             pl.BlockSpec((n, cols), lambda i: (0, jnp.maximum(i - tiles, 0))),
@@ -244,27 +277,35 @@
         compiler_params=kernel_params(),
         cost_estimate=brief(),
         name="restore",
-    )(where, ids_column, *[parts[c][d] for d in range(experts) for c in range(PARTS)])
+    )(where, ids_column, *flat)
 
 
 def expert_kernel(pieces, experts, capacity, part_index, where_ref, *refs):
-    att_refs, refs = refs[:experts], refs[experts:]
-    grad_refs, refs = refs[:experts], refs[experts:]
-    w_refs, refs = refs[:pieces], refs[pieces:]
+    count = 1 if SENT_STACKED[part_index] else experts
+    att_refs, refs = refs[:count], refs[count:]
+    grad_ref, own_ref, refs = refs[0], refs[1], refs[2:]
+    count = pieces // 2 + 2
+    w_refs, refs = refs[:count], refs[count:]
     gate_hbm, up_hbm, down_hbm, gain_ref, ids_ref, weight_ref = refs[:6]
     refs = refs[6:]
-    out_refs, refs = refs[:experts], refs[experts:]
+    count = 1 if BACK_STACKED[part_index] else experts
+    out_refs, refs = refs[:count], refs[count:]
     normed_ref, back_ref, units_ref, back_gate_ref, back_up_ref = refs[:5]
     w_scr, gate_scr, up_scr, down_scr, hidden_scr, back_in_scr, sems = refs[5:]
-    part, width = grad_refs[0].shape
+    _, part, width = grad_ref.shape
     rows = experts * part
-    att_cols = att_refs[0].shape[2]
-    piece = w_refs[0].shape[1]
+    att_cols = att_refs[0].shape[-1]
+    piece = w_scr.shape[3]
     ff = units_ref.shape[1]
     piece_index, owner = where_ref[2], where_ref[1]
-
+    sources = [jnp.bitwise_xor(owner, d) for d in range(experts)]
+
+    own, own_core, *chips, cores = w_refs
+    blocks = [own, own_core]
+    for j, chip in enumerate(chips):
+        blocks += [chip, cores.at[j]]
     copies = [
-        pltpu.make_async_copy(w_refs[m], w_scr.at[m], sems.at[m]) for m in range(pieces)
+        pltpu.make_async_copy(block, w_scr.at[m], sems.at[m]) for m, block in enumerate(blocks)
     ]
     first = pieces
     weight_copies = (
@@ -279,27 +320,26 @@
 
     n = ids_ref.shape[2]
     weights = []
-    for s in range(experts):
-        target = slots_row(ids_ref[s], capacity)
+    for s, source in enumerate(sources):
+        target = slots_row(ids_ref[source], capacity)
         slot = iota((part, n), 0) + (owner * capacity + part_index * part)
         weights.append(
             jnp.sum(
-                jnp.where(slot.astype(F32) == target, weight_ref[s], 0.0), axis=1, keepdims=True
+                jnp.where(slot.astype(F32) == target, weight_ref[source], 0.0),
+                axis=1,
+                keepdims=True,
             )
         )
-        grads = grad_refs[s][...].astype(F32)
+        grads = grad_ref[source].astype(F32)
         back_ref[s * part : (s + 1) * part, :] = (weights[s] * grads).astype(BF16)
 
     for m in range(pieces):
         copies[m].wait()
+        column = pl.multiple_of(jnp.bitwise_xor(piece_index, m) * piece, piece)
         total = jnp.zeros((rows, piece), F32)
         for d in range(experts):
-            source = lax.rem(owner - d + experts, experts)
-            at = pl.multiple_of(source * att_cols, att_cols)
-            total += dot(
-                att_refs[d][...].reshape(rows, att_cols), w_scr[m, pl.ds(at, att_cols), :]
-            )
-        column = pl.multiple_of(jnp.bitwise_xor(piece_index, m) * piece, piece)
+            block = own_ref[:, pl.ds(column, piece)] if d == 0 else w_scr[m, d - 1]
+            total += dot(entry(att_refs, d, owner)[...].reshape(rows, att_cols), block)
         hidden_scr[:, pl.ds(column, piece)] = total.astype(BF16)
 
     squares = jnp.zeros((rows, 1), F32)
@@ -331,7 +371,7 @@
         result = dot(units_ref[...], down_scr[:, t : t + PIECE]).astype(BF16).astype(F32)
         layer = (hidden + weight * result).astype(BF16)
         for s in range(experts):
-            out_refs[s][:, t : t + PIECE] = layer[s * part : (s + 1) * part]
+            entry(out_refs, s, owner)[:, t : t + PIECE] = layer[s * part : (s + 1) * part]
         back_in = dot(back_gate_ref[...], gate_scr[t : t + PIECE, :], ((1,), (1,)))
         back_in += dot(back_up_ref[...], up_scr[t : t + PIECE, :], ((1,), (1,)))
         back_in = back_in.astype(BF16)
@@ -344,35 +384,39 @@
         scaled = back_in_scr[:, t : t + PIECE].astype(F32) * gain_ref[:, t : t + PIECE]
         change = inv * (scaled - unit * moment)
         for s in range(experts):
-            grads = grad_refs[s][:, t : t + PIECE].astype(F32)
-            out_refs[s][:, width + t : width + t + PIECE] = (
+            grads = grad_ref[sources[s], :, t : t + PIECE].astype(F32)
+            entry(out_refs, s, owner)[:, width + t : width + t + PIECE] = (
                 grads + change[s * part : (s + 1) * part]
             ).astype(BF16)
 
 
-def expert_part(where, att, grads, projection, gate, up, down, gain, ids, weights, capacity, index):
-    experts, part, att_cols = att[0].shape
-    pieces = len(projection)
-    depth, piece = projection[0].shape
-    width = grads[0].shape[1]
+def expert_part(
+    where, att, grads, own, projection, gate, up, down, gain, ids, weights, capacity, index
+):
+    experts, part, att_cols = att[0].shape[-3:]
+    pieces = 2 * (len(projection) - 2)
+    piece = projection[0].shape[-1]
+    width = grads.shape[2]
     ff = gate.shape[2]
     rows = experts * part
     n = ids.shape[2]
     out = lambda *shape: jax.ShapeDtypeStruct(shape, BF16)
+    back = arrays(BACK_STACKED[index], experts, (part, 2 * width))
     in_hbm = pl.BlockSpec(memory_space=pl.ANY)
     outs = pl.pallas_call(
         functools.partial(expert_kernel, pieces, experts, capacity, index),
         grid=(1,),
         in_specs=[smem()]
-        + [whole(experts, part, att_cols)] * experts
-        + [pl.BlockSpec((part, width), lambda i: (index, 0))] * experts
-        + [in_hbm] * (pieces + 3)
+        + [whole(*x.shape) for x in att]
+        + [pl.BlockSpec((experts, part, width), lambda i: (0, index, 0))]
+        + [whole(*own.shape)]
+        + [in_hbm] * (len(projection) + 3)
         + [whole(1, width), whole(experts, 1, n), whole(experts, 1, n)],
-        out_specs=[whole(part, 2 * width)] * experts
+        out_specs=[whole(*shape) for shape in back]
         + [whole(rows, width)] * 2
         + [whole(rows, ff)] * 3,
         scratch_shapes=[
-            pltpu.VMEM((pieces, depth, piece), BF16),
+            pltpu.VMEM((pieces, experts - 1, att_cols, piece), BF16),
             pltpu.VMEM((width, ff), BF16),
             pltpu.VMEM((width, ff), BF16),
             pltpu.VMEM((ff, width), BF16),
@@ -380,12 +424,12 @@
             pltpu.VMEM((rows, width), BF16),
             pltpu.SemaphoreType.DMA((pieces + 3,)),
         ],
-        out_shape=[out(part, 2 * width)] * experts + [out(rows, width)] * 2 + [out(rows, ff)] * 3,
+        out_shape=[out(*shape) for shape in back] + [out(rows, width)] * 2 + [out(rows, ff)] * 3,
         compiler_params=kernel_params(),
         cost_estimate=brief(),
         name="expert",
-    )(where, *att, *grads, *projection, gate, up, down, gain, ids, weights)
-    return outs[:experts], outs[experts:]
+    )(where, *att, grads, own, *projection, gate, up, down, gain, ids, weights)
+    return outs[: len(back)], outs[len(back) :]
 
 
 def weight_kernel(count, *refs):
@@ -445,17 +489,23 @@
     return lax.ppermute(value, "ctx", [(i, i ^ mask) for i in range(count)])
 
 
-def shift(value, by):
+def to_owner(value, mask):
     count = lax.axis_size("exp")
-    return lax.ppermute(value, "exp", [(i, (i + by) % count) for i in range(count)])
+    return lax.ppermute(value, "exp", [(i, i ^ mask) for i in range(count)])
+
+
+def to_owners(values):
+    if len(values) == 1:
+        return [lax.all_to_all(values[0], "exp", 0, 0, tiled=True)]
+    return [values[0]] + [to_owner(values[d], d) for d in range(len(values) - 1, 0, -1)][::-1]
 
 
 def from_chips(value, count):
-    return [value] + [partner(value, m) for m in range(2, count, 2)]
-
-
-def with_cores(held):
-    return [x for value in held for x in (value, partner(value, 1))]
+    return [partner(value, m) for m in range(2, count, 2)]
+
+
+def with_cores(value, own_core, chips):
+    return [value, own_core, *chips, partner(jnp.stack(chips), 1)]
 
 
 def halved(value, bits, order, ctx):
@@ -501,30 +551,37 @@
     piece_index = ctx % pieces
     where = jnp.stack([ctx, owner, piece_index]).astype(jnp.int32)
 
+    ids_f = expert_ids.astype(F32)
+    info = jnp.stack([ids_f[:, 0], gate_weights[:, 0]])
+    info = lax.all_gather(info, "exp")
+    ids_all, weights_all = info[:, 0:1, :], info[:, 1:2, :]
+
+    grads = place(ids_f.reshape(1, n), grad_out, experts, capacity)
+
     first_column = (owner * heads_dev // group) * HEAD_SIZE
     keys = lax.dynamic_slice_in_dim(rotated_key_heads, first_column, HEAD_SIZE, 2)
     values = lax.dynamic_slice_in_dim(value_head_rows, first_column, HEAD_SIZE, 2)
-    key_values = jnp.concatenate([keys, values], axis=2)
-    key_values = with_cores(from_chips(key_values, ctx_count))
-
-    ids_f = expert_ids.astype(F32)
-    info = jnp.stack([ids_f[:, 0], gate_weights[:, 0]])
-    info = jnp.stack([info] + [shift(info, d) for d in range(1, experts)])
-    ids_all, weights_all = info[:, 0:1, :], info[:, 1:2, :]
-
-    grads = place(where, ids_f.reshape(1, n), grad_out, experts, capacity)
-    grads = [grads[0]] + [shift(grads[d], d) for d in range(1, experts)]
+    own = jnp.concatenate([keys, values], axis=2)
+    grads = lax.all_to_all(grads, "exp", 0, 0, tiled=True)
+    chips = from_chips(own, ctx_count)
 
     mine = lax.dynamic_slice_in_dim(out_proj, piece_index * piece, piece, 1)
-    mine = lax.all_gather(mine, "exp", axis=0, tiled=True)
-    mine, key_values = lax.optimization_barrier((mine, key_values))
-    projection = from_chips(mine, pieces)
+    mine = lax.all_gather(mine, "exp", axis=0)
+    mine, chips = lax.optimization_barrier((mine, chips))
+    key_values = with_cores(own, partner(own, 1), chips)
+    mine = jnp.concatenate(
+        [lax.dynamic_slice_in_dim(mine, owner ^ d, 1, 0) for d in range(1, exp_count)]
+    )
+    own_core = partner(mine, 1)
+    chips = from_chips(mine, pieces)
 
     attended = attend(where, queries, key_values, ids_all, capacity)
-    arrived = [[sent[0]] + [shift(sent[d], d) for d in range(1, experts)] for sent in attended[:1]]
-    projection, later = lax.optimization_barrier((projection, attended[1:]))
-    projection = with_cores(projection)
-    arrived += [[sent[0]] + [shift(sent[d], d) for d in range(1, experts)] for sent in later]
+    attended[0], grads = lax.optimization_barrier((attended[0], grads))
+    arrived = [to_owners(attended[0])]
+    chips, attended[1] = lax.optimization_barrier((chips, attended[1]))
+    projection = with_cores(mine, own_core, chips)
+    arrived[0], later = lax.optimization_barrier((arrived[0], attended[1]))
+    arrived.append(to_owners(later))
 
     rows, kept = [], []
     for index, att in enumerate(arrived):
@@ -532,6 +589,7 @@
             where,
             att,
             grads,
+            out_proj,
             projection,
             expert_gate,
             expert_up,
@@ -544,7 +602,7 @@
         )
         rows.append(out)
         kept.append(saved)
-    returned = [[rows[0][0]] + [shift(rows[0][d], -d) for d in range(1, experts)]]
+    returned = [to_owners(rows[0])]
 
     rows_dev = width // ctx_count
     ff = expert_gate.shape[2]
@@ -552,17 +610,14 @@
         (gone,) = weight_blocks(where, *zip(*kept), first=1)
         near = partner(gone, 1)
         (stay,) = weight_blocks(where, *zip(*kept), first=0)
-        pair = [(stay[j].astype(F32) + near[j].astype(F32)) for j in range(ctx_count // 2)]
-        far = [x.astype(BF16) for x in pair[1:]]
-        far, later = lax.optimization_barrier((far, rows[1:]))
-        far = [partner(x, 2 * j + 2) for j, x in enumerate(far)]
-        total = sum([x.astype(F32) for x in far], pair[0])
+        pair = [(stay[j].astype(F32) + near[j].astype(F32)).astype(BF16) for j in range(len(stay))]
+        far = [partner(x, 2 * j + 2) for j, x in enumerate(pair[1:])]
+        total = sum([x.astype(F32) for x in far], pair[0].astype(F32))
         grad_gate, grad_up = total[0][None], total[1][None]
         grad_down = total[2].reshape(PIECE, ff // PIECE, PIECE).transpose(1, 0, 2)
         grad_down = grad_down.reshape(1, ff, PIECE)
     else:
         gone = weight_blocks(where, *zip(*kept))
-        later = rows[1:]
         part_gate, part_up = [x.reshape(ctx_count, rows_dev, ff) for x in gone[:2]]
         part_down = gone[2].reshape(width // PIECE, ff, PIECE // rows_dev, rows_dev)
         part_down = part_down.transpose(0, 2, 1, 3).reshape(ctx_count, ff, rows_dev)
@@ -570,7 +625,7 @@
         grad_gate, grad_up, grad_down = [
             halved(x, bits, order, ctx)[None] for x in (part_gate, part_up, part_down)
         ]
-    returned += [[out[0]] + [shift(out[d], -d) for d in range(1, experts)] for out in later]
+    returned += [to_owners(out) for out in rows[1:]]
     returned, grad_gate, grad_up, grad_down = lax.optimization_barrier(
         (returned, grad_gate, grad_up, grad_down)
     )

time: 303 us -> 329 us (1.086)
  blocking collectives: 0 us -> 20.1 us
  other arithmetic: 7.77 us -> 14.2 us
  starting transfers between devices: 39 us -> 34.6 us
    ppermute x18 -> x6, waiting for transfers between devices: 100 us -> 42.4 us  [to_owner(): return lax.ppermute(value, 'exp', [(i, i ^ mask) for i in range(count)])]
    ppermute x18 -> x14, waiting for transfers between devices: 45.6 us -> 71.2 us  [partner(): return lax.ppermute(value, 'ctx', [(i, i ^ mask) for i in range(count)])]
    ppermute x18 -> x6, starting transfers between devices: 27.2 us -> 6.83 us  [to_owner(): return lax.ppermute(value, 'exp', [(i, i ^ mask) for i in range(count)])]
    all_to_all x0 -> x3, waiting for transfers between devices: none -> 20.1 us  [the longest x2 20.1 us: to_owners(): return [lax.all_to_all(values[0], 'exp', 0, 0, tiled=True)]]
    all_gather x0 -> x1, blocking collectives: none -> 20.1 us  [on_device(): info = lax.all_gather(info, 'exp')]
    all_to_all x0 -> x3, starting transfers between devices: none -> 16.9 us  [the longest x2 11.5 us: to_owners(): return [lax.all_to_all(values[0], 'exp', 0, 0, tiled=True)]]
    all_gather x1, waiting for transfers between devices: 0.01 us -> 12.6 us  [on_device(): mine = lax.all_gather(mine, 'exp', axis=0)]
    another operation x2, other arithmetic: 0.02 us -> 5.84 us  [with_cores(): return [value, own_core, *chips, partner(jnp.stack(chips), 1)]]
  transfers between devices with their start and end apart: 37 -> 24, of which waited for: 17 -> 13; matrix products, arithmetic and copies ran while one was open for 3% -> 7% of each run, Pallas kernels for 18% -> 11%
where the time goes in v4:
time: 329 us; the launch traced here: 327 us
  waiting for transfers between devices  146 us (44%)
  Pallas kernels  84.9 us (26%)
  starting transfers between devices  34.6 us (11%)
  blocking collectives  20.1 us (6%)
  between operations  14.3 us (4%)
  other arithmetic  14.2 us (4%)
  local copies, waits for them, and re-layouts  12.9 us (4%)
    ppermute x14, waiting for transfers between devices, partner(): return lax.ppermute(value, 'ctx', [(i, i ^ mask) for i in range(count)])  71.2 us
    ppermute x6, waiting for transfers between devices, to_owner(): return lax.ppermute(value, 'exp', [(i, i ^ mask) for i in range(count)])  42.4 us
    pallas_call x2, Pallas kernels, expert_part(): pl.pallas_call(functools.partial(expert_kernel, pieces, experts, capacity...  35.1 us
    pallas_call x1, Pallas kernels, attend(): pl.pallas_call(functools.partial(attend_kernel, experts, capacity, heads,...  25.5 us
    all_to_all x2, waiting for transfers between devices, to_owners(): return [lax.all_to_all(values[0], 'exp', 0, 0, tiled=True)]  20.1 us
    all_gather x1, blocking collectives, on_device(): info = lax.all_gather(info, 'exp')  20.1 us
    pallas_call x2, Pallas kernels, weight_blocks(): pl.pallas_call(lambda where_ref, *refs: weight_kernel(count, *refs), grid...  15.3 us
    all_gather x1, waiting for transfers between devices, on_device(): mine = lax.all_gather(mine, 'exp', axis=0)  12.6 us
  transfers between devices with their start and end apart: 24, of which 13 were waited for; matrix products, arithmetic and copies ran while one was open for 7% of the time, Pallas kernels for 11%

profile of v4, /device:TPU:22, one launch (start us, length us, event | category | flops | bytes accessed | tf_op | source)
XLA Modules:
  0.0 327.3 jit_solution(12340209673658025790)
XLA Ops:
  13.6 5.3 %all-to-all-start = ((bf16[4,128,2048]{2,1,0:T(8,128)(2,1)}), bf16[4,128,2048]{2,1,0:T(8,128)(2,1)S(1)}, u32[]{:S(2)}, u32[]{:S(2)}) async-start(bf16[4,128,2048]{2,1,0:T(8,128)(2,1)} %place.1), calls=%async_computation | async-start | bytes 4194304 | tf_op jit(solution)/shard_map/all_to_all | solution.py:565
  23.6 12.3 %collective-permute-done.3.refs_4_ = bf16[4,256,256]{2,1,0:T(8,128)(2,1)S(1)} collective-permute-done((bf16[4,256,256]{2,1,0:T(8,128)(2,1)S(1)}, bf16[4,256,256]{2,1,0:T(8,128)(2,1)S(1)}, u32[]{:S(2)}, u32[]{:S(2)}) %collective-permute-start.3) | collective-permute-done | bytes 524320 | tf_op jit(solution)/shard_map/ppermute | solution.py:489
  35.9 8.8 %collective-permute-done.2.refs_3_ = bf16[4,256,256]{2,1,0:T(8,128)(2,1)S(1)} collective-permute-done((bf16[4,256,256]{2,1,0:T(8,128)(2,1)S(1)}, bf16[4,256,256]{2,1,0:T(8,128)(2,1)S(1)}, u32[]{:S(2)}, u32[]{:S(2)}) %collective-permute-start.2) | collective-permute-done | bytes 524320 | tf_op jit(solution)/shard_map/ppermute | solution.py:489
  45.5 12.6 %all-gather.5.cloned.1.call-done = bf16[2048,256]{1,0:T(8,128)(2,1)} async-done(((bf16[512,256]{1,0:T(8,128)(2,1)}), bf16[2048,256]{1,0:T(8,128)(2,1)}) %all-gather.5.cloned.1.call-update) | async-done | bytes 1048592 | tf_op jit(solution)/shard_map/all_gather | solution.py:569
  65.6 20.1 %all-gather.2 = f32[4,2,256]{2,1,0:T(2,128)S(1)} all-gather(f32[1,2,256]{2,1,0:T(2,128)S(1)} %maximum_bitcast_fusion), channel_id=2, replica_groups=mesh['ctx'=8,'exp'=4] {'exp'}, dimensions={0}, use_global_device_ids=true | all-gather | bytes 10240 | tf_op jit(solution)/shard_map/all_gather | solution.py:556
  87.7 25.5 %attend.1 = (bf16[4,64,512]{2,1,0:T(8,128)(2,1)}, bf16[4,64,512]{2,1,0:T(8,128)(2,1)}, bf16[4,64,512]{2,1,0:T(8,128)(2,1)}, bf16[4,64,512]{2,1,0:T(8,128)(2,1)}, bf16[4,4,64,512]{3,2,1,0:T(8,128)(2,1)}) custom-call(s32[3]{0:T(128)} %pad_add_fusion.where_ref, bf16[4,256,512]{2,1,0:T(8,128)(2,1)} %q_ref.1, ...), custom_call_target="tpu_custom_call" | custom-call | flops 1000 | bytes 1000 | tf_op jit(solution)/shard_map/attend/pallas_call | solution.py:172
  120.8 9.1 %collective-permute-done.5.refs_1_ = bf16[4,64,512]{2,1,0:T(8,128)(2,1)S(1)} collective-permute-done((bf16[4,64,512]{2,1,0:T(8,128)(2,1)}, bf16[4,64,512]{2,1,0:T(8,128)(2,1)S(1)}, u32[]{:S(2)}, u32[]{:S(2)}) %collective-permute-start.5) | collective-permute-done | bytes 262176 | tf_op jit(solution)/shard_map/ppermute | solution.py:494
  129.9 8.6 %collective-permute-done.6.refs_2_ = bf16[4,64,512]{2,1,0:T(8,128)(2,1)S(1)} collective-permute-done((bf16[4,64,512]{2,1,0:T(8,128)(2,1)}, bf16[4,64,512]{2,1,0:T(8,128)(2,1)S(1)}, u32[]{:S(2)}, u32[]{:S(2)}) %collective-permute-start.6) | collective-permute-done | bytes 262176 | tf_op jit(solution)/shard_map/ppermute | solution.py:494
  138.5 6.1 %collective-permute-done.7.refs_3_ = bf16[4,64,512]{2,1,0:T(8,128)(2,1)} collective-permute-done((bf16[4,64,512]{2,1,0:T(8,128)(2,1)}, bf16[4,64,512]{2,1,0:T(8,128)(2,1)}, u32[]{:S(2)}, u32[]{:S(2)}) %collective-permute-start.7) | collective-permute-done | bytes 262176 | tf_op jit(solution)/shard_map/ppermute | solution.py:494
  144.6 4.4 %all-to-all-start.2 = ((bf16[4,4,64,512]{3,2,1,0:T(8,128)(2,1)}), bf16[4,4,64,512]{3,2,1,0:T(8,128)(2,1)}, u32[]{:S(2)}, u32[]{:S(2)}) async-start(bf16[4,4,64,512]{3,2,1,0:T(8,128)(2,1)} %get-tuple-element.76), calls=%async_computation.2 | async-start | bytes 2097152 | tf_op jit(solution)/shard_map/all_to_all | solution.py:499
  151.6 20.1 %all-to-all-done.2.refs_0_ = bf16[4,4,64,512]{3,2,1,0:T(8,128)(2,1)} async-done(((bf16[4,4,64,512]{3,2,1,0:T(8,128)(2,1)}), bf16[4,4,64,512]{3,2,1,0:T(8,128)(2,1)}, u32[]{:S(2)}, u32[]{:S(2)}) %all-to-all-start.2) | async-done | bytes 1048608 | tf_op jit(solution)/shard_map/all_to_all | solution.py:499
  171.7 17.4 %expert.3 = (bf16[64,4096]{1,0:T(8,128)(2,1)}, bf16[64,4096]{1,0:T(8,128)(2,1)}, bf16[64,4096]{1,0:T(8,128)(2,1)}, bf16[64,4096]{1,0:T(8,128)(2,1)}, bf16[256,20...) custom-call(s32[3]{0:T(128)} %pad_add_fusion.where_ref, ...), custom_call_target="tpu_custom_call" | custom-call | flops 1000 | bytes 1000 | tf_op jit(solution)/shard_map/expert/pallas_call | solution.py:406
  189.2 17.7 %expert.2 = (bf16[4,64,4096]{2,1,0:T(8,128)(2,1)}, bf16[256,2048]{1,0:T(8,128)(2,1)}, bf16[256,2048]{1,0:T(8,128)(2,1)}, bf16[256,768]{1,0:T(8,128)(2,1)}, bf16[...) custom-call(s32[3]{0:T(128)} %pad_add_fusion.where_ref, bf16[4,64,512]{2,1,0:T(8,128)(2,1)} %get-tuple-element.67.refs_0_, ...), custom_call_target="tpu_custom_call" | custom-call | flops 1000 | bytes 1000 | tf_op jit(solution)/shard_map/expert/pallas_call | solution.py:406
  206.9 7.7 %weight_grads.3 = bf16[4,3,256,768]{3,2,1,0:T(8,128)(2,1)} custom-call(s32[3]{0:T(128)} %pad_add_fusion.where_ref, bf16[256,2048]{1,0:T(8,128)(2,1)} %get-tuple-element.81.refs_0_, bf16[256,2048]{1,0:T(8,128)(2,1)} %get-tuple-element.82.refs_1_, bf16[256,2048]{1,0:T(8,128)(2,1)} %get-tuple-element.83.refs_2_, bf16[256,2048]{1,0:T(8,128)(2,1)} %get-tuple-element.84.refs_3_, ...), custom_call_target="tpu_custom_call" | custom-call | flops 1000 | bytes 1000 | tf_op jit(solution)/shard_map/weight_grads/pallas_call | solution.py:469
  214.5 7.1 %all-to-all-start.1 = ((bf16[4,64,4096]{2,1,0:T(8,128)(2,1)}), bf16[4,64,4096]{2,1,0:T(8,128)(2,1)S(1)}, u32[]{:S(2)}, u32[]{:S(2)}) async-start(bf16[4,64,4096]{2,1,0:T(8,128)(2,1)} %get-tuple-element.75), calls=%async_computation.1 | async-start | bytes 4194304 | tf_op jit(solution)/shard_map/all_to_all | solution.py:499
  221.6 7.7 %weight_grads.2 = bf16[4,3,256,768]{3,2,1,0:T(8,128)(2,1)} custom-call(s32[3]{0:T(128)} %pad_add_fusion.where_ref, bf16[256,2048]{1,0:T(8,128)(2,1)} %get-tuple-element.81.refs_0_, bf16[256,2048]{1,0:T(8,128)(2,1)} %get-tuple-element.82.refs_1_, bf16[256,2048]{1,0:T(8,128)(2,1)} %get-tuple-element.83.refs_2_, bf16[256,2048]{1,0:T(8,128)(2,1)} %get-tuple-element.84.refs_3_, ...), custom_call_target="tpu_custom_call" | custom-call | flops 1000 | bytes 1000 | tf_op jit(solution)/shard_map/weight_grads/pallas_call | solution.py:469
  229.3 4.0 %fusion.3 = (bf16[3,256,768]{2,1,0:T(8,128)(2,1)S(1)}, bf16[3,256,768]{2,1,0:T(8,128)(2,1)S(1)}, bf16[3,256,768]{2,1,0:T(8,128)(2,1)S(1)}) fusion(bf16[4,3,256,768]{3,2,1,0:T(8,128)(2,1)} %collective-permute-done.16, bf16[4,3,256,768]{3,2,1,0:T(8,128)(2,1)} %weight_grads.2), kind=kLoop, calls=%fused_computation.10 | loop fusion | flops 7077888 | bytes 10616832 | tf_op jit(solution)/shard_map/convert_element_type | solution.py:613
  233.4 3.4 %collective-permute-start.18 = (bf16[3,256,768]{2,1,0:T(8,128)(2,1)S(1)}, bf16[3,256,768]{2,1,0:T(8,128)(2,1)S(1)}, u32[]{:S(2)}, u32[]{:S(2)}) collective-permute-start(bf16[3,256,768]{2,1,0:T(8,128)(2,1)S(1)} %get-tuple-element.103), channel_id=1, source_target_pairs={{0,16},{4,20},{8,24},{12,28},{16,0},{20,4},{24,8},{28,12},{1,17},{... | collective-permute-start | bytes 3538952 | tf_op jit(solution)/shard_map/ppermute | solution.py:489
  239.5 22.7 %collective-permute-done.17 = bf16[3,256,768]{2,1,0:T(8,128)(2,1)S(1)} collective-permute-done((bf16[3,256,768]{2,1,0:T(8,128)(2,1)S(1)}, bf16[3,256,768]{2,1,0:T(8,128)(2,1)S(1)}, u32[]{:S(2)}, u32[]{:S(2)}) %collective-permute-start.17) | collective-permute-done | bytes 1179680 | tf_op jit(solution)/shard_map/ppermute | solution.py:489
  262.7 21.7 %collective-permute-done.19 = bf16[3,256,768]{2,1,0:T(8,128)(2,1)S(1)} collective-permute-done((bf16[3,256,768]{2,1,0:T(8,128)(2,1)S(1)}, bf16[3,256,768]{2,1,0:T(8,128)(2,1)S(1)}, u32[]{:S(2)}, u32[]{:S(2)}) %collective-permute-start.19) | collective-permute-done | bytes 1179680 | tf_op jit(solution)/shard_map/ppermute | solution.py:489
  284.4 3.3 %collective-permute-done.18 = bf16[3,256,768]{2,1,0:T(8,128)(2,1)S(1)} collective-permute-done((bf16[3,256,768]{2,1,0:T(8,128)(2,1)S(1)}, bf16[3,256,768]{2,1,0:T(8,128)(2,1)S(1)}, u32[]{:S(2)}, u32[]{:S(2)}) %collective-permute-start.18) | collective-permute-done | bytes 1179680 | tf_op jit(solution)/shard_map/ppermute | solution.py:489
  294.8 6.8 %collective-permute-done.14.refs_3_ = bf16[64,4096]{1,0:T(8,128)(2,1)} collective-permute-done((bf16[64,4096]{1,0:T(8,128)(2,1)}, bf16[64,4096]{1,0:T(8,128)(2,1)}, u32[]{:S(2)}, u32[]{:S(2)}) %collective-permute-start.14) | collective-permute-done | bytes 524320 | tf_op jit(solution)/shard_map/ppermute | solution.py:494
  301.6 11.7 %collective-permute-done.15.refs_4_ = bf16[64,4096]{1,0:T(8,128)(2,1)} collective-permute-done((bf16[64,4096]{1,0:T(8,128)(2,1)}, bf16[64,4096]{1,0:T(8,128)(2,1)}, u32[]{:S(2)}, u32[]{:S(2)}) %collective-permute-start.15) | collective-permute-done | bytes 524320 | tf_op jit(solution)/shard_map/ppermute | solution.py:494
  314.7 5.8 %restore.1 = (bf16[256,2048]{1,0:T(8,128)(2,1)}, bf16[256,2048]{1,0:T(8,128)(2,1)}) custom-call(s32[3]{0:T(128)} %pad_add_fusion.where_ref, f32[256,1]{1,0:T(8,128)} %convert_element_type.72.ids_ref, bf16[4,64,4096]{2,1,0:T(8,128)(2,1)} %copy-done.1, bf16[64,4096]{1,0:T(8,128)(2,1)} %get-tuple-element.92.refs_1_, ...), custom_call_target="tpu_custom_call" | custom-call | flops 1000 | bytes 1000 | tf_op jit(solution)/shard_map/restore/pallas_call | solution.py:263
  (75 shorter events, 43.1 us)
Async XLA Ops:
  7.2 50.9 %all-gather.5.cloned.1.call-start = ((), (), s32[]{:S(2)}) async-start(), calls=%async_computation.3 | async-start | bytes 1310720 | tf_op jit(solution)/shard_map/all_gather | solution.py:569
  13.6 102.9 %all-to-all-start = ((bf16[4,128,2048]{2,1,0:T(8,128)(2,1)}), bf16[4,128,2048]{2,1,0:T(8,128)(2,1)S(1)}, u32[]{:S(2)}, u32[]{:S(2)}) async-start(bf16[4,128,2048]{2,1,0:T(8,128)(2,1)} %place.1), calls=%async_computation | async-start | bytes 4194304 | tf_op jit(solution)/shard_map/all_to_all | solution.py:565
  20.1 15.8 %collective-permute-start.3 = (bf16[4,256,256]{2,1,0:T(8,128)(2,1)S(1)}, bf16[4,256,256]{2,1,0:T(8,128)(2,1)S(1)}, u32[]{:S(2)}, u32[]{:S(2)}) collective-permute-start(bf16[4,256,256]{2,1,0:T(8,128)(2,1)S(1)} %pad_maximum_fusion.3.refs_0_), channel_id=1, source_target_pairs={{0,24},{4,28},{8,16},{12,20},{16,8},{20,12},{24,0},{28,4},{1,25},{... | collective-permute-start | bytes 1572872 | tf_op jit(solution)/shard_map/ppermute | solution.py:489
  20.6 24.1 %collective-permute-start.2 = (bf16[4,256,256]{2,1,0:T(8,128)(2,1)S(1)}, bf16[4,256,256]{2,1,0:T(8,128)(2,1)S(1)}, u32[]{:S(2)}, u32[]{:S(2)}) collective-permute-start(bf16[4,256,256]{2,1,0:T(8,128)(2,1)S(1)} %pad_maximum_fusion.3.refs_0_), channel_id=1, source_target_pairs={{0,16},{4,20},{8,24},{12,28},{16,0},{20,4},{24,8},{28,12},{1,17},{... | collective-permute-start | bytes 1572872 | tf_op jit(solution)/shard_map/ppermute | solution.py:489
  22.1 23.3 %collective-permute-start.1 = (bf16[4,256,256]{2,1,0:T(8,128)(2,1)S(1)}, bf16[4,256,256]{2,1,0:T(8,128)(2,1)}, u32[]{:S(2)}, u32[]{:S(2)}) collective-permute-start(bf16[4,256,256]{2,1,0:T(8,128)(2,1)S(1)} %pad_maximum_fusion.3.refs_0_), channel_id=1, source_target_pairs={{0,8},{4,12},{8,0},{12,4},{16,24},{20,28},{24,16},{28,20},{1,9},{5... | collective-permute-start | bytes 1572872 | tf_op jit(solution)/shard_map/ppermute | solution.py:489
  60.6 26.3 %collective-permute-start.4 = (bf16[3,4,256,256]{3,2,1,0:T(8,128)(2,1)}, bf16[3,4,256,256]{3,2,1,0:T(8,128)(2,1)}, u32[]{:S(2)}, u32[]{:S(2)}) collective-permute-start(bf16[3,4,256,256]{3,2,1,0:T(8,128)(2,1)} %pad_maximum_fusion.1), channel_id=1, source_target_pairs={{0,4},{4,0},{8,12},{12,8},{16,20},{20,16},{24,28},{28,24},{1,5},{5... | collective-permute-start | bytes 4718600 | tf_op jit(solution)/shard_map/ppermute | solution.py:489
  62.0 51.2 %collective-permute-start.10 = (bf16[3,512,256]{2,1,0:T(8,128)(2,1)S(1)}, bf16[3,512,256]{2,1,0:T(8,128)(2,1)}, u32[]{:S(2)}, u32[]{:S(2)}) collective-permute-start(bf16[3,512,256]{2,1,0:T(8,128)(2,1)S(1)} %pad_maximum_fusion.2.refs_6_.refs_3_), channel_id=1, source_target_pairs={{0,24},{4,28},{8,16},{12,20},{16,8},{20,12},{24,0},{28,4},{1,25},{... | collective-permute-start | bytes 2359304 | tf_op jit(solution)/shard_map/ppermute | solution.py:489
  62.7 50.6 %collective-permute-start.9 = (bf16[3,512,256]{2,1,0:T(8,128)(2,1)S(1)}, bf16[3,512,256]{2,1,0:T(8,128)(2,1)}, u32[]{:S(2)}, u32[]{:S(2)}) collective-permute-start(bf16[3,512,256]{2,1,0:T(8,128)(2,1)S(1)} %pad_maximum_fusion.2.refs_6_.refs_3_), channel_id=1, source_target_pairs={{0,16},{4,20},{8,24},{12,28},{16,0},{20,4},{24,8},{28,12},{1,17},{... | collective-permute-start | bytes 2359304 | tf_op jit(solution)/shard_map/ppermute | solution.py:489
  64.1 49.1 %collective-permute-start.8 = (bf16[3,512,256]{2,1,0:T(8,128)(2,1)S(1)}, bf16[3,512,256]{2,1,0:T(8,128)(2,1)}, u32[]{:S(2)}, u32[]{:S(2)}) collective-permute-start(bf16[3,512,256]{2,1,0:T(8,128)(2,1)S(1)} %pad_maximum_fusion.2.refs_6_.refs_3_), channel_id=1, source_target_pairs={{0,8},{4,12},{8,0},{12,4},{16,24},{20,28},{24,16},{28,20},{1,9},{5... | collective-permute-start | bytes 2359304 | tf_op jit(solution)/shard_map/ppermute | solution.py:489
  65.6 21.4 %collective-permute-start = (bf16[4,256,256]{2,1,0:T(8,128)(2,1)S(1)}, bf16[4,256,256]{2,1,0:T(8,128)(2,1)S(1)}, u32[]{:S(2)}, u32[]{:S(2)}) collective-permute-start(bf16[4,256,256]{2,1,0:T(8,128)(2,1)S(1)} %pad_maximum_fusion.3.refs_0_), channel_id=1, source_target_pairs={{0,4},{4,0},{8,12},{12,8},{16,20},{20,16},{24,28},{28,24},{1,5},{5... | collective-permute-start | bytes 1572872 | tf_op jit(solution)/shard_map/ppermute | solution.py:489
  116.5 55.2 %collective-permute-start.12 = (bf16[3,3,512,256]{3,2,1,0:T(8,128)(2,1)}, bf16[3,3,512,256]{3,2,1,0:T(8,128)(2,1)}, u32[]{:S(2)}, u32[]{:S(2)}) collective-permute-start(bf16[3,3,512,256]{3,2,1,0:T(8,128)(2,1)} %pad_maximum_fusion), channel_id=1, source_target_pairs={{0,4},{4,0},{8,12},{12,8},{16,20},{20,16},{24,28},{28,24},{1,5},{5... | collective-permute-start | bytes 7077896 | tf_op jit(solution)/shard_map/ppermute | solution.py:489
  116.6 13.3 %collective-permute-start.5 = (bf16[4,64,512]{2,1,0:T(8,128)(2,1)}, bf16[4,64,512]{2,1,0:T(8,128)(2,1)S(1)}, u32[]{:S(2)}, u32[]{:S(2)}) collective-permute-start(bf16[4,64,512]{2,1,0:T(8,128)(2,1)} %get-tuple-element.61), channel_id=1, source_target_pairs={{0,1},{1,0},{2,3},{3,2},{4,5},{5,4},{6,7},{7,6},{8,9},{9,8},{10,11... | collective-permute-start | bytes 786440 | tf_op jit(solution)/shard_map/ppermute | solution.py:494
  118.1 20.4 %collective-permute-start.6 = (bf16[4,64,512]{2,1,0:T(8,128)(2,1)}, bf16[4,64,512]{2,1,0:T(8,128)(2,1)S(1)}, u32[]{:S(2)}, u32[]{:S(2)}) collective-permute-start(bf16[4,64,512]{2,1,0:T(8,128)(2,1)} %get-tuple-element.62), channel_id=1, source_target_pairs={{0,2},{1,3},{2,0},{3,1},{4,6},{5,7},{6,4},{7,5},{8,10},{9,11},{10,... | collective-permute-start | bytes 786440 | tf_op jit(solution)/shard_map/ppermute | solution.py:494
  120.3 24.3 %collective-permute-start.7 = (bf16[4,64,512]{2,1,0:T(8,128)(2,1)}, bf16[4,64,512]{2,1,0:T(8,128)(2,1)}, u32[]{:S(2)}, u32[]{:S(2)}) collective-permute-start(bf16[4,64,512]{2,1,0:T(8,128)(2,1)} %get-tuple-element.63), channel_id=1, source_target_pairs={{0,3},{1,2},{2,1},{3,0},{4,7},{5,6},{6,5},{7,4},{8,11},{9,10},{10,... | collective-permute-start | bytes 786440 | tf_op jit(solution)/shard_map/ppermute | solution.py:494
  144.6 27.1 %all-to-all-start.2 = ((bf16[4,4,64,512]{3,2,1,0:T(8,128)(2,1)}), bf16[4,4,64,512]{3,2,1,0:T(8,128)(2,1)}, u32[]{:S(2)}, u32[]{:S(2)}) async-start(bf16[4,4,64,512]{3,2,1,0:T(8,128)(2,1)} %get-tuple-element.76), calls=%async_computation.2 | async-start | bytes 2097152 | tf_op jit(solution)/shard_map/all_to_all | solution.py:499
  149.1 2.5 collective-permute-start.11
  214.5 14.8 %collective-permute-start.16 = (bf16[4,3,256,768]{3,2,1,0:T(8,128)(2,1)}, bf16[4,3,256,768]{3,2,1,0:T(8,128)(2,1)}, u32[]{:S(2)}, u32[]{:S(2)}) collective-permute-start(bf16[4,3,256,768]{3,2,1,0:T(8,128)(2,1)} %weight_grads.3), channel_id=1, source_target_pairs={{0,4},{4,0},{8,12},{12,8},{16,20},{20,16},{24,28},{28,24},{1,5},{5... | collective-permute-start | bytes 14155784 | tf_op jit(solution)/shard_map/ppermute | solution.py:489
  214.5 98.8 %all-to-all-start.1 = ((bf16[4,64,4096]{2,1,0:T(8,128)(2,1)}), bf16[4,64,4096]{2,1,0:T(8,128)(2,1)S(1)}, u32[]{:S(2)}, u32[]{:S(2)}) async-start(bf16[4,64,4096]{2,1,0:T(8,128)(2,1)} %get-tuple-element.75), calls=%async_computation.1 | async-start | bytes 4194304 | tf_op jit(solution)/shard_map/all_to_all | solution.py:499
  233.3 28.9 %collective-permute-start.17 = (bf16[3,256,768]{2,1,0:T(8,128)(2,1)S(1)}, bf16[3,256,768]{2,1,0:T(8,128)(2,1)S(1)}, u32[]{:S(2)}, u32[]{:S(2)}) collective-permute-start(bf16[3,256,768]{2,1,0:T(8,128)(2,1)S(1)} %get-tuple-element.101), channel_id=1, source_target_pairs={{0,8},{4,12},{8,0},{12,4},{16,24},{20,28},{24,16},{28,20},{1,9},{5... | collective-permute-start | bytes 3538952 | tf_op jit(solution)/shard_map/ppermute | solution.py:489
  233.4 51.1 %collective-permute-start.19 = (bf16[3,256,768]{2,1,0:T(8,128)(2,1)S(1)}, bf16[3,256,768]{2,1,0:T(8,128)(2,1)S(1)}, u32[]{:S(2)}, u32[]{:S(2)}) collective-permute-start(bf16[3,256,768]{2,1,0:T(8,128)(2,1)S(1)} %get-tuple-element.102), channel_id=1, source_target_pairs={{0,24},{4,28},{8,16},{12,20},{16,8},{20,12},{24,0},{28,4},{1,25},{... | collective-permute-start | bytes 3538952 | tf_op jit(solution)/shard_map/ppermute | solution.py:489
  233.4 54.3 %collective-permute-start.18 = (bf16[3,256,768]{2,1,0:T(8,128)(2,1)S(1)}, bf16[3,256,768]{2,1,0:T(8,128)(2,1)S(1)}, u32[]{:S(2)}, u32[]{:S(2)}) collective-permute-start(bf16[3,256,768]{2,1,0:T(8,128)(2,1)S(1)} %get-tuple-element.103), channel_id=1, source_target_pairs={{0,16},{4,20},{8,24},{12,28},{16,0},{20,4},{24,8},{28,12},{1,17},{... | collective-permute-start | bytes 3538952 | tf_op jit(solution)/shard_map/ppermute | solution.py:489
  237.5 57.3 %collective-permute-start.13 = (bf16[64,4096]{1,0:T(8,128)(2,1)}, bf16[64,4096]{1,0:T(8,128)(2,1)}, u32[]{:S(2)}, u32[]{:S(2)}) collective-permute-start(bf16[64,4096]{1,0:T(8,128)(2,1)} %get-tuple-element.78), channel_id=1, source_target_pairs={{0,1},{1,0},{2,3},{3,2},{4,5},{5,4},{6,7},{7,6},{8,9},{9,8},{10,11... | collective-permute-start | bytes 1572872 | tf_op jit(solution)/shard_map/ppermute | solution.py:494
  239.0 62.7 %collective-permute-start.14 = (bf16[64,4096]{1,0:T(8,128)(2,1)}, bf16[64,4096]{1,0:T(8,128)(2,1)}, u32[]{:S(2)}, u32[]{:S(2)}) collective-permute-start(bf16[64,4096]{1,0:T(8,128)(2,1)} %get-tuple-element.79), channel_id=1, source_target_pairs={{0,2},{1,3},{2,0},{3,1},{4,6},{5,7},{6,4},{7,5},{8,10},{9,11},{10,... | collective-permute-start | bytes 1572872 | tf_op jit(solution)/shard_map/ppermute | solution.py:494
  262.2 51.2 %collective-permute-start.15 = (bf16[64,4096]{1,0:T(8,128)(2,1)}, bf16[64,4096]{1,0:T(8,128)(2,1)}, u32[]{:S(2)}, u32[]{:S(2)}) collective-permute-start(bf16[64,4096]{1,0:T(8,128)(2,1)} %get-tuple-element.80), channel_id=1, source_target_pairs={{0,3},{1,2},{2,1},{3,0},{4,7},{5,6},{6,5},{7,4},{8,11},{9,10},{10,... | collective-permute-start | bytes 1572872 | tf_op jit(solution)/shard_map/ppermute | solution.py:494
  (12 other events, 341.8 us)
Sparse Core Ops, SparseCore 0:
  10.1 47.9 all-gather.4

commit v5 on v3

v5 whole, which is shorter than its diff:
```python
import functools
import math

import jax
import jax.numpy as jnp
from jax import lax
from jax.experimental import pallas as pl
from jax.experimental.pallas import tpu as pltpu
from jax.sharding import PartitionSpec as P

LOCAL_QUERY_HEADS = 16
LOCAL_KEY_HEADS = 2
HEAD_SIZE = 128
PIECE = 256
PARTS = 2

epsilon = 1e-06
masked_score = -1e30
F32 = jnp.float32
BF16 = jnp.bfloat16
VMEM_LIMIT = 60 << 20


def dot(a, b, contract=((1,), (0,))):
    return lax.dot_general(a, b, (contract, ((), ())), preferred_element_type=F32)


def iota(shape, dim):
    return lax.broadcasted_iota(jnp.int32, shape, dim)


def slots_row(ids_row, capacity):
    n = ids_row.shape[1]
    names = iota((16, n), 0).astype(F32)
    chosen = names == ids_row
    before = (iota((n, n), 0) < iota((n, n), 1)).astype(F32).astype(BF16)
    earlier = dot(jnp.where(chosen, 1.0, 0.0).astype(BF16), before)
    return jnp.sum(jnp.where(chosen, earlier + names * capacity, 0.0), axis=0, keepdims=True)


def slots_column(ids_column, capacity):
    n = ids_column.shape[0]
    names = iota((n, 128), 1).astype(F32)
    chosen = names == ids_column
    before = (iota((n, n), 1) < iota((n, n), 0)).astype(F32).astype(BF16)
    earlier = dot(before, jnp.where(chosen, 1.0, 0.0).astype(BF16))
    return jnp.sum(jnp.where(chosen, earlier + names * capacity, 0.0), axis=1, keepdims=True)


def one_hot(matches):
    return jnp.where(matches, 1.0, 0.0).astype(BF16)


def shifted_slots(position, owner, experts, capacity):
    expert = jnp.bitwise_xor(position // capacity, owner)
    return (expert * capacity + lax.rem(position, capacity)).astype(F32)


def kernel_params():
    return pltpu.CompilerParams(vmem_limit_bytes=VMEM_LIMIT)


def brief():
    return pl.CostEstimate(flops=1000, bytes_accessed=1000, transcendentals=0)


def whole(*shape):
    return pl.BlockSpec(shape, lambda *_: (0,) * len(shape))


def smem():
    return pl.BlockSpec(memory_space=pltpu.SMEM)


def attend_kernel(experts, capacity, heads, n_ctx, where_ref, q_ref, ids_ref, *refs):
    count = n_ctx // 2 + 1
    *chips, cores = refs[:count]
    refs = refs[count:]
    blocks = []
    for j, chip in enumerate(chips):
        blocks += [chip, cores.at[j]]
    out_refs, refs = refs[: experts * PARTS], refs[experts * PARTS :]
    k_scr, v_scr, best_scr, acc_scr, att_scr = refs
    ctx, owner = where_ref[0], where_ref[1]
    seq = pl.program_id(0)
    block = q_ref.shape[1]
    tile = 2 * block
    factor = math.log2(math.e) / math.sqrt(HEAD_SIZE)

    @pl.when(seq == 0)
    def _():
        v_scr[:, :, HEAD_SIZE:] = jnp.ones((n_ctx, block, HEAD_SIZE), BF16)

    for m in range(n_ctx):
        index = jnp.bitwise_xor(ctx, m)
        k_scr[index] = blocks[m][0, :, :HEAD_SIZE]
        v_scr[index, :, :HEAD_SIZE] = blocks[m][0, :, HEAD_SIZE:]

    def fold(t, last):
        key_tile = k_scr[pl.ds(2 * t, 2)].reshape(tile, HEAD_SIZE)
        value_tile = v_scr[pl.ds(2 * t, 2)].reshape(tile, 2 * HEAD_SIZE)
        for h in range(heads):
            q = q_ref[0, :, h * HEAD_SIZE : (h + 1) * HEAD_SIZE]
            s = dot(q, key_tile, ((1,), (1,)))
            if last:
                key_pos = iota((block, tile), 1) + t * tile
                query_pos = iota((block, tile), 0) + ctx * block
                s = jnp.where(key_pos <= query_pos, s, masked_score)
            best = jnp.max(s, axis=1, keepdims=True)
            if not last:
                old = best_scr[h]
                best = jnp.maximum(old, best)
            p = jnp.exp2((s - best) * factor)
            blended = dot(p.astype(BF16), value_tile)
            if last:
                acc_scr[h] = blended
            else:
                acc_scr[h] = acc_scr[h] * jnp.exp2((old - best) * factor) + blended
            best_scr[h] = best

    fold(ctx // 2, True)

    @pl.loop(0, ctx // 2)
    def _(t):
        fold(t, False)

    for h in range(heads):
        acc = acc_scr[h]
        att = acc[:, :HEAD_SIZE] / acc[:, HEAD_SIZE:]
        att_scr[:, h * HEAD_SIZE : (h + 1) * HEAD_SIZE] = att.astype(BF16)

    n = ids_ref.shape[2]
    part = capacity // PARTS
    per_seq = block // n
    position = iota((experts * capacity, n), 0)
    slots = shifted_slots(position, owner, experts, capacity)
    for b in range(per_seq):
        source = seq * per_seq + b
        target = slots_row(ids_ref[source], capacity)
        picked = dot(one_hot(slots == target), att_scr[b * n : (b + 1) * n, :]).astype(BF16)
        for d in range(experts):
            rank = jnp.bitwise_xor(jnp.bitwise_xor(owner, d), source)
            for c in range(PARTS):
                first = d * capacity + c * part
                out_refs[c * experts + d][rank] = picked[first : first + part]


def attend(where, queries, key_values, ids, capacity):
    seqs, block, width = queries.shape
    n_ctx = 2 * (len(key_values) - 1)
    experts, _, n = ids.shape
    heads = width // HEAD_SIZE
    part = capacity // PARTS
    by_seq = pl.BlockSpec((1, block, 2 * HEAD_SIZE), lambda s: (s, 0, 0))
    outs = pl.pallas_call(
        functools.partial(attend_kernel, experts, capacity, heads, n_ctx),
        grid=(seqs,),
        in_specs=[
            smem(),
            pl.BlockSpec((1, block, width), lambda s: (s, 0, 0)),
            whole(experts, 1, n),
        ]
        + [by_seq] * (len(key_values) - 1)
        + [pl.BlockSpec((n_ctx // 2, 1, block, 2 * HEAD_SIZE), lambda s: (0, s, 0, 0))],
        out_specs=[whole(experts, part, width)] * (PARTS * experts),
        scratch_shapes=[
            pltpu.VMEM((n_ctx, block, HEAD_SIZE), BF16),
            pltpu.VMEM((n_ctx, block, 2 * HEAD_SIZE), BF16),
            pltpu.VMEM((heads, block, 1), F32),
            pltpu.VMEM((heads, block, 2 * HEAD_SIZE), F32),
            pltpu.VMEM((block, width), BF16),
        ],
        out_shape=[jax.ShapeDtypeStruct((experts, part, width), BF16)] * (PARTS * experts),
        compiler_params=kernel_params(),
        cost_estimate=brief(),
        name="attend",
    )(where, queries, ids, *key_values)
    return [outs[c * experts : (c + 1) * experts] for c in range(PARTS)]


def place_kernel(experts, capacity, where_ref, ids_ref, rows_ref, *refs):
    out_refs, pick_scr = refs[:-1], refs[-1]

    @pl.when(pl.program_id(0) == 0)
    def _():
        position = iota(pick_scr.shape, 0)
        slots = shifted_slots(position, where_ref[1], experts, capacity)
        pick_scr[...] = one_hot(slots == slots_row(ids_ref[...], capacity))

    picked = dot(pick_scr[...], rows_ref[...]).astype(BF16)
    for d, ref in enumerate(out_refs):
        ref[...] = picked[d * capacity : (d + 1) * capacity]


def place(where, ids_row, rows, experts, capacity):
    n, width = rows.shape
    cols = min(width, 1024)
    return pl.pallas_call(
        functools.partial(place_kernel, experts, capacity),
        grid=(width // cols,),
        in_specs=[smem(), whole(1, n), pl.BlockSpec((n, cols), lambda i: (0, i))],
        out_specs=[pl.BlockSpec((capacity, cols), lambda i: (0, i))] * experts,
        out_shape=[jax.ShapeDtypeStruct((capacity, width), BF16)] * experts,
        scratch_shapes=[pltpu.VMEM((experts * capacity, n), BF16)],
        compiler_params=kernel_params(),
        cost_estimate=brief(),
        name="place",
    )(where, ids_row, rows)


def restore_kernel(experts, capacity, where_ref, ids_ref, *refs):
    *parts, out_ref, pick_scr = refs

    @pl.when(pl.program_id(0) == 0)
    def _():
        slots = shifted_slots(iota(pick_scr.shape, 1), where_ref[1], experts, capacity)
        pick_scr[...] = one_hot(slots == slots_column(ids_ref[...], capacity))

    rows = jnp.concatenate([ref[...] for ref in parts], axis=0)
    out_ref[...] = dot(pick_scr[...], rows).astype(BF16)


def restore(where, ids_column, parts, experts, capacity):
    n = ids_column.shape[0]
    part, width = parts[0][0].shape
    cols = min(width, 1024)
    return pl.pallas_call(
        functools.partial(restore_kernel, experts, capacity),
        grid=(width // cols,),
        in_specs=[smem(), whole(n, 1)]
        + [pl.BlockSpec((part, cols), lambda i: (0, i))] * (experts * PARTS),
        out_specs=pl.BlockSpec((n, cols), lambda i: (0, i)),
        out_shape=jax.ShapeDtypeStruct((n, width), BF16),
        scratch_shapes=[pltpu.VMEM((n, experts * capacity), BF16)],
        compiler_params=kernel_params(),
        cost_estimate=brief(),
        name="restore",
    )(where, ids_column, *[parts[c][d] for d in range(experts) for c in range(PARTS)])


def expert_kernel(experts, capacity, part_index, swap, where_ref, *refs):
    att_refs, refs = refs[:experts], refs[experts:]
    grad_refs, refs = refs[:experts], refs[experts:]
    own_ref, same_hbm, other_hbm, gate_hbm, up_hbm, down_hbm = refs[:6]
    gain_ref, ids_ref, weight_ref, refs = refs[6], refs[7], refs[8], refs[9:]
    layer_refs, refs = refs[:experts], refs[experts:]
    change_refs, refs = refs[:experts], refs[experts:]
    saved_refs, refs = refs[: 1 + swap], refs[1 + swap :]
    w_scr, gate_scr, up_scr, down_scr, hidden_scr, normed_ref, back_ref, back_in_scr, sems = refs
    part, width = grad_refs[0].shape
    rows = experts * part
    att_cols = att_refs[0].shape[-1]
    pieces, _, _, piece = w_scr.shape
    ff = gate_scr.shape[1]
    core, owner = jnp.bitwise_and(where_ref[0], 1), where_ref[1]
    sources = [jnp.bitwise_xor(owner, d) for d in range(experts)]
    units_at, gate_at, up_at, normed_at = 0, ff, 2 * ff, 3 * ff

    copies = []
    for q in range(pieces // 2):
        for ref in (same_hbm, other_hbm):
            m = len(copies)
            copies.append(pltpu.make_async_copy(ref.at[q], w_scr.at[m], sems.at[m]))
    weight_copies = (
        pltpu.make_async_copy(gate_hbm.at[0], gate_scr, sems.at[pieces]),
        pltpu.make_async_copy(up_hbm.at[0], up_scr, sems.at[pieces + 1]),
        pltpu.make_async_copy(down_hbm.at[0], down_scr, sems.at[pieces + 2]),
    )
    for copy in copies:
        copy.start()
    for copy in weight_copies:
        copy.start()

    n = ids_ref.shape[2]
    weights = []
    for s, source in enumerate(sources):
        target = slots_row(ids_ref[source], capacity)
        slot = iota((part, n), 0) + (owner * capacity + part_index * part)
        weights.append(
            jnp.sum(
                jnp.where(slot.astype(F32) == target, weight_ref[source], 0.0),
                axis=1,
                keepdims=True,
            )
        )
        grads = grad_refs[s][...].astype(F32)
        back_ref[s * part : (s + 1) * part, :] = (weights[s] * grads).astype(BF16)

    for m in range(pieces):
        copies[m].wait()
        index = m + core if m % 2 == 0 else m - core
        column = pl.multiple_of(index * piece, piece)
        total = jnp.zeros((rows, piece), F32)
        for d in range(experts):
            block = own_ref[:, pl.ds(column, piece)] if d == 0 else w_scr[m, d - 1]
            total += dot(att_refs[d][...].reshape(rows, att_cols), block)
        hidden_scr[:, pl.ds(column, piece)] = total.astype(BF16)

    squares = jnp.zeros((rows, 1), F32)
    for t in range(0, width, PIECE):
        hidden = hidden_scr[:, t : t + PIECE].astype(F32)
        squares += jnp.sum(hidden * hidden, axis=1, keepdims=True)
    inv = lax.rsqrt(squares / width + epsilon)
    for t in range(0, width, PIECE):
        hidden = hidden_scr[:, t : t + PIECE].astype(F32)
        normed_ref[:, t : t + PIECE] = (hidden * inv * gain_ref[:, t : t + PIECE]).astype(BF16)

    for copy in weight_copies:
        copy.wait()
    for f in range(0, ff, 256):
        gate_act = dot(normed_ref[...], gate_scr[:, f : f + 256])
        up_act = dot(normed_ref[...], up_scr[:, f : f + 256])
        back_units = dot(back_ref[...], down_scr[f : f + 256, :], ((1,), (1,)))
        sigma = 1.0 / (1.0 + jnp.exp(-gate_act))
        gated = gate_act * sigma
        units = (gated * up_act).astype(BF16)
        back_gate = back_units * up_act * sigma * (1.0 + gate_act * (1.0 - sigma))
        back_gate = back_gate.astype(BF16)
        back_up = (back_units * gated).astype(BF16)
        for ref in saved_refs:
            ref[:, units_at + f : units_at + f + 256] = units
            ref[:, gate_at + f : gate_at + f + 256] = back_gate
            ref[:, up_at + f : up_at + f + 256] = back_up

    saved = saved_refs[0]
    half = width // len(saved_refs)
    for c, ref in enumerate(saved_refs):
        for t in range(half // PIECE):
            if swap:
                block = 2 * t + (core if c == 0 else 1 - core)
                column = pl.multiple_of(block * PIECE, PIECE)
            else:
                column = t * PIECE
            at = normed_at + t * PIECE
            ref[:, at : at + PIECE] = normed_ref[:, pl.ds(column, PIECE)]
            ref[:, at + half : at + half + PIECE] = back_ref[:, pl.ds(column, PIECE)]

    weight = jnp.concatenate(weights, axis=0)
    moment = jnp.zeros((rows, 1), F32)
    for t in range(0, width, PIECE):
        hidden = hidden_scr[:, t : t + PIECE].astype(F32)
        result = dot(saved[:, units_at:gate_at], down_scr[:, t : t + PIECE])
        layer = (hidden + weight * result.astype(BF16).astype(F32)).astype(BF16)
        for s in range(experts):
            layer_refs[s][:, t : t + PIECE] = layer[s * part : (s + 1) * part]
        back_in = dot(saved[:, gate_at:up_at], gate_scr[t : t + PIECE, :], ((1,), (1,)))
        back_in += dot(saved[:, up_at:normed_at], up_scr[t : t + PIECE, :], ((1,), (1,)))
        back_in = back_in.astype(BF16)
        back_in_scr[:, t : t + PIECE] = back_in
        scaled = back_in.astype(F32) * gain_ref[:, t : t + PIECE]
        moment += jnp.sum(scaled * (hidden * inv), axis=1, keepdims=True)
    moment = moment / width
    for t in range(0, width, PIECE):
        unit = hidden_scr[:, t : t + PIECE].astype(F32) * inv
        scaled = back_in_scr[:, t : t + PIECE].astype(F32) * gain_ref[:, t : t + PIECE]
        change = inv * (scaled - unit * moment)
        for s in range(experts):
            grads = grad_refs[s][:, t : t + PIECE].astype(F32)
            change_refs[s][:, t : t + PIECE] = (
                grads + change[s * part : (s + 1) * part]
            ).astype(BF16)


def expert_part(
    where, att, grads, own, same, other, gate, up, down, gain, ids, weights, capacity, index, swap
):
    experts, part, att_cols = att[0].shape
    pieces = 2 * same.shape[0]
    piece = same.shape[-1]
    width = grads[0].shape[1]
    ff = gate.shape[2]
    rows = experts * part
    n = ids.shape[2]
    half = width // 2 if swap else width
    out = lambda *shape: jax.ShapeDtypeStruct(shape, BF16)
    in_hbm = pl.BlockSpec(memory_space=pl.ANY)
    outs = pl.pallas_call(
        functools.partial(expert_kernel, experts, capacity, index, swap),
        grid=(1,),
        in_specs=[smem()]
        + [whole(*x.shape) for x in att]
        + [pl.BlockSpec((part, width), lambda i: (index, 0))] * experts
        + [whole(*own.shape)]
        + [in_hbm] * 5
        + [whole(1, width), whole(experts, 1, n), whole(experts, 1, n)],
        out_specs=[whole(part, width)] * (2 * experts)
        + [whole(rows, 3 * ff + 2 * half)] * (1 + swap),
        scratch_shapes=[
            pltpu.VMEM((pieces, experts - 1, att_cols, piece), BF16),
            pltpu.VMEM((width, ff), BF16),
            pltpu.VMEM((width, ff), BF16),
            pltpu.VMEM((ff, width), BF16),
            pltpu.VMEM((rows, width), BF16),
            pltpu.VMEM((rows, width), BF16),
            pltpu.VMEM((rows, width), BF16),
            pltpu.VMEM((rows, width), BF16),
            pltpu.SemaphoreType.DMA((pieces + 3,)),
        ],
        out_shape=[out(part, width)] * (2 * experts)
        + [out(rows, 3 * ff + 2 * half)] * (1 + swap),
        compiler_params=kernel_params(),
        cost_estimate=brief(),
        name="expert",
    )(where, *att, *grads, own, same, other, gate, up, down, gain, ids, weights)
    return outs[:experts], outs[experts : 2 * experts], outs[2 * experts :]


def weight_kernel(count, *refs):
    units, back_gate, back_up, normed, back = [refs[i * count : (i + 1) * count] for i in range(5)]
    out_ref = refs[5 * count]
    first = ((0,), (0,))

    def total(left, right):
        return sum(dot(a[...], b[...], first) for a, b in zip(left, right)).astype(BF16)

    out_ref[0, 0] = total(normed, back_gate)
    out_ref[0, 1] = total(normed, back_up)
    down = total(units, back)
    cols = down.shape[1]
    for t in range(0, down.shape[0], cols):
        out_ref[0, 2, :, t : t + cols] = down[t : t + cols]


def weight_blocks(saved, blocks, ff):
    count = len(saved)
    rows, total = saved[0].shape
    normed_at = 3 * ff // PIECE
    back_at = normed_at + blocks
    thin = lambda at: [pl.BlockSpec((rows, PIECE), lambda i: (0, at + i))] * count
    full = lambda at: [pl.BlockSpec((rows, ff), lambda i: (0, at))] * count
    return pl.pallas_call(
        functools.partial(weight_kernel, count),
        grid=(blocks,),
        in_specs=full(0) + full(1) + full(2) + thin(normed_at) + thin(back_at),
        out_specs=pl.BlockSpec((1, 3, PIECE, ff), lambda i: (i, 0, 0, 0)),
        out_shape=jax.ShapeDtypeStruct((blocks, 3, PIECE, ff), BF16),
        compiler_params=kernel_params(),
        cost_estimate=brief(),
        name="weight_grads",
    )(*saved * 5)


def partner(value, mask):
    count = lax.axis_size("ctx")
    return lax.ppermute(value, "ctx", [(i, i ^ mask) for i in range(count)])


def to_owner(value, mask):
    count = lax.axis_size("exp")
    return lax.ppermute(value, "exp", [(i, i ^ mask) for i in range(count)])


def to_owners(values):
    return [values[0]] + [to_owner(values[d], d) for d in range(len(values) - 1, 0, -1)][::-1]


def chip_groups(count):
    return [
        list(range(first + core, first + count, 2))
        for first in range(0, lax.axis_size("ctx"), count)
        for core in range(2)
    ]


def after(value, *others):
    return lax.optimization_barrier((value, others))[0]


def halved(value, bits, order, ctx):
    shape = value.shape[1:]
    held = value.reshape((2,) * bits + shape)
    for place_in_order, bit in enumerate(order):
        axis = bits - 1 - bit
        mine = (ctx >> bit) & 1
        gone = lax.dynamic_slice_in_dim(held, 1 - mine, 1, axis)
        kept = lax.dynamic_slice_in_dim(held, mine, 1, axis)
        held = kept.astype(F32) + partner(gone, 1 << bit).astype(F32)
        if place_in_order < bits - 1:
            held = held.astype(BF16)
    return held.reshape(shape)


def on_device(
    queries,
    rotated_key_heads,
    value_head_rows,
    out_proj,
    norm_gain,
    expert_ids,
    gate_weights,
    expert_gate,
    expert_up,
    expert_down,
    grad_out,
):
    heads_dev = queries.shape[2] // HEAD_SIZE
    group = LOCAL_QUERY_HEADS // LOCAL_KEY_HEADS
    exp_count = lax.axis_size("exp")
    ctx_count = lax.axis_size("ctx")
    owner = lax.axis_index("exp")
    ctx = lax.axis_index("ctx")
    bits = ctx_count.bit_length() - 1
    n, _ = expert_ids.shape
    width = grad_out.shape[1]
    experts = exp_count
    capacity = min(n, 2 * n // experts)
    pieces = min(ctx_count, width // PIECE)
    piece = width // pieces
    piece_index = ctx % pieces
    where = jnp.stack([ctx, owner, piece_index]).astype(jnp.int32)

    ids_f = expert_ids.astype(F32)
    info = jnp.stack([ids_f[:, 0], gate_weights[:, 0]])
    info = jnp.broadcast_to(info[None], (exp_count,) + info.shape)
    info = lax.all_to_all(info, "exp", 0, 0, tiled=True)
    ids_all, weights_all = info[:, 0:1, :], info[:, 1:2, :]

    mine = lax.dynamic_slice_in_dim(out_proj, piece_index * piece, piece, 1)
    projection = to_owners([mine] * exp_count)[1:]

    first_column = (owner * heads_dev // group) * HEAD_SIZE
    keys = lax.dynamic_slice_in_dim(rotated_key_heads, first_column, HEAD_SIZE, 2)
    values = lax.dynamic_slice_in_dim(value_head_rows, first_column, HEAD_SIZE, 2)
    own = jnp.concatenate([keys, values], axis=2)
    chips = [own] + [partner(own, m) for m in range(2, ctx_count, 2)]
    key_values = chips + [partner(jnp.stack(chips), 1)]

    grads = place(where, ids_f.reshape(1, n), grad_out, experts, capacity)
    grads = to_owners(after(grads, projection))

    projection = after(jnp.stack(projection), chips)
    projection = jnp.broadcast_to(projection[None], (pieces // 2,) + projection.shape)
    same = lax.all_to_all(
        projection, "ctx", 0, 0, axis_index_groups=chip_groups(pieces), tiled=True
    )

    sent = attend(where, after(queries, grads[1]), key_values, ids_all, capacity)
    arrived = to_owners(after(sent[0], grads))
    later = after(sent[1], arrived, same)
    same = after(same, arrived[1])
    other = partner(same, 1)

    rows_dev = width // ctx_count
    ff = expert_gate.shape[2]
    swap = rows_dev == PIECE

    def run(index, arrived):
        return expert_part(
            where,
            arrived,
            grads,
            out_proj,
            same,
            other,
            expert_gate,
            expert_up,
            expert_down,
            norm_gain.reshape(1, width),
            ids_all,
            weights_all,
            capacity,
            index,
            swap,
        )

    layer_a, change_a, saved_a = run(0, arrived)
    layer_a = to_owners(layer_a)
    layer_b, change_b, saved_b = run(1, to_owners(later))
    if swap:
        saved = [saved_a[0], partner(saved_a[1], 1)]
        saved += [saved_b[0], partner(after(saved_b[1], layer_a), 1)]
        change_a = to_owners(after(change_a, layer_a))
        parts = weight_blocks(saved, width // PIECE // 2, ff)
        layer_b = after(layer_b, parts)
        parts = lax.all_to_all(
            parts, "ctx", 0, 0, axis_index_groups=chip_groups(ctx_count), tiled=True
        )
        total = jnp.sum(parts.astype(F32), axis=0)
        grad_gate, grad_up = total[0][None], total[1][None]
        grad_down = total[2].reshape(PIECE, ff // PIECE, PIECE).transpose(1, 0, 2)
        grad_down = grad_down.reshape(1, ff, PIECE)
    else:
        change_a = to_owners(after(change_a, layer_a))
        blocks = width // PIECE
        parts = weight_blocks(list(saved_a) + list(saved_b), blocks, ff)
        part_down = parts[:, 2].reshape(blocks, PIECE, ff // PIECE, PIECE).transpose(0, 2, 1, 3)
        part_down = part_down.reshape(blocks, ff, PIECE // rows_dev, rows_dev)
        part_down = part_down.transpose(0, 2, 1, 3).reshape(ctx_count, ff, rows_dev)
        order = list(range(bits))
        grad_gate, grad_up, grad_down = [
            halved(x.reshape((ctx_count,) + shape), bits, order, ctx)[None]
            for x, shape in (
                (parts[:, 0], (rows_dev, ff)),
                (parts[:, 1], (rows_dev, ff)),
                (part_down, (ff, rows_dev)),
            )
        ]
    layer_b = to_owners(after(layer_b, change_a))
    change_b = to_owners(after(change_b, layer_b[1:2]))
    layer_out = restore(where, ids_f, [layer_a, layer_b], experts, capacity)
    change_b = after(change_b, layer_out, grad_gate, grad_up, grad_down)
    grad_hidden = restore(where, ids_f, [change_a, change_b], experts, capacity)
    return (layer_out, grad_hidden, grad_gate, grad_up, grad_down)


def solution(mesh):
    in_specs = (
        P(None, "ctx", "exp"),
        P(None, "ctx", None),
        P(None, "ctx", None),
        P("exp", None),
        P(),
        P(("ctx", "exp"), None),
        P(("ctx", "exp"), None),
        P("exp", None, None),
        P("exp", None, None),
        P("exp", None, None),
        P(("ctx", "exp"), None),
    )
    out_specs = (
        P(("ctx", "exp"), None),
        P(("ctx", "exp"), None),
        P("exp", "ctx", None),
        P("exp", "ctx", None),
        P("exp", None, "ctx"),
    )
    return jax.shard_map(
        on_device, mesh=mesh, in_specs=in_specs, out_specs=out_specs, check_vma=False
    )
```

time: 303 us -> 274 us (0.904); the launches traced: 299 us -> 273 us
  waiting for transfers between devices: 146 us -> 122 us
  between operations: 14.4 us -> 1.09 us
  starting transfers between devices: 39 us -> 50 us
    ppermute x18 -> x7, waiting for transfers between devices: 45.6 us -> 14.7 us  [partner(): return lax.ppermute(value, 'ctx', [(i, i ^ mask) for i in range(count)])]
    all_to_all x0 -> x3, starting transfers between devices: none -> 13.7 us  [the longest x1 5.31 us: on_device(): lax.all_to_all(parts, 'ctx', 0, 0, axis_index_groups=chip_groups(ctx_coun...]
    ppermute x18 -> x7, starting transfers between devices: 11.7 us -> 3.56 us  [partner(): return lax.ppermute(value, 'ctx', [(i, i ^ mask) for i in range(count)])]
    ppermute x18 -> x24, waiting for transfers between devices: 100 us -> 106 us  [to_owner(): return lax.ppermute(value, 'exp', [(i, i ^ mask) for i in range(count)])]
    ppermute x18 -> x24, starting transfers between devices: 27.2 us -> 32.8 us  [to_owner(): return lax.ppermute(value, 'exp', [(i, i ^ mask) for i in range(count)])]
    convert_element_type x1 -> x0, other arithmetic: 3.96 us -> none  [on_device(): far = [x.astype(BF16) for x in pair[1:]]]
    reduce_sum x0 -> x1, other arithmetic: none -> 3.34 us  [on_device(): total = jnp.sum(parts.astype(F32), axis=0)]
  transfers between devices with their start and end apart: 37 -> 34, of which waited for: 17 -> 17; matrix products, arithmetic and copies ran while one was open for 3% -> 5% of each run, Pallas kernels for 18% -> 25%
where the time goes in v5:
time: 274 us; the launch traced here: 273 us
  waiting for transfers between devices  122 us (45%)
  Pallas kernels  81.1 us (30%)
  starting transfers between devices  50 us (18%)
  local copies, waits for them, and re-layouts  12.1 us (4%)
  other arithmetic  7.49 us (3%)
    ppermute x24, waiting for transfers between devices, to_owner(): return lax.ppermute(value, 'exp', [(i, i ^ mask) for i in range(count)])  106 us
    pallas_call x2, Pallas kernels, expert_part(): pl.pallas_call(functools.partial(expert_kernel, experts, capacity, index,...  35.3 us
    ppermute x24, starting transfers between devices, to_owner(): return lax.ppermute(value, 'exp', [(i, i ^ mask) for i in range(count)])  32.8 us
    pallas_call x1, Pallas kernels, attend(): pl.pallas_call(functools.partial(attend_kernel, experts, capacity, heads,...  25.5 us
    ppermute x7, waiting for transfers between devices, partner(): return lax.ppermute(value, 'ctx', [(i, i ^ mask) for i in range(count)])  14.7 us
    pallas_call x1, Pallas kernels, weight_blocks(): pl.pallas_call(functools.partial(weight_kernel, count), grid=(blocks,), i...  10.1 us
    pallas_call x2, Pallas kernels, restore(): pl.pallas_call(functools.partial(restore_kernel, experts, capacity), grid...  7.1 us
  transfers between devices with their start and end apart: 34, of which 17 were waited for; matrix products, arithmetic and copies ran while one was open for 5% of the time, Pallas kernels for 25%

profile of v5, /device:TPU:22, one launch (start us, length us, event | category | flops | bytes accessed | tf_op | source)
XLA Modules:
  0.0 273.4 jit_solution(16688105151985146051)
XLA Ops:
  6.9 3.5 %collective-permute-start.1 = (bf16[512,256]{1,0:T(8,128)(2,1)S(1)}, bf16[512,256]{1,0:T(8,128)(2,1)S(1)}, u32[]{:S(2)}, u32[]{:S(2)}) collective-permute-start(bf16[512,256]{1,0:T(8,128)(2,1)S(1)} %constant_dynamic-slice_fusion.2), channel_id=1, source_target_pairs={{0,2},{1,3},{2,0},{3,1},{4,6},{5,7},{6,4},{7,5},{8,10},{9,11},{10,... | collective-permute-start | bytes 786440 | tf_op jit(solution)/shard_map/ppermute | solution.py:450
  10.6 7.0 %collective-permute-done.6.refs_3_ = bf16[4,256,256]{2,1,0:T(8,128)(2,1)S(1)} collective-permute-done((bf16[4,256,256]{2,1,0:T(8,128)(2,1)S(1)}, bf16[4,256,256]{2,1,0:T(8,128)(2,1)S(1)}, u32[]{:S(2)}, u32[]{:S(2)}) %collective-permute-start.6) | collective-permute-done | bytes 524320 | tf_op jit(solution)/shard_map/ppermute | solution.py:445
  19.8 4.2 %all-to-all-start = ((f32[4,2,256]{2,1,0:T(2,128)}), f32[4,2,256]{2,1,0:T(2,128)S(1)}, u32[]{:S(2)}, u32[]{:S(2)}) async-start(f32[4,2,256]{2,1,0:T(2,128)} %broadcast_in_dim.4), calls=%async_computation | async-start | bytes 16384 | tf_op jit(solution)/shard_map/all_to_all | solution.py:515
  32.6 4.2 %all-to-all-start.1 = ((bf16[4,3,512,256]{3,2,1,0:T(8,128)(2,1)}), bf16[4,3,512,256]{3,2,1,0:T(8,128)(2,1)S(1)}, u32[]{:S(2)}, u32[]{:S(2)}) async-start(bf16[4,3,512,256]{3,2,1,0:T(8,128)(2,1)} %broadcast_in_dim.5), calls=%async_computation.1 | async-start | bytes 6291456 | tf_op jit(solution)/shard_map/all_to_all | solution.py:533
  45.1 18.5 %collective-permute-done.3.refs_5_ = bf16[128,2048]{1,0:T(8,128)(2,1)} collective-permute-done((bf16[128,2048]{1,0:T(8,128)(2,1)}, bf16[128,2048]{1,0:T(8,128)(2,1)}, u32[]{:S(2)}, u32[]{:S(2)}) %collective-permute-start.3) | collective-permute-done | bytes 524320 | tf_op jit(solution)/shard_map/ppermute | solution.py:450
  63.6 25.5 %attend.1 = (bf16[4,64,512]{2,1,0:T(8,128)(2,1)}, bf16[4,64,512]{2,1,0:T(8,128)(2,1)}, bf16[4,64,512]{2,1,0:T(8,128)(2,1)}, bf16[4,64,512]{2,1,0:T(8,128)(2,1)},...) custom-call(s32[3]{0:T(128)} %pad_add_fusion.where_ref, ...), custom_call_target="tpu_custom_call" | custom-call | flops 1000 | bytes 1000 | tf_op jit(solution)/shard_map/attend/pallas_call | solution.py:155
  91.7 5.6 %collective-permute-done.10.refs_1_ = bf16[4,64,512]{2,1,0:T(8,128)(2,1)} collective-permute-done((bf16[4,64,512]{2,1,0:T(8,128)(2,1)}, bf16[4,64,512]{2,1,0:T(8,128)(2,1)}, u32[]{:S(2)}, u32[]{:S(2)}) %collective-permute-start.10) | collective-permute-done | bytes 262176 | tf_op jit(solution)/shard_map/ppermute | solution.py:450
  100.5 16.1 %collective-permute-done.11.refs_2_ = bf16[4,64,512]{2,1,0:T(8,128)(2,1)S(1)} collective-permute-done((bf16[4,64,512]{2,1,0:T(8,128)(2,1)}, bf16[4,64,512]{2,1,0:T(8,128)(2,1)S(1)}, u32[]{:S(2)}, u32[]{:S(2)}) %collective-permute-start.11) | collective-permute-done | bytes 262176 | tf_op jit(solution)/shard_map/ppermute | solution.py:450
  116.6 7.3 %collective-permute-done.12.refs_3_ = bf16[4,64,512]{2,1,0:T(8,128)(2,1)S(1)} collective-permute-done((bf16[4,64,512]{2,1,0:T(8,128)(2,1)}, bf16[4,64,512]{2,1,0:T(8,128)(2,1)S(1)}, u32[]{:S(2)}, u32[]{:S(2)}) %collective-permute-start.12) | collective-permute-done | bytes 262176 | tf_op jit(solution)/shard_map/ppermute | solution.py:450
  129.1 17.6 %expert.2 = (bf16[64,2048]{1,0:T(8,128)(2,1)}, bf16[64,2048]{1,0:T(8,128)(2,1)}, bf16[64,2048]{1,0:T(8,128)(2,1)}, bf16[64,2048]{1,0:T(8,128)(2,1)}, bf16[64,204...) custom-call(s32[3]{0:T(128)} %pad_add_fusion.where_ref, ...), custom_call_target="tpu_custom_call" | custom-call | flops 1000 | bytes 1000 | tf_op jit(solution)/shard_map/expert/pallas_call | solution.py:377
  151.1 17.7 %expert.3 = (bf16[64,2048]{1,0:T(8,128)(2,1)}, bf16[64,2048]{1,0:T(8,128)(2,1)}, bf16[64,2048]{1,0:T(8,128)(2,1)}, bf16[64,2048]{1,0:T(8,128)(2,1)}, bf16[64,204...) custom-call(s32[3]{0:T(128)} %pad_add_fusion.where_ref, ...), custom_call_target="tpu_custom_call" | custom-call | flops 1000 | bytes 1000 | tf_op jit(solution)/shard_map/expert/pallas_call | solution.py:377
  168.8 4.2 %collective-permute-done.20.refs_6_ = bf16[64,2048]{1,0:T(8,128)(2,1)S(1)} collective-permute-done((bf16[64,2048]{1,0:T(8,128)(2,1)}, bf16[64,2048]{1,0:T(8,128)(2,1)S(1)}, u32[]{:S(2)}, u32[]{:S(2)}) %collective-permute-start.20) | collective-permute-done | bytes 262176 | tf_op jit(solution)/shard_map/ppermute | solution.py:450
  173.0 4.7 %collective-permute-done.21.refs_3_.refs_7_.refs_11_.refs_15_.refs_19_ = bf16[256,4352]{1,0:T(8,128)(2,1)} collective-permute-done((bf16[256,4352]{1,0:T(8,128)(2,1)}, bf16[256,4352]{1,0:T(8,128)(2,1)}, u32[]{:S(2)}, u32[]{:S(2)}) %collective-permute-start.21) | collective-permute-done | bytes 2228256 | tf_op jit(solution)/shard_map/ppermute | solution.py:445
  177.7 10.1 %weight_grads.1 = bf16[4,3,256,768]{3,2,1,0:T(8,128)(2,1)} custom-call(bf16[256,4352]{1,0:T(8,128)(2,1)} %get-tuple-element.105.refs_0_.refs_4_.refs_8_.refs_12_.refs_16_, bf16[256,4352]{1,0:T(8,128)(2,1)} %copy-done, bf16[256,4352]{1,0:T(8,128)(2,1)} %get-tuple-element.107.refs_2_.refs_6_.refs_10_.refs_14_.refs_18_, ...), custom_call_target="tpu_custom_call" | custom-call | flops 1000 | bytes 1000 | tf_op jit(solution)/shard_map/weight_grads/pallas_call | solution.py:431
  187.9 5.3 %all-to-all-start.2 = ((bf16[4,3,256,768]{3,2,1,0:T(8,128)(2,1)}), bf16[4,3,256,768]{3,2,1,0:T(8,128)(2,1)}, u32[]{:S(2)}, u32[]{:S(2)}) async-start(bf16[4,3,256,768]{3,2,1,0:T(8,128)(2,1)} %weight_grads.1), calls=%async_computation.2 | async-start | bytes 9437184 | tf_op jit(solution)/shard_map/all_to_all | solution.py:575
  196.8 6.9 %collective-permute-done.22.refs_2_ = bf16[64,2048]{1,0:T(8,128)(2,1)S(1)} collective-permute-done((bf16[64,2048]{1,0:T(8,128)(2,1)S(1)}, bf16[64,2048]{1,0:T(8,128)(2,1)S(1)}, u32[]{:S(2)}, u32[]{:S(2)}) %collective-permute-start.22) | collective-permute-done | bytes 262176 | tf_op jit(solution)/shard_map/ppermute | solution.py:450
  203.7 9.3 %collective-permute-done.23.refs_4_ = bf16[64,2048]{1,0:T(8,128)(2,1)S(1)} collective-permute-done((bf16[64,2048]{1,0:T(8,128)(2,1)S(1)}, bf16[64,2048]{1,0:T(8,128)(2,1)S(1)}, u32[]{:S(2)}, u32[]{:S(2)}) %collective-permute-start.23) | collective-permute-done | bytes 262176 | tf_op jit(solution)/shard_map/ppermute | solution.py:450
  213.1 6.7 %collective-permute-done.24.refs_6_ = bf16[64,2048]{1,0:T(8,128)(2,1)S(1)} collective-permute-done((bf16[64,2048]{1,0:T(8,128)(2,1)S(1)}, bf16[64,2048]{1,0:T(8,128)(2,1)S(1)}, u32[]{:S(2)}, u32[]{:S(2)}) %collective-permute-start.24) | collective-permute-done | bytes 262176 | tf_op jit(solution)/shard_map/ppermute | solution.py:450
  223.9 5.1 %collective-permute-done.25.refs_3_ = bf16[64,2048]{1,0:T(8,128)(2,1)S(1)} collective-permute-done((bf16[64,2048]{1,0:T(8,128)(2,1)S(1)}, bf16[64,2048]{1,0:T(8,128)(2,1)S(1)}, u32[]{:S(2)}, u32[]{:S(2)}) %collective-permute-start.25) | collective-permute-done | bytes 262176 | tf_op jit(solution)/shard_map/ppermute | solution.py:450
  232.7 6.7 %collective-permute-done.26.refs_5_ = bf16[64,2048]{1,0:T(8,128)(2,1)S(1)} collective-permute-done((bf16[64,2048]{1,0:T(8,128)(2,1)S(1)}, bf16[64,2048]{1,0:T(8,128)(2,1)S(1)}, u32[]{:S(2)}, u32[]{:S(2)}) %collective-permute-start.26) | collective-permute-done | bytes 262176 | tf_op jit(solution)/shard_map/ppermute | solution.py:450
  239.5 19.1 %collective-permute-done.27.refs_7_ = bf16[64,2048]{1,0:T(8,128)(2,1)S(1)} collective-permute-done((bf16[64,2048]{1,0:T(8,128)(2,1)S(1)}, bf16[64,2048]{1,0:T(8,128)(2,1)S(1)}, u32[]{:S(2)}, u32[]{:S(2)}) %collective-permute-start.27) | collective-permute-done | bytes 262176 | tf_op jit(solution)/shard_map/ppermute | solution.py:450
  259.3 3.5 %restore.2 = bf16[256,2048]{1,0:T(8,128)(2,1)} custom-call(s32[3]{0:T(128)} %pad_add_fusion.where_ref, f32[256,1]{1,0:T(8,128)} %convert_element_type.6.ids_ref, bf16[64,2048]{1,0:T(8,128)(2,1)} %get-tuple-element.92.refs_0_, bf16[64,2048]{1,0:T(8,128)(2,1)} %get-tuple-element.125.refs_1_, bf16[64,2048]{1,0:T(8,128)(2,1)} %copy-done.8, ...), custom_call_target="tpu_custom_call" | custom-call | flops 1000 | bytes 1000 | tf_op jit(solution)/shard_map/restore/pallas_call | solution.py:227
  262.8 3.3 %convert_reduce_fusion = f32[3,256,768]{2,1,0:T(8,128)S(1)} fusion(bf16[4,3,256,768]{3,2,1,0:T(8,128)(2,1)} %all-to-all-done.2), kind=kLoop, calls=%fused_computation | loop fusion | flops 4128768 | bytes 7077888 | tf_op jit(solution)/shard_map/reduce_sum | solution.py:578
  269.8 3.5 %restore.3 = bf16[256,2048]{1,0:T(8,128)(2,1)} custom-call(s32[3]{0:T(128)} %pad_add_fusion.where_ref, f32[256,1]{1,0:T(8,128)} %convert_element_type.6.ids_ref, bf16[64,2048]{1,0:T(8,128)(2,1)} %get-tuple-element.121.refs_0_, bf16[64,2048]{1,0:T(8,128)(2,1)} %get-tuple-element.137.refs_1_, bf16[64,2048]{1,0:T(8,128)(2,1)} %copy-done.11, ...), custom_call_target="tpu_custom_call" | custom-call | flops 1000 | bytes 1000 | tf_op jit(solution)/shard_map/restore/pallas_call | solution.py:227
  (136 shorter events, 56.6 us)
Async XLA Ops:
  2.4 24.6 %collective-permute-start.5 = (bf16[4,256,256]{2,1,0:T(8,128)(2,1)S(1)}, bf16[4,256,256]{2,1,0:T(8,128)(2,1)S(1)}, u32[]{:S(2)}, u32[]{:S(2)}) collective-permute-start(bf16[4,256,256]{2,1,0:T(8,128)(2,1)S(1)} %get-tuple-element.155.refs_0_), channel_id=1, source_target_pairs={{0,16},{4,20},{8,24},{12,28},{16,0},{20,4},{24,8},{28,12},{1,17},{... | collective-permute-start | bytes 1572872 | tf_op jit(solution)/shard_map/ppermute | solution.py:445
  3.9 23.1 %collective-permute-start.4 = (bf16[4,256,256]{2,1,0:T(8,128)(2,1)S(1)}, bf16[4,256,256]{2,1,0:T(8,128)(2,1)S(1)}, u32[]{:S(2)}, u32[]{:S(2)}) collective-permute-start(bf16[4,256,256]{2,1,0:T(8,128)(2,1)S(1)} %get-tuple-element.155.refs_0_), channel_id=1, source_target_pairs={{0,8},{4,12},{8,0},{12,4},{16,24},{20,28},{24,16},{28,20},{1,9},{5... | collective-permute-start | bytes 1572872 | tf_op jit(solution)/shard_map/ppermute | solution.py:445
  6.4 22.3 %collective-permute-start.2 = (bf16[512,256]{1,0:T(8,128)(2,1)S(1)}, bf16[512,256]{1,0:T(8,128)(2,1)S(1)}, u32[]{:S(2)}, u32[]{:S(2)}) collective-permute-start(bf16[512,256]{1,0:T(8,128)(2,1)S(1)} %constant_dynamic-slice_fusion.2), channel_id=1, source_target_pairs={{0,3},{1,2},{2,1},{3,0},{4,7},{5,6},{6,5},{7,4},{8,11},{9,10},{10,... | collective-permute-start | bytes 786440 | tf_op jit(solution)/shard_map/ppermute | solution.py:450
  6.9 21.8 %collective-permute-start.1 = (bf16[512,256]{1,0:T(8,128)(2,1)S(1)}, bf16[512,256]{1,0:T(8,128)(2,1)S(1)}, u32[]{:S(2)}, u32[]{:S(2)}) collective-permute-start(bf16[512,256]{1,0:T(8,128)(2,1)S(1)} %constant_dynamic-slice_fusion.2), channel_id=1, source_target_pairs={{0,2},{1,3},{2,0},{3,1},{4,6},{5,7},{6,4},{7,5},{8,10},{9,11},{10,... | collective-permute-start | bytes 786440 | tf_op jit(solution)/shard_map/ppermute | solution.py:450
  28.7 34.9 %collective-permute-start.7 = (bf16[4,4,256,256]{3,2,1,0:T(8,128)(2,1)}, bf16[4,4,256,256]{3,2,1,0:T(8,128)(2,1)}, u32[]{:S(2)}, u32[]{:S(2)}) collective-permute-start(bf16[4,4,256,256]{3,2,1,0:T(8,128)(2,1)} %pad_maximum_fusion), channel_id=1, source_target_pairs={{0,4},{4,0},{8,12},{12,8},{16,20},{20,16},{24,28},{28,24},{1,5},{5... | collective-permute-start | bytes 6291464 | tf_op jit(solution)/shard_map/ppermute | solution.py:445
  32.6 64.7 %all-to-all-start.1 = ((bf16[4,3,512,256]{3,2,1,0:T(8,128)(2,1)}), bf16[4,3,512,256]{3,2,1,0:T(8,128)(2,1)S(1)}, u32[]{:S(2)}, u32[]{:S(2)}) async-start(bf16[4,3,512,256]{3,2,1,0:T(8,128)(2,1)} %broadcast_in_dim.5), calls=%async_computation.1 | async-start | bytes 6291456 | tf_op jit(solution)/shard_map/all_to_all | solution.py:533
  40.4 23.2 %collective-permute-start.3 = (bf16[128,2048]{1,0:T(8,128)(2,1)}, bf16[128,2048]{1,0:T(8,128)(2,1)}, u32[]{:S(2)}, u32[]{:S(2)}) collective-permute-start(bf16[128,2048]{1,0:T(8,128)(2,1)} %get-tuple-element.77), channel_id=1, source_target_pairs={{0,1},{1,0},{2,3},{3,2},{4,5},{5,4},{6,7},{7,6},{8,9},{9,8},{10,11... | collective-permute-start | bytes 1572872 | tf_op jit(solution)/shard_map/ppermute | solution.py:450
  43.0 46.2 %collective-permute-start.8 = (bf16[128,2048]{1,0:T(8,128)(2,1)}, bf16[128,2048]{1,0:T(8,128)(2,1)S(1)}, u32[]{:S(2)}, u32[]{:S(2)}) collective-permute-start(bf16[128,2048]{1,0:T(8,128)(2,1)} %get-tuple-element.84), channel_id=1, source_target_pairs={{0,2},{1,3},{2,0},{3,1},{4,6},{5,7},{6,4},{7,5},{8,10},{9,11},{10,... | collective-permute-start | bytes 1572872 | tf_op jit(solution)/shard_map/ppermute | solution.py:450
  43.0 46.6 %collective-permute-start.9 = (bf16[128,2048]{1,0:T(8,128)(2,1)}, bf16[128,2048]{1,0:T(8,128)(2,1)}, u32[]{:S(2)}, u32[]{:S(2)}) collective-permute-start(bf16[128,2048]{1,0:T(8,128)(2,1)} %get-tuple-element.85), channel_id=1, source_target_pairs={{0,3},{1,2},{2,1},{3,0},{4,7},{5,6},{6,5},{7,4},{8,11},{9,10},{10,... | collective-permute-start | bytes 1572872 | tf_op jit(solution)/shard_map/ppermute | solution.py:450
  97.2 30.2 %collective-permute-start.13 = (bf16[4,3,512,256]{3,2,1,0:T(8,128)(2,1)S(1)}, bf16[4,3,512,256]{3,2,1,0:T(8,128)(2,1)S(1)}, u32[]{:S(2)}, u32[]{:S(2)}) collective-permute-start(bf16[4,3,512,256]{3,2,1,0:T(8,128)(2,1)S(1)} %all-to-all-done.1.refs_9_), channel_id=1, source_target_pairs={{0,4},{4,0},{8,12},{12,8},{16,20},{20,16},{24,28},{28,24},{1,5},{5... | collective-permute-start | bytes 9437192 | tf_op jit(solution)/shard_map/ppermute | solution.py:445
  98.7 25.2 %collective-permute-start.12 = (bf16[4,64,512]{2,1,0:T(8,128)(2,1)}, bf16[4,64,512]{2,1,0:T(8,128)(2,1)S(1)}, u32[]{:S(2)}, u32[]{:S(2)}) collective-permute-start(bf16[4,64,512]{2,1,0:T(8,128)(2,1)} %get-tuple-element.89), channel_id=1, source_target_pairs={{0,3},{1,2},{2,1},{3,0},{4,7},{5,6},{6,5},{7,4},{8,11},{9,10},{10,... | collective-permute-start | bytes 786440 | tf_op jit(solution)/shard_map/ppermute | solution.py:450
  123.9 24.8 %collective-permute-start.14 = (bf16[4,64,512]{2,1,0:T(8,128)(2,1)}, bf16[4,64,512]{2,1,0:T(8,128)(2,1)S(1)}, u32[]{:S(2)}, u32[]{:S(2)}) collective-permute-start(bf16[4,64,512]{2,1,0:T(8,128)(2,1)} %get-tuple-element.98), channel_id=1, source_target_pairs={{0,1},{1,0},{2,3},{3,2},{4,5},{5,4},{6,7},{7,6},{8,9},{9,8},{10,11... | collective-permute-start | bytes 786440 | tf_op jit(solution)/shard_map/ppermute | solution.py:450
  123.9 26.3 %collective-permute-start.15 = (bf16[4,64,512]{2,1,0:T(8,128)(2,1)}, bf16[4,64,512]{2,1,0:T(8,128)(2,1)S(1)}, u32[]{:S(2)}, u32[]{:S(2)}) collective-permute-start(bf16[4,64,512]{2,1,0:T(8,128)(2,1)} %get-tuple-element.99), channel_id=1, source_target_pairs={{0,2},{1,3},{2,0},{3,1},{4,6},{5,7},{6,4},{7,5},{8,10},{9,11},{10,... | collective-permute-start | bytes 786440 | tf_op jit(solution)/shard_map/ppermute | solution.py:450
  125.9 25.2 %collective-permute-start.16 = (bf16[4,64,512]{2,1,0:T(8,128)(2,1)}, bf16[4,64,512]{2,1,0:T(8,128)(2,1)}, u32[]{:S(2)}, u32[]{:S(2)}) collective-permute-start(bf16[4,64,512]{2,1,0:T(8,128)(2,1)} %get-tuple-element.100), channel_id=1, source_target_pairs={{0,3},{1,2},{2,1},{3,0},{4,7},{5,6},{6,5},{7,4},{8,11},{9,10},{10,... | collective-permute-start | bytes 786440 | tf_op jit(solution)/shard_map/ppermute | solution.py:450
  146.7 22.1 %collective-permute-start.18 = (bf16[64,2048]{1,0:T(8,128)(2,1)}, bf16[64,2048]{1,0:T(8,128)(2,1)S(1)}, u32[]{:S(2)}, u32[]{:S(2)}) collective-permute-start(bf16[64,2048]{1,0:T(8,128)(2,1)} %get-tuple-element.109), channel_id=1, source_target_pairs={{0,1},{1,0},{2,3},{3,2},{4,5},{5,4},{6,7},{7,6},{8,9},{9,8},{10,11... | collective-permute-start | bytes 786440 | tf_op jit(solution)/shard_map/ppermute | solution.py:450
  147.7 21.1 %collective-permute-start.19 = (bf16[64,2048]{1,0:T(8,128)(2,1)}, bf16[64,2048]{1,0:T(8,128)(2,1)S(1)}, u32[]{:S(2)}, u32[]{:S(2)}) collective-permute-start(bf16[64,2048]{1,0:T(8,128)(2,1)} %get-tuple-element.110), channel_id=1, source_target_pairs={{0,2},{1,3},{2,0},{3,1},{4,6},{5,7},{6,4},{7,5},{8,10},{9,11},{10,... | collective-permute-start | bytes 786440 | tf_op jit(solution)/shard_map/ppermute | solution.py:450
  148.7 24.3 %collective-permute-start.20 = (bf16[64,2048]{1,0:T(8,128)(2,1)}, bf16[64,2048]{1,0:T(8,128)(2,1)S(1)}, u32[]{:S(2)}, u32[]{:S(2)}) collective-permute-start(bf16[64,2048]{1,0:T(8,128)(2,1)} %get-tuple-element.111), channel_id=1, source_target_pairs={{0,3},{1,2},{2,1},{3,0},{4,7},{5,6},{6,5},{7,4},{8,11},{9,10},{10,... | collective-permute-start | bytes 786440 | tf_op jit(solution)/shard_map/ppermute | solution.py:450
  151.0 22.1 %collective-permute-start.17 = (bf16[256,4352]{1,0:T(8,128)(2,1)}, bf16[256,4352]{1,0:T(8,128)(2,1)S(1)}, u32[]{:S(2)}, u32[]{:S(2)}) collective-permute-start(bf16[256,4352]{1,0:T(8,128)(2,1)} %get-tuple-element.106), channel_id=1, source_target_pairs={{0,4},{4,0},{8,12},{12,8},{16,20},{20,16},{24,28},{28,24},{1,5},{5... | collective-permute-start | bytes 6684680 | tf_op jit(solution)/shard_map/ppermute | solution.py:445
  187.9 74.9 %all-to-all-start.2 = ((bf16[4,3,256,768]{3,2,1,0:T(8,128)(2,1)}), bf16[4,3,256,768]{3,2,1,0:T(8,128)(2,1)}, u32[]{:S(2)}, u32[]{:S(2)}) async-start(bf16[4,3,256,768]{3,2,1,0:T(8,128)(2,1)} %weight_grads.1), calls=%async_computation.2 | async-start | bytes 9437184 | tf_op jit(solution)/shard_map/all_to_all | solution.py:575
  195.1 24.6 %collective-permute-start.24 = (bf16[64,2048]{1,0:T(8,128)(2,1)S(1)}, bf16[64,2048]{1,0:T(8,128)(2,1)S(1)}, u32[]{:S(2)}, u32[]{:S(2)}) collective-permute-start(bf16[64,2048]{1,0:T(8,128)(2,1)S(1)} %copy-done.28), channel_id=1, source_target_pairs={{0,3},{1,2},{2,1},{3,0},{4,7},{5,6},{6,5},{7,4},{8,11},{9,10},{10,... | collective-permute-start | bytes 786440 | tf_op jit(solution)/shard_map/ppermute | solution.py:450
  221.6 37.0 %collective-permute-start.27 = (bf16[64,2048]{1,0:T(8,128)(2,1)S(1)}, bf16[64,2048]{1,0:T(8,128)(2,1)S(1)}, u32[]{:S(2)}, u32[]{:S(2)}) collective-permute-start(bf16[64,2048]{1,0:T(8,128)(2,1)S(1)} %copy-done.29), channel_id=1, source_target_pairs={{0,3},{1,2},{2,1},{3,0},{4,7},{5,6},{6,5},{7,4},{8,11},{9,10},{10,... | collective-permute-start | bytes 786440 | tf_op jit(solution)/shard_map/ppermute | solution.py:450
  229.0 39.9 %collective-permute-start.28 = (bf16[64,2048]{1,0:T(8,128)(2,1)}, bf16[64,2048]{1,0:T(8,128)(2,1)S(1)}, u32[]{:S(2)}, u32[]{:S(2)}) collective-permute-start(bf16[64,2048]{1,0:T(8,128)(2,1)} %get-tuple-element.134), channel_id=1, source_target_pairs={{0,1},{1,0},{2,3},{3,2},{4,5},{5,4},{6,7},{7,6},{8,9},{9,8},{10,11... | collective-permute-start | bytes 786440 | tf_op jit(solution)/shard_map/ppermute | solution.py:450
  231.3 37.7 %collective-permute-start.29 = (bf16[64,2048]{1,0:T(8,128)(2,1)}, bf16[64,2048]{1,0:T(8,128)(2,1)S(1)}, u32[]{:S(2)}, u32[]{:S(2)}) collective-permute-start(bf16[64,2048]{1,0:T(8,128)(2,1)} %get-tuple-element.135), channel_id=1, source_target_pairs={{0,2},{1,3},{2,0},{3,1},{4,6},{5,7},{6,4},{7,5},{8,10},{9,11},{10,... | collective-permute-start | bytes 786440 | tf_op jit(solution)/shard_map/ppermute | solution.py:450
  231.7 37.2 %collective-permute-start.30 = (bf16[64,2048]{1,0:T(8,128)(2,1)S(1)}, bf16[64,2048]{1,0:T(8,128)(2,1)S(1)}, u32[]{:S(2)}, u32[]{:S(2)}) collective-permute-start(bf16[64,2048]{1,0:T(8,128)(2,1)S(1)} %copy-done.27), channel_id=1, source_target_pairs={{0,3},{1,2},{2,1},{3,0},{4,7},{5,6},{6,5},{7,4},{8,11},{9,10},{10,... | collective-permute-start | bytes 786440 | tf_op jit(solution)/shard_map/ppermute | solution.py:450
  (44 other events, 707.1 us)

commit v6 on v5

--- a/solution.py
+++ b/solution.py
@@ -252,7 +252,8 @@
     att_cols = att_refs[0].shape[-1]
     pieces, _, _, piece = w_scr.shape
     ff = gate_scr.shape[1]
-    core, owner = jnp.bitwise_and(where_ref[0], 1), where_ref[1]
+    ctx, owner = where_ref[0], where_ref[1]
+    core = jnp.bitwise_and(ctx, 1)
     sources = [jnp.bitwise_xor(owner, d) for d in range(experts)]
     units_at, gate_at, up_at, normed_at = 0, ff, 2 * ff, 3 * ff
 
@@ -327,8 +328,7 @@
     for c, ref in enumerate(saved_refs):
         for t in range(half // PIECE):
             if swap:
-                block = 2 * t + (core if c == 0 else 1 - core)
-                column = pl.multiple_of(block * PIECE, PIECE)
+                column = pl.multiple_of(jnp.bitwise_xor(ctx, 2 * t + c) * PIECE, PIECE)
             else:
                 column = t * PIECE
             at = normed_at + t * PIECE
@@ -407,33 +407,40 @@
 
 def weight_kernel(count, *refs):
     units, back_gate, back_up, normed, back = [refs[i * count : (i + 1) * count] for i in range(5)]
-    out_ref = refs[5 * count]
+    outs = refs[5 * count :]
     first = ((0,), (0,))
 
     def total(left, right):
         return sum(dot(a[...], b[...], first) for a, b in zip(left, right)).astype(BF16)
 
-    out_ref[0, 0] = total(normed, back_gate)
-    out_ref[0, 1] = total(normed, back_up)
-    down = total(units, back)
+    gate, up, down = total(normed, back_gate), total(normed, back_up), total(units, back)
     cols = down.shape[1]
-    for t in range(0, down.shape[0], cols):
-        out_ref[0, 2, :, t : t + cols] = down[t : t + cols]
-
-
-def weight_blocks(saved, blocks, ff):
+    part = gate.shape[0] // len(outs)
+    for c, ref in enumerate(outs):
+        rows = slice(c * part, (c + 1) * part)
+        ref[0, 0] = gate[rows]
+        ref[0, 1] = up[rows]
+        for t in range(0, down.shape[0], cols):
+            ref[0, 2, :, t : t + cols] = down[t + c * part : t + (c + 1) * part]
+
+
+def weight_blocks(saved, blocks, ff, split):
     count = len(saved)
     rows, total = saved[0].shape
     normed_at = 3 * ff // PIECE
     back_at = normed_at + blocks
     thin = lambda at: [pl.BlockSpec((rows, PIECE), lambda i: (0, at + i))] * count
     full = lambda at: [pl.BlockSpec((rows, ff), lambda i: (0, at))] * count
+    part = PIECE // 2 if split else PIECE
+    shuffled = lambda i: (i % 2 * (blocks // 2) + i // 2, 0, 0, 0)
+    plain = lambda i: (i, 0, 0, 0)
+    orders = [shuffled, plain] if split else [plain]
     return pl.pallas_call(
         functools.partial(weight_kernel, count),
         grid=(blocks,),
         in_specs=full(0) + full(1) + full(2) + thin(normed_at) + thin(back_at),
-        out_specs=pl.BlockSpec((1, 3, PIECE, ff), lambda i: (i, 0, 0, 0)),
-        out_shape=jax.ShapeDtypeStruct((blocks, 3, PIECE, ff), BF16),
+        out_specs=[pl.BlockSpec((1, 3, part, ff), order) for order in orders],
+        out_shape=[jax.ShapeDtypeStruct((blocks, 3, part, ff), BF16) for _ in orders],
         compiler_params=kernel_params(),
         cost_estimate=brief(),
         name="weight_grads",
@@ -523,10 +530,11 @@
     values = lax.dynamic_slice_in_dim(value_head_rows, first_column, HEAD_SIZE, 2)
     own = jnp.concatenate([keys, values], axis=2)
     chips = [own] + [partner(own, m) for m in range(2, ctx_count, 2)]
-    key_values = chips + [partner(jnp.stack(chips), 1)]
 
     grads = place(where, ids_f.reshape(1, n), grad_out, experts, capacity)
-    grads = to_owners(after(grads, projection))
+    grads = to_owners(grads)
+
+    key_values = chips + [partner(after(jnp.stack(chips), grads[1]), 1)]
 
     projection = after(jnp.stack(projection), chips)
     projection = jnp.broadcast_to(projection[None], (pieces // 2,) + projection.shape)
@@ -534,10 +542,10 @@
         projection, "ctx", 0, 0, axis_index_groups=chip_groups(pieces), tiled=True
     )
 
-    sent = attend(where, after(queries, grads[1]), key_values, ids_all, capacity)
+    sent = attend(where, queries, key_values, ids_all, capacity)
     arrived = to_owners(after(sent[0], grads))
-    later = after(sent[1], arrived, same)
-    same = after(same, arrived[1])
+    later = after(sent[1], arrived[1], same)
+    same = after(same, sent[0], grads[2:])
     other = partner(same, 1)
 
     rows_dev = width // ctx_count
@@ -569,20 +577,28 @@
     if swap:
         saved = [saved_a[0], partner(saved_a[1], 1)]
         saved += [saved_b[0], partner(after(saved_b[1], layer_a), 1)]
-        change_a = to_owners(after(change_a, layer_a))
-        parts = weight_blocks(saved, width // PIECE // 2, ff)
-        layer_b = after(layer_b, parts)
-        parts = lax.all_to_all(
-            parts, "ctx", 0, 0, axis_index_groups=chip_groups(ctx_count), tiled=True
-        )
-        total = jnp.sum(parts.astype(F32), axis=0)
+        change_a = to_owners(after(change_a, layer_a[1]))
+        parts = weight_blocks(saved, ctx_count // 2, ff, True)
+        parts = after(parts, change_a)
+        half = ctx_count // 4
+        masks = (2, 4), (4, 2)
+        near = [partner(x[half:], m[0]) for x, m in zip(parts, masks)]
+        layer_b = to_owners(after(layer_b, change_a[1]))
+        near = after(near, layer_b[1])
+        sums = [x[:half].astype(F32) + y.astype(F32) for x, y in zip(parts, near)]
+        gone = [x[1].astype(BF16) for x in sums]
+        change_b = after(change_b, gone)
+        far = [partner(x, m[1]) for x, m in zip(gone, masks)]
+        total = [x[0] + y.astype(F32) for x, y in zip(sums, far)]
+        total = jnp.concatenate(total, axis=1)
         grad_gate, grad_up = total[0][None], total[1][None]
         grad_down = total[2].reshape(PIECE, ff // PIECE, PIECE).transpose(1, 0, 2)
         grad_down = grad_down.reshape(1, ff, PIECE)
     else:
-        change_a = to_owners(after(change_a, layer_a))
+        change_a = to_owners(after(change_a, layer_a[1]))
+        layer_b = to_owners(after(layer_b, change_a[1]))
         blocks = width // PIECE
-        parts = weight_blocks(list(saved_a) + list(saved_b), blocks, ff)
+        (parts,) = weight_blocks(list(saved_a) + list(saved_b), blocks, ff, False)
         part_down = parts[:, 2].reshape(blocks, PIECE, ff // PIECE, PIECE).transpose(0, 2, 1, 3)
         part_down = part_down.reshape(blocks, ff, PIECE // rows_dev, rows_dev)
         part_down = part_down.transpose(0, 2, 1, 3).reshape(ctx_count, ff, rows_dev)
@@ -595,7 +611,6 @@
                 (part_down, (ff, rows_dev)),
             )
         ]
-    layer_b = to_owners(after(layer_b, change_a))
     change_b = to_owners(after(change_b, layer_b[1:2]))
     layer_out = restore(where, ids_f, [layer_a, layer_b], experts, capacity)
     change_b = after(change_b, layer_out, grad_gate, grad_up, grad_down)

time: 274 us -> 300 us (1.095)
  waiting for transfers between devices: 122 us -> 145 us
  starting transfers between devices: 50 us -> 45.1 us
  local copies, waits for them, and re-layouts: 12.1 us -> 16.5 us
    ppermute x24, waiting for transfers between devices: 106 us -> 119 us  [to_owner(): return lax.ppermute(value, 'exp', [(i, i ^ mask) for i in range(count)])]
    all_to_all x1 -> x0, starting transfers between devices: 5.31 us -> none  [on_device(): lax.all_to_all(parts, 'ctx', 0, 0, axis_index_groups=chip_groups(ctx_coun...]
    all_to_all x1, waiting for transfers between devices: 0.83 us -> 6.09 us  [on_device(): info = lax.all_to_all(info, 'exp', 0, 0, tiled=True)]
    ppermute x7 -> x11, waiting for transfers between devices: 14.7 us -> 19.5 us  [partner(): return lax.ppermute(value, 'ctx', [(i, i ^ mask) for i in range(count)])]
    reduce_sum x1 -> x0, other arithmetic: 3.34 us -> none  [on_device(): total = jnp.sum(parts.astype(F32), axis=0)]
    unnamed x69, local copies, waits for them, and re-layouts: 4.21 us -> 7.47 us
    ppermute x7 -> x11, starting transfers between devices: 3.56 us -> 6.43 us  [partner(): return lax.ppermute(value, 'ctx', [(i, i ^ mask) for i in range(count)])]
  transfers between devices with their start and end apart: 34 -> 37, of which waited for: 17 -> 19; matrix products, arithmetic and copies ran while one was open for 5% -> 5% of each run, Pallas kernels for 25% -> 26%
where the time goes in v6:
time: 300 us; the launch traced here: 298 us
  waiting for transfers between devices  145 us (48%)
  Pallas kernels  81.2 us (27%)
  starting transfers between devices  45.1 us (15%)
  local copies, waits for them, and re-layouts  16.5 us (6%)
  other arithmetic  9.47 us (3%)
    ppermute x24, waiting for transfers between devices, to_owner(): return lax.ppermute(value, 'exp', [(i, i ^ mask) for i in range(count)])  119 us
    pallas_call x2, Pallas kernels, expert_part(): pl.pallas_call(functools.partial(expert_kernel, experts, capacity, index,...  35.4 us
    ppermute x24, starting transfers between devices, to_owner(): return lax.ppermute(value, 'exp', [(i, i ^ mask) for i in range(count)])  30.3 us
    pallas_call x1, Pallas kernels, attend(): pl.pallas_call(functools.partial(attend_kernel, experts, capacity, heads,...  25.5 us
    ppermute x11, waiting for transfers between devices, partner(): return lax.ppermute(value, 'ctx', [(i, i ^ mask) for i in range(count)])  19.5 us
    pallas_call x1, Pallas kernels, weight_blocks(): pl.pallas_call(functools.partial(weight_kernel, count), grid=(blocks,), i...  10 us
    unnamed x69, local copies, waits for them, and re-layouts  7.47 us
    pallas_call x2, Pallas kernels, restore(): pl.pallas_call(functools.partial(restore_kernel, experts, capacity), grid...  7.11 us
  transfers between devices with their start and end apart: 37, of which 19 were waited for; matrix products, arithmetic and copies ran while one was open for 5% of the time, Pallas kernels for 26%

profile of v6, /device:TPU:22, one launch (start us, length us, event | category | flops | bytes accessed | tf_op | source)
XLA Modules:
  0.0 298.4 jit_solution(14275369232181228239)
XLA Ops:
  11.1 11.1 %collective-permute-done.12 = bf16[512,256]{1,0:T(8,128)(2,1)S(1)} collective-permute-done((bf16[512,256]{1,0:T(8,128)(2,1)S(1)}, bf16[512,256]{1,0:T(8,128)(2,1)S(1)}, u32[]{:S(2)}, u32[]{:S(2)}) %collective-permute-start.12) | collective-permute-done | bytes 262176 | tf_op jit(solution)/shard_map/ppermute | solution.py:457
  30.1 4.2 %all-to-all-start = ((f32[4,2,256]{2,1,0:T(2,128)}), f32[4,2,256]{2,1,0:T(2,128)S(1)}, u32[]{:S(2)}, u32[]{:S(2)}) async-start(f32[4,2,256]{2,1,0:T(2,128)} %broadcast_in_dim.4), calls=%async_computation | async-start | bytes 16384 | tf_op jit(solution)/shard_map/all_to_all | solution.py:522
  36.2 6.1 %all-to-all-done = f32[4,2,256]{2,1,0:T(2,128)S(1)} async-done(((f32[4,2,256]{2,1,0:T(2,128)}), f32[4,2,256]{2,1,0:T(2,128)S(1)}, u32[]{:S(2)}, u32[]{:S(2)}) %all-to-all-start) | async-done | bytes 8224 | tf_op jit(solution)/shard_map/all_to_all | solution.py:522
  44.2 4.2 %all-to-all-start.1 = ((bf16[4,3,512,256]{3,2,1,0:T(8,128)(2,1)}), bf16[4,3,512,256]{3,2,1,0:T(8,128)(2,1)S(1)}, u32[]{:S(2)}, u32[]{:S(2)}) async-start(bf16[4,3,512,256]{3,2,1,0:T(8,128)(2,1)} %broadcast_in_dim.5), calls=%async_computation.1 | async-start | bytes 6291456 | tf_op jit(solution)/shard_map/all_to_all | solution.py:541
  54.9 25.5 %attend.1 = (bf16[4,64,512]{2,1,0:T(8,128)(2,1)}, bf16[4,64,512]{2,1,0:T(8,128)(2,1)}, bf16[4,64,512]{2,1,0:T(8,128)(2,1)}, bf16[4,64,512]{2,1,0:T(8,128)(2,1)},...) custom-call(s32[3]{0:T(128)} %pad_add_fusion.where_ref, ...), custom_call_target="tpu_custom_call" | custom-call | flops 1000 | bytes 1000 | tf_op jit(solution)/shard_map/attend/pallas_call | solution.py:155
  80.4 6.8 %collective-permute-done.5.refs_6_ = bf16[128,2048]{1,0:T(8,128)(2,1)S(1)} collective-permute-done((bf16[128,2048]{1,0:T(8,128)(2,1)}, bf16[128,2048]{1,0:T(8,128)(2,1)S(1)}, u32[]{:S(2)}, u32[]{:S(2)}) %collective-permute-start.5) | collective-permute-done | bytes 524320 | tf_op jit(solution)/shard_map/ppermute | solution.py:457
  87.9 11.6 %collective-permute-done.6.refs_7_ = bf16[128,2048]{1,0:T(8,128)(2,1)} collective-permute-done((bf16[128,2048]{1,0:T(8,128)(2,1)}, bf16[128,2048]{1,0:T(8,128)(2,1)}, u32[]{:S(2)}, u32[]{:S(2)}) %collective-permute-start.6) | collective-permute-done | bytes 524320 | tf_op jit(solution)/shard_map/ppermute | solution.py:457
  103.1 8.3 %collective-permute-done.7.refs_1_ = bf16[4,64,512]{2,1,0:T(8,128)(2,1)S(1)} collective-permute-done((bf16[4,64,512]{2,1,0:T(8,128)(2,1)}, bf16[4,64,512]{2,1,0:T(8,128)(2,1)S(1)}, u32[]{:S(2)}, u32[]{:S(2)}) %collective-permute-start.7) | collective-permute-done | bytes 262176 | tf_op jit(solution)/shard_map/ppermute | solution.py:457
  114.2 6.5 %collective-permute-done.8.refs_2_ = bf16[4,64,512]{2,1,0:T(8,128)(2,1)S(1)} collective-permute-done((bf16[4,64,512]{2,1,0:T(8,128)(2,1)}, bf16[4,64,512]{2,1,0:T(8,128)(2,1)S(1)}, u32[]{:S(2)}, u32[]{:S(2)}) %collective-permute-start.8) | collective-permute-done | bytes 262176 | tf_op jit(solution)/shard_map/ppermute | solution.py:457
  121.3 17.3 %collective-permute-done.9.refs_3_ = bf16[4,64,512]{2,1,0:T(8,128)(2,1)S(1)} collective-permute-done((bf16[4,64,512]{2,1,0:T(8,128)(2,1)}, bf16[4,64,512]{2,1,0:T(8,128)(2,1)S(1)}, u32[]{:S(2)}, u32[]{:S(2)}) %collective-permute-start.9) | collective-permute-done | bytes 262176 | tf_op jit(solution)/shard_map/ppermute | solution.py:457
  140.4 17.6 %expert.2 = (bf16[64,2048]{1,0:T(8,128)(2,1)}, bf16[64,2048]{1,0:T(8,128)(2,1)}, bf16[64,2048]{1,0:T(8,128)(2,1)}, bf16[64,2048]{1,0:T(8,128)(2,1)}, bf16[64,204...) custom-call(s32[3]{0:T(128)} %pad_add_fusion.where_ref, ...), custom_call_target="tpu_custom_call" | custom-call | flops 1000 | bytes 1000 | tf_op jit(solution)/shard_map/expert/pallas_call | solution.py:377
  162.2 17.8 %expert.3 = (bf16[64,2048]{1,0:T(8,128)(2,1)}, bf16[64,2048]{1,0:T(8,128)(2,1)}, bf16[64,2048]{1,0:T(8,128)(2,1)}, bf16[64,2048]{1,0:T(8,128)(2,1)}, bf16[64,204...) custom-call(s32[3]{0:T(128)} %pad_add_fusion.where_ref, ...), custom_call_target="tpu_custom_call" | custom-call | flops 1000 | bytes 1000 | tf_op jit(solution)/shard_map/expert/pallas_call | solution.py:377
  182.5 3.8 %collective-permute-start.26 = (bf16[64,2048]{1,0:T(8,128)(2,1)}, bf16[64,2048]{1,0:T(8,128)(2,1)S(1)}, u32[]{:S(2)}, u32[]{:S(2)}) collective-permute-start(bf16[64,2048]{1,0:T(8,128)(2,1)} %get-tuple-element.127), channel_id=1, source_target_pairs={{0,2},{1,3},{2,0},{3,1},{4,6},{5,7},{6,4},{7,5},{8,10},{9,11},{10,... | collective-permute-start | bytes 786440 | tf_op jit(solution)/shard_map/ppermute | solution.py:457
  187.7 10.0 %weight_grads.1 = (bf16[4,3,128,768]{3,2,1,0:T(8,128)(2,1)}, bf16[4,3,128,768]{3,2,1,0:T(8,128)(2,1)}) custom-call(bf16[256,4352]{1,0:T(8,128)(2,1)} %get-tuple-element.120.refs_0_.refs_4_.refs_8_.refs_12_.refs_16_, bf16[256,4352]{1,0:T(8,128)(2,1)} %copy-done, bf16[256,4352]{1,0:T(8,128)(2,1)} %get-tuple-element.122.refs_2_.refs_6_.refs_10_.refs_14_.refs_18_, ...), custom_call_target="tpu_custom_call" | custom-call | flops 1000 | bytes 1000 | tf_op jit(solution)/shard_map/weight_grads/pallas_call | solution.py:438
  197.8 6.9 %collective-permute-done.26.refs_4_ = bf16[64,2048]{1,0:T(8,128)(2,1)S(1)} collective-permute-done((bf16[64,2048]{1,0:T(8,128)(2,1)}, bf16[64,2048]{1,0:T(8,128)(2,1)S(1)}, u32[]{:S(2)}, u32[]{:S(2)}) %collective-permute-start.26) | collective-permute-done | bytes 262176 | tf_op jit(solution)/shard_map/ppermute | solution.py:457
  204.6 4.2 %collective-permute-done.27.refs_6_ = bf16[64,2048]{1,0:T(8,128)(2,1)S(1)} collective-permute-done((bf16[64,2048]{1,0:T(8,128)(2,1)S(1)}, bf16[64,2048]{1,0:T(8,128)(2,1)S(1)}, u32[]{:S(2)}, u32[]{:S(2)}) %collective-permute-start.27) | collective-permute-done | bytes 262176 | tf_op jit(solution)/shard_map/ppermute | solution.py:457
  211.1 6.8 %collective-permute-done.19.refs_3_ = bf16[64,2048]{1,0:T(8,128)(2,1)S(1)} collective-permute-done((bf16[64,2048]{1,0:T(8,128)(2,1)}, bf16[64,2048]{1,0:T(8,128)(2,1)S(1)}, u32[]{:S(2)}, u32[]{:S(2)}) %collective-permute-start.19) | collective-permute-done | bytes 262176 | tf_op jit(solution)/shard_map/ppermute | solution.py:457
  217.9 19.1 %collective-permute-done.29 = bf16[2,3,128,768]{3,2,1,0:T(8,128)(2,1)S(1)} collective-permute-done((bf16[2,3,128,768]{3,2,1,0:T(8,128)(2,1)S(1)}, bf16[2,3,128,768]{3,2,1,0:T(8,128)(2,1)S(1)}, u32[]{:S(2)}, u32[]{:S(2)}) %collective-permute-start.29) | collective-permute-done | bytes 1179680 | tf_op jit(solution)/shard_map/ppermute | solution.py:452
  245.4 13.8 %collective-permute-done.21.refs_5_ = bf16[64,2048]{1,0:T(8,128)(2,1)S(1)} collective-permute-done((bf16[64,2048]{1,0:T(8,128)(2,1)S(1)}, bf16[64,2048]{1,0:T(8,128)(2,1)S(1)}, u32[]{:S(2)}, u32[]{:S(2)}) %collective-permute-start.21) | collective-permute-done | bytes 262176 | tf_op jit(solution)/shard_map/ppermute | solution.py:457
  259.2 5.7 %collective-permute-done.23.refs_7_ = bf16[64,2048]{1,0:T(8,128)(2,1)} collective-permute-done((bf16[64,2048]{1,0:T(8,128)(2,1)S(1)}, bf16[64,2048]{1,0:T(8,128)(2,1)}, u32[]{:S(2)}, u32[]{:S(2)}) %collective-permute-start.23) | collective-permute-done | bytes 262176 | tf_op jit(solution)/shard_map/ppermute | solution.py:457
  265.0 3.6 %restore.2 = bf16[256,2048]{1,0:T(8,128)(2,1)} custom-call(s32[3]{0:T(128)} %pad_add_fusion.where_ref, f32[256,1]{1,0:T(8,128)} %convert_element_type.29.ids_ref, bf16[64,2048]{1,0:T(8,128)(2,1)} %get-tuple-element.90.refs_0_, bf16[64,2048]{1,0:T(8,128)(2,1)} %get-tuple-element.109.refs_1_, bf16[64,2048]{1,0:T(8,128)(2,1)} %copy-done.14, ...), custom_call_target="tpu_custom_call" | custom-call | flops 1000 | bytes 1000 | tf_op jit(solution)/shard_map/restore/pallas_call | solution.py:227
  278.1 10.0 %collective-permute-done.31.refs_5_ = bf16[64,2048]{1,0:T(8,128)(2,1)S(1)} collective-permute-done((bf16[64,2048]{1,0:T(8,128)(2,1)}, bf16[64,2048]{1,0:T(8,128)(2,1)S(1)}, u32[]{:S(2)}, u32[]{:S(2)}) %collective-permute-start.31) | collective-permute-done | bytes 262176 | tf_op jit(solution)/shard_map/ppermute | solution.py:457
  288.1 6.8 %collective-permute-done.32.refs_7_ = bf16[64,2048]{1,0:T(8,128)(2,1)} collective-permute-done((bf16[64,2048]{1,0:T(8,128)(2,1)}, bf16[64,2048]{1,0:T(8,128)(2,1)}, u32[]{:S(2)}, u32[]{:S(2)}) %collective-permute-start.32) | collective-permute-done | bytes 262176 | tf_op jit(solution)/shard_map/ppermute | solution.py:457
  294.8 3.6 %restore.3 = bf16[256,2048]{1,0:T(8,128)(2,1)} custom-call(s32[3]{0:T(128)} %pad_add_fusion.where_ref, f32[256,1]{1,0:T(8,128)} %convert_element_type.29.ids_ref, bf16[64,2048]{1,0:T(8,128)(2,1)} %get-tuple-element.115.refs_0_, bf16[64,2048]{1,0:T(8,128)(2,1)} %get-tuple-element.141.refs_1_, bf16[64,2048]{1,0:T(8,128)(2,1)} %copy-done.16, ...), custom_call_target="tpu_custom_call" | custom-call | flops 1000 | bytes 1000 | tf_op jit(solution)/shard_map/restore/pallas_call | solution.py:227
  (149 shorter events, 66.1 us)
Async XLA Ops:
  2.2 24.6 %collective-permute-start.11 = (bf16[512,256]{1,0:T(8,128)(2,1)S(1)}, bf16[512,256]{1,0:T(8,128)(2,1)S(1)}, u32[]{:S(2)}, u32[]{:S(2)}) collective-permute-start(bf16[512,256]{1,0:T(8,128)(2,1)S(1)} %constant_dynamic-slice_fusion), channel_id=1, source_target_pairs={{0,2},{1,3},{2,0},{3,1},{4,6},{5,7},{6,4},{7,5},{8,10},{9,11},{10,... | collective-permute-start | bytes 786440 | tf_op jit(solution)/shard_map/ppermute | solution.py:457
  7.6 28.5 %collective-permute-start.2 = (bf16[4,256,256]{2,1,0:T(8,128)(2,1)S(1)}, bf16[4,256,256]{2,1,0:T(8,128)(2,1)S(1)}, u32[]{:S(2)}, u32[]{:S(2)}) collective-permute-start(bf16[4,256,256]{2,1,0:T(8,128)(2,1)S(1)} %get-tuple-element.149.refs_0_), channel_id=1, source_target_pairs={{0,24},{4,28},{8,16},{12,20},{16,8},{20,12},{24,0},{28,4},{1,25},{... | collective-permute-start | bytes 1572872 | tf_op jit(solution)/shard_map/ppermute | solution.py:452
  8.1 28.1 %collective-permute-start.1 = (bf16[4,256,256]{2,1,0:T(8,128)(2,1)S(1)}, bf16[4,256,256]{2,1,0:T(8,128)(2,1)S(1)}, u32[]{:S(2)}, u32[]{:S(2)}) collective-permute-start(bf16[4,256,256]{2,1,0:T(8,128)(2,1)S(1)} %get-tuple-element.149.refs_0_), channel_id=1, source_target_pairs={{0,16},{4,20},{8,24},{12,28},{16,0},{20,4},{24,8},{28,12},{1,17},{... | collective-permute-start | bytes 1572872 | tf_op jit(solution)/shard_map/ppermute | solution.py:452
  9.6 26.6 %collective-permute-start = (bf16[4,256,256]{2,1,0:T(8,128)(2,1)S(1)}, bf16[4,256,256]{2,1,0:T(8,128)(2,1)S(1)}, u32[]{:S(2)}, u32[]{:S(2)}) collective-permute-start(bf16[4,256,256]{2,1,0:T(8,128)(2,1)S(1)} %get-tuple-element.149.refs_0_), channel_id=1, source_target_pairs={{0,8},{4,12},{8,0},{12,4},{16,24},{20,28},{24,16},{28,20},{1,9},{5... | collective-permute-start | bytes 1572872 | tf_op jit(solution)/shard_map/ppermute | solution.py:452
  26.7 23.5 %collective-permute-start.3 = (bf16[128,2048]{1,0:T(8,128)(2,1)}, bf16[128,2048]{1,0:T(8,128)(2,1)}, u32[]{:S(2)}, u32[]{:S(2)}) collective-permute-start(bf16[128,2048]{1,0:T(8,128)(2,1)} %get-tuple-element.75), channel_id=1, source_target_pairs={{0,1},{1,0},{2,3},{3,2},{4,5},{5,4},{6,7},{7,6},{8,9},{9,8},{10,11... | collective-permute-start | bytes 1572872 | tf_op jit(solution)/shard_map/ppermute | solution.py:457
  44.2 55.3 %all-to-all-start.1 = ((bf16[4,3,512,256]{3,2,1,0:T(8,128)(2,1)}), bf16[4,3,512,256]{3,2,1,0:T(8,128)(2,1)S(1)}, u32[]{:S(2)}, u32[]{:S(2)}) async-start(bf16[4,3,512,256]{3,2,1,0:T(8,128)(2,1)} %broadcast_in_dim.5), calls=%async_computation.1 | async-start | bytes 6291456 | tf_op jit(solution)/shard_map/all_to_all | solution.py:541
  50.3 36.9 %collective-permute-start.5 = (bf16[128,2048]{1,0:T(8,128)(2,1)}, bf16[128,2048]{1,0:T(8,128)(2,1)S(1)}, u32[]{:S(2)}, u32[]{:S(2)}) collective-permute-start(bf16[128,2048]{1,0:T(8,128)(2,1)} %get-tuple-element.82), channel_id=1, source_target_pairs={{0,2},{1,3},{2,0},{3,1},{4,6},{5,7},{6,4},{7,5},{8,10},{9,11},{10,... | collective-permute-start | bytes 1572872 | tf_op jit(solution)/shard_map/ppermute | solution.py:457
  52.9 46.6 %collective-permute-start.6 = (bf16[128,2048]{1,0:T(8,128)(2,1)}, bf16[128,2048]{1,0:T(8,128)(2,1)}, u32[]{:S(2)}, u32[]{:S(2)}) collective-permute-start(bf16[128,2048]{1,0:T(8,128)(2,1)} %get-tuple-element.83), channel_id=1, source_target_pairs={{0,3},{1,2},{2,1},{3,0},{4,7},{5,6},{6,5},{7,4},{8,11},{9,10},{10,... | collective-permute-start | bytes 1572872 | tf_op jit(solution)/shard_map/ppermute | solution.py:457
  99.5 39.1 %collective-permute-start.13 = (bf16[4,3,512,256]{3,2,1,0:T(8,128)(2,1)S(1)}, bf16[4,3,512,256]{3,2,1,0:T(8,128)(2,1)S(1)}, u32[]{:S(2)}, u32[]{:S(2)}) collective-permute-start(bf16[4,3,512,256]{3,2,1,0:T(8,128)(2,1)S(1)} %all-to-all-done.1.refs_9_), channel_id=1, source_target_pairs={{0,4},{4,0},{8,12},{12,8},{16,20},{20,16},{24,28},{28,24},{1,5},{5... | collective-permute-start | bytes 9437192 | tf_op jit(solution)/shard_map/ppermute | solution.py:452
  102.4 36.2 %collective-permute-start.9 = (bf16[4,64,512]{2,1,0:T(8,128)(2,1)}, bf16[4,64,512]{2,1,0:T(8,128)(2,1)S(1)}, u32[]{:S(2)}, u32[]{:S(2)}) collective-permute-start(bf16[4,64,512]{2,1,0:T(8,128)(2,1)} %get-tuple-element.87), channel_id=1, source_target_pairs={{0,3},{1,2},{2,1},{3,0},{4,7},{5,6},{6,5},{7,4},{8,11},{9,10},{10,... | collective-permute-start | bytes 786440 | tf_op jit(solution)/shard_map/ppermute | solution.py:457
  111.4 49.4 %collective-permute-start.14 = (bf16[4,64,512]{2,1,0:T(8,128)(2,1)}, bf16[4,64,512]{2,1,0:T(8,128)(2,1)S(1)}, u32[]{:S(2)}, u32[]{:S(2)}) collective-permute-start(bf16[4,64,512]{2,1,0:T(8,128)(2,1)} %get-tuple-element.96), channel_id=1, source_target_pairs={{0,1},{1,0},{2,3},{3,2},{4,5},{5,4},{6,7},{7,6},{8,9},{9,8},{10,11... | collective-permute-start | bytes 786440 | tf_op jit(solution)/shard_map/ppermute | solution.py:457
  113.8 47.7 %collective-permute-start.15 = (bf16[4,64,512]{2,1,0:T(8,128)(2,1)}, bf16[4,64,512]{2,1,0:T(8,128)(2,1)S(1)}, u32[]{:S(2)}, u32[]{:S(2)}) collective-permute-start(bf16[4,64,512]{2,1,0:T(8,128)(2,1)} %get-tuple-element.97), channel_id=1, source_target_pairs={{0,2},{1,3},{2,0},{3,1},{4,6},{5,7},{6,4},{7,5},{8,10},{9,11},{10,... | collective-permute-start | bytes 786440 | tf_op jit(solution)/shard_map/ppermute | solution.py:457
  120.7 41.5 %collective-permute-start.16 = (bf16[4,64,512]{2,1,0:T(8,128)(2,1)}, bf16[4,64,512]{2,1,0:T(8,128)(2,1)}, u32[]{:S(2)}, u32[]{:S(2)}) collective-permute-start(bf16[4,64,512]{2,1,0:T(8,128)(2,1)} %get-tuple-element.98), channel_id=1, source_target_pairs={{0,3},{1,2},{2,1},{3,0},{4,7},{5,6},{6,5},{7,4},{8,11},{9,10},{10,... | collective-permute-start | bytes 786440 | tf_op jit(solution)/shard_map/ppermute | solution.py:457
  157.9 22.1 %collective-permute-start.17 = (bf16[64,2048]{1,0:T(8,128)(2,1)}, bf16[64,2048]{1,0:T(8,128)(2,1)S(1)}, u32[]{:S(2)}, u32[]{:S(2)}) collective-permute-start(bf16[64,2048]{1,0:T(8,128)(2,1)} %get-tuple-element.107), channel_id=1, source_target_pairs={{0,1},{1,0},{2,3},{3,2},{4,5},{5,4},{6,7},{7,6},{8,9},{9,8},{10,11... | collective-permute-start | bytes 786440 | tf_op jit(solution)/shard_map/ppermute | solution.py:457
  158.0 22.1 %collective-permute-start.20 = (bf16[64,2048]{1,0:T(8,128)(2,1)}, bf16[64,2048]{1,0:T(8,128)(2,1)S(1)}, u32[]{:S(2)}, u32[]{:S(2)}) collective-permute-start(bf16[64,2048]{1,0:T(8,128)(2,1)} %get-tuple-element.111), channel_id=1, source_target_pairs={{0,2},{1,3},{2,0},{3,1},{4,6},{5,7},{6,4},{7,5},{8,10},{9,11},{10,... | collective-permute-start | bytes 786440 | tf_op jit(solution)/shard_map/ppermute | solution.py:457
  162.2 24.1 %collective-permute-start.24 = (bf16[256,4352]{1,0:T(8,128)(2,1)}, bf16[256,4352]{1,0:T(8,128)(2,1)S(1)}, u32[]{:S(2)}, u32[]{:S(2)}) collective-permute-start(bf16[256,4352]{1,0:T(8,128)(2,1)} %get-tuple-element.121), channel_id=1, source_target_pairs={{0,4},{4,0},{8,12},{12,8},{16,20},{20,16},{24,28},{28,24},{1,5},{5... | collective-permute-start | bytes 6684680 | tf_op jit(solution)/shard_map/ppermute | solution.py:452
  182.5 22.1 %collective-permute-start.26 = (bf16[64,2048]{1,0:T(8,128)(2,1)}, bf16[64,2048]{1,0:T(8,128)(2,1)S(1)}, u32[]{:S(2)}, u32[]{:S(2)}) collective-permute-start(bf16[64,2048]{1,0:T(8,128)(2,1)} %get-tuple-element.127), channel_id=1, source_target_pairs={{0,2},{1,3},{2,0},{3,1},{4,6},{5,7},{6,4},{7,5},{8,10},{9,11},{10,... | collective-permute-start | bytes 786440 | tf_op jit(solution)/shard_map/ppermute | solution.py:457
  186.3 22.5 %collective-permute-start.27 = (bf16[64,2048]{1,0:T(8,128)(2,1)S(1)}, bf16[64,2048]{1,0:T(8,128)(2,1)S(1)}, u32[]{:S(2)}, u32[]{:S(2)}) collective-permute-start(bf16[64,2048]{1,0:T(8,128)(2,1)S(1)} %copy-done.33), channel_id=1, source_target_pairs={{0,3},{1,2},{2,1},{3,0},{4,7},{5,6},{6,5},{7,4},{8,11},{9,10},{10,... | collective-permute-start | bytes 786440 | tf_op jit(solution)/shard_map/ppermute | solution.py:457
  210.4 26.6 %collective-permute-start.29 = (bf16[2,3,128,768]{3,2,1,0:T(8,128)(2,1)S(1)}, bf16[2,3,128,768]{3,2,1,0:T(8,128)(2,1)S(1)}, u32[]{:S(2)}, u32[]{:S(2)}) collective-permute-start(bf16[2,3,128,768]{3,2,1,0:T(8,128)(2,1)S(1)} %slice.45), channel_id=1, source_target_pairs={{0,16},{4,20},{8,24},{12,28},{16,0},{20,4},{24,8},{28,12},{1,17},{... | collective-permute-start | bytes 3538952 | tf_op jit(solution)/shard_map/ppermute | solution.py:452
  211.1 26.2 %collective-permute-start.28 = (bf16[2,3,128,768]{3,2,1,0:T(8,128)(2,1)S(1)}, bf16[2,3,128,768]{3,2,1,0:T(8,128)(2,1)S(1)}, u32[]{:S(2)}, u32[]{:S(2)}) collective-permute-start(bf16[2,3,128,768]{3,2,1,0:T(8,128)(2,1)S(1)} %slice.44), channel_id=1, source_target_pairs={{0,8},{4,12},{8,0},{12,4},{16,24},{20,28},{24,16},{28,20},{1,9},{5... | collective-permute-start | bytes 3538952 | tf_op jit(solution)/shard_map/ppermute | solution.py:452
  238.5 33.6 %collective-permute-start.33 = (bf16[3,128,768]{2,1,0:T(8,128)(2,1)}, bf16[3,128,768]{2,1,0:T(8,128)(2,1)}, u32[]{:S(2)}, u32[]{:S(2)}) collective-permute-start(bf16[3,128,768]{2,1,0:T(8,128)(2,1)} %fusion.4), channel_id=1, source_target_pairs={{0,16},{4,20},{8,24},{12,28},{16,0},{20,4},{24,8},{28,12},{1,17},{... | collective-permute-start | bytes 1769480 | tf_op jit(solution)/shard_map/ppermute | solution.py:452
  241.7 31.6 %collective-permute-start.34 = (bf16[3,128,768]{2,1,0:T(8,128)(2,1)S(1)}, bf16[3,128,768]{2,1,0:T(8,128)(2,1)S(1)}, u32[]{:S(2)}, u32[]{:S(2)}) collective-permute-start(bf16[3,128,768]{2,1,0:T(8,128)(2,1)S(1)} %fusion.5), channel_id=1, source_target_pairs={{0,8},{4,12},{8,0},{12,4},{16,24},{20,28},{24,16},{28,20},{1,9},{5... | collective-permute-start | bytes 1769480 | tf_op jit(solution)/shard_map/ppermute | solution.py:452
  242.3 22.7 %collective-permute-start.23 = (bf16[64,2048]{1,0:T(8,128)(2,1)S(1)}, bf16[64,2048]{1,0:T(8,128)(2,1)}, u32[]{:S(2)}, u32[]{:S(2)}) collective-permute-start(bf16[64,2048]{1,0:T(8,128)(2,1)S(1)} %copy-done.31), channel_id=1, source_target_pairs={{0,3},{1,2},{2,1},{3,0},{4,7},{5,6},{6,5},{7,4},{8,11},{9,10},{10,... | collective-permute-start | bytes 786440 | tf_op jit(solution)/shard_map/ppermute | solution.py:457
  269.7 25.1 %collective-permute-start.32 = (bf16[64,2048]{1,0:T(8,128)(2,1)}, bf16[64,2048]{1,0:T(8,128)(2,1)}, u32[]{:S(2)}, u32[]{:S(2)}) collective-permute-start(bf16[64,2048]{1,0:T(8,128)(2,1)} %get-tuple-element.140), channel_id=1, source_target_pairs={{0,3},{1,2},{2,1},{3,0},{4,7},{5,6},{6,5},{7,4},{8,11},{9,10},{10,... | collective-permute-start | bytes 786440 | tf_op jit(solution)/shard_map/ppermute | solution.py:457
  (47 other events, 575.4 us)

commit v7 on v6

--- a/solution.py
+++ b/solution.py
@@ -208,43 +208,64 @@
     )(where, ids_row, rows)
 
 
-def restore_kernel(experts, capacity, where_ref, ids_ref, *refs):
-    *parts, out_ref, pick_scr = refs
-
-    @pl.when(pl.program_id(0) == 0)
+def restore_kernel(experts, capacity, tiles, where_ref, ids_ref, *refs):
+    *parts, layer_ref, grad_ref, pick_scr = refs
+    step = pl.program_id(0)
+
+    @pl.when(step == 0)
     def _():
         slots = shifted_slots(iota(pick_scr.shape, 1), where_ref[1], experts, capacity)
         pick_scr[...] = one_hot(slots == slots_column(ids_ref[...], capacity))
 
-    rows = jnp.concatenate([ref[...] for ref in parts], axis=0)
-    out_ref[...] = dot(pick_scr[...], rows).astype(BF16)
-
-
-def restore(where, ids_column, parts, experts, capacity):
+    def rows(early, late):
+        both = [ref[...] for pair in zip(early, late) for ref in pair]
+        return dot(pick_scr[...], jnp.concatenate(both, axis=0)).astype(BF16)
+
+    layer_a, change_a, now = [parts[i * experts : (i + 1) * experts] for i in range(3)]
+
+    @pl.when(step < tiles)
+    def _():
+        layer_ref[...] = rows(layer_a, now)
+
+    @pl.when(step >= tiles)
+    def _():
+        grad_ref[...] = rows(change_a, now)
+
+
+def restore(where, ids_column, layer_a, change_a, packed, experts, capacity):
     n = ids_column.shape[0]
-    part, width = parts[0][0].shape
+    part, width = layer_a[0].shape
     cols = min(width, 1024)
+    tiles = width // cols
+    first = lambda i: (0, jnp.minimum(i, tiles - 1))
+    second = lambda i: (0, jnp.maximum(i - tiles, 0))
+    block = lambda at: [pl.BlockSpec((part, cols), at)] * experts
     return pl.pallas_call(
-        functools.partial(restore_kernel, experts, capacity),
-        grid=(width // cols,),
-        in_specs=[smem(), whole(n, 1)]
-        + [pl.BlockSpec((part, cols), lambda i: (0, i))] * (experts * PARTS),
-        out_specs=pl.BlockSpec((n, cols), lambda i: (0, i)),
-        out_shape=jax.ShapeDtypeStruct((n, width), BF16),
+        functools.partial(restore_kernel, experts, capacity, tiles),
+        grid=(2 * tiles,),
+        in_specs=[smem(), whole(n, 1)] + block(first) + block(second) + block(lambda i: (0, i)),
+        out_specs=[pl.BlockSpec((n, cols), first), pl.BlockSpec((n, cols), second)],
+        out_shape=[jax.ShapeDtypeStruct((n, width), BF16)] * 2,
         scratch_shapes=[pltpu.VMEM((n, experts * capacity), BF16)],
         compiler_params=kernel_params(),
         cost_estimate=brief(),
         name="restore",
-    )(where, ids_column, *[parts[c][d] for d in range(experts) for c in range(PARTS)])
+    )(where, ids_column, *layer_a, *change_a, *packed)
 
 
 def expert_kernel(experts, capacity, part_index, swap, where_ref, *refs):
     att_refs, refs = refs[:experts], refs[experts:]
     grad_refs, refs = refs[:experts], refs[experts:]
+    width_of = grad_refs[0].shape[1]
     own_ref, same_hbm, other_hbm, gate_hbm, up_hbm, down_hbm = refs[:6]
     gain_ref, ids_ref, weight_ref, refs = refs[6], refs[7], refs[8], refs[9:]
-    layer_refs, refs = refs[:experts], refs[experts:]
-    change_refs, refs = refs[:experts], refs[experts:]
+    if part_index == 0:
+        layer_refs, refs = refs[:experts], refs[experts:]
+        change_refs, refs = refs[:experts], refs[experts:]
+    else:
+        packed_refs, refs = refs[:experts], refs[experts:]
+        layer_refs = [ref.at[:, :width_of] for ref in packed_refs]
+        change_refs = [ref.at[:, width_of:] for ref in packed_refs]
     saved_refs, refs = refs[: 1 + swap], refs[1 + swap :]
     w_scr, gate_scr, up_scr, down_scr, hidden_scr, normed_ref, back_ref, back_in_scr, sems = refs
     part, width = grad_refs[0].shape
@@ -362,7 +383,7 @@
 
 
 def expert_part(
-    where, att, grads, own, same, other, gate, up, down, gain, ids, weights, capacity, index, swap
+    where, att, grads, own, same, other, gate, up, down, gain, ids, weights, capacity, swap, index
 ):
     experts, part, att_cols = att[0].shape
     pieces = 2 * same.shape[0]
@@ -373,6 +394,7 @@
     n = ids.shape[2]
     half = width // 2 if swap else width
     out = lambda *shape: jax.ShapeDtypeStruct(shape, BF16)
+    rows_out = [out(part, width)] * (2 * experts) if index == 0 else [out(part, 2 * width)] * experts
     in_hbm = pl.BlockSpec(memory_space=pl.ANY)
     outs = pl.pallas_call(
         functools.partial(expert_kernel, experts, capacity, index, swap),
@@ -383,7 +405,7 @@
         + [whole(*own.shape)]
         + [in_hbm] * 5
         + [whole(1, width), whole(experts, 1, n), whole(experts, 1, n)],
-        out_specs=[whole(part, width)] * (2 * experts)
+        out_specs=[whole(*x.shape) for x in rows_out]
         + [whole(rows, 3 * ff + 2 * half)] * (1 + swap),
         scratch_shapes=[
             pltpu.VMEM((pieces, experts - 1, att_cols, piece), BF16),
@@ -396,13 +418,13 @@
             pltpu.VMEM((rows, width), BF16),
             pltpu.SemaphoreType.DMA((pieces + 3,)),
         ],
-        out_shape=[out(part, width)] * (2 * experts)
+        out_shape=rows_out
         + [out(rows, 3 * ff + 2 * half)] * (1 + swap),
         compiler_params=kernel_params(),
         cost_estimate=brief(),
         name="expert",
     )(where, *att, *grads, own, same, other, gate, up, down, gain, ids, weights)
-    return outs[:experts], outs[experts : 2 * experts], outs[2 * experts :]
+    return outs[: len(rows_out)], outs[len(rows_out) :]
 
 
 def weight_kernel(count, *refs):
@@ -530,11 +552,10 @@
     values = lax.dynamic_slice_in_dim(value_head_rows, first_column, HEAD_SIZE, 2)
     own = jnp.concatenate([keys, values], axis=2)
     chips = [own] + [partner(own, m) for m in range(2, ctx_count, 2)]
+    key_values = chips + [partner(jnp.stack(chips), 1)]
 
     grads = place(where, ids_f.reshape(1, n), grad_out, experts, capacity)
-    grads = to_owners(grads)
-
-    key_values = chips + [partner(after(jnp.stack(chips), grads[1]), 1)]
+    grads = to_owners(after(grads, projection))
 
     projection = after(jnp.stack(projection), chips)
     projection = jnp.broadcast_to(projection[None], (pieces // 2,) + projection.shape)
@@ -543,16 +564,16 @@
     )
 
     sent = attend(where, queries, key_values, ids_all, capacity)
-    arrived = to_owners(after(sent[0], grads))
-    later = after(sent[1], arrived[1], same)
-    same = after(same, sent[0], grads[2:])
+    arrived = to_owners(after(sent[0], grads[2:]))
+    later = after(sent[1], arrived, same)
+    same = after(same, sent[0], grads[1:])
     other = partner(same, 1)
 
     rows_dev = width // ctx_count
     ff = expert_gate.shape[2]
     swap = rows_dev == PIECE
 
-    def run(index, arrived):
+    def run(arrived, index):
         return expert_part(
             where,
             arrived,
@@ -567,36 +588,33 @@
             ids_all,
             weights_all,
             capacity,
+            swap,
             index,
-            swap,
         )
 
-    layer_a, change_a, saved_a = run(0, arrived)
-    layer_a = to_owners(layer_a)
-    layer_b, change_b, saved_b = run(1, to_owners(later))
+    rows_a, saved_a = run(arrived, 0)
+    layer_a = to_owners(rows_a[:experts])
+    change_a = to_owners(after(rows_a[experts:], layer_a[1]))
+    rows_b, saved_b = run(to_owners(later), 1)
+    packed = to_owners(rows_b)
     if swap:
         saved = [saved_a[0], partner(saved_a[1], 1)]
         saved += [saved_b[0], partner(after(saved_b[1], layer_a), 1)]
-        change_a = to_owners(after(change_a, layer_a[1]))
         parts = weight_blocks(saved, ctx_count // 2, ff, True)
         parts = after(parts, change_a)
         half = ctx_count // 4
         masks = (2, 4), (4, 2)
         near = [partner(x[half:], m[0]) for x, m in zip(parts, masks)]
-        layer_b = to_owners(after(layer_b, change_a[1]))
-        near = after(near, layer_b[1])
         sums = [x[:half].astype(F32) + y.astype(F32) for x, y in zip(parts, near)]
         gone = [x[1].astype(BF16) for x in sums]
-        change_b = after(change_b, gone)
         far = [partner(x, m[1]) for x, m in zip(gone, masks)]
+        packed = after(packed, gone)
         total = [x[0] + y.astype(F32) for x, y in zip(sums, far)]
         total = jnp.concatenate(total, axis=1)
         grad_gate, grad_up = total[0][None], total[1][None]
         grad_down = total[2].reshape(PIECE, ff // PIECE, PIECE).transpose(1, 0, 2)
         grad_down = grad_down.reshape(1, ff, PIECE)
     else:
-        change_a = to_owners(after(change_a, layer_a[1]))
-        layer_b = to_owners(after(layer_b, change_a[1]))
         blocks = width // PIECE
         (parts,) = weight_blocks(list(saved_a) + list(saved_b), blocks, ff, False)
         part_down = parts[:, 2].reshape(blocks, PIECE, ff // PIECE, PIECE).transpose(0, 2, 1, 3)
@@ -611,10 +629,7 @@
                 (part_down, (ff, rows_dev)),
             )
         ]
-    change_b = to_owners(after(change_b, layer_b[1:2]))
-    layer_out = restore(where, ids_f, [layer_a, layer_b], experts, capacity)
-    change_b = after(change_b, layer_out, grad_gate, grad_up, grad_down)
-    grad_hidden = restore(where, ids_f, [change_a, change_b], experts, capacity)
+    layer_out, grad_hidden = restore(where, ids_f, layer_a, change_a, packed, experts, capacity)
     return (layer_out, grad_hidden, grad_gate, grad_up, grad_down)
 
 

time: 300 us -> 263 us (0.88)
  waiting for transfers between devices: 145 us -> 112 us
  starting transfers between devices: 45.1 us -> 41.1 us
    ppermute x24 -> x21, waiting for transfers between devices: 119 us -> 88 us  [to_owner(): return lax.ppermute(value, 'exp', [(i, i ^ mask) for i in range(count)])]
    all_to_all x1, waiting for transfers between devices: 6.09 us -> 0.01 us  [on_device(): info = lax.all_to_all(info, 'exp', 0, 0, tiled=True)]
    ppermute x11, waiting for transfers between devices: 19.5 us -> 24.2 us  [partner(): return lax.ppermute(value, 'ctx', [(i, i ^ mask) for i in range(count)])]
    ppermute x24 -> x21, starting transfers between devices: 30.3 us -> 25.9 us  [to_owner(): return lax.ppermute(value, 'exp', [(i, i ^ mask) for i in range(count)])]
    unnamed x69 -> x57, local copies, waits for them, and re-layouts: 7.47 us -> 5.33 us
    pallas_call x2 -> x1, Pallas kernels: 7.11 us -> 5.96 us  [restore(): pl.pallas_call(functools.partial(restore_kernel, experts, capacity, tiles...]
  transfers between devices with their start and end apart: 37 -> 34, of which waited for: 19 -> 14; matrix products, arithmetic and copies ran while one was open for 5% -> 5% of each run, Pallas kernels for 26% -> 31%
where the time goes in v7:
time: 263 us; the launch traced here: 259 us
  waiting for transfers between devices  112 us (43%)
  Pallas kernels  80.3 us (31%)
  starting transfers between devices  41.1 us (16%)
  local copies, waits for them, and re-layouts  14.6 us (6%)
  other arithmetic  9.74 us (4%)
    ppermute x21, waiting for transfers between devices, to_owner(): return lax.ppermute(value, 'exp', [(i, i ^ mask) for i in range(count)])  88 us
    pallas_call x2, Pallas kernels, expert_part(): pl.pallas_call(functools.partial(expert_kernel, experts, capacity, index,...  35.7 us
    ppermute x21, starting transfers between devices, to_owner(): return lax.ppermute(value, 'exp', [(i, i ^ mask) for i in range(count)])  25.9 us
    pallas_call x1, Pallas kernels, attend(): pl.pallas_call(functools.partial(attend_kernel, experts, capacity, heads,...  25.5 us
    ppermute x11, waiting for transfers between devices, partner(): return lax.ppermute(value, 'ctx', [(i, i ^ mask) for i in range(count)])  24.2 us
    pallas_call x1, Pallas kernels, weight_blocks(): pl.pallas_call(functools.partial(weight_kernel, count), grid=(blocks,), i...  10 us
    pallas_call x1, Pallas kernels, restore(): pl.pallas_call(functools.partial(restore_kernel, experts, capacity, tiles...  5.96 us
    all_to_all x1, starting transfers between devices, on_device(): info = lax.all_to_all(info, 'exp', 0, 0, tiled=True)  5.65 us
  transfers between devices with their start and end apart: 34, of which 14 were waited for; matrix products, arithmetic and copies ran while one was open for 5% of the time, Pallas kernels for 31%

profile of v7, /device:TPU:22, one launch (start us, length us, event | category | flops | bytes accessed | tf_op | source)
XLA Modules:
  0.0 259.0 jit_solution(1294600496177829199)
XLA Ops:
  7.6 3.5 %collective-permute-start.5 = (bf16[512,256]{1,0:T(8,128)(2,1)S(1)}, bf16[512,256]{1,0:T(8,128)(2,1)S(1)}, u32[]{:S(2)}, u32[]{:S(2)}) collective-permute-start(bf16[512,256]{1,0:T(8,128)(2,1)S(1)} %constant_dynamic-slice_fusion), channel_id=1, source_target_pairs={{0,2},{1,3},{2,0},{3,1},{4,6},{5,7},{6,4},{7,5},{8,10},{9,11},{10,... | collective-permute-start | bytes 786440 | tf_op jit(solution)/shard_map/ppermute | solution.py:479
  11.1 11.1 %collective-permute-done.6 = bf16[512,256]{1,0:T(8,128)(2,1)S(1)} collective-permute-done((bf16[512,256]{1,0:T(8,128)(2,1)S(1)}, bf16[512,256]{1,0:T(8,128)(2,1)S(1)}, u32[]{:S(2)}, u32[]{:S(2)}) %collective-permute-start.6) | collective-permute-done | bytes 262176 | tf_op jit(solution)/shard_map/ppermute | solution.py:479
  23.0 5.7 %all-to-all-start = ((f32[4,2,256]{2,1,0:T(2,128)}), f32[4,2,256]{2,1,0:T(2,128)S(1)}, u32[]{:S(2)}, u32[]{:S(2)}) async-start(f32[4,2,256]{2,1,0:T(2,128)} %broadcast_in_dim.4), calls=%async_computation | async-start | bytes 16384 | tf_op jit(solution)/shard_map/all_to_all | solution.py:544
  34.9 4.2 %all-to-all-start.1 = ((bf16[4,3,512,256]{3,2,1,0:T(8,128)(2,1)}), bf16[4,3,512,256]{3,2,1,0:T(8,128)(2,1)S(1)}, u32[]{:S(2)}, u32[]{:S(2)}) async-start(bf16[4,3,512,256]{3,2,1,0:T(8,128)(2,1)} %broadcast_in_dim.5), calls=%async_computation.1 | async-start | bytes 6291456 | tf_op jit(solution)/shard_map/all_to_all | solution.py:562
  39.1 3.1 %pad_maximum_fusion = bf16[4,4,256,256]{3,2,1,0:T(8,128)(2,1)} fusion(bf16[1,4,256,256]{3,2,1,0:T(8,128)(2,1)} %bitcast.31, bf16[1,4,256,256]{3,2,1,0:T(8,128)(2,1)} %bitcast.32, bf16[1,4,256,256]{3,2,1,0:T(8,128)(2,1)} %bitcast.33, bf16[1,4,256,256]{3,2,1,0:T(8,128)(2,1)} %get-tuple-element.122), kind=kLoop, calls=%fused_computation.6 | loop fusion | flops 3145728 | bytes 4194304 | tf_op jit(solution)/shard_map/stack | solution.py:555
  42.9 3.1 %place.1 = (bf16[128,2048]{1,0:T(8,128)(2,1)}, bf16[128,2048]{1,0:T(8,128)(2,1)}, bf16[128,2048]{1,0:T(8,128)(2,1)}, bf16[128,2048]{1,0:T(8,128)(2,1)}) custom-call(s32[3]{0:T(128)} %pad_add_fusion.where_ref, f32[1,256]{1,0:T(1,128)} %bitcast.41, bf16[256,2048]{1,0:T(8,128)(2,1)} %rows_ref.1), custom_call_target="tpu_custom_call" | custom-call | flops 1000 | bytes 1000 | tf_op jit(solution)/shard_map/place/pallas_call | solution.py:198
  51.0 25.5 %attend.1 = (bf16[4,64,512]{2,1,0:T(8,128)(2,1)}, bf16[4,64,512]{2,1,0:T(8,128)(2,1)}, bf16[4,64,512]{2,1,0:T(8,128)(2,1)}, bf16[4,64,512]{2,1,0:T(8,128)(2,1)},...) custom-call(s32[3]{0:T(128)} %pad_add_fusion.where_ref, ...), custom_call_target="tpu_custom_call" | custom-call | flops 1000 | bytes 1000 | tf_op jit(solution)/shard_map/attend/pallas_call | solution.py:155
  76.5 6.4 %collective-permute-done.7.refs_6_ = bf16[128,2048]{1,0:T(8,128)(2,1)S(1)} collective-permute-done((bf16[128,2048]{1,0:T(8,128)(2,1)}, bf16[128,2048]{1,0:T(8,128)(2,1)S(1)}, u32[]{:S(2)}, u32[]{:S(2)}) %collective-permute-start.7) | collective-permute-done | bytes 524320 | tf_op jit(solution)/shard_map/ppermute | solution.py:479
  82.9 12.4 %collective-permute-done.8.refs_7_ = bf16[128,2048]{1,0:T(8,128)(2,1)} collective-permute-done((bf16[128,2048]{1,0:T(8,128)(2,1)}, bf16[128,2048]{1,0:T(8,128)(2,1)}, u32[]{:S(2)}, u32[]{:S(2)}) %collective-permute-start.8) | collective-permute-done | bytes 524320 | tf_op jit(solution)/shard_map/ppermute | solution.py:479
  98.9 8.3 %collective-permute-done.9.refs_1_ = bf16[4,64,512]{2,1,0:T(8,128)(2,1)S(1)} collective-permute-done((bf16[4,64,512]{2,1,0:T(8,128)(2,1)}, bf16[4,64,512]{2,1,0:T(8,128)(2,1)S(1)}, u32[]{:S(2)}, u32[]{:S(2)}) %collective-permute-start.9) | collective-permute-done | bytes 262176 | tf_op jit(solution)/shard_map/ppermute | solution.py:479
  107.2 9.2 %collective-permute-done.10.refs_2_ = bf16[4,64,512]{2,1,0:T(8,128)(2,1)S(1)} collective-permute-done((bf16[4,64,512]{2,1,0:T(8,128)(2,1)}, bf16[4,64,512]{2,1,0:T(8,128)(2,1)S(1)}, u32[]{:S(2)}, u32[]{:S(2)}) %collective-permute-start.10) | collective-permute-done | bytes 262176 | tf_op jit(solution)/shard_map/ppermute | solution.py:479
  116.5 5.9 %collective-permute-done.11.refs_3_ = bf16[4,64,512]{2,1,0:T(8,128)(2,1)S(1)} collective-permute-done((bf16[4,64,512]{2,1,0:T(8,128)(2,1)}, bf16[4,64,512]{2,1,0:T(8,128)(2,1)S(1)}, u32[]{:S(2)}, u32[]{:S(2)}) %collective-permute-start.11) | collective-permute-done | bytes 262176 | tf_op jit(solution)/shard_map/ppermute | solution.py:479
  122.4 2.8 %collective-permute-start.21 = (bf16[4,64,512]{2,1,0:T(8,128)(2,1)}, bf16[4,64,512]{2,1,0:T(8,128)(2,1)S(1)}, u32[]{:S(2)}, u32[]{:S(2)}) collective-permute-start(bf16[4,64,512]{2,1,0:T(8,128)(2,1)} %get-tuple-element.98), channel_id=1, source_target_pairs={{0,2},{1,3},{2,0},{3,1},{4,6},{5,7},{6,4},{7,5},{8,10},{9,11},{10,... | collective-permute-start | bytes 786440 | tf_op jit(solution)/shard_map/ppermute | solution.py:479
  127.6 17.7 %expert.2 = (bf16[64,2048]{1,0:T(8,128)(2,1)}, bf16[64,2048]{1,0:T(8,128)(2,1)}, bf16[64,2048]{1,0:T(8,128)(2,1)}, bf16[64,2048]{1,0:T(8,128)(2,1)}, bf16[64,204...) custom-call(s32[3]{0:T(128)} %pad_add_fusion.where_ref, ...), custom_call_target="tpu_custom_call" | custom-call | flops 1000 | bytes 1000 | tf_op jit(solution)/shard_map/expert/pallas_call | solution.py:399
  149.5 18.0 %expert.3 = (bf16[64,4096]{1,0:T(8,128)(2,1)}, bf16[64,4096]{1,0:T(8,128)(2,1)}, bf16[64,4096]{1,0:T(8,128)(2,1)}, bf16[64,4096]{1,0:T(8,128)(2,1)}, bf16[256,43...) custom-call(s32[3]{0:T(128)} %pad_add_fusion.where_ref, bf16[4,64,512]{2,1,0:T(8,128)(2,1)} %get-tuple-element.96.refs_0_, ...), custom_call_target="tpu_custom_call" | custom-call | flops 1000 | bytes 1000 | tf_op jit(solution)/shard_map/expert/pallas_call | solution.py:399
  167.6 3.1 %collective-permute-done.16.refs_3_ = bf16[64,2048]{1,0:T(8,128)(2,1)S(1)} collective-permute-done((bf16[64,2048]{1,0:T(8,128)(2,1)}, bf16[64,2048]{1,0:T(8,128)(2,1)S(1)}, u32[]{:S(2)}, u32[]{:S(2)}) %collective-permute-start.16) | collective-permute-done | bytes 262176 | tf_op jit(solution)/shard_map/ppermute | solution.py:479
  170.8 2.8 %collective-permute-start.18 = (bf16[64,2048]{1,0:T(8,128)(2,1)}, bf16[64,2048]{1,0:T(8,128)(2,1)S(1)}, u32[]{:S(2)}, u32[]{:S(2)}) collective-permute-start(bf16[64,2048]{1,0:T(8,128)(2,1)} %get-tuple-element.90), channel_id=1, source_target_pairs={{0,2},{1,3},{2,0},{3,1},{4,6},{5,7},{6,4},{7,5},{8,10},{9,11},{10,... | collective-permute-start | bytes 786440 | tf_op jit(solution)/shard_map/ppermute | solution.py:479
  175.6 10.0 %weight_grads.1 = (bf16[4,3,128,768]{3,2,1,0:T(8,128)(2,1)}, bf16[4,3,128,768]{3,2,1,0:T(8,128)(2,1)}) custom-call(bf16[256,4352]{1,0:T(8,128)(2,1)} %get-tuple-element.104.refs_0_.refs_4_.refs_8_.refs_12_.refs_16_, bf16[256,4352]{1,0:T(8,128)(2,1)} %copy-done, bf16[256,4352]{1,0:T(8,128)(2,1)} %get-tuple-element.106.refs_2_.refs_6_.refs_10_.refs_14_.refs_18_, ...), custom_call_target="tpu_custom_call" | custom-call | flops 1000 | bytes 1000 | tf_op jit(solution)/shard_map/weight_grads/pallas_call | solution.py:460
  185.7 6.1 %collective-permute-done.18.refs_6_ = bf16[64,2048]{1,0:T(8,128)(2,1)S(1)} collective-permute-done((bf16[64,2048]{1,0:T(8,128)(2,1)}, bf16[64,2048]{1,0:T(8,128)(2,1)S(1)}, u32[]{:S(2)}, u32[]{:S(2)}) %collective-permute-start.18) | collective-permute-done | bytes 262176 | tf_op jit(solution)/shard_map/ppermute | solution.py:479
  191.8 6.0 %collective-permute-done.19.refs_7_ = bf16[64,2048]{1,0:T(8,128)(2,1)S(1)} collective-permute-done((bf16[64,2048]{1,0:T(8,128)(2,1)}, bf16[64,2048]{1,0:T(8,128)(2,1)S(1)}, u32[]{:S(2)}, u32[]{:S(2)}) %collective-permute-start.19) | collective-permute-done | bytes 262176 | tf_op jit(solution)/shard_map/ppermute | solution.py:479
  203.6 23.0 %collective-permute-done.29 = bf16[2,3,128,768]{3,2,1,0:T(8,128)(2,1)S(1)} collective-permute-done((bf16[2,3,128,768]{3,2,1,0:T(8,128)(2,1)S(1)}, bf16[2,3,128,768]{3,2,1,0:T(8,128)(2,1)S(1)}, u32[]{:S(2)}, u32[]{:S(2)}) %collective-permute-start.29) | collective-permute-done | bytes 1179680 | tf_op jit(solution)/shard_map/ppermute | solution.py:474
  231.1 7.0 %collective-permute-done.24.refs_10_ = bf16[64,4096]{1,0:T(8,128)(2,1)} collective-permute-done((bf16[64,4096]{1,0:T(8,128)(2,1)}, bf16[64,4096]{1,0:T(8,128)(2,1)}, u32[]{:S(2)}, u32[]{:S(2)}) %collective-permute-start.24) | collective-permute-done | bytes 524320 | tf_op jit(solution)/shard_map/ppermute | solution.py:479
  238.1 10.3 %collective-permute-done.25.refs_11_ = bf16[64,4096]{1,0:T(8,128)(2,1)} collective-permute-done((bf16[64,4096]{1,0:T(8,128)(2,1)}, bf16[64,4096]{1,0:T(8,128)(2,1)}, u32[]{:S(2)}, u32[]{:S(2)}) %collective-permute-start.25) | collective-permute-done | bytes 524320 | tf_op jit(solution)/shard_map/ppermute | solution.py:479
  248.3 6.0 %restore.1 = (bf16[256,2048]{1,0:T(8,128)(2,1)}, bf16[256,2048]{1,0:T(8,128)(2,1)}) custom-call(s32[3]{0:T(128)} %pad_add_fusion.where_ref, f32[256,1]{1,0:T(8,128)} %convert_element_type.29.ids_ref, bf16[64,2048]{1,0:T(8,128)(2,1)} %get-tuple-element.80.refs_0_, bf16[64,2048]{1,0:T(8,128)(2,1)} %copy-done.12, bf16[64,2048]{1,0:T(8,128)(2,1)} %copy-done.13, ...), custom_call_target="tpu_custom_call" | custom-call | flops 1000 | bytes 1000 | tf_op jit(solution)/shard_map/restore/pallas_call | solution.py:243
  (130 shorter events, 46.8 us)
Async XLA Ops:
  4.1 28.7 %collective-permute-start.2 = (bf16[4,256,256]{2,1,0:T(8,128)(2,1)S(1)}, bf16[4,256,256]{2,1,0:T(8,128)(2,1)S(1)}, u32[]{:S(2)}, u32[]{:S(2)}) collective-permute-start(bf16[4,256,256]{2,1,0:T(8,128)(2,1)S(1)} %get-tuple-element.123.refs_0_), channel_id=1, source_target_pairs={{0,24},{4,28},{8,16},{12,20},{16,8},{20,12},{24,0},{28,4},{1,25},{... | collective-permute-start | bytes 1572872 | tf_op jit(solution)/shard_map/ppermute | solution.py:474
  4.6 28.2 %collective-permute-start.1 = (bf16[4,256,256]{2,1,0:T(8,128)(2,1)S(1)}, bf16[4,256,256]{2,1,0:T(8,128)(2,1)S(1)}, u32[]{:S(2)}, u32[]{:S(2)}) collective-permute-start(bf16[4,256,256]{2,1,0:T(8,128)(2,1)S(1)} %get-tuple-element.123.refs_0_), channel_id=1, source_target_pairs={{0,16},{4,20},{8,24},{12,28},{16,0},{20,4},{24,8},{28,12},{1,17},{... | collective-permute-start | bytes 1572872 | tf_op jit(solution)/shard_map/ppermute | solution.py:474
  6.1 26.7 %collective-permute-start = (bf16[4,256,256]{2,1,0:T(8,128)(2,1)S(1)}, bf16[4,256,256]{2,1,0:T(8,128)(2,1)S(1)}, u32[]{:S(2)}, u32[]{:S(2)}) collective-permute-start(bf16[4,256,256]{2,1,0:T(8,128)(2,1)S(1)} %get-tuple-element.123.refs_0_), channel_id=1, source_target_pairs={{0,8},{4,12},{8,0},{12,4},{16,24},{20,28},{24,16},{28,20},{1,9},{5... | collective-permute-start | bytes 1572872 | tf_op jit(solution)/shard_map/ppermute | solution.py:474
  34.9 60.4 %all-to-all-start.1 = ((bf16[4,3,512,256]{3,2,1,0:T(8,128)(2,1)}), bf16[4,3,512,256]{3,2,1,0:T(8,128)(2,1)S(1)}, u32[]{:S(2)}, u32[]{:S(2)}) async-start(bf16[4,3,512,256]{3,2,1,0:T(8,128)(2,1)} %broadcast_in_dim.5), calls=%async_computation.1 | async-start | bytes 6291456 | tf_op jit(solution)/shard_map/all_to_all | solution.py:562
  46.0 36.9 %collective-permute-start.7 = (bf16[128,2048]{1,0:T(8,128)(2,1)}, bf16[128,2048]{1,0:T(8,128)(2,1)S(1)}, u32[]{:S(2)}, u32[]{:S(2)}) collective-permute-start(bf16[128,2048]{1,0:T(8,128)(2,1)} %get-tuple-element.70), channel_id=1, source_target_pairs={{0,2},{1,3},{2,0},{3,1},{4,6},{5,7},{6,4},{7,5},{8,10},{9,11},{10,... | collective-permute-start | bytes 1572872 | tf_op jit(solution)/shard_map/ppermute | solution.py:479
  48.5 46.8 %collective-permute-start.8 = (bf16[128,2048]{1,0:T(8,128)(2,1)}, bf16[128,2048]{1,0:T(8,128)(2,1)}, u32[]{:S(2)}, u32[]{:S(2)}) collective-permute-start(bf16[128,2048]{1,0:T(8,128)(2,1)} %get-tuple-element.71), channel_id=1, source_target_pairs={{0,3},{1,2},{2,1},{3,0},{4,7},{5,6},{6,5},{7,4},{8,11},{9,10},{10,... | collective-permute-start | bytes 1572872 | tf_op jit(solution)/shard_map/ppermute | solution.py:479
  49.9 45.4 %collective-permute-start.12 = (bf16[128,2048]{1,0:T(8,128)(2,1)}, bf16[128,2048]{1,0:T(8,128)(2,1)}, u32[]{:S(2)}, u32[]{:S(2)}) collective-permute-start(bf16[128,2048]{1,0:T(8,128)(2,1)} %get-tuple-element.77), channel_id=1, source_target_pairs={{0,1},{1,0},{2,3},{3,2},{4,5},{5,4},{6,7},{7,6},{8,9},{9,8},{10,11... | collective-permute-start | bytes 1572872 | tf_op jit(solution)/shard_map/ppermute | solution.py:479
  95.3 30.6 %collective-permute-start.13 = (bf16[4,3,512,256]{3,2,1,0:T(8,128)(2,1)S(1)}, bf16[4,3,512,256]{3,2,1,0:T(8,128)(2,1)S(1)}, u32[]{:S(2)}, u32[]{:S(2)}) collective-permute-start(bf16[4,3,512,256]{3,2,1,0:T(8,128)(2,1)S(1)} %all-to-all-done.1.refs_9_), channel_id=1, source_target_pairs={{0,4},{4,0},{8,12},{12,8},{16,20},{20,16},{24,28},{28,24},{1,5},{5... | collective-permute-start | bytes 9437192 | tf_op jit(solution)/shard_map/ppermute | solution.py:474
  98.2 24.2 %collective-permute-start.11 = (bf16[4,64,512]{2,1,0:T(8,128)(2,1)}, bf16[4,64,512]{2,1,0:T(8,128)(2,1)S(1)}, u32[]{:S(2)}, u32[]{:S(2)}) collective-permute-start(bf16[4,64,512]{2,1,0:T(8,128)(2,1)} %get-tuple-element.75), channel_id=1, source_target_pairs={{0,3},{1,2},{2,1},{3,0},{4,7},{5,6},{6,5},{7,4},{8,11},{9,10},{10,... | collective-permute-start | bytes 786440 | tf_op jit(solution)/shard_map/ppermute | solution.py:479
  122.4 25.7 %collective-permute-start.20 = (bf16[4,64,512]{2,1,0:T(8,128)(2,1)}, bf16[4,64,512]{2,1,0:T(8,128)(2,1)S(1)}, u32[]{:S(2)}, u32[]{:S(2)}) collective-permute-start(bf16[4,64,512]{2,1,0:T(8,128)(2,1)} %get-tuple-element.97), channel_id=1, source_target_pairs={{0,1},{1,0},{2,3},{3,2},{4,5},{5,4},{6,7},{7,6},{8,9},{9,8},{10,11... | collective-permute-start | bytes 786440 | tf_op jit(solution)/shard_map/ppermute | solution.py:479
  122.4 26.5 %collective-permute-start.21 = (bf16[4,64,512]{2,1,0:T(8,128)(2,1)}, bf16[4,64,512]{2,1,0:T(8,128)(2,1)S(1)}, u32[]{:S(2)}, u32[]{:S(2)}) collective-permute-start(bf16[4,64,512]{2,1,0:T(8,128)(2,1)} %get-tuple-element.98), channel_id=1, source_target_pairs={{0,2},{1,3},{2,0},{3,1},{4,6},{5,7},{6,4},{7,5},{8,10},{9,11},{10,... | collective-permute-start | bytes 786440 | tf_op jit(solution)/shard_map/ppermute | solution.py:479
  125.2 24.4 %collective-permute-start.22 = (bf16[4,64,512]{2,1,0:T(8,128)(2,1)}, bf16[4,64,512]{2,1,0:T(8,128)(2,1)}, u32[]{:S(2)}, u32[]{:S(2)}) collective-permute-start(bf16[4,64,512]{2,1,0:T(8,128)(2,1)} %get-tuple-element.99), channel_id=1, source_target_pairs={{0,3},{1,2},{2,1},{3,0},{4,7},{5,6},{6,5},{7,4},{8,11},{9,10},{10,... | collective-permute-start | bytes 786440 | tf_op jit(solution)/shard_map/ppermute | solution.py:479
  145.3 22.3 %collective-permute-start.14 = (bf16[64,2048]{1,0:T(8,128)(2,1)}, bf16[64,2048]{1,0:T(8,128)(2,1)S(1)}, u32[]{:S(2)}, u32[]{:S(2)}) collective-permute-start(bf16[64,2048]{1,0:T(8,128)(2,1)} %get-tuple-element.81), channel_id=1, source_target_pairs={{0,1},{1,0},{2,3},{3,2},{4,5},{5,4},{6,7},{7,6},{8,9},{9,8},{10,11... | collective-permute-start | bytes 786440 | tf_op jit(solution)/shard_map/ppermute | solution.py:479
  146.3 21.3 %collective-permute-start.15 = (bf16[64,2048]{1,0:T(8,128)(2,1)}, bf16[64,2048]{1,0:T(8,128)(2,1)S(1)}, u32[]{:S(2)}, u32[]{:S(2)}) collective-permute-start(bf16[64,2048]{1,0:T(8,128)(2,1)} %get-tuple-element.82), channel_id=1, source_target_pairs={{0,2},{1,3},{2,0},{3,1},{4,6},{5,7},{6,4},{7,5},{8,10},{9,11},{10,... | collective-permute-start | bytes 786440 | tf_op jit(solution)/shard_map/ppermute | solution.py:479
  148.1 22.6 %collective-permute-start.16 = (bf16[64,2048]{1,0:T(8,128)(2,1)}, bf16[64,2048]{1,0:T(8,128)(2,1)S(1)}, u32[]{:S(2)}, u32[]{:S(2)}) collective-permute-start(bf16[64,2048]{1,0:T(8,128)(2,1)} %get-tuple-element.83), channel_id=1, source_target_pairs={{0,3},{1,2},{2,1},{3,0},{4,7},{5,6},{6,5},{7,4},{8,11},{9,10},{10,... | collective-permute-start | bytes 786440 | tf_op jit(solution)/shard_map/ppermute | solution.py:479
  149.5 24.7 %collective-permute-start.26 = (bf16[256,4352]{1,0:T(8,128)(2,1)}, bf16[256,4352]{1,0:T(8,128)(2,1)S(1)}, u32[]{:S(2)}, u32[]{:S(2)}) collective-permute-start(bf16[256,4352]{1,0:T(8,128)(2,1)} %get-tuple-element.105), channel_id=1, source_target_pairs={{0,4},{4,0},{8,12},{12,8},{16,20},{20,16},{24,28},{28,24},{1,5},{5... | collective-permute-start | bytes 6684680 | tf_op jit(solution)/shard_map/ppermute | solution.py:474
  173.5 24.2 %collective-permute-start.19 = (bf16[64,2048]{1,0:T(8,128)(2,1)}, bf16[64,2048]{1,0:T(8,128)(2,1)S(1)}, u32[]{:S(2)}, u32[]{:S(2)}) collective-permute-start(bf16[64,2048]{1,0:T(8,128)(2,1)} %get-tuple-element.91), channel_id=1, source_target_pairs={{0,3},{1,2},{2,1},{3,0},{4,7},{5,6},{6,5},{7,4},{8,11},{9,10},{10,... | collective-permute-start | bytes 786440 | tf_op jit(solution)/shard_map/ppermute | solution.py:479
  199.3 27.3 %collective-permute-start.29 = (bf16[2,3,128,768]{3,2,1,0:T(8,128)(2,1)S(1)}, bf16[2,3,128,768]{3,2,1,0:T(8,128)(2,1)S(1)}, u32[]{:S(2)}, u32[]{:S(2)}) collective-permute-start(bf16[2,3,128,768]{3,2,1,0:T(8,128)(2,1)S(1)} %slice.47), channel_id=1, source_target_pairs={{0,16},{4,20},{8,24},{12,28},{16,0},{20,4},{24,8},{28,12},{1,17},{... | collective-permute-start | bytes 3538952 | tf_op jit(solution)/shard_map/ppermute | solution.py:474
  200.0 28.3 %collective-permute-start.28 = (bf16[2,3,128,768]{3,2,1,0:T(8,128)(2,1)S(1)}, bf16[2,3,128,768]{3,2,1,0:T(8,128)(2,1)S(1)}, u32[]{:S(2)}, u32[]{:S(2)}) collective-permute-start(bf16[2,3,128,768]{3,2,1,0:T(8,128)(2,1)S(1)} %slice.44), channel_id=1, source_target_pairs={{0,8},{4,12},{8,0},{12,4},{16,24},{20,28},{24,16},{28,20},{1,9},{5... | collective-permute-start | bytes 3538952 | tf_op jit(solution)/shard_map/ppermute | solution.py:474
  200.1 31.0 %collective-permute-start.23 = (bf16[64,4096]{1,0:T(8,128)(2,1)}, bf16[64,4096]{1,0:T(8,128)(2,1)}, u32[]{:S(2)}, u32[]{:S(2)}) collective-permute-start(bf16[64,4096]{1,0:T(8,128)(2,1)} %get-tuple-element.101), channel_id=1, source_target_pairs={{0,1},{1,0},{2,3},{3,2},{4,5},{5,4},{6,7},{7,6},{8,9},{9,8},{10,11... | collective-permute-start | bytes 1572872 | tf_op jit(solution)/shard_map/ppermute | solution.py:479
  200.2 37.9 %collective-permute-start.24 = (bf16[64,4096]{1,0:T(8,128)(2,1)}, bf16[64,4096]{1,0:T(8,128)(2,1)}, u32[]{:S(2)}, u32[]{:S(2)}) collective-permute-start(bf16[64,4096]{1,0:T(8,128)(2,1)} %get-tuple-element.102), channel_id=1, source_target_pairs={{0,2},{1,3},{2,0},{3,1},{4,6},{5,7},{6,4},{7,5},{8,10},{9,11},{10,... | collective-permute-start | bytes 1572872 | tf_op jit(solution)/shard_map/ppermute | solution.py:479
  202.9 45.4 %collective-permute-start.25 = (bf16[64,4096]{1,0:T(8,128)(2,1)}, bf16[64,4096]{1,0:T(8,128)(2,1)}, u32[]{:S(2)}, u32[]{:S(2)}) collective-permute-start(bf16[64,4096]{1,0:T(8,128)(2,1)} %get-tuple-element.103), channel_id=1, source_target_pairs={{0,3},{1,2},{2,1},{3,0},{4,7},{5,6},{6,5},{7,4},{8,11},{9,10},{10,... | collective-permute-start | bytes 1572872 | tf_op jit(solution)/shard_map/ppermute | solution.py:479
  227.8 26.6 %collective-permute-start.31 = (bf16[3,128,768]{2,1,0:T(8,128)(2,1)}, bf16[3,128,768]{2,1,0:T(8,128)(2,1)}, u32[]{:S(2)}, u32[]{:S(2)}) collective-permute-start(bf16[3,128,768]{2,1,0:T(8,128)(2,1)} %fusion.5), channel_id=1, source_target_pairs={{0,8},{4,12},{8,0},{12,4},{16,24},{20,28},{24,16},{28,20},{1,9},{5... | collective-permute-start | bytes 1769480 | tf_op jit(solution)/shard_map/ppermute | solution.py:474
  230.1 25.6 %collective-permute-start.30 = (bf16[3,128,768]{2,1,0:T(8,128)(2,1)S(1)}, bf16[3,128,768]{2,1,0:T(8,128)(2,1)S(1)}, u32[]{:S(2)}, u32[]{:S(2)}) collective-permute-start(bf16[3,128,768]{2,1,0:T(8,128)(2,1)S(1)} %fusion.4), channel_id=1, source_target_pairs={{0,16},{4,20},{8,24},{12,28},{16,0},{20,4},{24,8},{28,12},{1,17},{... | collective-permute-start | bytes 1769480 | tf_op jit(solution)/shard_map/ppermute | solution.py:474
  (38 other events, 453.2 us)

commit v8 on v7

--- a/solution.py
+++ b/solution.py
@@ -99,24 +99,27 @@
     def fold(t, last):
         key_tile = k_scr[pl.ds(2 * t, 2)].reshape(tile, HEAD_SIZE)
         value_tile = v_scr[pl.ds(2 * t, 2)].reshape(tile, 2 * HEAD_SIZE)
-        for h in range(heads):
-            q = q_ref[0, :, h * HEAD_SIZE : (h + 1) * HEAD_SIZE]
-            s = dot(q, key_tile, ((1,), (1,)))
+        every = range(heads)
+        s = [
+            dot(q_ref[0, :, h * HEAD_SIZE : (h + 1) * HEAD_SIZE], key_tile, ((1,), (1,)))
+            for h in every
+        ]
+        if last:
+            key_pos = iota((block, tile), 1) + t * tile
+            query_pos = iota((block, tile), 0) + ctx * block
+            s = [jnp.where(key_pos <= query_pos, x, masked_score) for x in s]
+        best = [jnp.max(x, axis=1, keepdims=True) for x in s]
+        if not last:
+            old = [best_scr[h] for h in every]
+            best = [jnp.maximum(x, y) for x, y in zip(old, best)]
+        p = [jnp.exp2((x - y) * factor).astype(BF16) for x, y in zip(s, best)]
+        blended = [dot(x, value_tile) for x in p]
+        for h in every:
             if last:
-                key_pos = iota((block, tile), 1) + t * tile
-                query_pos = iota((block, tile), 0) + ctx * block
-                s = jnp.where(key_pos <= query_pos, s, masked_score)
-            best = jnp.max(s, axis=1, keepdims=True)
-            if not last:
-                old = best_scr[h]
-                best = jnp.maximum(old, best)
-            p = jnp.exp2((s - best) * factor)
-            blended = dot(p.astype(BF16), value_tile)
-            if last:
-                acc_scr[h] = blended
+                acc_scr[h] = blended[h]
             else:
-                acc_scr[h] = acc_scr[h] * jnp.exp2((old - best) * factor) + blended
-            best_scr[h] = best
+                acc_scr[h] = acc_scr[h] * jnp.exp2((old[h] - best[h]) * factor) + blended[h]
+            best_scr[h] = best[h]
 
     fold(ctx // 2, True)
 
@@ -483,6 +486,14 @@
     return [values[0]] + [to_owner(values[d], d) for d in range(len(values) - 1, 0, -1)][::-1]
 
 
+def in_two_hops(values):
+    if len(values) != 4:
+        return to_owners(values)
+    near = to_owner(jnp.stack(values[1:3]), 1)
+    far = to_owner(values[3], 3)
+    return [values[0], near[0], to_owner(near[1], 3), far]
+
+
 def chip_groups(count):
     return [
         list(range(first + core, first + count, 2))
@@ -545,7 +556,8 @@
     ids_all, weights_all = info[:, 0:1, :], info[:, 1:2, :]
 
     mine = lax.dynamic_slice_in_dim(out_proj, piece_index * piece, piece, 1)
-    projection = to_owners([mine] * exp_count)[1:]
+    mine = lax.all_gather(mine, "exp")
+    projection = [lax.dynamic_index_in_dim(mine, owner ^ d, 0, False) for d in range(1, exp_count)]
 
     first_column = (owner * heads_dev // group) * HEAD_SIZE
     keys = lax.dynamic_slice_in_dim(rotated_key_heads, first_column, HEAD_SIZE, 2)
@@ -555,7 +567,7 @@
     key_values = chips + [partner(jnp.stack(chips), 1)]
 
     grads = place(where, ids_f.reshape(1, n), grad_out, experts, capacity)
-    grads = to_owners(after(grads, projection))
+    grads = to_owners(grads)
 
     projection = after(jnp.stack(projection), chips)
     projection = jnp.broadcast_to(projection[None], (pieces // 2,) + projection.shape)
@@ -563,10 +575,10 @@
         projection, "ctx", 0, 0, axis_index_groups=chip_groups(pieces), tiled=True
     )
 
-    sent = attend(where, queries, key_values, ids_all, capacity)
-    arrived = to_owners(after(sent[0], grads[2:]))
+    sent = attend(where, after(queries, grads[1:]), key_values, ids_all, capacity)
+    arrived = in_two_hops(sent[0])
     later = after(sent[1], arrived, same)
-    same = after(same, sent[0], grads[1:])
+    same = after(same, sent[0])
     other = partner(same, 1)
 
     rows_dev = width // ctx_count
@@ -594,9 +606,9 @@
 
     rows_a, saved_a = run(arrived, 0)
     layer_a = to_owners(rows_a[:experts])
-    change_a = to_owners(after(rows_a[experts:], layer_a[1]))
+    change_a = in_two_hops(after(rows_a[experts:], layer_a[1]))
     rows_b, saved_b = run(to_owners(later), 1)
-    packed = to_owners(rows_b)
+    packed = in_two_hops(rows_b)
     if swap:
         saved = [saved_a[0], partner(saved_a[1], 1)]
         saved += [saved_b[0], partner(after(saved_b[1], layer_a), 1)]

time: 263 us -> 326 us (1.24)
  waiting for transfers between devices: 112 us -> 152 us
  between operations: 1.05 us -> 14.5 us
  Pallas kernels: 80.3 us -> 87.2 us
  local copies, waits for them, and re-layouts: 14.6 us -> 21.4 us
  starting transfers between devices: 41.1 us -> 34.9 us
  other arithmetic: 9.74 us -> 13.5 us
    ppermute x21 -> x18, waiting for transfers between devices: 88 us -> 119 us  [to_owner(): return lax.ppermute(value, 'exp', [(i, i ^ mask) for i in range(count)])]
    all_gather x0 -> x1, waiting for transfers between devices: none -> 18.3 us  [on_device(): mine = lax.all_gather(mine, 'exp')]
    ppermute x11, waiting for transfers between devices: 24.2 us -> 14.6 us  [partner(): return lax.ppermute(value, 'ctx', [(i, i ^ mask) for i in range(count)])]
    pallas_call x1, Pallas kernels: 25.5 us -> 32.6 us  [attend(): pl.pallas_call(functools.partial(attend_kernel, experts, capacity, heads,...]
    ppermute x21 -> x18, starting transfers between devices: 25.9 us -> 18.9 us  [to_owner(): return lax.ppermute(value, 'exp', [(i, i ^ mask) for i in range(count)])]
    another operation x0 -> x3, other arithmetic: none -> 4.74 us  [in_two_hops(): near = to_owner(jnp.stack(values[1:3]), 1)]
    squeeze x0 -> x3, local copies, waits for them, and re-layouts: none -> 3.56 us  [in_two_hops(): return [values[0], near[0], to_owner(near[1], 3), far]]
    unnamed x57 -> x49, local copies, waits for them, and re-layouts: 5.33 us -> 6.57 us
  transfers between devices with their start and end apart: 34 -> 32, of which waited for: 14 -> 14; matrix products, arithmetic and copies ran while one was open for 5% -> 7% of each run, Pallas kernels for 31% -> 27%
where the time goes in v8:
time: 326 us; the launch traced here: 323 us
  waiting for transfers between devices  152 us (47%)
  Pallas kernels  87.2 us (27%)
  starting transfers between devices  34.9 us (11%)
  local copies, waits for them, and re-layouts  21.4 us (7%)
  between operations  14.5 us (4%)
  other arithmetic  13.5 us (4%)
    ppermute x18, waiting for transfers between devices, to_owner(): return lax.ppermute(value, 'exp', [(i, i ^ mask) for i in range(count)])  119 us
    pallas_call x2, Pallas kernels, expert_part(): pl.pallas_call(functools.partial(expert_kernel, experts, capacity, index,...  35.5 us
    pallas_call x1, Pallas kernels, attend(): pl.pallas_call(functools.partial(attend_kernel, experts, capacity, heads,...  32.6 us
    ppermute x18, starting transfers between devices, to_owner(): return lax.ppermute(value, 'exp', [(i, i ^ mask) for i in range(count)])  18.9 us
    all_gather x1, waiting for transfers between devices, on_device(): mine = lax.all_gather(mine, 'exp')  18.3 us
    ppermute x11, waiting for transfers between devices, partner(): return lax.ppermute(value, 'ctx', [(i, i ^ mask) for i in range(count)])  14.6 us
    pallas_call x1, Pallas kernels, weight_blocks(): pl.pallas_call(functools.partial(weight_kernel, count), grid=(blocks,), i...  10 us
    unnamed x49, local copies, waits for them, and re-layouts  6.57 us
  transfers between devices with their start and end apart: 32, of which 14 were waited for; matrix products, arithmetic and copies ran while one was open for 7% of the time, Pallas kernels for 27%

profile of v8, /device:TPU:22, one launch (start us, length us, event | category | flops | bytes accessed | tf_op | source)
XLA Modules:
  0.0 323.0 jit_solution(9541267215403996770)
XLA Ops:
  15.3 5.2 %all-to-all-start = ((f32[4,2,256]{2,1,0:T(2,128)}), f32[4,2,256]{2,1,0:T(2,128)S(1)}, u32[]{:S(2)}, u32[]{:S(2)}) async-start(f32[4,2,256]{2,1,0:T(2,128)} %broadcast_in_dim.4), calls=%async_computation | async-start | bytes 16384 | tf_op jit(solution)/shard_map/all_to_all | solution.py:555
  20.5 18.3 %all-gather.3.cloned.1.call-done = bf16[2048,256]{1,0:T(8,128)(2,1)} async-done(((bf16[512,256]{1,0:T(8,128)(2,1)}), bf16[2048,256]{1,0:T(8,128)(2,1)}) %all-gather.3.cloned.1.call-update) | async-done | bytes 1048592 | tf_op jit(solution)/shard_map/all_gather | solution.py:559
  42.3 4.2 %all-to-all-start.1 = ((bf16[4,3,512,256]{3,2,1,0:T(8,128)(2,1)}), bf16[4,3,512,256]{3,2,1,0:T(8,128)(2,1)S(1)}, u32[]{:S(2)}, u32[]{:S(2)}) async-start(bf16[4,3,512,256]{3,2,1,0:T(8,128)(2,1)} %broadcast_in_dim.5), calls=%async_computation.1 | async-start | bytes 6291456 | tf_op jit(solution)/shard_map/all_to_all | solution.py:574
  46.5 3.1 pad_maximum_fusion
  50.3 3.1 place.1
  57.5 19.1 %collective-permute-done.refs_5_ = bf16[128,2048]{1,0:T(8,128)(2,1)} collective-permute-done((bf16[128,2048]{1,0:T(8,128)(2,1)}, bf16[128,2048]{1,0:T(8,128)(2,1)}, u32[]{:S(2)}, u32[]{:S(2)}) %collective-permute-start) | collective-permute-done | bytes 524320 | tf_op jit(solution)/shard_map/ppermute | solution.py:482
  76.6 14.3 %collective-permute-done.1.refs_6_ = bf16[128,2048]{1,0:T(8,128)(2,1)} collective-permute-done((bf16[128,2048]{1,0:T(8,128)(2,1)}, bf16[128,2048]{1,0:T(8,128)(2,1)}, u32[]{:S(2)}, u32[]{:S(2)}) %collective-permute-start.1) | collective-permute-done | bytes 524320 | tf_op jit(solution)/shard_map/ppermute | solution.py:482
  90.9 12.1 %collective-permute-done.2.refs_7_ = bf16[128,2048]{1,0:T(8,128)(2,1)} collective-permute-done((bf16[128,2048]{1,0:T(8,128)(2,1)}, bf16[128,2048]{1,0:T(8,128)(2,1)}, u32[]{:S(2)}, u32[]{:S(2)}) %collective-permute-start.2) | collective-permute-done | bytes 524320 | tf_op jit(solution)/shard_map/ppermute | solution.py:482
  103.0 32.6 %attend.1 = (bf16[4,64,512]{2,1,0:T(8,128)(2,1)}, bf16[4,64,512]{2,1,0:T(8,128)(2,1)}, bf16[4,64,512]{2,1,0:T(8,128)(2,1)}, bf16[4,64,512]{2,1,0:T(8,128)(2,1)},...) custom-call(s32[3]{0:T(128)} %pad_add_fusion.where_ref, ...), custom_call_target="tpu_custom_call" | custom-call | flops 1000 | bytes 1000 | tf_op jit(solution)/shard_map/attend/pallas_call | solution.py:158
  138.2 13.8 %collective-permute-done.7 = bf16[2,4,64,512]{3,2,1,0:T(8,128)(2,1)S(1)} collective-permute-done((bf16[2,4,64,512]{3,2,1,0:T(8,128)(2,1)S(1)}, bf16[2,4,64,512]{3,2,1,0:T(8,128)(2,1)S(1)}, u32[]{:S(2)}, u32[]{:S(2)}) %collective-permute-start.7) | collective-permute-done | bytes 524320 | tf_op jit(solution)/shard_map/ppermute | solution.py:482
  153.7 14.7 %collective-permute-done.8.refs_2_ = bf16[4,64,512]{2,1,0:T(8,128)(2,1)S(1)} collective-permute-done((bf16[4,64,512]{2,1,0:T(8,128)(2,1)S(1)}, bf16[4,64,512]{2,1,0:T(8,128)(2,1)S(1)}, u32[]{:S(2)}, u32[]{:S(2)}) %collective-permute-start.8) | collective-permute-done | bytes 262176 | tf_op jit(solution)/shard_map/ppermute | solution.py:482
  168.4 2.5 collective-permute-start.18
  173.5 17.5 %expert.2 = (bf16[64,2048]{1,0:T(8,128)(2,1)}, bf16[64,2048]{1,0:T(8,128)(2,1)}, bf16[64,2048]{1,0:T(8,128)(2,1)}, bf16[64,2048]{1,0:T(8,128)(2,1)}, bf16[64,204...) custom-call(s32[3]{0:T(128)} %pad_add_fusion.where_ref, ...), custom_call_target="tpu_custom_call" | custom-call | flops 1000 | bytes 1000 | tf_op jit(solution)/shard_map/expert/pallas_call | solution.py:402
  195.5 18.0 %expert.3 = (bf16[64,4096]{1,0:T(8,128)(2,1)}, bf16[64,4096]{1,0:T(8,128)(2,1)}, bf16[64,4096]{1,0:T(8,128)(2,1)}, bf16[64,4096]{1,0:T(8,128)(2,1)}, bf16[256,43...) custom-call(s32[3]{0:T(128)} %pad_add_fusion.where_ref, bf16[4,64,512]{2,1,0:T(8,128)(2,1)} %get-tuple-element.82.refs_0_, ...), custom_call_target="tpu_custom_call" | custom-call | flops 1000 | bytes 1000 | tf_op jit(solution)/shard_map/expert/pallas_call | solution.py:402
  213.6 3.8 %collective-permute-done.13.refs_3_ = bf16[64,2048]{1,0:T(8,128)(2,1)S(1)} collective-permute-done((bf16[64,2048]{1,0:T(8,128)(2,1)}, bf16[64,2048]{1,0:T(8,128)(2,1)S(1)}, u32[]{:S(2)}, u32[]{:S(2)}) %collective-permute-start.13) | collective-permute-done | bytes 262176 | tf_op jit(solution)/shard_map/ppermute | solution.py:482
  219.3 2.3 pad_maximum_fusion.1
  224.6 9.5 %collective-permute-done.14 = bf16[2,64,2048]{2,1,0:T(8,128)(2,1)S(1)} collective-permute-done((bf16[2,64,2048]{2,1,0:T(8,128)(2,1)S(1)}, bf16[2,64,2048]{2,1,0:T(8,128)(2,1)S(1)}, u32[]{:S(2)}, u32[]{:S(2)}) %collective-permute-start.14) | collective-permute-done | bytes 524320 | tf_op jit(solution)/shard_map/ppermute | solution.py:482
  237.3 10.0 %weight_grads.1 = (bf16[4,3,128,768]{3,2,1,0:T(8,128)(2,1)}, bf16[4,3,128,768]{3,2,1,0:T(8,128)(2,1)}) custom-call(bf16[256,4352]{1,0:T(8,128)(2,1)} %get-tuple-element.90.refs_0_.refs_4_.refs_8_.refs_12_.refs_16_, bf16[256,4352]{1,0:T(8,128)(2,1)} %copy-done, bf16[256,4352]{1,0:T(8,128)(2,1)} %get-tuple-element.92.refs_2_.refs_6_.refs_10_.refs_14_.refs_18_, ...), custom_call_target="tpu_custom_call" | custom-call | flops 1000 | bytes 1000 | tf_op jit(solution)/shard_map/weight_grads/pallas_call | solution.py:463
  250.2 6.4 %collective-permute-done.20 = bf16[2,64,4096]{2,1,0:T(8,128)(2,1)} collective-permute-done((bf16[2,64,4096]{2,1,0:T(8,128)(2,1)}, bf16[2,64,4096]{2,1,0:T(8,128)(2,1)}, u32[]{:S(2)}, u32[]{:S(2)}) %collective-permute-start.20) | collective-permute-done | bytes 1048608 | tf_op jit(solution)/shard_map/ppermute | solution.py:482
  259.8 14.5 %collective-permute-done.26 = bf16[2,3,128,768]{3,2,1,0:T(8,128)(2,1)S(1)} collective-permute-done((bf16[2,3,128,768]{3,2,1,0:T(8,128)(2,1)S(1)}, bf16[2,3,128,768]{3,2,1,0:T(8,128)(2,1)S(1)}, u32[]{:S(2)}, u32[]{:S(2)}) %collective-permute-start.26) | collective-permute-done | bytes 1179680 | tf_op jit(solution)/shard_map/ppermute | solution.py:477
  277.2 2.8 collective-permute-start.27
  280.7 17.3 %collective-permute-done.22.refs_11_ = bf16[64,4096]{1,0:T(8,128)(2,1)} collective-permute-done((bf16[64,4096]{1,0:T(8,128)(2,1)}, bf16[64,4096]{1,0:T(8,128)(2,1)}, u32[]{:S(2)}, u32[]{:S(2)}) %collective-permute-start.22) | collective-permute-done | bytes 524320 | tf_op jit(solution)/shard_map/ppermute | solution.py:482
  298.0 7.6 %collective-permute-done.21.refs_10_ = bf16[64,4096]{1,0:T(8,128)(2,1)} collective-permute-done((bf16[64,4096]{1,0:T(8,128)(2,1)S(1)}, bf16[64,4096]{1,0:T(8,128)(2,1)}, u32[]{:S(2)}, u32[]{:S(2)}) %collective-permute-start.21) | collective-permute-done | bytes 524320 | tf_op jit(solution)/shard_map/ppermute | solution.py:482
  305.6 6.0 %restore.1 = (bf16[256,2048]{1,0:T(8,128)(2,1)}, bf16[256,2048]{1,0:T(8,128)(2,1)}) custom-call(s32[3]{0:T(128)} %pad_add_fusion.where_ref, f32[256,1]{1,0:T(8,128)} %convert_element_type.29.ids_ref, bf16[64,2048]{1,0:T(8,128)(2,1)} %get-tuple-element.66.refs_0_, bf16[64,2048]{1,0:T(8,128)(2,1)} %copy-done.11, bf16[64,2048]{1,0:T(8,128)(2,1)} %copy-done.12, ...), custom_call_target="tpu_custom_call" | custom-call | flops 1000 | bytes 1000 | tf_op jit(solution)/shard_map/restore/pallas_call | solution.py:246
  (126 shorter events, 49.9 us)
Async XLA Ops:
  7.2 31.6 %all-gather.3.cloned.1.call-start = ((), (), s32[]{:S(2)}) async-start(), calls=%async_computation.2 | async-start | bytes 1310720 | tf_op jit(solution)/shard_map/all_gather | solution.py:559
  10.9 29.1 %collective-permute-start.5 = (bf16[4,256,256]{2,1,0:T(8,128)(2,1)S(1)}, bf16[4,256,256]{2,1,0:T(8,128)(2,1)S(1)}, u32[]{:S(2)}, u32[]{:S(2)}) collective-permute-start(bf16[4,256,256]{2,1,0:T(8,128)(2,1)S(1)} %get-tuple-element.118.refs_0_), channel_id=1, source_target_pairs={{0,24},{4,28},{8,16},{12,20},{16,8},{20,12},{24,0},{28,4},{1,25},{... | collective-permute-start | bytes 1572872 | tf_op jit(solution)/shard_map/ppermute | solution.py:477
  11.4 28.7 %collective-permute-start.4 = (bf16[4,256,256]{2,1,0:T(8,128)(2,1)S(1)}, bf16[4,256,256]{2,1,0:T(8,128)(2,1)S(1)}, u32[]{:S(2)}, u32[]{:S(2)}) collective-permute-start(bf16[4,256,256]{2,1,0:T(8,128)(2,1)S(1)} %get-tuple-element.118.refs_0_), channel_id=1, source_target_pairs={{0,16},{4,20},{8,24},{12,28},{16,0},{20,4},{24,8},{28,12},{1,17},{... | collective-permute-start | bytes 1572872 | tf_op jit(solution)/shard_map/ppermute | solution.py:477
  12.9 27.2 %collective-permute-start.3 = (bf16[4,256,256]{2,1,0:T(8,128)(2,1)S(1)}, bf16[4,256,256]{2,1,0:T(8,128)(2,1)S(1)}, u32[]{:S(2)}, u32[]{:S(2)}) collective-permute-start(bf16[4,256,256]{2,1,0:T(8,128)(2,1)S(1)} %get-tuple-element.118.refs_0_), channel_id=1, source_target_pairs={{0,8},{4,12},{8,0},{12,4},{16,24},{20,28},{24,16},{28,20},{1,9},{5... | collective-permute-start | bytes 1572872 | tf_op jit(solution)/shard_map/ppermute | solution.py:477
  15.3 24.8 %all-to-all-start = ((f32[4,2,256]{2,1,0:T(2,128)}), f32[4,2,256]{2,1,0:T(2,128)S(1)}, u32[]{:S(2)}, u32[]{:S(2)}) async-start(f32[4,2,256]{2,1,0:T(2,128)} %broadcast_in_dim.4), calls=%async_computation | async-start | bytes 16384 | tf_op jit(solution)/shard_map/all_to_all | solution.py:555
  42.3 93.3 %all-to-all-start.1 = ((bf16[4,3,512,256]{3,2,1,0:T(8,128)(2,1)}), bf16[4,3,512,256]{3,2,1,0:T(8,128)(2,1)S(1)}, u32[]{:S(2)}, u32[]{:S(2)}) async-start(bf16[4,3,512,256]{3,2,1,0:T(8,128)(2,1)} %broadcast_in_dim.5), calls=%async_computation.1 | async-start | bytes 6291456 | tf_op jit(solution)/shard_map/all_to_all | solution.py:574
  49.6 53.4 %collective-permute-start.6 = (bf16[4,4,256,256]{3,2,1,0:T(8,128)(2,1)}, bf16[4,4,256,256]{3,2,1,0:T(8,128)(2,1)}, u32[]{:S(2)}, u32[]{:S(2)}) collective-permute-start(bf16[4,4,256,256]{3,2,1,0:T(8,128)(2,1)} %pad_maximum_fusion), channel_id=1, source_target_pairs={{0,4},{4,0},{8,12},{12,8},{16,20},{20,16},{24,28},{28,24},{1,5},{5... | collective-permute-start | bytes 6291464 | tf_op jit(solution)/shard_map/ppermute | solution.py:477
  53.4 23.2 %collective-permute-start = (bf16[128,2048]{1,0:T(8,128)(2,1)}, bf16[128,2048]{1,0:T(8,128)(2,1)}, u32[]{:S(2)}, u32[]{:S(2)}) collective-permute-start(bf16[128,2048]{1,0:T(8,128)(2,1)} %get-tuple-element.55), channel_id=1, source_target_pairs={{0,1},{1,0},{2,3},{3,2},{4,5},{5,4},{6,7},{7,6},{8,9},{9,8},{10,11... | collective-permute-start | bytes 1572872 | tf_op jit(solution)/shard_map/ppermute | solution.py:482
  53.9 37.0 %collective-permute-start.1 = (bf16[128,2048]{1,0:T(8,128)(2,1)}, bf16[128,2048]{1,0:T(8,128)(2,1)}, u32[]{:S(2)}, u32[]{:S(2)}) collective-permute-start(bf16[128,2048]{1,0:T(8,128)(2,1)} %get-tuple-element.56), channel_id=1, source_target_pairs={{0,2},{1,3},{2,0},{3,1},{4,6},{5,7},{6,4},{7,5},{8,10},{9,11},{10,... | collective-permute-start | bytes 1572872 | tf_op jit(solution)/shard_map/ppermute | solution.py:482
  55.8 47.2 %collective-permute-start.2 = (bf16[128,2048]{1,0:T(8,128)(2,1)}, bf16[128,2048]{1,0:T(8,128)(2,1)}, u32[]{:S(2)}, u32[]{:S(2)}) collective-permute-start(bf16[128,2048]{1,0:T(8,128)(2,1)} %get-tuple-element.57), channel_id=1, source_target_pairs={{0,3},{1,2},{2,1},{3,0},{4,7},{5,6},{6,5},{7,4},{8,11},{9,10},{10,... | collective-permute-start | bytes 1572872 | tf_op jit(solution)/shard_map/ppermute | solution.py:482
  135.6 36.3 %collective-permute-start.10 = (bf16[4,3,512,256]{3,2,1,0:T(8,128)(2,1)S(1)}, bf16[4,3,512,256]{3,2,1,0:T(8,128)(2,1)S(1)}, u32[]{:S(2)}, u32[]{:S(2)}) collective-permute-start(bf16[4,3,512,256]{3,2,1,0:T(8,128)(2,1)S(1)} %all-to-all-done.1.refs_9_), channel_id=1, source_target_pairs={{0,4},{4,0},{8,12},{12,8},{16,20},{20,16},{24,28},{28,24},{1,5},{5... | collective-permute-start | bytes 9437192 | tf_op jit(solution)/shard_map/ppermute | solution.py:477
  168.4 25.3 %collective-permute-start.17 = (bf16[4,64,512]{2,1,0:T(8,128)(2,1)}, bf16[4,64,512]{2,1,0:T(8,128)(2,1)S(1)}, u32[]{:S(2)}, u32[]{:S(2)}) collective-permute-start(bf16[4,64,512]{2,1,0:T(8,128)(2,1)} %get-tuple-element.83), channel_id=1, source_target_pairs={{0,1},{1,0},{2,3},{3,2},{4,5},{5,4},{6,7},{7,6},{8,9},{9,8},{10,11... | collective-permute-start | bytes 786440 | tf_op jit(solution)/shard_map/ppermute | solution.py:482
  168.4 26.3 %collective-permute-start.18 = (bf16[4,64,512]{2,1,0:T(8,128)(2,1)}, bf16[4,64,512]{2,1,0:T(8,128)(2,1)S(1)}, u32[]{:S(2)}, u32[]{:S(2)}) collective-permute-start(bf16[4,64,512]{2,1,0:T(8,128)(2,1)} %get-tuple-element.84), channel_id=1, source_target_pairs={{0,2},{1,3},{2,0},{3,1},{4,6},{5,7},{6,4},{7,5},{8,10},{9,11},{10,... | collective-permute-start | bytes 786440 | tf_op jit(solution)/shard_map/ppermute | solution.py:482
  170.9 24.6 %collective-permute-start.19 = (bf16[4,64,512]{2,1,0:T(8,128)(2,1)}, bf16[4,64,512]{2,1,0:T(8,128)(2,1)}, u32[]{:S(2)}, u32[]{:S(2)}) collective-permute-start(bf16[4,64,512]{2,1,0:T(8,128)(2,1)} %get-tuple-element.85), channel_id=1, source_target_pairs={{0,3},{1,2},{2,1},{3,0},{4,7},{5,6},{6,5},{7,4},{8,11},{9,10},{10,... | collective-permute-start | bytes 786440 | tf_op jit(solution)/shard_map/ppermute | solution.py:482
  193.7 23.7 %collective-permute-start.13 = (bf16[64,2048]{1,0:T(8,128)(2,1)}, bf16[64,2048]{1,0:T(8,128)(2,1)S(1)}, u32[]{:S(2)}, u32[]{:S(2)}) collective-permute-start(bf16[64,2048]{1,0:T(8,128)(2,1)} %get-tuple-element.69), channel_id=1, source_target_pairs={{0,3},{1,2},{2,1},{3,0},{4,7},{5,6},{6,5},{7,4},{8,11},{9,10},{10,... | collective-permute-start | bytes 786440 | tf_op jit(solution)/shard_map/ppermute | solution.py:482
  195.4 40.5 %collective-permute-start.23 = (bf16[256,4352]{1,0:T(8,128)(2,1)}, bf16[256,4352]{1,0:T(8,128)(2,1)S(1)}, u32[]{:S(2)}, u32[]{:S(2)}) collective-permute-start(bf16[256,4352]{1,0:T(8,128)(2,1)} %get-tuple-element.91), channel_id=1, source_target_pairs={{0,4},{4,0},{8,12},{12,8},{16,20},{20,16},{24,28},{28,24},{1,5},{5... | collective-permute-start | bytes 6684680 | tf_op jit(solution)/shard_map/ppermute | solution.py:477
  221.5 35.1 %collective-permute-start.20 = (bf16[2,64,4096]{2,1,0:T(8,128)(2,1)}, bf16[2,64,4096]{2,1,0:T(8,128)(2,1)}, u32[]{:S(2)}, u32[]{:S(2)}) collective-permute-start(bf16[2,64,4096]{2,1,0:T(8,128)(2,1)} %pad_maximum_fusion.1), channel_id=1, source_target_pairs={{0,1},{1,0},{2,3},{3,2},{4,5},{5,4},{6,7},{7,6},{8,9},{9,8},{10,11... | collective-permute-start | bytes 3145736 | tf_op jit(solution)/shard_map/ppermute | solution.py:482
  223.5 23.8 %collective-permute-start.16 = (bf16[64,2048]{1,0:T(8,128)(2,1)}, bf16[64,2048]{1,0:T(8,128)(2,1)S(1)}, u32[]{:S(2)}, u32[]{:S(2)}) collective-permute-start(bf16[64,2048]{1,0:T(8,128)(2,1)} %get-tuple-element.77), channel_id=1, source_target_pairs={{0,3},{1,2},{2,1},{3,0},{4,7},{5,6},{6,5},{7,4},{8,11},{9,10},{10,... | collective-permute-start | bytes 786440 | tf_op jit(solution)/shard_map/ppermute | solution.py:482
  248.9 25.3 %collective-permute-start.26 = (bf16[2,3,128,768]{3,2,1,0:T(8,128)(2,1)S(1)}, bf16[2,3,128,768]{3,2,1,0:T(8,128)(2,1)S(1)}, u32[]{:S(2)}, u32[]{:S(2)}) collective-permute-start(bf16[2,3,128,768]{3,2,1,0:T(8,128)(2,1)S(1)} %slice.71), channel_id=1, source_target_pairs={{0,16},{4,20},{8,24},{12,28},{16,0},{20,4},{24,8},{28,12},{1,17},{... | collective-permute-start | bytes 3538952 | tf_op jit(solution)/shard_map/ppermute | solution.py:477
  249.0 48.9 %collective-permute-start.22 = (bf16[64,4096]{1,0:T(8,128)(2,1)}, bf16[64,4096]{1,0:T(8,128)(2,1)}, u32[]{:S(2)}, u32[]{:S(2)}) collective-permute-start(bf16[64,4096]{1,0:T(8,128)(2,1)} %get-tuple-element.89), channel_id=1, source_target_pairs={{0,3},{1,2},{2,1},{3,0},{4,7},{5,6},{6,5},{7,4},{8,11},{9,10},{10,... | collective-permute-start | bytes 1572872 | tf_op jit(solution)/shard_map/ppermute | solution.py:482
  250.1 25.3 %collective-permute-start.25 = (bf16[2,3,128,768]{3,2,1,0:T(8,128)(2,1)S(1)}, bf16[2,3,128,768]{3,2,1,0:T(8,128)(2,1)S(1)}, u32[]{:S(2)}, u32[]{:S(2)}) collective-permute-start(bf16[2,3,128,768]{3,2,1,0:T(8,128)(2,1)S(1)} %slice.68), channel_id=1, source_target_pairs={{0,8},{4,12},{8,0},{12,4},{16,24},{20,28},{24,16},{28,20},{1,9},{5... | collective-permute-start | bytes 3538952 | tf_op jit(solution)/shard_map/ppermute | solution.py:477
  258.7 46.8 %collective-permute-start.21 = (bf16[64,4096]{1,0:T(8,128)(2,1)S(1)}, bf16[64,4096]{1,0:T(8,128)(2,1)}, u32[]{:S(2)}, u32[]{:S(2)}) collective-permute-start(bf16[64,4096]{1,0:T(8,128)(2,1)S(1)} %get-tuple-element.108), channel_id=1, source_target_pairs={{0,3},{1,2},{2,1},{3,0},{4,7},{5,6},{6,5},{7,4},{8,11},{9,10},{10,... | collective-permute-start | bytes 1572872 | tf_op jit(solution)/shard_map/ppermute | solution.py:482
  275.4 36.1 %collective-permute-start.28 = (bf16[3,128,768]{2,1,0:T(8,128)(2,1)}, bf16[3,128,768]{2,1,0:T(8,128)(2,1)}, u32[]{:S(2)}, u32[]{:S(2)}) collective-permute-start(bf16[3,128,768]{2,1,0:T(8,128)(2,1)} %fusion.5), channel_id=1, source_target_pairs={{0,8},{4,12},{8,0},{12,4},{16,24},{20,28},{24,16},{28,20},{1,9},{5... | collective-permute-start | bytes 1769480 | tf_op jit(solution)/shard_map/ppermute | solution.py:477
  277.2 35.6 %collective-permute-start.27 = (bf16[3,128,768]{2,1,0:T(8,128)(2,1)S(1)}, bf16[3,128,768]{2,1,0:T(8,128)(2,1)S(1)}, u32[]{:S(2)}, u32[]{:S(2)}) collective-permute-start(bf16[3,128,768]{2,1,0:T(8,128)(2,1)S(1)} %fusion.4), channel_id=1, source_target_pairs={{0,16},{4,20},{8,24},{12,28},{16,0},{20,4},{24,8},{28,12},{1,17},{... | collective-permute-start | bytes 1769480 | tf_op jit(solution)/shard_map/ppermute | solution.py:477
  (32 other events, 382.5 us)
Sparse Core Ops, SparseCore 0:
  10.2 28.5 all-gather.2

commit v9 on v7

--- a/solution.py
+++ b/solution.py
@@ -136,7 +136,7 @@
     slots = shifted_slots(position, owner, experts, capacity)
     for b in range(per_seq):
         source = seq * per_seq + b
-        target = slots_row(ids_ref[source], capacity)
+        target = slots_row(ids_ref[jnp.bitwise_xor(owner, source)], capacity)
         picked = dot(one_hot(slots == target), att_scr[b * n : (b + 1) * n, :]).astype(BF16)
         for d in range(experts):
             rank = jnp.bitwise_xor(jnp.bitwise_xor(owner, d), source)
@@ -178,34 +178,29 @@
     return [outs[c * experts : (c + 1) * experts] for c in range(PARTS)]
 
 
-def place_kernel(experts, capacity, where_ref, ids_ref, rows_ref, *refs):
-    out_refs, pick_scr = refs[:-1], refs[-1]
-
+def place_kernel(capacity, ids_ref, rows_ref, out_ref, pick_scr):
     @pl.when(pl.program_id(0) == 0)
     def _():
         position = iota(pick_scr.shape, 0)
-        slots = shifted_slots(position, where_ref[1], experts, capacity)
-        pick_scr[...] = one_hot(slots == slots_row(ids_ref[...], capacity))
-
-    picked = dot(pick_scr[...], rows_ref[...]).astype(BF16)
-    for d, ref in enumerate(out_refs):
-        ref[...] = picked[d * capacity : (d + 1) * capacity]
-
-
-def place(where, ids_row, rows, experts, capacity):
+        pick_scr[...] = one_hot(position.astype(F32) == slots_row(ids_ref[...], capacity))
+
+    out_ref[...] = dot(pick_scr[...], rows_ref[...]).astype(BF16).reshape(out_ref.shape)
+
+
+def place(ids_row, rows, experts, capacity):
     n, width = rows.shape
     cols = min(width, 1024)
     return pl.pallas_call(
-        functools.partial(place_kernel, experts, capacity),
+        functools.partial(place_kernel, capacity),
         grid=(width // cols,),
-        in_specs=[smem(), whole(1, n), pl.BlockSpec((n, cols), lambda i: (0, i))],
-        out_specs=[pl.BlockSpec((capacity, cols), lambda i: (0, i))] * experts,
-        out_shape=[jax.ShapeDtypeStruct((capacity, width), BF16)] * experts,
+        in_specs=[whole(1, n), pl.BlockSpec((n, cols), lambda i: (0, i))],
+        out_specs=pl.BlockSpec((experts, capacity, cols), lambda i: (0, 0, i)),
+        out_shape=jax.ShapeDtypeStruct((experts, capacity, width), BF16),
         scratch_shapes=[pltpu.VMEM((experts * capacity, n), BF16)],
         compiler_params=kernel_params(),
         cost_estimate=brief(),
         name="place",
-    )(where, ids_row, rows)
+    )(ids_row, rows)
 
 
 def restore_kernel(experts, capacity, tiles, where_ref, ids_ref, *refs):
@@ -253,12 +248,14 @@
     )(where, ids_column, *layer_a, *change_a, *packed)
 
 
-def expert_kernel(experts, capacity, part_index, swap, where_ref, *refs):
+def expert_kernel(pieces, experts, capacity, part_index, swap, where_ref, *refs):
     att_refs, refs = refs[:experts], refs[experts:]
-    grad_refs, refs = refs[:experts], refs[experts:]
-    width_of = grad_refs[0].shape[1]
-    own_ref, same_hbm, other_hbm, gate_hbm, up_hbm, down_hbm = refs[:6]
-    gain_ref, ids_ref, weight_ref, refs = refs[6], refs[7], refs[8], refs[9:]
+    grad_ref, refs = refs[0], refs[1:]
+    width_of = grad_ref.shape[2]
+    own_ref, refs = refs[0], refs[1:]
+    same_hbms, refs = refs[: pieces // 2], refs[pieces // 2 :]
+    other_hbm, gate_hbm, up_hbm, down_hbm = refs[:4]
+    gain_ref, ids_ref, weight_ref, refs = refs[4], refs[5], refs[6], refs[7:]
     if part_index == 0:
         layer_refs, refs = refs[:experts], refs[experts:]
         change_refs, refs = refs[:experts], refs[experts:]
@@ -268,21 +265,20 @@
         change_refs = [ref.at[:, width_of:] for ref in packed_refs]
     saved_refs, refs = refs[: 1 + swap], refs[1 + swap :]
     w_scr, gate_scr, up_scr, down_scr, hidden_scr, normed_ref, back_ref, back_in_scr, sems = refs
-    part, width = grad_refs[0].shape
+    _, part, width = grad_ref.shape
     rows = experts * part
     att_cols = att_refs[0].shape[-1]
-    pieces, _, _, piece = w_scr.shape
+    piece = w_scr.shape[3]
     ff = gate_scr.shape[1]
     ctx, owner = where_ref[0], where_ref[1]
-    core = jnp.bitwise_and(ctx, 1)
     sources = [jnp.bitwise_xor(owner, d) for d in range(experts)]
     units_at, gate_at, up_at, normed_at = 0, ff, 2 * ff, 3 * ff
 
     copies = []
     for q in range(pieces // 2):
-        for ref in (same_hbm, other_hbm):
+        for block in (same_hbms[q], other_hbm.at[q]):
             m = len(copies)
-            copies.append(pltpu.make_async_copy(ref.at[q], w_scr.at[m], sems.at[m]))
+            copies.append(pltpu.make_async_copy(block, w_scr.at[m], sems.at[m]))
     weight_copies = (
         pltpu.make_async_copy(gate_hbm.at[0], gate_scr, sems.at[pieces]),
         pltpu.make_async_copy(up_hbm.at[0], up_scr, sems.at[pieces + 1]),
@@ -296,22 +292,21 @@
     n = ids_ref.shape[2]
     weights = []
     for s, source in enumerate(sources):
-        target = slots_row(ids_ref[source], capacity)
+        target = slots_row(ids_ref[s], capacity)
         slot = iota((part, n), 0) + (owner * capacity + part_index * part)
         weights.append(
             jnp.sum(
-                jnp.where(slot.astype(F32) == target, weight_ref[source], 0.0),
+                jnp.where(slot.astype(F32) == target, weight_ref[s], 0.0),
                 axis=1,
                 keepdims=True,
             )
         )
-        grads = grad_refs[s][...].astype(F32)
+        grads = grad_ref[source].astype(F32)
         back_ref[s * part : (s + 1) * part, :] = (weights[s] * grads).astype(BF16)
 
     for m in range(pieces):
         copies[m].wait()
-        index = m + core if m % 2 == 0 else m - core
-        column = pl.multiple_of(index * piece, piece)
+        column = pl.multiple_of(jnp.bitwise_xor(where_ref[2], m) * piece, piece)
         total = jnp.zeros((rows, piece), F32)
         for d in range(experts):
             block = own_ref[:, pl.ds(column, piece)] if d == 0 else w_scr[m, d - 1]
@@ -376,7 +371,7 @@
         scaled = back_in_scr[:, t : t + PIECE].astype(F32) * gain_ref[:, t : t + PIECE]
         change = inv * (scaled - unit * moment)
         for s in range(experts):
-            grads = grad_refs[s][:, t : t + PIECE].astype(F32)
+            grads = grad_ref[sources[s], :, t : t + PIECE].astype(F32)
             change_refs[s][:, t : t + PIECE] = (
                 grads + change[s * part : (s + 1) * part]
             ).astype(BF16)
@@ -386,9 +381,9 @@
     where, att, grads, own, same, other, gate, up, down, gain, ids, weights, capacity, swap, index
 ):
     experts, part, att_cols = att[0].shape
-    pieces = 2 * same.shape[0]
-    piece = same.shape[-1]
-    width = grads[0].shape[1]
+    pieces = 2 * len(same)
+    piece = same[0].shape[-1]
+    width = grads.shape[2]
     ff = gate.shape[2]
     rows = experts * part
     n = ids.shape[2]
@@ -397,13 +392,13 @@
     rows_out = [out(part, width)] * (2 * experts) if index == 0 else [out(part, 2 * width)] * experts
     in_hbm = pl.BlockSpec(memory_space=pl.ANY)
     outs = pl.pallas_call(
-        functools.partial(expert_kernel, experts, capacity, index, swap),
+        functools.partial(expert_kernel, pieces, experts, capacity, index, swap),
         grid=(1,),
         in_specs=[smem()]
         + [whole(*x.shape) for x in att]
-        + [pl.BlockSpec((part, width), lambda i: (index, 0))] * experts
+        + [pl.BlockSpec((experts, part, width), lambda i: (0, index, 0))]
         + [whole(*own.shape)]
-        + [in_hbm] * 5
+        + [in_hbm] * (len(same) + 4)
         + [whole(1, width), whole(experts, 1, n), whole(experts, 1, n)],
         out_specs=[whole(*x.shape) for x in rows_out]
         + [whole(rows, 3 * ff + 2 * half)] * (1 + swap),
@@ -423,7 +418,7 @@
         compiler_params=kernel_params(),
         cost_estimate=brief(),
         name="expert",
-    )(where, *att, *grads, own, same, other, gate, up, down, gain, ids, weights)
+    )(where, *att, grads, own, *same, other, gate, up, down, gain, ids, weights)
     return outs[: len(rows_out)], outs[len(rows_out) :]
 
 
@@ -481,14 +476,6 @@
 
 def to_owners(values):
     return [values[0]] + [to_owner(values[d], d) for d in range(len(values) - 1, 0, -1)][::-1]
-
-
-def chip_groups(count):
-    return [
-        list(range(first + core, first + count, 2))
-        for first in range(0, lax.axis_size("ctx"), count)
-        for core in range(2)
-    ]
 
 
 def after(value, *others):
@@ -539,13 +526,18 @@
     where = jnp.stack([ctx, owner, piece_index]).astype(jnp.int32)
 
     ids_f = expert_ids.astype(F32)
-    info = jnp.stack([ids_f[:, 0], gate_weights[:, 0]])
-    info = jnp.broadcast_to(info[None], (exp_count,) + info.shape)
-    info = lax.all_to_all(info, "exp", 0, 0, tiled=True)
-    ids_all, weights_all = info[:, 0:1, :], info[:, 1:2, :]
-
+    gates = gate_weights[:, 0]
+    high = lax.optimization_barrier(gates.astype(BF16))
+    middle = lax.optimization_barrier((gates - high.astype(F32)).astype(BF16))
+    low = (gates - high.astype(F32) - middle.astype(F32)).astype(BF16)
+    info = jnp.stack([ids_f[:, 0].astype(BF16), high, middle, low])
+    info = jnp.pad(info, ((0, 12), (0, piece - n)))
     mine = lax.dynamic_slice_in_dim(out_proj, piece_index * piece, piece, 1)
-    projection = to_owners([mine] * exp_count)[1:]
+    depth = mine.shape[0]
+    arrivals = to_owners([jnp.concatenate([mine, info])] * exp_count)
+    projection = [x[:depth] for x in arrivals[1:]]
+    info = jnp.stack([x[depth : depth + 4, :n] for x in arrivals]).astype(F32)
+    ids_all, weights_all = info[:, 0:1], info[:, 1:2] + info[:, 2:3] + info[:, 3:4]
 
     first_column = (owner * heads_dev // group) * HEAD_SIZE
     keys = lax.dynamic_slice_in_dim(rotated_key_heads, first_column, HEAD_SIZE, 2)
@@ -554,20 +546,17 @@
     chips = [own] + [partner(own, m) for m in range(2, ctx_count, 2)]
     key_values = chips + [partner(jnp.stack(chips), 1)]
 
-    grads = place(where, ids_f.reshape(1, n), grad_out, experts, capacity)
-    grads = to_owners(after(grads, projection))
+    grads = place(ids_f.reshape(1, n), grad_out, experts, capacity)
+    grads = lax.all_to_all(grads, "exp", 0, 0, tiled=True)
 
     projection = after(jnp.stack(projection), chips)
-    projection = jnp.broadcast_to(projection[None], (pieces // 2,) + projection.shape)
-    same = lax.all_to_all(
-        projection, "ctx", 0, 0, axis_index_groups=chip_groups(pieces), tiled=True
-    )
+    same = [projection] + [partner(projection, m) for m in range(2, pieces, 2)]
 
     sent = attend(where, queries, key_values, ids_all, capacity)
-    arrived = to_owners(after(sent[0], grads[2:]))
+    arrived = to_owners(after(sent[0], grads))
     later = after(sent[1], arrived, same)
-    same = after(same, sent[0], grads[1:])
-    other = partner(same, 1)
+    same = after(same, sent[0])
+    other = partner(jnp.stack(same), 1)
 
     rows_dev = width // ctx_count
     ff = expert_gate.shape[2]

time: 263 us -> 255 us (0.970)
  waiting for transfers between devices: 112 us -> 107 us
    ppermute x21 -> x18, waiting for transfers between devices: 88 us -> 57.8 us  [to_owner(): return lax.ppermute(value, 'exp', [(i, i ^ mask) for i in range(count)])]
    ppermute x11 -> x14, waiting for transfers between devices: 24.2 us -> 47.4 us  [partner(): return lax.ppermute(value, 'ctx', [(i, i ^ mask) for i in range(count)])]
    ppermute x11 -> x14, starting transfers between devices: 5.28 us -> 10.9 us  [partner(): return lax.ppermute(value, 'ctx', [(i, i ^ mask) for i in range(count)])]
    another operation x0 -> x9, local copies, waits for them, and re-layouts: none -> 4.96 us  [the longest x3 2.9 us: on_device(): projection = after(jnp.stack(projection), chips)]
    all_to_all x2 -> x1, starting transfers between devices: 9.85 us -> 6.18 us  [on_device(): grads = lax.all_to_all(grads, 'exp', 0, 0, tiled=True)]
    ppermute x21 -> x18, starting transfers between devices: 25.9 us -> 22.5 us  [to_owner(): return lax.ppermute(value, 'exp', [(i, i ^ mask) for i in range(count)])]
    another operation x1 -> x3, other arithmetic: 0.01 us -> 3.17 us  [the longest x1 3.15 us: on_device(): other = partner(jnp.stack(same), 1)]
    broadcast_in_dim x2 -> x0, local copies, waits for them, and re-layouts: 2.67 us -> none  [the longest x1 2.08 us: on_device(): jnp.broadcast_to(projection[None], (pieces // 2,) + projection.shape)]
  transfers between devices with their start and end apart: 34 -> 33, of which waited for: 14 -> 15; matrix products, arithmetic and copies ran while one was open for 5% -> 6% of each run, Pallas kernels for 31% -> 32%
where the time goes in v9:
time: 255 us; the launch traced here: 253 us
  waiting for transfers between devices  107 us (42%)
  Pallas kernels  80.9 us (32%)
  starting transfers between devices  39.7 us (16%)
  local copies, waits for them, and re-layouts  14.1 us (6%)
  other arithmetic  10.4 us (4%)
    ppermute x18, waiting for transfers between devices, to_owner(): return lax.ppermute(value, 'exp', [(i, i ^ mask) for i in range(count)])  57.8 us
    ppermute x14, waiting for transfers between devices, partner(): return lax.ppermute(value, 'ctx', [(i, i ^ mask) for i in range(count)])  47.4 us
    pallas_call x2, Pallas kernels, expert_part(): pl.pallas_call(functools.partial(expert_kernel, pieces, experts, capacity...  36.1 us
    pallas_call x1, Pallas kernels, attend(): pl.pallas_call(functools.partial(attend_kernel, experts, capacity, heads,...  25.5 us
    ppermute x18, starting transfers between devices, to_owner(): return lax.ppermute(value, 'exp', [(i, i ^ mask) for i in range(count)])  22.5 us
    ppermute x14, starting transfers between devices, partner(): return lax.ppermute(value, 'ctx', [(i, i ^ mask) for i in range(count)])  10.9 us
    pallas_call x1, Pallas kernels, weight_blocks(): pl.pallas_call(functools.partial(weight_kernel, count), grid=(blocks,), i...  10.1 us
    all_to_all x1, starting transfers between devices, on_device(): grads = lax.all_to_all(grads, 'exp', 0, 0, tiled=True)  6.18 us
  transfers between devices with their start and end apart: 33, of which 15 were waited for; matrix products, arithmetic and copies ran while one was open for 6% of the time, Pallas kernels for 32%

profile of v9, /device:TPU:22, one launch (start us, length us, event | category | flops | bytes accessed | tf_op | source)
XLA Modules:
  0.0 253.0 jit_solution(86371382827399517)
XLA Ops:
  7.3 10.3 %collective-permute-done.5.refs_3_ = bf16[4,256,256]{2,1,0:T(8,128)(2,1)S(1)} collective-permute-done((bf16[4,256,256]{2,1,0:T(8,128)(2,1)S(1)}, bf16[4,256,256]{2,1,0:T(8,128)(2,1)S(1)}, u32[]{:S(2)}, u32[]{:S(2)}) %collective-permute-start.5) | collective-permute-done | bytes 524320 | tf_op jit(solution)/shard_map/ppermute | solution.py:469
  17.6 9.4 %collective-permute-done.4.refs_2_ = bf16[4,256,256]{2,1,0:T(8,128)(2,1)S(1)} collective-permute-done((bf16[4,256,256]{2,1,0:T(8,128)(2,1)S(1)}, bf16[4,256,256]{2,1,0:T(8,128)(2,1)S(1)}, u32[]{:S(2)}, u32[]{:S(2)}) %collective-permute-start.4) | collective-permute-done | bytes 524320 | tf_op jit(solution)/shard_map/ppermute | solution.py:469
  30.7 3.2 %place.1 = bf16[4,128,2048]{2,1,0:T(8,128)(2,1)} custom-call(f32[1,256]{1,0:T(1,128)} %bitcast.54, bf16[256,2048]{1,0:T(8,128)(2,1)} %rows_ref.1), custom_call_target="tpu_custom_call" | custom-call | flops 1000 | bytes 1000 | tf_op jit(solution)/shard_map/place/pallas_call | solution.py:193
  33.9 6.2 %all-to-all-start = ((bf16[4,128,2048]{2,1,0:T(8,128)(2,1)}), bf16[4,128,2048]{2,1,0:T(8,128)(2,1)S(1)}, u32[]{:S(2)}, u32[]{:S(2)}) async-start(bf16[4,128,2048]{2,1,0:T(8,128)(2,1)} %place.1), calls=%async_computation | async-start | bytes 4194304 | tf_op jit(solution)/shard_map/all_to_all | solution.py:550
  51.2 25.5 %attend.1 = (bf16[4,64,512]{2,1,0:T(8,128)(2,1)}, bf16[4,64,512]{2,1,0:T(8,128)(2,1)}, bf16[4,64,512]{2,1,0:T(8,128)(2,1)}, bf16[4,64,512]{2,1,0:T(8,128)(2,1)},...) custom-call(s32[3]{0:T(128)} %pad_add_fusion.where_ref, ...), custom_call_target="tpu_custom_call" | custom-call | flops 1000 | bytes 1000 | tf_op jit(solution)/shard_map/attend/pallas_call | solution.py:155
  76.7 4.8 %collective-permute-done.11.refs_8_ = bf16[3,512,256]{2,1,0:T(8,128)(2,1)} collective-permute-done((bf16[3,512,256]{2,1,0:T(8,128)(2,1)S(1)}, bf16[3,512,256]{2,1,0:T(8,128)(2,1)}, u32[]{:S(2)}, u32[]{:S(2)}) %collective-permute-start.11) | collective-permute-done | bytes 786464 | tf_op jit(solution)/shard_map/ppermute | solution.py:469
  81.5 3.1 %pad_maximum_fusion = bf16[4,3,512,256]{3,2,1,0:T(8,128)(2,1)} fusion(bf16[1,3,512,256]{3,2,1,0:T(8,128)(2,1)} %bitcast.18, bf16[1,3,512,256]{3,2,1,0:T(8,128)(2,1)} %bitcast.17, bf16[1,3,512,256]{3,2,1,0:T(8,128)(2,1)} %bitcast.16, bf16[1,3,512,256]{3,2,1,0:T(8,128)(2,1)S(1)} %bitcast.45), kind=kLoop, calls=%fused_computation | loop fusion | flops 4718592 | bytes 6291456 | tf_op jit(solution)/shard_map/stack | solution.py:559
  86.3 4.5 %collective-permute-start.7 = (bf16[4,64,512]{2,1,0:T(8,128)(2,1)}, bf16[4,64,512]{2,1,0:T(8,128)(2,1)S(1)}, u32[]{:S(2)}, u32[]{:S(2)}) collective-permute-start(bf16[4,64,512]{2,1,0:T(8,128)(2,1)} %get-tuple-element.62), channel_id=1, source_target_pairs={{0,1},{1,0},{2,3},{3,2},{4,5},{5,4},{6,7},{7,6},{8,9},{9,8},{10,11... | collective-permute-start | bytes 786440 | tf_op jit(solution)/shard_map/ppermute | solution.py:474
  92.3 8.7 %collective-permute-done.7.refs_1_ = bf16[4,64,512]{2,1,0:T(8,128)(2,1)S(1)} collective-permute-done((bf16[4,64,512]{2,1,0:T(8,128)(2,1)}, bf16[4,64,512]{2,1,0:T(8,128)(2,1)S(1)}, u32[]{:S(2)}, u32[]{:S(2)}) %collective-permute-start.7) | collective-permute-done | bytes 262176 | tf_op jit(solution)/shard_map/ppermute | solution.py:474
  101.0 7.7 %collective-permute-done.8.refs_2_ = bf16[4,64,512]{2,1,0:T(8,128)(2,1)S(1)} collective-permute-done((bf16[4,64,512]{2,1,0:T(8,128)(2,1)S(1)}, bf16[4,64,512]{2,1,0:T(8,128)(2,1)S(1)}, u32[]{:S(2)}, u32[]{:S(2)}) %collective-permute-start.8) | collective-permute-done | bytes 262176 | tf_op jit(solution)/shard_map/ppermute | solution.py:474
  108.7 6.7 %collective-permute-done.9.refs_3_ = bf16[4,64,512]{2,1,0:T(8,128)(2,1)S(1)} collective-permute-done((bf16[4,64,512]{2,1,0:T(8,128)(2,1)S(1)}, bf16[4,64,512]{2,1,0:T(8,128)(2,1)S(1)}, u32[]{:S(2)}, u32[]{:S(2)}) %collective-permute-start.9) | collective-permute-done | bytes 262176 | tf_op jit(solution)/shard_map/ppermute | solution.py:474
  115.4 2.0 collective-permute-start.21
  118.9 17.9 %expert.2 = (bf16[64,2048]{1,0:T(8,128)(2,1)}, bf16[64,2048]{1,0:T(8,128)(2,1)}, bf16[64,2048]{1,0:T(8,128)(2,1)}, bf16[64,2048]{1,0:T(8,128)(2,1)}, bf16[64,204...) custom-call(s32[3]{0:T(128)} %pad_add_fusion.where_ref, ...), custom_call_target="tpu_custom_call" | custom-call | flops 1000 | bytes 1000 | tf_op jit(solution)/shard_map/expert/pallas_call | solution.py:394
  140.4 4.4 %collective-permute-done.22.refs_3_ = bf16[4,64,512]{2,1,0:T(8,128)(2,1)S(1)} collective-permute-done((bf16[4,64,512]{2,1,0:T(8,128)(2,1)}, bf16[4,64,512]{2,1,0:T(8,128)(2,1)S(1)}, u32[]{:S(2)}, u32[]{:S(2)}) %collective-permute-start.22) | collective-permute-done | bytes 262176 | tf_op jit(solution)/shard_map/ppermute | solution.py:474
  145.5 18.2 %expert.3 = (bf16[64,4096]{1,0:T(8,128)(2,1)}, bf16[64,4096]{1,0:T(8,128)(2,1)}, bf16[64,4096]{1,0:T(8,128)(2,1)}, bf16[64,4096]{1,0:T(8,128)(2,1)}, bf16[256,43...) custom-call(s32[3]{0:T(128)} %pad_add_fusion.where_ref, bf16[4,64,512]{2,1,0:T(8,128)(2,1)} %get-tuple-element.86.refs_0_, ...), custom_call_target="tpu_custom_call" | custom-call | flops 1000 | bytes 1000 | tf_op jit(solution)/shard_map/expert/pallas_call | solution.py:394
  165.6 1.9 collective-permute-start.19
  168.9 10.1 %weight_grads.1 = (bf16[4,3,128,768]{3,2,1,0:T(8,128)(2,1)}, bf16[4,3,128,768]{3,2,1,0:T(8,128)(2,1)}) custom-call(bf16[256,4352]{1,0:T(8,128)(2,1)} %get-tuple-element.94.refs_0_.refs_4_.refs_8_.refs_12_.refs_16_, bf16[256,4352]{1,0:T(8,128)(2,1)} %copy-done, bf16[256,4352]{1,0:T(8,128)(2,1)} %get-tuple-element.96.refs_2_.refs_6_.refs_10_.refs_14_.refs_18_, ...), custom_call_target="tpu_custom_call" | custom-call | flops 1000 | bytes 1000 | tf_op jit(solution)/shard_map/weight_grads/pallas_call | solution.py:455
  179.0 4.7 %collective-permute-done.18.refs_6_ = bf16[64,2048]{1,0:T(8,128)(2,1)S(1)} collective-permute-done((bf16[64,2048]{1,0:T(8,128)(2,1)}, bf16[64,2048]{1,0:T(8,128)(2,1)S(1)}, u32[]{:S(2)}, u32[]{:S(2)}) %collective-permute-start.18) | collective-permute-done | bytes 262176 | tf_op jit(solution)/shard_map/ppermute | solution.py:474
  183.7 7.2 %collective-permute-done.19.refs_7_ = bf16[64,2048]{1,0:T(8,128)(2,1)S(1)} collective-permute-done((bf16[64,2048]{1,0:T(8,128)(2,1)}, bf16[64,2048]{1,0:T(8,128)(2,1)S(1)}, u32[]{:S(2)}, u32[]{:S(2)}) %collective-permute-start.19) | collective-permute-done | bytes 262176 | tf_op jit(solution)/shard_map/ppermute | solution.py:474
  196.1 1.8 collective-permute-start.25
  197.9 21.8 %collective-permute-done.29 = bf16[2,3,128,768]{3,2,1,0:T(8,128)(2,1)S(1)} collective-permute-done((bf16[2,3,128,768]{3,2,1,0:T(8,128)(2,1)S(1)}, bf16[2,3,128,768]{3,2,1,0:T(8,128)(2,1)S(1)}, u32[]{:S(2)}, u32[]{:S(2)}) %collective-permute-start.29) | collective-permute-done | bytes 1179680 | tf_op jit(solution)/shard_map/ppermute | solution.py:469
  225.1 6.2 %collective-permute-done.24.refs_10_ = bf16[64,4096]{1,0:T(8,128)(2,1)} collective-permute-done((bf16[64,4096]{1,0:T(8,128)(2,1)}, bf16[64,4096]{1,0:T(8,128)(2,1)}, u32[]{:S(2)}, u32[]{:S(2)}) %collective-permute-start.24) | collective-permute-done | bytes 524320 | tf_op jit(solution)/shard_map/ppermute | solution.py:474
  231.3 11.0 %collective-permute-done.25.refs_11_ = bf16[64,4096]{1,0:T(8,128)(2,1)} collective-permute-done((bf16[64,4096]{1,0:T(8,128)(2,1)}, bf16[64,4096]{1,0:T(8,128)(2,1)}, u32[]{:S(2)}, u32[]{:S(2)}) %collective-permute-start.25) | collective-permute-done | bytes 524320 | tf_op jit(solution)/shard_map/ppermute | solution.py:474
  242.3 6.0 %restore.1 = (bf16[256,2048]{1,0:T(8,128)(2,1)}, bf16[256,2048]{1,0:T(8,128)(2,1)}) custom-call(s32[3]{0:T(128)} %pad_add_fusion.where_ref, f32[256,1]{1,0:T(8,128)} %convert_element_type.60.ids_ref, bf16[64,2048]{1,0:T(8,128)(2,1)} %get-tuple-element.70.refs_0_, bf16[64,2048]{1,0:T(8,128)(2,1)} %copy-done.11, bf16[64,2048]{1,0:T(8,128)(2,1)} %copy-done.12, ...), custom_call_target="tpu_custom_call" | custom-call | flops 1000 | bytes 1000 | tf_op jit(solution)/shard_map/restore/pallas_call | solution.py:238
  (143 shorter events, 48.6 us)
Async XLA Ops:
  2.4 24.6 %collective-permute-start.4 = (bf16[4,256,256]{2,1,0:T(8,128)(2,1)S(1)}, bf16[4,256,256]{2,1,0:T(8,128)(2,1)S(1)}, u32[]{:S(2)}, u32[]{:S(2)}) collective-permute-start(bf16[4,256,256]{2,1,0:T(8,128)(2,1)S(1)} %get-tuple-element.113.refs_0_), channel_id=1, source_target_pairs={{0,16},{4,20},{8,24},{12,28},{16,0},{20,4},{24,8},{28,12},{1,17},{... | collective-permute-start | bytes 1572872 | tf_op jit(solution)/shard_map/ppermute | solution.py:469
  3.9 23.1 %collective-permute-start.3 = (bf16[4,256,256]{2,1,0:T(8,128)(2,1)S(1)}, bf16[4,256,256]{2,1,0:T(8,128)(2,1)S(1)}, u32[]{:S(2)}, u32[]{:S(2)}) collective-permute-start(bf16[4,256,256]{2,1,0:T(8,128)(2,1)S(1)} %get-tuple-element.113.refs_0_), channel_id=1, source_target_pairs={{0,8},{4,12},{8,0},{12,4},{16,24},{20,28},{24,16},{28,20},{1,9},{5... | collective-permute-start | bytes 1572872 | tf_op jit(solution)/shard_map/ppermute | solution.py:469
  6.8 34.0 %collective-permute-start.2 = (bf16[528,256]{1,0:T(8,128)(2,1)S(1)}, bf16[528,256]{1,0:T(8,128)(2,1)}, u32[]{:S(2)}, u32[]{:S(2)}) collective-permute-start(bf16[528,256]{1,0:T(8,128)(2,1)S(1)} %fusion.7), channel_id=1, source_target_pairs={{0,3},{1,2},{2,1},{3,0},{4,7},{5,6},{6,5},{7,4},{8,11},{9,10},{10,... | collective-permute-start | bytes 811016 | tf_op jit(solution)/shard_map/ppermute | solution.py:474
  33.9 52.4 %all-to-all-start = ((bf16[4,128,2048]{2,1,0:T(8,128)(2,1)}), bf16[4,128,2048]{2,1,0:T(8,128)(2,1)S(1)}, u32[]{:S(2)}, u32[]{:S(2)}) async-start(bf16[4,128,2048]{2,1,0:T(8,128)(2,1)} %place.1), calls=%async_computation | async-start | bytes 4194304 | tf_op jit(solution)/shard_map/all_to_all | solution.py:550
  45.0 31.7 %collective-permute-start.12 = (bf16[3,512,256]{2,1,0:T(8,128)(2,1)S(1)}, bf16[3,512,256]{2,1,0:T(8,128)(2,1)}, u32[]{:S(2)}, u32[]{:S(2)}) collective-permute-start(bf16[3,512,256]{2,1,0:T(8,128)(2,1)S(1)} %pad_maximum_fusion.3.refs_6_), channel_id=1, source_target_pairs={{0,24},{4,28},{8,16},{12,20},{16,8},{20,12},{24,0},{28,4},{1,25},{... | collective-permute-start | bytes 2359304 | tf_op jit(solution)/shard_map/ppermute | solution.py:469
  46.2 35.3 %collective-permute-start.11 = (bf16[3,512,256]{2,1,0:T(8,128)(2,1)S(1)}, bf16[3,512,256]{2,1,0:T(8,128)(2,1)}, u32[]{:S(2)}, u32[]{:S(2)}) collective-permute-start(bf16[3,512,256]{2,1,0:T(8,128)(2,1)S(1)} %pad_maximum_fusion.3.refs_6_), channel_id=1, source_target_pairs={{0,16},{4,20},{8,24},{12,28},{16,0},{20,4},{24,8},{28,12},{1,17},{... | collective-permute-start | bytes 2359304 | tf_op jit(solution)/shard_map/ppermute | solution.py:469
  47.7 33.8 %collective-permute-start.10 = (bf16[3,512,256]{2,1,0:T(8,128)(2,1)S(1)}, bf16[3,512,256]{2,1,0:T(8,128)(2,1)}, u32[]{:S(2)}, u32[]{:S(2)}) collective-permute-start(bf16[3,512,256]{2,1,0:T(8,128)(2,1)S(1)} %pad_maximum_fusion.3.refs_6_), channel_id=1, source_target_pairs={{0,8},{4,12},{8,0},{12,4},{16,24},{20,28},{24,16},{28,20},{1,9},{5... | collective-permute-start | bytes 2359304 | tf_op jit(solution)/shard_map/ppermute | solution.py:469
  84.7 34.2 %collective-permute-start.13 = (bf16[4,3,512,256]{3,2,1,0:T(8,128)(2,1)}, bf16[4,3,512,256]{3,2,1,0:T(8,128)(2,1)}, u32[]{:S(2)}, u32[]{:S(2)}) collective-permute-start(bf16[4,3,512,256]{3,2,1,0:T(8,128)(2,1)} %pad_maximum_fusion), channel_id=1, source_target_pairs={{0,4},{4,0},{8,12},{12,8},{16,20},{20,16},{24,28},{28,24},{1,5},{5... | collective-permute-start | bytes 9437192 | tf_op jit(solution)/shard_map/ppermute | solution.py:469
  90.8 24.7 %collective-permute-start.9 = (bf16[4,64,512]{2,1,0:T(8,128)(2,1)S(1)}, bf16[4,64,512]{2,1,0:T(8,128)(2,1)S(1)}, u32[]{:S(2)}, u32[]{:S(2)}) collective-permute-start(bf16[4,64,512]{2,1,0:T(8,128)(2,1)S(1)} %copy-done.26), channel_id=1, source_target_pairs={{0,3},{1,2},{2,1},{3,0},{4,7},{5,6},{6,5},{7,4},{8,11},{9,10},{10,... | collective-permute-start | bytes 786440 | tf_op jit(solution)/shard_map/ppermute | solution.py:474
  115.4 23.5 %collective-permute-start.20 = (bf16[4,64,512]{2,1,0:T(8,128)(2,1)}, bf16[4,64,512]{2,1,0:T(8,128)(2,1)S(1)}, u32[]{:S(2)}, u32[]{:S(2)}) collective-permute-start(bf16[4,64,512]{2,1,0:T(8,128)(2,1)} %get-tuple-element.87), channel_id=1, source_target_pairs={{0,1},{1,0},{2,3},{3,2},{4,5},{5,4},{6,7},{7,6},{8,9},{9,8},{10,11... | collective-permute-start | bytes 786440 | tf_op jit(solution)/shard_map/ppermute | solution.py:474
  115.4 25.0 %collective-permute-start.21 = (bf16[4,64,512]{2,1,0:T(8,128)(2,1)}, bf16[4,64,512]{2,1,0:T(8,128)(2,1)S(1)}, u32[]{:S(2)}, u32[]{:S(2)}) collective-permute-start(bf16[4,64,512]{2,1,0:T(8,128)(2,1)} %get-tuple-element.88), channel_id=1, source_target_pairs={{0,2},{1,3},{2,0},{3,1},{4,6},{5,7},{6,4},{7,5},{8,10},{9,11},{10,... | collective-permute-start | bytes 786440 | tf_op jit(solution)/shard_map/ppermute | solution.py:474
  117.4 27.4 %collective-permute-start.22 = (bf16[4,64,512]{2,1,0:T(8,128)(2,1)}, bf16[4,64,512]{2,1,0:T(8,128)(2,1)S(1)}, u32[]{:S(2)}, u32[]{:S(2)}) collective-permute-start(bf16[4,64,512]{2,1,0:T(8,128)(2,1)} %get-tuple-element.89), channel_id=1, source_target_pairs={{0,3},{1,2},{2,1},{3,0},{4,7},{5,6},{6,5},{7,4},{8,11},{9,10},{10,... | collective-permute-start | bytes 786440 | tf_op jit(solution)/shard_map/ppermute | solution.py:474
  136.9 26.9 %collective-permute-start.14 = (bf16[64,2048]{1,0:T(8,128)(2,1)}, bf16[64,2048]{1,0:T(8,128)(2,1)S(1)}, u32[]{:S(2)}, u32[]{:S(2)}) collective-permute-start(bf16[64,2048]{1,0:T(8,128)(2,1)} %get-tuple-element.71), channel_id=1, source_target_pairs={{0,1},{1,0},{2,3},{3,2},{4,5},{5,4},{6,7},{7,6},{8,9},{9,8},{10,11... | collective-permute-start | bytes 786440 | tf_op jit(solution)/shard_map/ppermute | solution.py:474
  137.8 26.0 %collective-permute-start.15 = (bf16[64,2048]{1,0:T(8,128)(2,1)}, bf16[64,2048]{1,0:T(8,128)(2,1)S(1)}, u32[]{:S(2)}, u32[]{:S(2)}) collective-permute-start(bf16[64,2048]{1,0:T(8,128)(2,1)} %get-tuple-element.72), channel_id=1, source_target_pairs={{0,2},{1,3},{2,0},{3,1},{4,6},{5,7},{6,4},{7,5},{8,10},{9,11},{10,... | collective-permute-start | bytes 786440 | tf_op jit(solution)/shard_map/ppermute | solution.py:474
  138.9 24.9 %collective-permute-start.16 = (bf16[64,2048]{1,0:T(8,128)(2,1)}, bf16[64,2048]{1,0:T(8,128)(2,1)S(1)}, u32[]{:S(2)}, u32[]{:S(2)}) collective-permute-start(bf16[64,2048]{1,0:T(8,128)(2,1)} %get-tuple-element.73), channel_id=1, source_target_pairs={{0,3},{1,2},{2,1},{3,0},{4,7},{5,6},{6,5},{7,4},{8,11},{9,10},{10,... | collective-permute-start | bytes 786440 | tf_op jit(solution)/shard_map/ppermute | solution.py:474
  140.4 27.0 %collective-permute-start.26 = (bf16[256,4352]{1,0:T(8,128)(2,1)}, bf16[256,4352]{1,0:T(8,128)(2,1)S(1)}, u32[]{:S(2)}, u32[]{:S(2)}) collective-permute-start(bf16[256,4352]{1,0:T(8,128)(2,1)} %get-tuple-element.95), channel_id=1, source_target_pairs={{0,4},{4,0},{8,12},{12,8},{16,20},{20,16},{24,28},{28,24},{1,5},{5... | collective-permute-start | bytes 6684680 | tf_op jit(solution)/shard_map/ppermute | solution.py:469
  165.6 25.3 %collective-permute-start.19 = (bf16[64,2048]{1,0:T(8,128)(2,1)}, bf16[64,2048]{1,0:T(8,128)(2,1)S(1)}, u32[]{:S(2)}, u32[]{:S(2)}) collective-permute-start(bf16[64,2048]{1,0:T(8,128)(2,1)} %get-tuple-element.81), channel_id=1, source_target_pairs={{0,3},{1,2},{2,1},{3,0},{4,7},{5,6},{6,5},{7,4},{8,11},{9,10},{10,... | collective-permute-start | bytes 786440 | tf_op jit(solution)/shard_map/ppermute | solution.py:474
  192.4 27.3 %collective-permute-start.29 = (bf16[2,3,128,768]{3,2,1,0:T(8,128)(2,1)S(1)}, bf16[2,3,128,768]{3,2,1,0:T(8,128)(2,1)S(1)}, u32[]{:S(2)}, u32[]{:S(2)}) collective-permute-start(bf16[2,3,128,768]{3,2,1,0:T(8,128)(2,1)S(1)} %slice.80), channel_id=1, source_target_pairs={{0,16},{4,20},{8,24},{12,28},{16,0},{20,4},{24,8},{28,12},{1,17},{... | collective-permute-start | bytes 3538952 | tf_op jit(solution)/shard_map/ppermute | solution.py:469
  193.8 28.3 %collective-permute-start.28 = (bf16[2,3,128,768]{3,2,1,0:T(8,128)(2,1)S(1)}, bf16[2,3,128,768]{3,2,1,0:T(8,128)(2,1)S(1)}, u32[]{:S(2)}, u32[]{:S(2)}) collective-permute-start(bf16[2,3,128,768]{3,2,1,0:T(8,128)(2,1)S(1)} %slice.77), channel_id=1, source_target_pairs={{0,8},{4,12},{8,0},{12,4},{16,24},{20,28},{24,16},{28,20},{1,9},{5... | collective-permute-start | bytes 3538952 | tf_op jit(solution)/shard_map/ppermute | solution.py:469
  194.4 30.7 %collective-permute-start.23 = (bf16[64,4096]{1,0:T(8,128)(2,1)}, bf16[64,4096]{1,0:T(8,128)(2,1)}, u32[]{:S(2)}, u32[]{:S(2)}) collective-permute-start(bf16[64,4096]{1,0:T(8,128)(2,1)} %get-tuple-element.91), channel_id=1, source_target_pairs={{0,1},{1,0},{2,3},{3,2},{4,5},{5,4},{6,7},{7,6},{8,9},{9,8},{10,11... | collective-permute-start | bytes 1572872 | tf_op jit(solution)/shard_map/ppermute | solution.py:474
  194.4 36.8 %collective-permute-start.24 = (bf16[64,4096]{1,0:T(8,128)(2,1)}, bf16[64,4096]{1,0:T(8,128)(2,1)}, u32[]{:S(2)}, u32[]{:S(2)}) collective-permute-start(bf16[64,4096]{1,0:T(8,128)(2,1)} %get-tuple-element.92), channel_id=1, source_target_pairs={{0,2},{1,3},{2,0},{3,1},{4,6},{5,7},{6,4},{7,5},{8,10},{9,11},{10,... | collective-permute-start | bytes 1572872 | tf_op jit(solution)/shard_map/ppermute | solution.py:474
  196.1 46.2 %collective-permute-start.25 = (bf16[64,4096]{1,0:T(8,128)(2,1)}, bf16[64,4096]{1,0:T(8,128)(2,1)}, u32[]{:S(2)}, u32[]{:S(2)}) collective-permute-start(bf16[64,4096]{1,0:T(8,128)(2,1)} %get-tuple-element.93), channel_id=1, source_target_pairs={{0,3},{1,2},{2,1},{3,0},{4,7},{5,6},{6,5},{7,4},{8,11},{9,10},{10,... | collective-permute-start | bytes 1572872 | tf_op jit(solution)/shard_map/ppermute | solution.py:474
  220.9 27.4 %collective-permute-start.31 = (bf16[3,128,768]{2,1,0:T(8,128)(2,1)}, bf16[3,128,768]{2,1,0:T(8,128)(2,1)}, u32[]{:S(2)}, u32[]{:S(2)}) collective-permute-start(bf16[3,128,768]{2,1,0:T(8,128)(2,1)} %fusion.5), channel_id=1, source_target_pairs={{0,8},{4,12},{8,0},{12,4},{16,24},{20,28},{24,16},{28,20},{1,9},{5... | collective-permute-start | bytes 1769480 | tf_op jit(solution)/shard_map/ppermute | solution.py:469
  223.8 25.7 %collective-permute-start.30 = (bf16[3,128,768]{2,1,0:T(8,128)(2,1)S(1)}, bf16[3,128,768]{2,1,0:T(8,128)(2,1)S(1)}, u32[]{:S(2)}, u32[]{:S(2)}) collective-permute-start(bf16[3,128,768]{2,1,0:T(8,128)(2,1)S(1)} %fusion.4), channel_id=1, source_target_pairs={{0,16},{4,20},{8,24},{12,28},{16,0},{20,4},{24,8},{28,12},{1,17},{... | collective-permute-start | bytes 1769480 | tf_op jit(solution)/shard_map/ppermute | solution.py:469
  (37 other events, 479.6 us)

commit v10 on v9

--- a/solution.py
+++ b/solution.py
@@ -68,11 +68,17 @@
     return pl.BlockSpec(shape, lambda *_: (0,) * len(shape))
 
 
+def route_rows(route, n):
+    last = route.shape[0] // 16 - 1
+    return pl.BlockSpec((16, n), lambda *_: (last, 0))
+
+
 def smem():
     return pl.BlockSpec(memory_space=pltpu.SMEM)
 
 
-def attend_kernel(experts, capacity, heads, n_ctx, where_ref, q_ref, ids_ref, *refs):
+def attend_kernel(experts, capacity, heads, n_ctx, where_ref, q_ref, *refs):
+    route_refs, refs = refs[:experts], refs[experts:]
     count = n_ctx // 2 + 1
     *chips, cores = refs[:count]
     refs = refs[count:]
@@ -80,7 +86,7 @@
     for j, chip in enumerate(chips):
         blocks += [chip, cores.at[j]]
     out_refs, refs = refs[: experts * PARTS], refs[experts * PARTS :]
-    k_scr, v_scr, best_scr, acc_scr, att_scr = refs
+    k_scr, v_scr, best_scr, acc_scr, att_scr, ids_scr = refs
     ctx, owner = where_ref[0], where_ref[1]
     seq = pl.program_id(0)
     block = q_ref.shape[1]
@@ -90,6 +96,8 @@
     @pl.when(seq == 0)
     def _():
         v_scr[:, :, HEAD_SIZE:] = jnp.ones((n_ctx, block, HEAD_SIZE), BF16)
+        for d, ref in enumerate(route_refs):
+            ids_scr[d] = ref[...].astype(F32)[0:1]
 
     for m in range(n_ctx):
         index = jnp.bitwise_xor(ctx, m)
@@ -129,14 +137,14 @@
         att = acc[:, :HEAD_SIZE] / acc[:, HEAD_SIZE:]
         att_scr[:, h * HEAD_SIZE : (h + 1) * HEAD_SIZE] = att.astype(BF16)
 
-    n = ids_ref.shape[2]
+    n = ids_scr.shape[2]
     part = capacity // PARTS
     per_seq = block // n
     position = iota((experts * capacity, n), 0)
     slots = shifted_slots(position, owner, experts, capacity)
     for b in range(per_seq):
         source = seq * per_seq + b
-        target = slots_row(ids_ref[jnp.bitwise_xor(owner, source)], capacity)
+        target = slots_row(ids_scr[jnp.bitwise_xor(owner, source)], capacity)
         picked = dot(one_hot(slots == target), att_scr[b * n : (b + 1) * n, :]).astype(BF16)
         for d in range(experts):
             rank = jnp.bitwise_xor(jnp.bitwise_xor(owner, d), source)
@@ -145,10 +153,10 @@
                 out_refs[c * experts + d][rank] = picked[first : first + part]
 
 
-def attend(where, queries, key_values, ids, capacity):
+def attend(where, queries, key_values, routes, n, capacity):
     seqs, block, width = queries.shape
     n_ctx = 2 * (len(key_values) - 1)
-    experts, _, n = ids.shape
+    experts = len(routes)
     heads = width // HEAD_SIZE
     part = capacity // PARTS
     by_seq = pl.BlockSpec((1, block, 2 * HEAD_SIZE), lambda s: (s, 0, 0))
@@ -158,8 +166,8 @@
         in_specs=[
             smem(),
             pl.BlockSpec((1, block, width), lambda s: (s, 0, 0)),
-            whole(experts, 1, n),
         ]
+        + [route_rows(x, n) for x in routes]
         + [by_seq] * (len(key_values) - 1)
         + [pl.BlockSpec((n_ctx // 2, 1, block, 2 * HEAD_SIZE), lambda s: (0, s, 0, 0))],
         out_specs=[whole(experts, part, width)] * (PARTS * experts),
@@ -169,12 +177,13 @@
             pltpu.VMEM((heads, block, 1), F32),
             pltpu.VMEM((heads, block, 2 * HEAD_SIZE), F32),
             pltpu.VMEM((block, width), BF16),
+            pltpu.VMEM((experts, 1, n), F32),
         ],
         out_shape=[jax.ShapeDtypeStruct((experts, part, width), BF16)] * (PARTS * experts),
         compiler_params=kernel_params(),
         cost_estimate=brief(),
         name="attend",
-    )(where, queries, ids, *key_values)
+    )(where, queries, *routes, *key_values)
     return [outs[c * experts : (c + 1) * experts] for c in range(PARTS)]
 
 
@@ -254,8 +263,8 @@
     width_of = grad_ref.shape[2]
     own_ref, refs = refs[0], refs[1:]
     same_hbms, refs = refs[: pieces // 2], refs[pieces // 2 :]
-    other_hbm, gate_hbm, up_hbm, down_hbm = refs[:4]
-    gain_ref, ids_ref, weight_ref, refs = refs[4], refs[5], refs[6], refs[7:]
+    other_hbm, gate_hbm, up_hbm, down_hbm, gain_ref = refs[:5]
+    route_refs, refs = refs[5 : 5 + experts], refs[5 + experts :]
     if part_index == 0:
         layer_refs, refs = refs[:experts], refs[experts:]
         change_refs, refs = refs[:experts], refs[experts:]
@@ -289,14 +298,15 @@
     for copy in weight_copies:
         copy.start()
 
-    n = ids_ref.shape[2]
+    n = route_refs[0].shape[1]
     weights = []
     for s, source in enumerate(sources):
-        target = slots_row(ids_ref[s], capacity)
+        route = route_refs[s][...].astype(F32)
+        target = slots_row(route[0:1], capacity)
         slot = iota((part, n), 0) + (owner * capacity + part_index * part)
         weights.append(
             jnp.sum(
-                jnp.where(slot.astype(F32) == target, weight_ref[s], 0.0),
+                jnp.where(slot.astype(F32) == target, route[1:2] + route[2:3] + route[3:4], 0.0),
                 axis=1,
                 keepdims=True,
             )
@@ -309,7 +319,7 @@
         column = pl.multiple_of(jnp.bitwise_xor(where_ref[2], m) * piece, piece)
         total = jnp.zeros((rows, piece), F32)
         for d in range(experts):
-            block = own_ref[:, pl.ds(column, piece)] if d == 0 else w_scr[m, d - 1]
+            block = own_ref[:, pl.ds(column, piece)] if d == 0 else w_scr[m, d - 1, :att_cols]
             total += dot(att_refs[d][...].reshape(rows, att_cols), block)
         hidden_scr[:, pl.ds(column, piece)] = total.astype(BF16)
 
@@ -378,7 +388,7 @@
 
 
 def expert_part(
-    where, att, grads, own, same, other, gate, up, down, gain, ids, weights, capacity, swap, index
+    where, att, grads, own, same, other, gate, up, down, gain, routes, n, capacity, swap, index
 ):
     experts, part, att_cols = att[0].shape
     pieces = 2 * len(same)
@@ -386,7 +396,6 @@
     width = grads.shape[2]
     ff = gate.shape[2]
     rows = experts * part
-    n = ids.shape[2]
     half = width // 2 if swap else width
     out = lambda *shape: jax.ShapeDtypeStruct(shape, BF16)
     rows_out = [out(part, width)] * (2 * experts) if index == 0 else [out(part, 2 * width)] * experts
@@ -399,11 +408,12 @@
         + [pl.BlockSpec((experts, part, width), lambda i: (0, index, 0))]
         + [whole(*own.shape)]
         + [in_hbm] * (len(same) + 4)
-        + [whole(1, width), whole(experts, 1, n), whole(experts, 1, n)],
+        + [whole(1, width)]
+        + [route_rows(x, n) for x in routes],
         out_specs=[whole(*x.shape) for x in rows_out]
         + [whole(rows, 3 * ff + 2 * half)] * (1 + swap),
         scratch_shapes=[
-            pltpu.VMEM((pieces, experts - 1, att_cols, piece), BF16),
+            pltpu.VMEM((pieces,) + same[0].shape, BF16),
             pltpu.VMEM((width, ff), BF16),
             pltpu.VMEM((width, ff), BF16),
             pltpu.VMEM((ff, width), BF16),
@@ -418,7 +428,7 @@
         compiler_params=kernel_params(),
         cost_estimate=brief(),
         name="expert",
-    )(where, *att, grads, own, *same, other, gate, up, down, gain, ids, weights)
+    )(where, *att, grads, own, *same, other, gate, up, down, gain, *routes)
     return outs[: len(rows_out)], outs[len(rows_out) :]
 
 
@@ -533,26 +543,22 @@
     info = jnp.stack([ids_f[:, 0].astype(BF16), high, middle, low])
     info = jnp.pad(info, ((0, 12), (0, piece - n)))
     mine = lax.dynamic_slice_in_dim(out_proj, piece_index * piece, piece, 1)
-    depth = mine.shape[0]
-    arrivals = to_owners([jnp.concatenate([mine, info])] * exp_count)
-    projection = [x[:depth] for x in arrivals[1:]]
-    info = jnp.stack([x[depth : depth + 4, :n] for x in arrivals]).astype(F32)
-    ids_all, weights_all = info[:, 0:1], info[:, 1:2] + info[:, 2:3] + info[:, 3:4]
+    routes = to_owners([jnp.concatenate([mine, info])] * exp_count)
 
     first_column = (owner * heads_dev // group) * HEAD_SIZE
     keys = lax.dynamic_slice_in_dim(rotated_key_heads, first_column, HEAD_SIZE, 2)
     values = lax.dynamic_slice_in_dim(value_head_rows, first_column, HEAD_SIZE, 2)
     own = jnp.concatenate([keys, values], axis=2)
     chips = [own] + [partner(own, m) for m in range(2, ctx_count, 2)]
-    key_values = chips + [partner(jnp.stack(chips), 1)]
 
     grads = place(ids_f.reshape(1, n), grad_out, experts, capacity)
+    key_values = chips + [partner(after(jnp.stack(chips), routes[1:], grads), 1)]
     grads = lax.all_to_all(grads, "exp", 0, 0, tiled=True)
 
-    projection = after(jnp.stack(projection), chips)
+    projection = after(jnp.stack(routes[1:]), chips)
     same = [projection] + [partner(projection, m) for m in range(2, pieces, 2)]
 
-    sent = attend(where, queries, key_values, ids_all, capacity)
+    sent = attend(where, queries, key_values, routes, n, capacity)
     arrived = to_owners(after(sent[0], grads))
     later = after(sent[1], arrived, same)
     same = after(same, sent[0])
@@ -574,8 +580,8 @@
             expert_up,
             expert_down,
             norm_gain.reshape(1, width),
-            ids_all,
-            weights_all,
+            routes,
+            n,
             capacity,
             swap,
             index,
@@ -618,7 +624,7 @@
                 (part_down, (ff, rows_dev)),
             )
         ]
-    layer_out, grad_hidden = restore(where, ids_f, layer_a, change_a, packed, experts, capacity)
+    layer_out, grad_hidden = restore(where, after(ids_f, grad_gate, grad_up, grad_down), layer_a, change_a, packed, experts, capacity)
     return (layer_out, grad_hidden, grad_gate, grad_up, grad_down)
 
 

time: 255 us -> 251 us (0.984); the launches traced: 253 us -> 246 us
  local copies, waits for them, and re-layouts: 14.1 us -> 7.87 us
    all_to_all x1, waiting for transfers between devices: 1.57 us -> 14.1 us  [on_device(): grads = lax.all_to_all(grads, 'exp', 0, 0, tiled=True)]
    ppermute x14, waiting for transfers between devices: 47.4 us -> 35.1 us  [partner(): return lax.ppermute(value, 'ctx', [(i, i ^ mask) for i in range(count)])]
    another operation x6 -> x0, local copies, waits for them, and re-layouts: 4.94 us -> none  [the longest x3 2.9 us: on_device(): projection = after(jnp.stack(projection), chips)]
  transfers between devices with their start and end apart: 33 -> 33, of which waited for: 15 -> 15; matrix products, arithmetic and copies ran while one was open for 6% -> 3% of each run, Pallas kernels for 32% -> 30%
where the time goes in v10:
time: 251 us; the launch traced here: 246 us
  waiting for transfers between devices  106 us (42%)
  Pallas kernels  80.9 us (32%)
  starting transfers between devices  41.8 us (17%)
  other arithmetic  8.59 us (3%)
  local copies, waits for them, and re-layouts  7.87 us (3%)
    ppermute x18, waiting for transfers between devices, to_owner(): return lax.ppermute(value, 'exp', [(i, i ^ mask) for i in range(count)])  56.5 us
    pallas_call x2, Pallas kernels, expert_part(): pl.pallas_call(functools.partial(expert_kernel, pieces, experts, capacity...  36.1 us
    ppermute x14, waiting for transfers between devices, partner(): return lax.ppermute(value, 'ctx', [(i, i ^ mask) for i in range(count)])  35.1 us
    pallas_call x1, Pallas kernels, attend(): pl.pallas_call(functools.partial(attend_kernel, experts, capacity, heads,...  25.5 us
    ppermute x18, starting transfers between devices, to_owner(): return lax.ppermute(value, 'exp', [(i, i ^ mask) for i in range(count)])  24.7 us
    all_to_all x1, waiting for transfers between devices, on_device(): grads = lax.all_to_all(grads, 'exp', 0, 0, tiled=True)  14.1 us
    pallas_call x1, Pallas kernels, weight_blocks(): pl.pallas_call(functools.partial(weight_kernel, count), grid=(blocks,), i...  10 us
    ppermute x14, starting transfers between devices, partner(): return lax.ppermute(value, 'ctx', [(i, i ^ mask) for i in range(count)])  9.93 us
  transfers between devices with their start and end apart: 33, of which 15 were waited for; matrix products, arithmetic and copies ran while one was open for 3% of the time, Pallas kernels for 30%

profile of v10, /device:TPU:22, one launch (start us, length us, event | category | flops | bytes accessed | tf_op | source)
XLA Modules:
  0.0 246.3 jit_solution(17705223474504437680)
XLA Ops:
  7.3 3.5 %collective-permute-start.1 = (bf16[528,256]{1,0:T(8,128)(2,1)S(1)}, bf16[528,256]{1,0:T(8,128)(2,1)S(1)}, u32[]{:S(2)}, u32[]{:S(2)}) collective-permute-start(bf16[528,256]{1,0:T(8,128)(2,1)S(1)} %pad_maximum_fusion.5.refs_0_.refs_15_), channel_id=1, source_target_pairs={{0,2},{1,3},{2,0},{3,1},{4,6},{5,7},{6,4},{7,5},{8,10},{9,11},{10,... | collective-permute-start | bytes 811016 | tf_op jit(solution)/shard_map/ppermute | solution.py:484
  10.8 6.8 %collective-permute-done.5.refs_7_ = bf16[4,256,256]{2,1,0:T(8,128)(2,1)S(1)} collective-permute-done((bf16[4,256,256]{2,1,0:T(8,128)(2,1)S(1)}, bf16[4,256,256]{2,1,0:T(8,128)(2,1)S(1)}, u32[]{:S(2)}, u32[]{:S(2)}) %collective-permute-start.5) | collective-permute-done | bytes 524320 | tf_op jit(solution)/shard_map/ppermute | solution.py:479
  19.2 3.2 %place.1 = bf16[4,128,2048]{2,1,0:T(8,128)(2,1)} custom-call(f32[1,256]{1,0:T(1,128)} %bitcast.46, bf16[256,2048]{1,0:T(8,128)(2,1)} %rows_ref.1), custom_call_target="tpu_custom_call" | custom-call | flops 1000 | bytes 1000 | tf_op jit(solution)/shard_map/place/pallas_call | solution.py:202
  22.4 4.6 %collective-permute-done.4.refs_6_ = bf16[4,256,256]{2,1,0:T(8,128)(2,1)S(1)} collective-permute-done((bf16[4,256,256]{2,1,0:T(8,128)(2,1)S(1)}, bf16[4,256,256]{2,1,0:T(8,128)(2,1)S(1)}, u32[]{:S(2)}, u32[]{:S(2)}) %collective-permute-start.4) | collective-permute-done | bytes 524320 | tf_op jit(solution)/shard_map/ppermute | solution.py:479
  33.3 7.2 %all-to-all-start = ((bf16[4,128,2048]{2,1,0:T(8,128)(2,1)}), bf16[4,128,2048]{2,1,0:T(8,128)(2,1)S(1)}, u32[]{:S(2)}, u32[]{:S(2)}) async-start(bf16[4,128,2048]{2,1,0:T(8,128)(2,1)} %place.1), calls=%async_computation | async-start | bytes 4194304 | tf_op jit(solution)/shard_map/all_to_all | solution.py:556
  41.2 25.5 %attend.1 = (bf16[4,64,512]{2,1,0:T(8,128)(2,1)}, bf16[4,64,512]{2,1,0:T(8,128)(2,1)}, bf16[4,64,512]{2,1,0:T(8,128)(2,1)}, bf16[4,64,512]{2,1,0:T(8,128)(2,1)},...) custom-call(s32[3]{0:T(128)} %pad_add_fusion.where_ref, ...), custom_call_target="tpu_custom_call" | custom-call | flops 1000 | bytes 1000 | tf_op jit(solution)/shard_map/attend/pallas_call | solution.py:163
  68.0 3.2 %pad_maximum_fusion = bf16[4,3,528,256]{3,2,1,0:T(8,128)(2,1)} fusion(bf16[1,3,528,256]{3,2,1,0:T(8,128)(2,1)} %bitcast.14, bf16[1,3,528,256]{3,2,1,0:T(8,128)(2,1)} %bitcast.13, bf16[1,3,528,256]{3,2,1,0:T(8,128)(2,1)} %bitcast.12, bf16[1,3,528,256]{3,2,1,0:T(8,128)(2,1)S(1)} %bitcast.34), kind=kLoop, calls=%fused_computation | loop fusion | flops 4866048 | bytes 6488064 | tf_op jit(solution)/shard_map/stack | solution.py:565
  71.2 14.1 %all-to-all-done.refs_4_ = bf16[4,128,2048]{2,1,0:T(8,128)(2,1)S(1)} async-done(((bf16[4,128,2048]{2,1,0:T(8,128)(2,1)}), bf16[4,128,2048]{2,1,0:T(8,128)(2,1)S(1)}, u32[]{:S(2)}, u32[]{:S(2)}) %all-to-all-start) | async-done | bytes 2097184 | tf_op jit(solution)/shard_map/all_to_all | solution.py:556
  89.3 7.7 %collective-permute-done.7.refs_1_ = bf16[4,64,512]{2,1,0:T(8,128)(2,1)S(1)} collective-permute-done((bf16[4,64,512]{2,1,0:T(8,128)(2,1)}, bf16[4,64,512]{2,1,0:T(8,128)(2,1)S(1)}, u32[]{:S(2)}, u32[]{:S(2)}) %collective-permute-start.7) | collective-permute-done | bytes 262176 | tf_op jit(solution)/shard_map/ppermute | solution.py:484
  97.0 9.7 %collective-permute-done.8.refs_2_ = bf16[4,64,512]{2,1,0:T(8,128)(2,1)S(1)} collective-permute-done((bf16[4,64,512]{2,1,0:T(8,128)(2,1)S(1)}, bf16[4,64,512]{2,1,0:T(8,128)(2,1)S(1)}, u32[]{:S(2)}, u32[]{:S(2)}) %collective-permute-start.8) | collective-permute-done | bytes 262176 | tf_op jit(solution)/shard_map/ppermute | solution.py:484
  106.7 4.6 %collective-permute-done.9.refs_3_ = bf16[4,64,512]{2,1,0:T(8,128)(2,1)S(1)} collective-permute-done((bf16[4,64,512]{2,1,0:T(8,128)(2,1)S(1)}, bf16[4,64,512]{2,1,0:T(8,128)(2,1)S(1)}, u32[]{:S(2)}, u32[]{:S(2)}) %collective-permute-start.9) | collective-permute-done | bytes 262176 | tf_op jit(solution)/shard_map/ppermute | solution.py:484
  111.4 3.0 %collective-permute-start.16 = (bf16[4,64,512]{2,1,0:T(8,128)(2,1)}, bf16[4,64,512]{2,1,0:T(8,128)(2,1)S(1)}, u32[]{:S(2)}, u32[]{:S(2)}) collective-permute-start(bf16[4,64,512]{2,1,0:T(8,128)(2,1)} %get-tuple-element.81), channel_id=1, source_target_pairs={{0,2},{1,3},{2,0},{3,1},{4,6},{5,7},{6,4},{7,5},{8,10},{9,11},{10,... | collective-permute-start | bytes 786440 | tf_op jit(solution)/shard_map/ppermute | solution.py:484
  114.9 17.9 %expert.2 = (bf16[64,2048]{1,0:T(8,128)(2,1)}, bf16[64,2048]{1,0:T(8,128)(2,1)}, bf16[64,2048]{1,0:T(8,128)(2,1)}, bf16[64,2048]{1,0:T(8,128)(2,1)}, bf16[64,204...) custom-call(s32[3]{0:T(128)} %pad_add_fusion.where_ref, ...), custom_call_target="tpu_custom_call" | custom-call | flops 1000 | bytes 1000 | tf_op jit(solution)/shard_map/expert/pallas_call | solution.py:403
  136.4 3.2 %collective-permute-done.17.refs_3_ = bf16[4,64,512]{2,1,0:T(8,128)(2,1)S(1)} collective-permute-done((bf16[4,64,512]{2,1,0:T(8,128)(2,1)}, bf16[4,64,512]{2,1,0:T(8,128)(2,1)S(1)}, u32[]{:S(2)}, u32[]{:S(2)}) %collective-permute-start.17) | collective-permute-done | bytes 262176 | tf_op jit(solution)/shard_map/ppermute | solution.py:484
  140.3 18.2 %expert.3 = (bf16[64,4096]{1,0:T(8,128)(2,1)}, bf16[64,4096]{1,0:T(8,128)(2,1)}, bf16[64,4096]{1,0:T(8,128)(2,1)}, bf16[64,4096]{1,0:T(8,128)(2,1)}, bf16[256,43...) custom-call(s32[3]{0:T(128)} %pad_add_fusion.where_ref, bf16[4,64,512]{2,1,0:T(8,128)(2,1)} %get-tuple-element.79.refs_0_, ...), custom_call_target="tpu_custom_call" | custom-call | flops 1000 | bytes 1000 | tf_op jit(solution)/shard_map/expert/pallas_call | solution.py:403
  158.7 4.3 %collective-permute-start.23 = (bf16[64,2048]{1,0:T(8,128)(2,1)}, bf16[64,2048]{1,0:T(8,128)(2,1)S(1)}, u32[]{:S(2)}, u32[]{:S(2)}) collective-permute-start(bf16[64,2048]{1,0:T(8,128)(2,1)} %get-tuple-element.98), channel_id=1, source_target_pairs={{0,2},{1,3},{2,0},{3,1},{4,6},{5,7},{6,4},{7,5},{8,10},{9,11},{10,... | collective-permute-start | bytes 786440 | tf_op jit(solution)/shard_map/ppermute | solution.py:484
  164.4 10.0 %weight_grads.1 = (bf16[4,3,128,768]{3,2,1,0:T(8,128)(2,1)}, bf16[4,3,128,768]{3,2,1,0:T(8,128)(2,1)}) custom-call(bf16[256,4352]{1,0:T(8,128)(2,1)} %get-tuple-element.73.refs_0_.refs_4_.refs_8_.refs_12_.refs_16_, bf16[256,4352]{1,0:T(8,128)(2,1)} %copy-done, bf16[256,4352]{1,0:T(8,128)(2,1)} %get-tuple-element.83.refs_2_.refs_6_.refs_10_.refs_14_.refs_18_, ...), custom_call_target="tpu_custom_call" | custom-call | flops 1000 | bytes 1000 | tf_op jit(solution)/shard_map/weight_grads/pallas_call | solution.py:465
  174.5 6.7 %collective-permute-done.23.refs_6_ = bf16[64,2048]{1,0:T(8,128)(2,1)S(1)} collective-permute-done((bf16[64,2048]{1,0:T(8,128)(2,1)}, bf16[64,2048]{1,0:T(8,128)(2,1)S(1)}, u32[]{:S(2)}, u32[]{:S(2)}) %collective-permute-start.23) | collective-permute-done | bytes 262176 | tf_op jit(solution)/shard_map/ppermute | solution.py:484
  181.2 4.8 %collective-permute-done.24.refs_7_ = bf16[64,2048]{1,0:T(8,128)(2,1)S(1)} collective-permute-done((bf16[64,2048]{1,0:T(8,128)(2,1)}, bf16[64,2048]{1,0:T(8,128)(2,1)S(1)}, u32[]{:S(2)}, u32[]{:S(2)}) %collective-permute-start.24) | collective-permute-done | bytes 262176 | tf_op jit(solution)/shard_map/ppermute | solution.py:484
  188.9 3.8 %collective-permute-start.30 = (bf16[64,4096]{1,0:T(8,128)(2,1)}, bf16[64,4096]{1,0:T(8,128)(2,1)S(1)}, u32[]{:S(2)}, u32[]{:S(2)}) collective-permute-start(bf16[64,4096]{1,0:T(8,128)(2,1)} %get-tuple-element.105), channel_id=1, source_target_pairs={{0,2},{1,3},{2,0},{3,1},{4,6},{5,7},{6,4},{7,5},{8,10},{9,11},{10,... | collective-permute-start | bytes 1572872 | tf_op jit(solution)/shard_map/ppermute | solution.py:484
  192.7 22.1 %collective-permute-done.27 = bf16[2,3,128,768]{3,2,1,0:T(8,128)(2,1)S(1)} collective-permute-done((bf16[2,3,128,768]{3,2,1,0:T(8,128)(2,1)S(1)}, bf16[2,3,128,768]{3,2,1,0:T(8,128)(2,1)S(1)}, u32[]{:S(2)}, u32[]{:S(2)}) %collective-permute-start.27) | collective-permute-done | bytes 1179680 | tf_op jit(solution)/shard_map/ppermute | solution.py:479
  217.9 10.0 %collective-permute-done.30.refs_10_ = bf16[64,4096]{1,0:T(8,128)(2,1)S(1)} collective-permute-done((bf16[64,4096]{1,0:T(8,128)(2,1)}, bf16[64,4096]{1,0:T(8,128)(2,1)S(1)}, u32[]{:S(2)}, u32[]{:S(2)}) %collective-permute-start.30) | collective-permute-done | bytes 524320 | tf_op jit(solution)/shard_map/ppermute | solution.py:484
  227.9 8.7 %collective-permute-done.31.refs_11_ = bf16[64,4096]{1,0:T(8,128)(2,1)S(1)} collective-permute-done((bf16[64,4096]{1,0:T(8,128)(2,1)}, bf16[64,4096]{1,0:T(8,128)(2,1)S(1)}, u32[]{:S(2)}, u32[]{:S(2)}) %collective-permute-start.31) | collective-permute-done | bytes 524320 | tf_op jit(solution)/shard_map/ppermute | solution.py:484
  240.2 6.0 %restore.1 = (bf16[256,2048]{1,0:T(8,128)(2,1)}, bf16[256,2048]{1,0:T(8,128)(2,1)}) custom-call(s32[3]{0:T(128)} %pad_add_fusion.where_ref, f32[256,1]{1,0:T(8,128)} %convert_element_type.57.ids_ref, bf16[64,2048]{1,0:T(8,128)(2,1)} %get-tuple-element.85.refs_0_, bf16[64,2048]{1,0:T(8,128)(2,1)} %copy-done.24, bf16[64,2048]{1,0:T(8,128)(2,1)} %copy-done.25, ...), custom_call_target="tpu_custom_call" | custom-call | flops 1000 | bytes 1000 | tf_op jit(solution)/shard_map/restore/pallas_call | solution.py:247
  (148 shorter events, 35.8 us)
Async XLA Ops:
  2.4 24.6 %collective-permute-start.4 = (bf16[4,256,256]{2,1,0:T(8,128)(2,1)S(1)}, bf16[4,256,256]{2,1,0:T(8,128)(2,1)S(1)}, u32[]{:S(2)}, u32[]{:S(2)}) collective-permute-start(bf16[4,256,256]{2,1,0:T(8,128)(2,1)S(1)} %get-tuple-element.117.refs_4_), channel_id=1, source_target_pairs={{0,16},{4,20},{8,24},{12,28},{16,0},{20,4},{24,8},{28,12},{1,17},{... | collective-permute-start | bytes 1572872 | tf_op jit(solution)/shard_map/ppermute | solution.py:479
  3.9 23.1 %collective-permute-start.3 = (bf16[4,256,256]{2,1,0:T(8,128)(2,1)S(1)}, bf16[4,256,256]{2,1,0:T(8,128)(2,1)S(1)}, u32[]{:S(2)}, u32[]{:S(2)}) collective-permute-start(bf16[4,256,256]{2,1,0:T(8,128)(2,1)S(1)} %get-tuple-element.117.refs_4_), channel_id=1, source_target_pairs={{0,8},{4,12},{8,0},{12,4},{16,24},{20,28},{24,16},{28,20},{1,9},{5... | collective-permute-start | bytes 1572872 | tf_op jit(solution)/shard_map/ppermute | solution.py:479
  6.8 21.9 %collective-permute-start.2 = (bf16[528,256]{1,0:T(8,128)(2,1)S(1)}, bf16[528,256]{1,0:T(8,128)(2,1)S(1)}, u32[]{:S(2)}, u32[]{:S(2)}) collective-permute-start(bf16[528,256]{1,0:T(8,128)(2,1)S(1)} %pad_maximum_fusion.5.refs_0_.refs_15_), channel_id=1, source_target_pairs={{0,3},{1,2},{2,1},{3,0},{4,7},{5,6},{6,5},{7,4},{8,11},{9,10},{10,... | collective-permute-start | bytes 811016 | tf_op jit(solution)/shard_map/ppermute | solution.py:484
  7.3 22.3 %collective-permute-start.1 = (bf16[528,256]{1,0:T(8,128)(2,1)S(1)}, bf16[528,256]{1,0:T(8,128)(2,1)S(1)}, u32[]{:S(2)}, u32[]{:S(2)}) collective-permute-start(bf16[528,256]{1,0:T(8,128)(2,1)S(1)} %pad_maximum_fusion.5.refs_0_.refs_15_), channel_id=1, source_target_pairs={{0,2},{1,3},{2,0},{3,1},{4,6},{5,7},{6,4},{7,5},{8,10},{9,11},{10,... | collective-permute-start | bytes 811016 | tf_op jit(solution)/shard_map/ppermute | solution.py:484
  29.8 37.0 %collective-permute-start.12 = (bf16[3,528,256]{2,1,0:T(8,128)(2,1)S(1)}, bf16[3,528,256]{2,1,0:T(8,128)(2,1)}, u32[]{:S(2)}, u32[]{:S(2)}) collective-permute-start(bf16[3,528,256]{2,1,0:T(8,128)(2,1)S(1)} %pad_maximum_fusion.2.refs_6_), channel_id=1, source_target_pairs={{0,24},{4,28},{8,16},{12,20},{16,8},{20,12},{24,0},{28,4},{1,25},{... | collective-permute-start | bytes 2433032 | tf_op jit(solution)/shard_map/ppermute | solution.py:479
  30.4 37.6 %collective-permute-start.11 = (bf16[3,528,256]{2,1,0:T(8,128)(2,1)S(1)}, bf16[3,528,256]{2,1,0:T(8,128)(2,1)}, u32[]{:S(2)}, u32[]{:S(2)}) collective-permute-start(bf16[3,528,256]{2,1,0:T(8,128)(2,1)S(1)} %pad_maximum_fusion.2.refs_6_), channel_id=1, source_target_pairs={{0,16},{4,20},{8,24},{12,28},{16,0},{20,4},{24,8},{28,12},{1,17},{... | collective-permute-start | bytes 2433032 | tf_op jit(solution)/shard_map/ppermute | solution.py:479
  31.8 36.2 %collective-permute-start.10 = (bf16[3,528,256]{2,1,0:T(8,128)(2,1)S(1)}, bf16[3,528,256]{2,1,0:T(8,128)(2,1)}, u32[]{:S(2)}, u32[]{:S(2)}) collective-permute-start(bf16[3,528,256]{2,1,0:T(8,128)(2,1)S(1)} %pad_maximum_fusion.2.refs_6_), channel_id=1, source_target_pairs={{0,8},{4,12},{8,0},{12,4},{16,24},{20,28},{24,16},{28,20},{1,9},{5... | collective-permute-start | bytes 2433032 | tf_op jit(solution)/shard_map/ppermute | solution.py:479
  33.3 52.0 %all-to-all-start = ((bf16[4,128,2048]{2,1,0:T(8,128)(2,1)}), bf16[4,128,2048]{2,1,0:T(8,128)(2,1)S(1)}, u32[]{:S(2)}, u32[]{:S(2)}) async-start(bf16[4,128,2048]{2,1,0:T(8,128)(2,1)} %place.1), calls=%async_computation | async-start | bytes 4194304 | tf_op jit(solution)/shard_map/all_to_all | solution.py:556
  71.2 43.6 %collective-permute-start.13 = (bf16[4,3,528,256]{3,2,1,0:T(8,128)(2,1)}, bf16[4,3,528,256]{3,2,1,0:T(8,128)(2,1)}, u32[]{:S(2)}, u32[]{:S(2)}) collective-permute-start(bf16[4,3,528,256]{3,2,1,0:T(8,128)(2,1)} %pad_maximum_fusion), channel_id=1, source_target_pairs={{0,4},{4,0},{8,12},{12,8},{16,20},{20,16},{24,28},{28,24},{1,5},{5... | collective-permute-start | bytes 9732104 | tf_op jit(solution)/shard_map/ppermute | solution.py:479
  88.7 22.6 %collective-permute-start.9 = (bf16[4,64,512]{2,1,0:T(8,128)(2,1)S(1)}, bf16[4,64,512]{2,1,0:T(8,128)(2,1)S(1)}, u32[]{:S(2)}, u32[]{:S(2)}) collective-permute-start(bf16[4,64,512]{2,1,0:T(8,128)(2,1)S(1)} %copy-done.33), channel_id=1, source_target_pairs={{0,3},{1,2},{2,1},{3,0},{4,7},{5,6},{6,5},{7,4},{8,11},{9,10},{10,... | collective-permute-start | bytes 786440 | tf_op jit(solution)/shard_map/ppermute | solution.py:484
  111.4 24.5 %collective-permute-start.15 = (bf16[4,64,512]{2,1,0:T(8,128)(2,1)}, bf16[4,64,512]{2,1,0:T(8,128)(2,1)S(1)}, u32[]{:S(2)}, u32[]{:S(2)}) collective-permute-start(bf16[4,64,512]{2,1,0:T(8,128)(2,1)} %get-tuple-element.80), channel_id=1, source_target_pairs={{0,1},{1,0},{2,3},{3,2},{4,5},{5,4},{6,7},{7,6},{8,9},{9,8},{10,11... | collective-permute-start | bytes 786440 | tf_op jit(solution)/shard_map/ppermute | solution.py:484
  111.4 25.0 %collective-permute-start.16 = (bf16[4,64,512]{2,1,0:T(8,128)(2,1)}, bf16[4,64,512]{2,1,0:T(8,128)(2,1)S(1)}, u32[]{:S(2)}, u32[]{:S(2)}) collective-permute-start(bf16[4,64,512]{2,1,0:T(8,128)(2,1)} %get-tuple-element.81), channel_id=1, source_target_pairs={{0,2},{1,3},{2,0},{3,1},{4,6},{5,7},{6,4},{7,5},{8,10},{9,11},{10,... | collective-permute-start | bytes 786440 | tf_op jit(solution)/shard_map/ppermute | solution.py:484
  114.3 25.2 %collective-permute-start.17 = (bf16[4,64,512]{2,1,0:T(8,128)(2,1)}, bf16[4,64,512]{2,1,0:T(8,128)(2,1)S(1)}, u32[]{:S(2)}, u32[]{:S(2)}) collective-permute-start(bf16[4,64,512]{2,1,0:T(8,128)(2,1)} %get-tuple-element.82), channel_id=1, source_target_pairs={{0,3},{1,2},{2,1},{3,0},{4,7},{5,6},{6,5},{7,4},{8,11},{9,10},{10,... | collective-permute-start | bytes 786440 | tf_op jit(solution)/shard_map/ppermute | solution.py:484
  132.8 25.7 %collective-permute-start.18 = (bf16[64,2048]{1,0:T(8,128)(2,1)}, bf16[64,2048]{1,0:T(8,128)(2,1)S(1)}, u32[]{:S(2)}, u32[]{:S(2)}) collective-permute-start(bf16[64,2048]{1,0:T(8,128)(2,1)} %get-tuple-element.86), channel_id=1, source_target_pairs={{0,1},{1,0},{2,3},{3,2},{4,5},{5,4},{6,7},{7,6},{8,9},{9,8},{10,11... | collective-permute-start | bytes 786440 | tf_op jit(solution)/shard_map/ppermute | solution.py:484
  133.8 24.7 %collective-permute-start.19 = (bf16[64,2048]{1,0:T(8,128)(2,1)}, bf16[64,2048]{1,0:T(8,128)(2,1)S(1)}, u32[]{:S(2)}, u32[]{:S(2)}) collective-permute-start(bf16[64,2048]{1,0:T(8,128)(2,1)} %get-tuple-element.87), channel_id=1, source_target_pairs={{0,2},{1,3},{2,0},{3,1},{4,6},{5,7},{6,4},{7,5},{8,10},{9,11},{10,... | collective-permute-start | bytes 786440 | tf_op jit(solution)/shard_map/ppermute | solution.py:484
  135.9 22.7 %collective-permute-start.20 = (bf16[64,2048]{1,0:T(8,128)(2,1)}, bf16[64,2048]{1,0:T(8,128)(2,1)S(1)}, u32[]{:S(2)}, u32[]{:S(2)}) collective-permute-start(bf16[64,2048]{1,0:T(8,128)(2,1)} %get-tuple-element.88), channel_id=1, source_target_pairs={{0,3},{1,2},{2,1},{3,0},{4,7},{5,6},{6,5},{7,4},{8,11},{9,10},{10,... | collective-permute-start | bytes 786440 | tf_op jit(solution)/shard_map/ppermute | solution.py:484
  136.4 26.6 %collective-permute-start.14 = (bf16[256,4352]{1,0:T(8,128)(2,1)}, bf16[256,4352]{1,0:T(8,128)(2,1)S(1)}, u32[]{:S(2)}, u32[]{:S(2)}) collective-permute-start(bf16[256,4352]{1,0:T(8,128)(2,1)} %get-tuple-element.74), channel_id=1, source_target_pairs={{0,4},{4,0},{8,12},{12,8},{16,20},{20,16},{24,28},{28,24},{1,5},{5... | collective-permute-start | bytes 6684680 | tf_op jit(solution)/shard_map/ppermute | solution.py:479
  158.7 22.5 %collective-permute-start.23 = (bf16[64,2048]{1,0:T(8,128)(2,1)}, bf16[64,2048]{1,0:T(8,128)(2,1)S(1)}, u32[]{:S(2)}, u32[]{:S(2)}) collective-permute-start(bf16[64,2048]{1,0:T(8,128)(2,1)} %get-tuple-element.98), channel_id=1, source_target_pairs={{0,2},{1,3},{2,0},{3,1},{4,6},{5,7},{6,4},{7,5},{8,10},{9,11},{10,... | collective-permute-start | bytes 786440 | tf_op jit(solution)/shard_map/ppermute | solution.py:484
  163.0 23.1 %collective-permute-start.24 = (bf16[64,2048]{1,0:T(8,128)(2,1)}, bf16[64,2048]{1,0:T(8,128)(2,1)S(1)}, u32[]{:S(2)}, u32[]{:S(2)}) collective-permute-start(bf16[64,2048]{1,0:T(8,128)(2,1)} %get-tuple-element.99), channel_id=1, source_target_pairs={{0,3},{1,2},{2,1},{3,0},{4,7},{5,6},{6,5},{7,4},{8,11},{9,10},{10,... | collective-permute-start | bytes 786440 | tf_op jit(solution)/shard_map/ppermute | solution.py:484
  187.6 27.3 %collective-permute-start.27 = (bf16[2,3,128,768]{3,2,1,0:T(8,128)(2,1)S(1)}, bf16[2,3,128,768]{3,2,1,0:T(8,128)(2,1)S(1)}, u32[]{:S(2)}, u32[]{:S(2)}) collective-permute-start(bf16[2,3,128,768]{3,2,1,0:T(8,128)(2,1)S(1)} %slice.40), channel_id=1, source_target_pairs={{0,16},{4,20},{8,24},{12,28},{16,0},{20,4},{24,8},{28,12},{1,17},{... | collective-permute-start | bytes 3538952 | tf_op jit(solution)/shard_map/ppermute | solution.py:479
  188.3 27.6 %collective-permute-start.25 = (bf16[2,3,128,768]{3,2,1,0:T(8,128)(2,1)S(1)}, bf16[2,3,128,768]{3,2,1,0:T(8,128)(2,1)S(1)}, u32[]{:S(2)}, u32[]{:S(2)}) collective-permute-start(bf16[2,3,128,768]{3,2,1,0:T(8,128)(2,1)S(1)} %slice.36), channel_id=1, source_target_pairs={{0,8},{4,12},{8,0},{12,4},{16,24},{20,28},{24,16},{28,20},{1,9},{5... | collective-permute-start | bytes 3538952 | tf_op jit(solution)/shard_map/ppermute | solution.py:479
  188.9 29.0 %collective-permute-start.29 = (bf16[64,4096]{1,0:T(8,128)(2,1)}, bf16[64,4096]{1,0:T(8,128)(2,1)S(1)}, u32[]{:S(2)}, u32[]{:S(2)}) collective-permute-start(bf16[64,4096]{1,0:T(8,128)(2,1)} %get-tuple-element.104), channel_id=1, source_target_pairs={{0,1},{1,0},{2,3},{3,2},{4,5},{5,4},{6,7},{7,6},{8,9},{9,8},{10,11... | collective-permute-start | bytes 1572872 | tf_op jit(solution)/shard_map/ppermute | solution.py:484
  188.9 39.0 %collective-permute-start.30 = (bf16[64,4096]{1,0:T(8,128)(2,1)}, bf16[64,4096]{1,0:T(8,128)(2,1)S(1)}, u32[]{:S(2)}, u32[]{:S(2)}) collective-permute-start(bf16[64,4096]{1,0:T(8,128)(2,1)} %get-tuple-element.105), channel_id=1, source_target_pairs={{0,2},{1,3},{2,0},{3,1},{4,6},{5,7},{6,4},{7,5},{8,10},{9,11},{10,... | collective-permute-start | bytes 1572872 | tf_op jit(solution)/shard_map/ppermute | solution.py:484
  192.7 43.9 %collective-permute-start.31 = (bf16[64,4096]{1,0:T(8,128)(2,1)}, bf16[64,4096]{1,0:T(8,128)(2,1)S(1)}, u32[]{:S(2)}, u32[]{:S(2)}) collective-permute-start(bf16[64,4096]{1,0:T(8,128)(2,1)} %get-tuple-element.106), channel_id=1, source_target_pairs={{0,3},{1,2},{2,1},{3,0},{4,7},{5,6},{6,5},{7,4},{8,11},{9,10},{10,... | collective-permute-start | bytes 1572872 | tf_op jit(solution)/shard_map/ppermute | solution.py:484
  (44 other events, 515.6 us)

commit v11 on v10

--- a/solution.py
+++ b/solution.py
@@ -561,7 +561,7 @@
     sent = attend(where, queries, key_values, routes, n, capacity)
     arrived = to_owners(after(sent[0], grads))
     later = after(sent[1], arrived, same)
-    same = after(same, sent[0])
+    same = after(same, sent[0], grads)
     other = partner(jnp.stack(same), 1)
 
     rows_dev = width // ctx_count

time: 251 us -> 291 us (1.16)
  waiting for transfers between devices: 106 us -> 151 us
  starting transfers between devices: 41.8 us -> 38.4 us
    ppermute x18, waiting for transfers between devices: 56.5 us -> 112 us  [to_owner(): return lax.ppermute(value, 'exp', [(i, i ^ mask) for i in range(count)])]
    all_to_all x1, waiting for transfers between devices: 14.1 us -> 0.01 us  [on_device(): grads = lax.all_to_all(grads, 'exp', 0, 0, tiled=True)]
    ppermute x14, waiting for transfers between devices: 35.1 us -> 38.8 us  [partner(): return lax.ppermute(value, 'ctx', [(i, i ^ mask) for i in range(count)])]
  transfers between devices with their start and end apart: 33 -> 33, of which waited for: 15 -> 15; matrix products, arithmetic and copies ran while one was open for 3% -> 2% of each run, Pallas kernels for 30% -> 26%
where the time goes in v11:
time: 291 us; the launch traced here: 288 us
  waiting for transfers between devices  151 us (52%)
  Pallas kernels  80.8 us (28%)
  starting transfers between devices  38.4 us (13%)
  other arithmetic  9.45 us (3%)
  local copies, waits for them, and re-layouts  6.81 us (2%)
    ppermute x18, waiting for transfers between devices, to_owner(): return lax.ppermute(value, 'exp', [(i, i ^ mask) for i in range(count)])  112 us
    ppermute x14, waiting for transfers between devices, partner(): return lax.ppermute(value, 'ctx', [(i, i ^ mask) for i in range(count)])  38.8 us
    pallas_call x2, Pallas kernels, expert_part(): pl.pallas_call(functools.partial(expert_kernel, pieces, experts, capacity...  36.1 us
    pallas_call x1, Pallas kernels, attend(): pl.pallas_call(functools.partial(attend_kernel, experts, capacity, heads,...  25.5 us
    ppermute x18, starting transfers between devices, to_owner(): return lax.ppermute(value, 'exp', [(i, i ^ mask) for i in range(count)])  22.1 us
    ppermute x14, starting transfers between devices, partner(): return lax.ppermute(value, 'ctx', [(i, i ^ mask) for i in range(count)])  11 us
    pallas_call x1, Pallas kernels, weight_blocks(): pl.pallas_call(functools.partial(weight_kernel, count), grid=(blocks,), i...  10 us
    pallas_call x1, Pallas kernels, restore(): pl.pallas_call(functools.partial(restore_kernel, experts, capacity, tiles...  5.96 us
  transfers between devices with their start and end apart: 33, of which 15 were waited for; matrix products, arithmetic and copies ran while one was open for 2% of the time, Pallas kernels for 26%

profile of v11, /device:TPU:22, one launch (start us, length us, event | category | flops | bytes accessed | tf_op | source)
XLA Modules:
  0.0 288.1 jit_solution(73382956111351299)
XLA Ops:
  6.9 3.2 %place.1 = bf16[4,128,2048]{2,1,0:T(8,128)(2,1)} custom-call(f32[1,256]{1,0:T(1,128)} %bitcast.43, bf16[256,2048]{1,0:T(8,128)(2,1)} %rows_ref.1), custom_call_target="tpu_custom_call" | custom-call | flops 1000 | bytes 1000 | tf_op jit(solution)/shard_map/place/pallas_call | solution.py:202
  10.1 5.3 %all-to-all-start = ((bf16[4,128,2048]{2,1,0:T(8,128)(2,1)}), bf16[4,128,2048]{2,1,0:T(8,128)(2,1)S(1)}, u32[]{:S(2)}, u32[]{:S(2)}) async-start(bf16[4,128,2048]{2,1,0:T(8,128)(2,1)} %place.1), calls=%async_computation | async-start | bytes 4194304 | tf_op jit(solution)/shard_map/all_to_all | solution.py:556
  17.3 3.3 %collective-permute-start.1 = (bf16[528,256]{1,0:T(8,128)(2,1)S(1)}, bf16[528,256]{1,0:T(8,128)(2,1)S(1)}, u32[]{:S(2)}, u32[]{:S(2)}) collective-permute-start(bf16[528,256]{1,0:T(8,128)(2,1)S(1)} %pad_maximum_fusion.5.refs_0_.refs_15_), channel_id=1, source_target_pairs={{0,2},{1,3},{2,0},{3,1},{4,6},{5,7},{6,4},{7,5},{8,10},{9,11},{10,... | collective-permute-start | bytes 811016 | tf_op jit(solution)/shard_map/ppermute | solution.py:484
  20.5 7.3 %collective-permute-done.4.refs_6_ = bf16[4,256,256]{2,1,0:T(8,128)(2,1)} collective-permute-done((bf16[4,256,256]{2,1,0:T(8,128)(2,1)S(1)}, bf16[4,256,256]{2,1,0:T(8,128)(2,1)}, u32[]{:S(2)}, u32[]{:S(2)}) %collective-permute-start.4) | collective-permute-done | bytes 524320 | tf_op jit(solution)/shard_map/ppermute | solution.py:479
  29.4 50.7 %collective-permute-done.2.refs_3_.refs_18_ = bf16[528,256]{1,0:T(8,128)(2,1)S(1)} collective-permute-done((bf16[528,256]{1,0:T(8,128)(2,1)S(1)}, bf16[528,256]{1,0:T(8,128)(2,1)S(1)}, u32[]{:S(2)}, u32[]{:S(2)}) %collective-permute-start.2) | collective-permute-done | bytes 270368 | tf_op jit(solution)/shard_map/ppermute | solution.py:484
  87.0 25.5 %attend.1 = (bf16[4,64,512]{2,1,0:T(8,128)(2,1)}, bf16[4,64,512]{2,1,0:T(8,128)(2,1)}, bf16[4,64,512]{2,1,0:T(8,128)(2,1)}, bf16[4,64,512]{2,1,0:T(8,128)(2,1)},...) custom-call(s32[3]{0:T(128)} %pad_add_fusion.where_ref, ...), custom_call_target="tpu_custom_call" | custom-call | flops 1000 | bytes 1000 | tf_op jit(solution)/shard_map/attend/pallas_call | solution.py:163
  112.5 8.5 %collective-permute-done.11.refs_8_ = bf16[3,528,256]{2,1,0:T(8,128)(2,1)} collective-permute-done((bf16[3,528,256]{2,1,0:T(8,128)(2,1)S(1)}, bf16[3,528,256]{2,1,0:T(8,128)(2,1)}, u32[]{:S(2)}, u32[]{:S(2)}) %collective-permute-start.11) | collective-permute-done | bytes 811040 | tf_op jit(solution)/shard_map/ppermute | solution.py:479
  121.1 2.8 pad_maximum_fusion
  128.2 9.8 %collective-permute-done.7.refs_1_ = bf16[4,64,512]{2,1,0:T(8,128)(2,1)S(1)} collective-permute-done((bf16[4,64,512]{2,1,0:T(8,128)(2,1)S(1)}, bf16[4,64,512]{2,1,0:T(8,128)(2,1)S(1)}, u32[]{:S(2)}, u32[]{:S(2)}) %collective-permute-start.7) | collective-permute-done | bytes 262176 | tf_op jit(solution)/shard_map/ppermute | solution.py:484
  138.0 7.5 %collective-permute-done.8.refs_2_ = bf16[4,64,512]{2,1,0:T(8,128)(2,1)S(1)} collective-permute-done((bf16[4,64,512]{2,1,0:T(8,128)(2,1)S(1)}, bf16[4,64,512]{2,1,0:T(8,128)(2,1)S(1)}, u32[]{:S(2)}, u32[]{:S(2)}) %collective-permute-start.8) | collective-permute-done | bytes 262176 | tf_op jit(solution)/shard_map/ppermute | solution.py:484
  145.5 6.2 %collective-permute-done.9.refs_3_ = bf16[4,64,512]{2,1,0:T(8,128)(2,1)S(1)} collective-permute-done((bf16[4,64,512]{2,1,0:T(8,128)(2,1)S(1)}, bf16[4,64,512]{2,1,0:T(8,128)(2,1)S(1)}, u32[]{:S(2)}, u32[]{:S(2)}) %collective-permute-start.9) | collective-permute-done | bytes 262176 | tf_op jit(solution)/shard_map/ppermute | solution.py:484
  151.7 2.9 %collective-permute-start.16 = (bf16[4,64,512]{2,1,0:T(8,128)(2,1)S(1)}, bf16[4,64,512]{2,1,0:T(8,128)(2,1)S(1)}, u32[]{:S(2)}, u32[]{:S(2)}) collective-permute-start(bf16[4,64,512]{2,1,0:T(8,128)(2,1)S(1)} %copy-done.29), channel_id=1, source_target_pairs={{0,2},{1,3},{2,0},{3,1},{4,6},{5,7},{6,4},{7,5},{8,10},{9,11},{10,... | collective-permute-start | bytes 786440 | tf_op jit(solution)/shard_map/ppermute | solution.py:484
  155.2 17.9 %expert.2 = (bf16[64,2048]{1,0:T(8,128)(2,1)}, bf16[64,2048]{1,0:T(8,128)(2,1)}, bf16[64,2048]{1,0:T(8,128)(2,1)}, bf16[64,2048]{1,0:T(8,128)(2,1)}, bf16[64,204...) custom-call(s32[3]{0:T(128)} %pad_add_fusion.where_ref, ...), custom_call_target="tpu_custom_call" | custom-call | flops 1000 | bytes 1000 | tf_op jit(solution)/shard_map/expert/pallas_call | solution.py:403
  176.7 2.7 collective-permute-done.17.refs_3_
  180.1 18.2 %expert.3 = (bf16[64,4096]{1,0:T(8,128)(2,1)}, bf16[64,4096]{1,0:T(8,128)(2,1)}, bf16[64,4096]{1,0:T(8,128)(2,1)}, bf16[64,4096]{1,0:T(8,128)(2,1)}, bf16[256,43...) custom-call(s32[3]{0:T(128)} %pad_add_fusion.where_ref, bf16[4,64,512]{2,1,0:T(8,128)(2,1)} %get-tuple-element.79.refs_0_, ...), custom_call_target="tpu_custom_call" | custom-call | flops 1000 | bytes 1000 | tf_op jit(solution)/shard_map/expert/pallas_call | solution.py:403
  200.1 2.9 %collective-permute-start.23 = (bf16[64,2048]{1,0:T(8,128)(2,1)}, bf16[64,2048]{1,0:T(8,128)(2,1)S(1)}, u32[]{:S(2)}, u32[]{:S(2)}) collective-permute-start(bf16[64,2048]{1,0:T(8,128)(2,1)} %get-tuple-element.98), channel_id=1, source_target_pairs={{0,2},{1,3},{2,0},{3,1},{4,6},{5,7},{6,4},{7,5},{8,10},{9,11},{10,... | collective-permute-start | bytes 786440 | tf_op jit(solution)/shard_map/ppermute | solution.py:484
  204.9 10.0 %weight_grads.1 = (bf16[4,3,128,768]{3,2,1,0:T(8,128)(2,1)}, bf16[4,3,128,768]{3,2,1,0:T(8,128)(2,1)}) custom-call(bf16[256,4352]{1,0:T(8,128)(2,1)} %get-tuple-element.73.refs_0_.refs_4_.refs_8_.refs_12_.refs_16_, bf16[256,4352]{1,0:T(8,128)(2,1)} %copy-done, bf16[256,4352]{1,0:T(8,128)(2,1)} %get-tuple-element.83.refs_2_.refs_6_.refs_10_.refs_14_.refs_18_, ...), custom_call_target="tpu_custom_call" | custom-call | flops 1000 | bytes 1000 | tf_op jit(solution)/shard_map/weight_grads/pallas_call | solution.py:465
  215.0 6.3 %collective-permute-done.23.refs_6_ = bf16[64,2048]{1,0:T(8,128)(2,1)S(1)} collective-permute-done((bf16[64,2048]{1,0:T(8,128)(2,1)}, bf16[64,2048]{1,0:T(8,128)(2,1)S(1)}, u32[]{:S(2)}, u32[]{:S(2)}) %collective-permute-start.23) | collective-permute-done | bytes 262176 | tf_op jit(solution)/shard_map/ppermute | solution.py:484
  221.3 5.8 %collective-permute-done.24.refs_7_ = bf16[64,2048]{1,0:T(8,128)(2,1)S(1)} collective-permute-done((bf16[64,2048]{1,0:T(8,128)(2,1)}, bf16[64,2048]{1,0:T(8,128)(2,1)S(1)}, u32[]{:S(2)}, u32[]{:S(2)}) %collective-permute-start.24) | collective-permute-done | bytes 262176 | tf_op jit(solution)/shard_map/ppermute | solution.py:484
  230.7 2.9 %collective-permute-start.30 = (bf16[64,4096]{1,0:T(8,128)(2,1)}, bf16[64,4096]{1,0:T(8,128)(2,1)S(1)}, u32[]{:S(2)}, u32[]{:S(2)}) collective-permute-start(bf16[64,4096]{1,0:T(8,128)(2,1)} %get-tuple-element.105), channel_id=1, source_target_pairs={{0,2},{1,3},{2,0},{3,1},{4,6},{5,7},{6,4},{7,5},{8,10},{9,11},{10,... | collective-permute-start | bytes 1572872 | tf_op jit(solution)/shard_map/ppermute | solution.py:484
  234.2 21.8 %collective-permute-done.27 = bf16[2,3,128,768]{3,2,1,0:T(8,128)(2,1)S(1)} collective-permute-done((bf16[2,3,128,768]{3,2,1,0:T(8,128)(2,1)S(1)}, bf16[2,3,128,768]{3,2,1,0:T(8,128)(2,1)S(1)}, u32[]{:S(2)}, u32[]{:S(2)}) %collective-permute-start.27) | collective-permute-done | bytes 1179680 | tf_op jit(solution)/shard_map/ppermute | solution.py:479
  259.3 9.5 %collective-permute-done.30.refs_10_ = bf16[64,4096]{1,0:T(8,128)(2,1)S(1)} collective-permute-done((bf16[64,4096]{1,0:T(8,128)(2,1)}, bf16[64,4096]{1,0:T(8,128)(2,1)S(1)}, u32[]{:S(2)}, u32[]{:S(2)}) %collective-permute-start.30) | collective-permute-done | bytes 524320 | tf_op jit(solution)/shard_map/ppermute | solution.py:484
  268.8 9.7 %collective-permute-done.31.refs_11_ = bf16[64,4096]{1,0:T(8,128)(2,1)S(1)} collective-permute-done((bf16[64,4096]{1,0:T(8,128)(2,1)}, bf16[64,4096]{1,0:T(8,128)(2,1)S(1)}, u32[]{:S(2)}, u32[]{:S(2)}) %collective-permute-start.31) | collective-permute-done | bytes 524320 | tf_op jit(solution)/shard_map/ppermute | solution.py:484
  282.0 6.0 %restore.1 = (bf16[256,2048]{1,0:T(8,128)(2,1)}, bf16[256,2048]{1,0:T(8,128)(2,1)}) custom-call(s32[3]{0:T(128)} %pad_add_fusion.where_ref, f32[256,1]{1,0:T(8,128)} %convert_element_type.57.ids_ref, bf16[64,2048]{1,0:T(8,128)(2,1)} %get-tuple-element.85.refs_0_, bf16[64,2048]{1,0:T(8,128)(2,1)} %copy-done.20, bf16[64,2048]{1,0:T(8,128)(2,1)} %copy-done.21, ...), custom_call_target="tpu_custom_call" | custom-call | flops 1000 | bytes 1000 | tf_op jit(solution)/shard_map/restore/pallas_call | solution.py:247
  (146 shorter events, 39.9 us)
Async XLA Ops:
  3.1 24.7 %collective-permute-start.4 = (bf16[4,256,256]{2,1,0:T(8,128)(2,1)S(1)}, bf16[4,256,256]{2,1,0:T(8,128)(2,1)}, u32[]{:S(2)}, u32[]{:S(2)}) collective-permute-start(bf16[4,256,256]{2,1,0:T(8,128)(2,1)S(1)} %get-tuple-element.117.refs_4_), channel_id=1, source_target_pairs={{0,16},{4,20},{8,24},{12,28},{16,0},{20,4},{24,8},{28,12},{1,17},{... | collective-permute-start | bytes 1572872 | tf_op jit(solution)/shard_map/ppermute | solution.py:479
  4.6 23.2 %collective-permute-start.3 = (bf16[4,256,256]{2,1,0:T(8,128)(2,1)S(1)}, bf16[4,256,256]{2,1,0:T(8,128)(2,1)}, u32[]{:S(2)}, u32[]{:S(2)}) collective-permute-start(bf16[4,256,256]{2,1,0:T(8,128)(2,1)S(1)} %get-tuple-element.117.refs_4_), channel_id=1, source_target_pairs={{0,8},{4,12},{8,0},{12,4},{16,24},{20,28},{24,16},{28,20},{1,9},{5... | collective-permute-start | bytes 1572872 | tf_op jit(solution)/shard_map/ppermute | solution.py:479
  10.1 110.9 %all-to-all-start = ((bf16[4,128,2048]{2,1,0:T(8,128)(2,1)}), bf16[4,128,2048]{2,1,0:T(8,128)(2,1)S(1)}, u32[]{:S(2)}, u32[]{:S(2)}) async-start(bf16[4,128,2048]{2,1,0:T(8,128)(2,1)} %place.1), calls=%async_computation | async-start | bytes 4194304 | tf_op jit(solution)/shard_map/all_to_all | solution.py:556
  16.6 63.5 %collective-permute-start.2 = (bf16[528,256]{1,0:T(8,128)(2,1)S(1)}, bf16[528,256]{1,0:T(8,128)(2,1)S(1)}, u32[]{:S(2)}, u32[]{:S(2)}) collective-permute-start(bf16[528,256]{1,0:T(8,128)(2,1)S(1)} %pad_maximum_fusion.5.refs_0_.refs_15_), channel_id=1, source_target_pairs={{0,3},{1,2},{2,1},{3,0},{4,7},{5,6},{6,5},{7,4},{8,11},{9,10},{10,... | collective-permute-start | bytes 811016 | tf_op jit(solution)/shard_map/ppermute | solution.py:484
  17.3 65.4 %collective-permute-start.1 = (bf16[528,256]{1,0:T(8,128)(2,1)S(1)}, bf16[528,256]{1,0:T(8,128)(2,1)S(1)}, u32[]{:S(2)}, u32[]{:S(2)}) collective-permute-start(bf16[528,256]{1,0:T(8,128)(2,1)S(1)} %pad_maximum_fusion.5.refs_0_.refs_15_), channel_id=1, source_target_pairs={{0,2},{1,3},{2,0},{3,1},{4,6},{5,7},{6,4},{7,5},{8,10},{9,11},{10,... | collective-permute-start | bytes 811016 | tf_op jit(solution)/shard_map/ppermute | solution.py:484
  20.5 62.1 %collective-permute-start = (bf16[528,256]{1,0:T(8,128)(2,1)S(1)}, bf16[528,256]{1,0:T(8,128)(2,1)S(1)}, u32[]{:S(2)}, u32[]{:S(2)}) collective-permute-start(bf16[528,256]{1,0:T(8,128)(2,1)S(1)} %pad_maximum_fusion.5.refs_0_.refs_15_), channel_id=1, source_target_pairs={{0,1},{1,0},{2,3},{3,2},{4,5},{5,4},{6,7},{7,6},{8,9},{9,8},{10,11... | collective-permute-start | bytes 811016 | tf_op jit(solution)/shard_map/ppermute | solution.py:484
  82.8 29.7 %collective-permute-start.12 = (bf16[3,528,256]{2,1,0:T(8,128)(2,1)S(1)}, bf16[3,528,256]{2,1,0:T(8,128)(2,1)}, u32[]{:S(2)}, u32[]{:S(2)}) collective-permute-start(bf16[3,528,256]{2,1,0:T(8,128)(2,1)S(1)} %pad_maximum_fusion.2.refs_6_), channel_id=1, source_target_pairs={{0,24},{4,28},{8,16},{12,20},{16,8},{20,12},{24,0},{28,4},{1,25},{... | collective-permute-start | bytes 2433032 | tf_op jit(solution)/shard_map/ppermute | solution.py:479
  83.3 37.7 %collective-permute-start.11 = (bf16[3,528,256]{2,1,0:T(8,128)(2,1)S(1)}, bf16[3,528,256]{2,1,0:T(8,128)(2,1)}, u32[]{:S(2)}, u32[]{:S(2)}) collective-permute-start(bf16[3,528,256]{2,1,0:T(8,128)(2,1)S(1)} %pad_maximum_fusion.2.refs_6_), channel_id=1, source_target_pairs={{0,16},{4,20},{8,24},{12,28},{16,0},{20,4},{24,8},{28,12},{1,17},{... | collective-permute-start | bytes 2433032 | tf_op jit(solution)/shard_map/ppermute | solution.py:479
  84.8 36.1 %collective-permute-start.10 = (bf16[3,528,256]{2,1,0:T(8,128)(2,1)S(1)}, bf16[3,528,256]{2,1,0:T(8,128)(2,1)}, u32[]{:S(2)}, u32[]{:S(2)}) collective-permute-start(bf16[3,528,256]{2,1,0:T(8,128)(2,1)S(1)} %pad_maximum_fusion.2.refs_6_), channel_id=1, source_target_pairs={{0,8},{4,12},{8,0},{12,4},{16,24},{20,28},{24,16},{28,20},{1,9},{5... | collective-permute-start | bytes 2433032 | tf_op jit(solution)/shard_map/ppermute | solution.py:479
  123.9 31.3 %collective-permute-start.13 = (bf16[4,3,528,256]{3,2,1,0:T(8,128)(2,1)S(1)}, bf16[4,3,528,256]{3,2,1,0:T(8,128)(2,1)}, u32[]{:S(2)}, u32[]{:S(2)}) collective-permute-start(bf16[4,3,528,256]{3,2,1,0:T(8,128)(2,1)S(1)} %pad_maximum_fusion), channel_id=1, source_target_pairs={{0,4},{4,0},{8,12},{12,8},{16,20},{20,16},{24,28},{28,24},{1,5},{5... | collective-permute-start | bytes 9732104 | tf_op jit(solution)/shard_map/ppermute | solution.py:479
  127.6 24.1 %collective-permute-start.9 = (bf16[4,64,512]{2,1,0:T(8,128)(2,1)S(1)}, bf16[4,64,512]{2,1,0:T(8,128)(2,1)S(1)}, u32[]{:S(2)}, u32[]{:S(2)}) collective-permute-start(bf16[4,64,512]{2,1,0:T(8,128)(2,1)S(1)} %copy-done.31), channel_id=1, source_target_pairs={{0,3},{1,2},{2,1},{3,0},{4,7},{5,6},{6,5},{7,4},{8,11},{9,10},{10,... | collective-permute-start | bytes 786440 | tf_op jit(solution)/shard_map/ppermute | solution.py:484
  151.7 24.4 %collective-permute-start.15 = (bf16[4,64,512]{2,1,0:T(8,128)(2,1)S(1)}, bf16[4,64,512]{2,1,0:T(8,128)(2,1)S(1)}, u32[]{:S(2)}, u32[]{:S(2)}) collective-permute-start(bf16[4,64,512]{2,1,0:T(8,128)(2,1)S(1)} %copy-done.30), channel_id=1, source_target_pairs={{0,1},{1,0},{2,3},{3,2},{4,5},{5,4},{6,7},{7,6},{8,9},{9,8},{10,11... | collective-permute-start | bytes 786440 | tf_op jit(solution)/shard_map/ppermute | solution.py:484
  151.7 25.0 %collective-permute-start.16 = (bf16[4,64,512]{2,1,0:T(8,128)(2,1)S(1)}, bf16[4,64,512]{2,1,0:T(8,128)(2,1)S(1)}, u32[]{:S(2)}, u32[]{:S(2)}) collective-permute-start(bf16[4,64,512]{2,1,0:T(8,128)(2,1)S(1)} %copy-done.29), channel_id=1, source_target_pairs={{0,2},{1,3},{2,0},{3,1},{4,6},{5,7},{6,4},{7,5},{8,10},{9,11},{10,... | collective-permute-start | bytes 786440 | tf_op jit(solution)/shard_map/ppermute | solution.py:484
  154.6 24.8 %collective-permute-start.17 = (bf16[4,64,512]{2,1,0:T(8,128)(2,1)}, bf16[4,64,512]{2,1,0:T(8,128)(2,1)S(1)}, u32[]{:S(2)}, u32[]{:S(2)}) collective-permute-start(bf16[4,64,512]{2,1,0:T(8,128)(2,1)} %get-tuple-element.82), channel_id=1, source_target_pairs={{0,3},{1,2},{2,1},{3,0},{4,7},{5,6},{6,5},{7,4},{8,11},{9,10},{10,... | collective-permute-start | bytes 786440 | tf_op jit(solution)/shard_map/ppermute | solution.py:484
  173.1 25.2 %collective-permute-start.18 = (bf16[64,2048]{1,0:T(8,128)(2,1)}, bf16[64,2048]{1,0:T(8,128)(2,1)S(1)}, u32[]{:S(2)}, u32[]{:S(2)}) collective-permute-start(bf16[64,2048]{1,0:T(8,128)(2,1)} %get-tuple-element.86), channel_id=1, source_target_pairs={{0,1},{1,0},{2,3},{3,2},{4,5},{5,4},{6,7},{7,6},{8,9},{9,8},{10,11... | collective-permute-start | bytes 786440 | tf_op jit(solution)/shard_map/ppermute | solution.py:484
  174.2 24.2 %collective-permute-start.19 = (bf16[64,2048]{1,0:T(8,128)(2,1)}, bf16[64,2048]{1,0:T(8,128)(2,1)S(1)}, u32[]{:S(2)}, u32[]{:S(2)}) collective-permute-start(bf16[64,2048]{1,0:T(8,128)(2,1)} %get-tuple-element.87), channel_id=1, source_target_pairs={{0,2},{1,3},{2,0},{3,1},{4,6},{5,7},{6,4},{7,5},{8,10},{9,11},{10,... | collective-permute-start | bytes 786440 | tf_op jit(solution)/shard_map/ppermute | solution.py:484
  176.1 24.0 %collective-permute-start.20 = (bf16[64,2048]{1,0:T(8,128)(2,1)}, bf16[64,2048]{1,0:T(8,128)(2,1)S(1)}, u32[]{:S(2)}, u32[]{:S(2)}) collective-permute-start(bf16[64,2048]{1,0:T(8,128)(2,1)} %get-tuple-element.88), channel_id=1, source_target_pairs={{0,3},{1,2},{2,1},{3,0},{4,7},{5,6},{6,5},{7,4},{8,11},{9,10},{10,... | collective-permute-start | bytes 786440 | tf_op jit(solution)/shard_map/ppermute | solution.py:484
  176.7 26.9 %collective-permute-start.14 = (bf16[256,4352]{1,0:T(8,128)(2,1)}, bf16[256,4352]{1,0:T(8,128)(2,1)S(1)}, u32[]{:S(2)}, u32[]{:S(2)}) collective-permute-start(bf16[256,4352]{1,0:T(8,128)(2,1)} %get-tuple-element.74), channel_id=1, source_target_pairs={{0,4},{4,0},{8,12},{12,8},{16,20},{20,16},{24,28},{28,24},{1,5},{5... | collective-permute-start | bytes 6684680 | tf_op jit(solution)/shard_map/ppermute | solution.py:479
  203.0 24.1 %collective-permute-start.24 = (bf16[64,2048]{1,0:T(8,128)(2,1)}, bf16[64,2048]{1,0:T(8,128)(2,1)S(1)}, u32[]{:S(2)}, u32[]{:S(2)}) collective-permute-start(bf16[64,2048]{1,0:T(8,128)(2,1)} %get-tuple-element.99), channel_id=1, source_target_pairs={{0,3},{1,2},{2,1},{3,0},{4,7},{5,6},{6,5},{7,4},{8,11},{9,10},{10,... | collective-permute-start | bytes 786440 | tf_op jit(solution)/shard_map/ppermute | solution.py:484
  228.6 27.3 %collective-permute-start.27 = (bf16[2,3,128,768]{3,2,1,0:T(8,128)(2,1)S(1)}, bf16[2,3,128,768]{3,2,1,0:T(8,128)(2,1)S(1)}, u32[]{:S(2)}, u32[]{:S(2)}) collective-permute-start(bf16[2,3,128,768]{3,2,1,0:T(8,128)(2,1)S(1)} %slice.40), channel_id=1, source_target_pairs={{0,16},{4,20},{8,24},{12,28},{16,0},{20,4},{24,8},{28,12},{1,17},{... | collective-permute-start | bytes 3538952 | tf_op jit(solution)/shard_map/ppermute | solution.py:479
  230.1 27.5 %collective-permute-start.25 = (bf16[2,3,128,768]{3,2,1,0:T(8,128)(2,1)S(1)}, bf16[2,3,128,768]{3,2,1,0:T(8,128)(2,1)S(1)}, u32[]{:S(2)}, u32[]{:S(2)}) collective-permute-start(bf16[2,3,128,768]{3,2,1,0:T(8,128)(2,1)S(1)} %slice.36), channel_id=1, source_target_pairs={{0,8},{4,12},{8,0},{12,4},{16,24},{20,28},{24,16},{28,20},{1,9},{5... | collective-permute-start | bytes 3538952 | tf_op jit(solution)/shard_map/ppermute | solution.py:479
  230.7 28.6 %collective-permute-start.29 = (bf16[64,4096]{1,0:T(8,128)(2,1)}, bf16[64,4096]{1,0:T(8,128)(2,1)S(1)}, u32[]{:S(2)}, u32[]{:S(2)}) collective-permute-start(bf16[64,4096]{1,0:T(8,128)(2,1)} %get-tuple-element.104), channel_id=1, source_target_pairs={{0,1},{1,0},{2,3},{3,2},{4,5},{5,4},{6,7},{7,6},{8,9},{9,8},{10,11... | collective-permute-start | bytes 1572872 | tf_op jit(solution)/shard_map/ppermute | solution.py:484
  230.7 38.1 %collective-permute-start.30 = (bf16[64,4096]{1,0:T(8,128)(2,1)}, bf16[64,4096]{1,0:T(8,128)(2,1)S(1)}, u32[]{:S(2)}, u32[]{:S(2)}) collective-permute-start(bf16[64,4096]{1,0:T(8,128)(2,1)} %get-tuple-element.105), channel_id=1, source_target_pairs={{0,2},{1,3},{2,0},{3,1},{4,6},{5,7},{6,4},{7,5},{8,10},{9,11},{10,... | collective-permute-start | bytes 1572872 | tf_op jit(solution)/shard_map/ppermute | solution.py:484
  233.6 44.9 %collective-permute-start.31 = (bf16[64,4096]{1,0:T(8,128)(2,1)}, bf16[64,4096]{1,0:T(8,128)(2,1)S(1)}, u32[]{:S(2)}, u32[]{:S(2)}) collective-permute-start(bf16[64,4096]{1,0:T(8,128)(2,1)} %get-tuple-element.106), channel_id=1, source_target_pairs={{0,3},{1,2},{2,1},{3,0},{4,7},{5,6},{6,5},{7,4},{8,11},{9,10},{10,... | collective-permute-start | bytes 1572872 | tf_op jit(solution)/shard_map/ppermute | solution.py:484
  (43 other events, 611.0 us)
